TPU v7x, 32 devices: a whole 2x2x4 slice. The times are simulated.
32 devices in a mesh: seq: 8 (over y, x, core), mp: 4 (over z).
Axes of the slice: x: 2, y: 2, z: 4, core: 2. Of those that a mesh axis runs over, the one named last changes fastest.
Arguments:
- x_branch: bfloat16 [2048, 8192], P('seq', 'mp'), may hold values from -6 to 6
- z_branch: bfloat16 [2048, 8192], P('seq', 'mp'), may hold values from -6 to 6
- conv_weight: float32 [4, 8192], P(None, 'mp'), may hold values from -3 to 3
- conv_bias: float32 [8192], P('mp'), may hold values from -0.5 to 0.5
- xproj_weight: bfloat16 [8192, 544], P('mp'), may hold values from -0.0625 to 0.0625
- dt_weight: bfloat16 [512, 8192], P(None, 'mp'), may hold values from -0.25 to 0.25
- dt_bias: float32 [8192], P('mp'), may hold values from -4 to -2
- decay_rate: float32 [16, 8192], P(None, 'mp'), may hold values from 0.0009765625 to 2
- skip_gain: float32 [8192], P('mp'), may hold values from 0.5 to 1.5
- query_rows: bfloat16 [2048, 8192], P('seq', 'mp'), may hold values from -6 to 6
- key_rows: bfloat16 [2048, 1024], P('seq', 'mp'), may hold values from -6 to 6
- value_rows: bfloat16 [2048, 1024], P('seq', 'mp'), may hold values from -6 to 6
- lengths: int32 [4], replicated, may hold values from 1 to 1024, as said below
- destination: int32 [2048], replicated, may hold values from 0 to 2047, as said below
Outputs:
- mamba_out: bfloat16 [2048, 8192], P('seq', 'mp')
- regrouped: bfloat16 [2048, 8192], P('seq', 'mp')
Inputs may be any that keep to these rules, and one draw needn't show every extreme that they name: The 4 lengths sum to 2048, and the second of them equals 1024. destination is a permutation of 0 to 2047. Cut each aligned block of 256 positions into 8 runs of 32 consecutive positions: each run goes in order to consecutive rows of one aligned target block, the runs of block i to the rows that start at i * 32 within their target blocks, and the 8 runs of one block go to 8 different target blocks.
All inputs are finite; a program needn't handle non-finite values.
Results may differ from a plain program's by a relative error of at most 0.02.
Values may be sent and summed in bfloat16 or wider, within the bound.
No kernel may reach another device: no remote copies, remote signals or barrier semaphores. Data moves between devices by JAX's collectives and lax.ppermute only.
A program may use at most 128 MiB of HBM per device.

v0:
```python
import functools

import jax
import jax.numpy as jnp
from jax import lax
from jax.experimental import pallas as pl
from jax.experimental.pallas import tpu as pltpu
from jax.sharding import PartitionSpec as P

HD = 128
LANES = 128
HALO = 16
LOG2E = 1.4426950408889634
RESET = 1e30
APART = 65536.0
VMEM_LIMIT = 32 * 1024 * 1024
VMEM_MOST = 56 * 1024 * 1024


def doc_edges(lengths_ref):
    starts, ends, total = [], [], 0
    for i in range(lengths_ref.shape[0]):
        starts.append(total)
        total = total + lengths_ref[i]
        ends.append(total)
    return starts, ends


def doc_start(places, starts):
    found = jnp.zeros_like(places)
    for start in starts[1:]:
        found = jnp.where(places >= start, start, found)
    return found


def channel_chunk(channels):
    return 512 if channels % 512 == 0 else channels


def pack_kernel(x_ref, k_ref, v_ref, halo_ref, kv_ref):
    width = k_ref.shape[1]
    halo_ref[...] = x_ref[...]
    kv_ref[:, :width] = k_ref[...]
    kv_ref[:, width:] = v_ref[...]


def pack(x_branch, key_rows, value_rows):
    tok, channels = x_branch.shape
    width = key_rows.shape[1]
    whole = lambda rows, columns: pl.BlockSpec((rows, columns), lambda i: (0, 0))
    return pl.pallas_call(
        pack_kernel,
        grid=(1,),
        in_specs=[
            pl.BlockSpec((HALO, channels), lambda i: (tok // HALO - 1, 0)),
            whole(tok, width),
            whole(tok, width),
        ],
        out_specs=[whole(HALO, channels), whole(tok, 2 * width)],
        out_shape=[
            jax.ShapeDtypeStruct((HALO, channels), x_branch.dtype),
            jax.ShapeDtypeStruct((tok, 2 * width), key_rows.dtype),
        ],
        compiler_params=pltpu.CompilerParams(vmem_limit_bytes=VMEM_MOST),
        cost_estimate=pl.CostEstimate(flops=0, bytes_accessed=16 * tok * width, transcendentals=0),
        name="pack",
    )(x_branch, key_rows, value_rows)


def conv_kernel(lengths_ref, x_ref, halo_ref, w_ref, b_ref, xp_ref, inner_ref, part_ref, ext, acc):
    tok, chunk = x_ref.shape
    starts, _ = doc_edges(lengths_ref)
    anchor = lax.axis_index("seq") * tok
    places = anchor + lax.broadcasted_iota(jnp.int32, (tok, LANES), 0)
    depth = places - doc_start(places, starts)
    ext[0:HALO, :] = halo_ref[...].astype(jnp.float32)
    ext[HALO:, :] = x_ref[...].astype(jnp.float32)
    for lane in range(0, chunk, LANES):
        cols = slice(lane, lane + LANES)
        total = b_ref[:, cols] + w_ref[0:1, cols] * ext[HALO:, cols]
        for lag in range(1, w_ref.shape[0]):
            window = ext[HALO - lag : HALO - lag + tok, cols]
            total += w_ref[lag : lag + 1, cols] * jnp.where(depth >= lag, window, 0.0)
        act = total * (0.5 + 0.5 * jnp.tanh(0.5 * total))
        inner_ref[:, cols] = act.astype(jnp.bfloat16)
    product = lax.dot_general(
        xp_ref[...], inner_ref[...], (((1,), (1,)), ((), ())), preferred_element_type=jnp.float32
    )
    at = pl.program_id(0)

    @pl.when(at == 0)
    def _():
        acc[...] = product

    @pl.when(at > 0)
    def _():
        acc[...] += product

    @pl.when(at == pl.num_programs(0) - 1)
    def _():
        part_ref[...] = acc[...].astype(jnp.bfloat16)


def conv_project(lengths, x_branch, halo, conv_weight, conv_bias, xproj_weight):
    tok, channels = x_branch.shape
    width = xproj_weight.shape[1]
    taps = conv_weight.shape[0]
    chunk = channel_chunk(channels)
    return pl.pallas_call(
        conv_kernel,
        grid=(channels // chunk,),
        in_specs=[
            pl.BlockSpec(memory_space=pltpu.SMEM),
            pl.BlockSpec((tok, chunk), lambda i: (0, i)),
            pl.BlockSpec((HALO, chunk), lambda i: (0, i)),
            pl.BlockSpec((taps, chunk), lambda i: (0, i)),
            pl.BlockSpec((1, chunk), lambda i: (0, i)),
            pl.BlockSpec((width, chunk), lambda i: (0, i)),
        ],
        out_specs=[
            pl.BlockSpec((tok, chunk), lambda i: (0, i)),
            pl.BlockSpec((width, tok), lambda i: (0, 0)),
        ],
        out_shape=[
            jax.ShapeDtypeStruct((tok, channels), jnp.bfloat16),
            jax.ShapeDtypeStruct((width, tok), jnp.bfloat16),
        ],
        scratch_shapes=[
            pltpu.VMEM((tok + HALO, chunk), jnp.float32),
            pltpu.VMEM((width, tok), jnp.float32),
        ],
        compiler_params=pltpu.CompilerParams(vmem_limit_bytes=VMEM_MOST),
        cost_estimate=pl.CostEstimate(
            flops=80 * tok * channels * width, bytes_accessed=8 * tok * channels, transcendentals=tok * channels
        ),
        name="conv_project",
    )(lengths, x_branch, halo, conv_weight, conv_bias.reshape(1, channels), xproj_weight.T)


def spread(columns):
    tok, k = columns.shape
    own = lax.broadcasted_iota(jnp.int32, (k, k), 0) == lax.broadcasted_iota(jnp.int32, (k, k), 1)
    picked = jnp.where(own[None], columns.astype(jnp.float32)[:, None, :], 0.0).reshape(tok * k, k)
    ones = jnp.ones((k, LANES), jnp.bfloat16)
    return jnp.dot(picked.astype(jnp.bfloat16), ones, preferred_element_type=jnp.float32)


def lane_tiles(value):
    return [value[:, i : i + LANES] for i in range(0, value.shape[1], LANES)]


ROWS = 8
UNROLL = 2 * ROWS


def fold_rows(parts, lane, group):
    row = parts[lane, pl.ds(group * ROWS, ROWS, stride=ROWS), :]
    for n in range(1, ROWS):
        row = row + parts[lane, pl.ds(group * ROWS + n, ROWS, stride=ROWS), :]
    return row


def halves(term):
    total = term[0:ROWS]
    for more in range(ROWS, term.shape[0], ROWS):
        total = total + term[more : more + ROWS]
    return total


def keep_terms(parts, terms):
    for i, of_lane in enumerate(terms):
        for u, term in enumerate(of_lane):
            parts[i, u * ROWS : (u + 1) * ROWS, :] = term


def local_kernel(
    lengths_ref,
    proj_ref,
    dtw_ref,
    bias_ref,
    rate_ref,
    skip_ref,
    inner_ref,
    y_ref,
    sum_ref,
    state_ref,
    low_cols,
    bc_spread,
    step_ref,
    drive_ref,
    parts,
    totals,
):
    tok, chunk = inner_ref.shape
    states = rate_ref.shape[0]
    low_rank = dtw_ref.shape[0]
    tiles = chunk // LANES
    starts, _ = doc_edges(lengths_ref)
    at = pl.program_id(0)

    @pl.when(at == 0)
    def _():
        low_cols[...] = proj_ref[:low_rank, :].astype(jnp.float32).T.astype(jnp.bfloat16)
        bc_spread[...] = spread(proj_ref[low_rank:, :].astype(jnp.float32).T)

    anchor = lax.axis_index("seq") * tok
    places = anchor + lax.broadcasted_iota(jnp.int32, (tok, LANES), 0)
    at_start = places == doc_start(places, starts)
    upto = lax.broadcasted_iota(jnp.int32, (tok, tok), 0) >= lax.broadcasted_iota(jnp.int32, (tok, tok), 1)
    upto = upto.astype(jnp.float32).astype(jnp.bfloat16)
    raw = jnp.dot(low_cols[...], dtw_ref[...], preferred_element_type=jnp.float32)
    for i in range(tiles):
        cols = slice(i * LANES, (i + 1) * LANES)
        biased = raw[:, cols] + bias_ref[:, cols]
        step = jnp.maximum(biased, 0.0) + jnp.log(1.0 + jnp.exp(-jnp.abs(biased)))
        drive = step * inner_ref[:, cols].astype(jnp.float32)
        drive_ref[:, :, cols] = drive.reshape(tok // ROWS, ROWS, LANES)
        step = jnp.where(at_start, RESET, step)
        step_ref[:, :, cols] = step.reshape(tok // ROWS, ROWS, LANES)
        summed = jnp.dot(upto, step.astype(jnp.bfloat16), preferred_element_type=jnp.float32)
        sum_ref[:, :, cols] = summed.reshape(tok // ROWS, ROWS, LANES)
        totals[at * tiles + i] = summed[tok - 1 : tok]
    rate2 = lane_tiles(rate_ref[...] * (-LOG2E))

    def body(turn, state):
        base = pl.multiple_of(turn * UNROLL, UNROLL)
        spread_at = pl.multiple_of(turn * UNROLL * 2 * states, UNROLL * 2 * states)
        state, terms = list(state), [[] for _ in range(tiles)]
        for first in range(0, tiles, 2):
            for u in range(UNROLL):
                tile = turn * (UNROLL // ROWS) + u // ROWS
                row = slice(u % ROWS, u % ROWS + 1)
                b_rows = bc_spread[pl.ds(spread_at + u * 2 * states, states), :]
                c_rows = bc_spread[pl.ds(spread_at + u * 2 * states + states, states), :]
                for i in range(first, min(first + 2, tiles)):
                    cols = slice(i * LANES, (i + 1) * LANES)
                    decay = jnp.exp2(rate2[i] * step_ref[tile, row, cols])
                    state[i] = decay * state[i] + b_rows * drive_ref[tile, row, cols]
                    terms[i].append(halves(c_rows * state[i]))
        keep_terms(parts, terms)
        for group in range(0, UNROLL, ROWS):
            for i in range(tiles):
                y_ref[pl.ds(base + group, ROWS), i * LANES : (i + 1) * LANES] = fold_rows(parts, i, group)
        return state

    end = lax.fori_loop(0, tok // UNROLL, body, [jnp.zeros_like(r) for r in rate2])
    y_ref[...] += skip_ref[...] * inner_ref[...].astype(jnp.float32)
    for i in range(tiles):
        state_ref[at * tiles + i] = end[i].astype(jnp.bfloat16)

    @pl.when(at == pl.num_programs(0) - 1)
    def _():
        lanes = totals.shape[0]
        row = lax.broadcasted_iota(jnp.int32, (states, LANES), 0)
        table = jnp.zeros((states, LANES), jnp.float32)
        for i in range(lanes):
            table = jnp.where(row == i, totals[i], table)
        high = table.astype(jnp.bfloat16)
        state_ref[lanes] = high
        state_ref[lanes + 1] = (table - high.astype(jnp.float32)).astype(jnp.bfloat16)


def local_scan(lengths, projected, dt_weight, dt_bias, decay_rate, skip_gain, inner_act):
    tok, channels = inner_act.shape
    low_rank = dt_weight.shape[0]
    states = decay_rate.shape[0]
    width = projected.shape[0]
    chunk = channel_chunk(channels)
    lanes = channels // LANES
    by_chunk = lambda rows: pl.BlockSpec((rows, chunk), lambda i: (0, i))
    return pl.pallas_call(
        local_kernel,
        grid=(channels // chunk,),
        in_specs=[
            pl.BlockSpec(memory_space=pltpu.SMEM),
            pl.BlockSpec((width, tok), lambda i: (0, 0)),
            by_chunk(low_rank),
            by_chunk(1),
            by_chunk(states),
            by_chunk(1),
            by_chunk(tok),
        ],
        out_specs=[
            by_chunk(tok),
            pl.BlockSpec((tok // ROWS, ROWS, chunk), lambda i: (0, 0, i)),
            pl.BlockSpec((lanes + 2, states, LANES), lambda i: (0, 0, 0)),
        ],
        out_shape=[
            jax.ShapeDtypeStruct((tok, channels), jnp.float32),
            jax.ShapeDtypeStruct((tok // ROWS, ROWS, channels), jnp.float32),
            jax.ShapeDtypeStruct((lanes + 2, states, LANES), jnp.bfloat16),
        ],
        scratch_shapes=[
            pltpu.VMEM((tok, low_rank), jnp.bfloat16),
            pltpu.VMEM((tok * 2 * states, LANES), jnp.float32),
            pltpu.VMEM((tok // ROWS, ROWS, chunk), jnp.float32),
            pltpu.VMEM((tok // ROWS, ROWS, chunk), jnp.float32),
            pltpu.VMEM((chunk // LANES, UNROLL * ROWS, LANES), jnp.float32),
            pltpu.VMEM((lanes, 1, LANES), jnp.float32),
        ],
        compiler_params=pltpu.CompilerParams(vmem_limit_bytes=VMEM_LIMIT),
        cost_estimate=pl.CostEstimate(
            flops=12 * tok * channels * states,
            bytes_accessed=12 * tok * channels,
            transcendentals=tok * channels * states,
        ),
        name="local_scan",
    )(
        lengths,
        projected,
        dt_weight,
        dt_bias.reshape(1, channels),
        decay_rate,
        skip_gain.reshape(1, channels),
        inner_act,
    )


def join_kernel(
    low_rank,
    reach,
    proj_ref,
    y_ref,
    sum_ref,
    z_ref,
    rate_ref,
    moved_ref,
    mine_ref,
    theirs_ref,
    out_ref,
    regrouped_ref,
    c_spread,
    parts,
):
    tok, chunk = y_ref.shape
    states = rate_ref.shape[0]
    tiles = chunk // LANES
    lanes = mine_ref.shape[1] - 2
    at = pl.program_id(0)

    @pl.when(at == 0)
    def _():
        c_spread[...] = spread(proj_ref[low_rank + states :, :].astype(jnp.float32).T).astype(jnp.bfloat16)

    regrouped_ref[...] = moved_ref[...]

    rate2 = lane_tiles(rate_ref[...] * (-LOG2E))
    row = lax.broadcasted_iota(jnp.int32, (states, LANES), 0)
    entering = [jnp.zeros_like(r) for r in rate2]
    odd = lax.rem(lax.axis_index("seq"), 2)
    for back in range(reach, 0, -1):
        ref, which = (mine_ref, back // 2) if back % 2 == 0 else (theirs_ref, (back + 1) // 2 - odd)
        table = ref[which, lanes].astype(jnp.float32) + ref[which, lanes + 1].astype(jnp.float32)
        for i, before in enumerate(entering):
            total = jnp.sum(jnp.where(row == at * tiles + i, table, 0.0), axis=0, keepdims=True)
            entering[i] = jnp.exp2(rate2[i] * total) * before + ref[which, at * tiles + i].astype(jnp.float32)
    entering = [e.astype(jnp.bfloat16) for e in entering]

    def body(turn, carry):
        rows = pl.ds(pl.multiple_of(turn * UNROLL, UNROLL), UNROLL)
        spread_at = pl.multiple_of(turn * UNROLL * states, UNROLL * states)
        terms = [[] for _ in range(tiles)]
        for first in range(0, tiles, 2):
            for u in range(UNROLL):
                tile = turn * (UNROLL // ROWS) + u // ROWS
                c_rows = c_spread[pl.ds(spread_at + u * states, states), :]
                for i in range(first, min(first + 2, tiles)):
                    power = rate2[i] * sum_ref[tile, u % ROWS : u % ROWS + 1, i * LANES : (i + 1) * LANES]
                    term = jnp.exp2(power.astype(jnp.bfloat16)) * entering[i] * c_rows
                    terms[i].append(halves(term.astype(jnp.float32)))
        keep_terms(parts, terms)
        for i in range(tiles):
            cols = slice(i * LANES, (i + 1) * LANES)
            more = jnp.concatenate([fold_rows(parts, i, group) for group in range(0, UNROLL, ROWS)], axis=0)
            z = z_ref[rows, cols].astype(jnp.float32)
            gate = z * (0.5 + 0.5 * jnp.tanh(0.5 * z))
            out_ref[rows, cols] = ((y_ref[rows, cols] + more) * gate).astype(jnp.bfloat16)
        return carry

    lax.fori_loop(0, tok // UNROLL, body, 0)


def join_states(projected, y, sums, z_branch, decay_rate, moved, mine, theirs, low_rank, reach):
    tok, channels = z_branch.shape
    states = decay_rate.shape[0]
    width = projected.shape[0]
    chunk = channel_chunk(channels)
    by_chunk = lambda rows: pl.BlockSpec((rows, chunk), lambda i: (0, i))
    return pl.pallas_call(
        functools.partial(join_kernel, low_rank, reach),
        grid=(channels // chunk,),
        in_specs=[
            pl.BlockSpec((width, tok), lambda i: (0, 0)),
            by_chunk(tok),
            pl.BlockSpec((tok // ROWS, ROWS, chunk), lambda i: (0, 0, i)),
            by_chunk(tok),
            by_chunk(states),
            by_chunk(tok),
            pl.BlockSpec(mine.shape, lambda i: (0, 0, 0, 0)),
            pl.BlockSpec(theirs.shape, lambda i: (0, 0, 0, 0)),
        ],
        out_specs=[by_chunk(tok), by_chunk(tok)],
        out_shape=[jax.ShapeDtypeStruct((tok, channels), jnp.bfloat16)] * 2,
        scratch_shapes=[
            pltpu.VMEM((tok * states, LANES), jnp.bfloat16),
            pltpu.VMEM((chunk // LANES, UNROLL * ROWS, LANES), jnp.float32),
        ],
        compiler_params=pltpu.CompilerParams(vmem_limit_bytes=VMEM_LIMIT),
        cost_estimate=pl.CostEstimate(
            flops=8 * tok * channels * states,
            bytes_accessed=14 * tok * channels,
            transcendentals=tok * channels * states,
        ),
        name="join_states",
    )(projected, y, sums, z_branch, decay_rate, moved, mine, theirs)


def attend_kernel(kv_local, first_group, lengths_ref, place_ref, q_ref, mine_ref, theirs_ref, *refs):
    out_ref, queries, scores, tops, acc = refs[-5:]
    tok = q_ref.shape[0]
    heads = q_ref.shape[1] // HD
    group = pl.program_id(0) + first_group
    position = lax.axis_index("seq")
    odd = lax.rem(position, 2)
    anchor = position * tok
    scale = LOG2E * HD**-0.5
    starts, ends = doc_edges(lengths_ref)
    lane = lax.broadcasted_iota(jnp.int32, (1, LANES), 1)
    first = jnp.full((1, LANES), 2**30, jnp.int32)
    last = jnp.zeros((1, LANES), jnp.int32)
    for i, (start, end) in enumerate(zip(starts, ends)):
        first = jnp.where(lane == i, start, first)
        last = jnp.where(lane == i, end, last)
    rows = lax.broadcasted_iota(jnp.int32, (tok, LANES), 0)

    def in_doc(base):
        return (rows + base >= first) & (rows + base < last)

    apart = jnp.where(in_doc(anchor) | (lane >= len(starts)), 0.0, -APART).astype(jnp.bfloat16)
    for head in range(heads):
        queries[head * tok : (head + 1) * tok, :HD] = q_ref[:, head * HD : (head + 1) * HD]
        queries[head * tok : (head + 1) * tok, HD:] = apart
    key_cols = pl.ds(pl.multiple_of(group * HD, HD), HD)
    value_cols = pl.ds(pl.multiple_of((group + kv_local) * HD, HD), HD)

    def rows_of(back, cols):
        if isinstance(back, int) and back == 0:
            return mine_ref[0, :, cols]
        ours = mine_ref[back // 2, :, cols]
        other = theirs_ref[(back + 1) // 2 - odd, :, cols]
        return jnp.where(lax.rem(back, 2) == 0, ours, other)

    def score(back):
        marks = jnp.where(in_doc(anchor - back * tok), 1.0, 0.0).astype(jnp.bfloat16)
        keys = jnp.concatenate([rows_of(back, key_cols), marks], axis=1)
        return lax.dot_general(queries[...], keys, (((1,), (1,)), ((), ())), preferred_element_type=jnp.float32)

    def widest(s):
        top = s[:, :LANES]
        for at in range(LANES, tok, LANES):
            top = jnp.maximum(top, s[:, at : at + LANES])
        return top

    own = score(0)
    causal = lax.broadcasted_iota(jnp.int32, (tok, tok), 1) <= lax.broadcasted_iota(jnp.int32, (tok, tok), 0)
    for head in range(heads):
        part = slice(head * tok, (head + 1) * tok)
        s = jnp.where(causal, own[part], -APART)
        scores[0, part, :] = s
        tops[part, :] = widest(s)

    begin = jnp.int32(0)
    for start in starts[1:]:
        begin = jnp.where(anchor >= start, start, begin)
    earlier = (anchor - begin + tok - 1) // tok

    def look(back, carry):
        s = score(back)
        scores[back] = s
        tops[...] = jnp.maximum(tops[...], widest(s))
        return carry

    lax.fori_loop(1, earlier + 1, look, 0)
    tops[...] = jnp.broadcast_to(jnp.max(tops[...], axis=1, keepdims=True) * scale, tops.shape)

    def weighted(back):
        values = jnp.concatenate([rows_of(back, value_cols), jnp.ones((tok, HD), jnp.bfloat16)], axis=1)
        top = tops[...]
        weights = [
            jnp.exp2((scores[back, :, at : at + LANES] * scale - top).astype(jnp.bfloat16))
            for at in range(0, tok, LANES)
        ]
        return jnp.dot(jnp.concatenate(weights, axis=1), values, preferred_element_type=jnp.float32)

    acc[...] = weighted(0)

    def absorb(back, carry):
        acc[...] += weighted(back)
        return carry

    lax.fori_loop(1, earlier + 1, absorb, 0)
    order = place_ref[pl.ds(position, 1), :]
    move = (lax.broadcasted_iota(jnp.int32, (tok, tok), 0) == order).astype(jnp.float32).astype(jnp.bfloat16)
    for head in range(heads):
        part = slice(head * tok, (head + 1) * tok)
        result = (acc[part, :HD] / acc[part, HD:]).astype(jnp.bfloat16)
        moved = jnp.dot(move, result, preferred_element_type=jnp.float32)
        out_ref[:, head * HD : (head + 1) * HD] = moved.astype(jnp.bfloat16)


def attend(lengths, send_place, query_rows, mine, theirs, groups, so_far):
    tok, width = query_rows.shape
    kv_local = mine.shape[2] // (2 * HD)
    share = width // kv_local
    heads = share // HD
    reach = 2 * (mine.shape[0] - 1)
    count = groups[1] - groups[0]
    whole = lambda a: pl.BlockSpec(a.shape, lambda i: (0,) * a.ndim)
    in_specs = [
        pl.BlockSpec(memory_space=pltpu.SMEM),
        whole(send_place),
        pl.BlockSpec((tok, share), lambda i: (0, i + groups[0])),
        whole(mine),
        whole(theirs),
    ]
    operands = [lengths, send_place, query_rows, mine, theirs]
    aliases = {}
    if so_far is not None:
        aliases = {len(operands): 0}
        in_specs.append(pl.BlockSpec(memory_space=pl.ANY))
        operands.append(so_far)
    return pl.pallas_call(
        functools.partial(attend_kernel, kv_local, groups[0]),
        grid=(count,),
        in_specs=in_specs,
        out_specs=pl.BlockSpec((tok, share), lambda i: (0, i + groups[0])),
        out_shape=jax.ShapeDtypeStruct((tok, width), jnp.bfloat16),
        scratch_shapes=[
            pltpu.VMEM((heads * tok, 2 * HD), jnp.bfloat16),
            pltpu.VMEM((reach + 1, heads * tok, tok), jnp.float32),
            pltpu.VMEM((heads * tok, LANES), jnp.float32),
            pltpu.VMEM((heads * tok, 2 * HD), jnp.float32),
        ],
        input_output_aliases=aliases,
        compiler_params=pltpu.CompilerParams(vmem_limit_bytes=VMEM_LIMIT // 2 + 4 * (reach + 1) * heads * tok * tok),
        cost_estimate=pl.CostEstimate(
            flops=4 * tok * share * count * tok * 4,
            bytes_accessed=8 * tok * share * count,
            transcendentals=tok * tok * 4 * heads * count,
        ),
        name="attend",
    )(*operands)


def shifted(value, steps):
    count = lax.axis_size("seq")
    return lax.ppermute(value, "seq", [(source, source + steps) for source in range(count - steps)])


def with_partner(held):
    mine = jnp.stack(held)
    count = lax.axis_size("seq")
    return mine, lax.ppermute(mine, "seq", [(source, source ^ 1) for source in range(count)])


def even_back(value, reach):
    return [value] + [shifted(value, 2 * k) for k in range(1, (reach + 1) // 2 + 1)]


def local(
    x_branch,
    z_branch,
    conv_weight,
    conv_bias,
    xproj_weight,
    dt_weight,
    dt_bias,
    decay_rate,
    skip_gain,
    query_rows,
    key_rows,
    value_rows,
    lengths,
    destination,
):
    tok = x_branch.shape[0]
    n_seq = lax.axis_size("seq")
    n_mp = lax.axis_size("mp")
    low_rank = dt_weight.shape[0]
    reach = n_seq // 2
    run_rows = tok // n_seq
    kv_local = key_rows.shape[1] // HD
    fence = lax.optimization_barrier

    halo, kv = pack(x_branch, key_rows, value_rows)
    earlier_rows = shifted(halo, 1)
    held = even_back(kv, reach)
    send_place = ((destination // tok) * run_rows + destination % run_rows).reshape(n_seq, tok)

    inner_act, partial = conv_project(lengths, x_branch, earlier_rows, conv_weight, conv_bias, xproj_weight)
    _, *held = fence((partial, *held))
    pieces = lax.all_to_all(partial, "mp", split_axis=0, concat_axis=0, tiled=True)
    mine, theirs = with_partner(held)
    early = max(kv_local // 2, 1)
    attended = attend(lengths, send_place, query_rows, mine, theirs, (0, early), None)
    pieces, attended = fence((pieces, attended))
    summed = jnp.sum(pieces.reshape(n_mp, -1, tok).astype(jnp.float32), axis=0).astype(jnp.bfloat16)
    copies = jnp.broadcast_to(summed[None], (n_mp,) + summed.shape).reshape(partial.shape)
    copies, attended = fence((copies, attended))
    projected = lax.all_to_all(copies, "mp", split_axis=0, concat_axis=0, tiled=True)
    if early < kv_local:
        attended = attend(lengths, send_place, query_rows, mine, theirs, (early, kv_local), attended)
    projected, attended = fence((projected, attended))
    regrouped = lax.all_to_all(attended, "seq", split_axis=0, concat_axis=0, tiled=True)

    y, sums, state = local_scan(lengths, projected, dt_weight, dt_bias, decay_rate, skip_gain, inner_act)
    own, other = with_partner(even_back(state, reach))
    return tuple(join_states(projected, y, sums, z_branch, decay_rate, regrouped, own, other, low_rank, reach))


def solution(mesh):
    placed = (
        P("seq", "mp"),
        P("seq", "mp"),
        P(None, "mp"),
        P("mp"),
        P("mp", None),
        P(None, "mp"),
        P("mp"),
        P(None, "mp"),
        P("mp"),
        P("seq", "mp"),
        P("seq", "mp"),
        P("seq", "mp"),
        P(),
        P(),
    )
    return jax.shard_map(
        local,
        mesh=mesh,
        in_specs=placed,
        out_specs=(P("seq", "mp"), P("seq", "mp")),
        check_vma=False,
    )
```

profile of v0, /device:TPU:0, one launch (start us, length us, event | category | flops | bytes accessed | tf_op | source)
XLA Modules:
  0.0 97.5 jit_solution(8917601445984447469)
XLA Ops:
  0.6 1.7 %pack.1 = (bf16[16,2048]{1,0:T(8,128)(2,1)}, bf16[256,512]{1,0:T(8,128)(2,1)}) custom-call(bf16[256,2048]{1,0:T(8,128)(2,1)} %x_ref.3, bf16[256,256]{1,0:T(8,128)(2,1)} %k_ref.1, bf16[256,256]{1,0:T(8,128)(2,1)} %v_ref.1), custom_call_target="tpu_custom_call" | custom-call | bytes 1048576 | tf_op jit(solution)/shard_map/pack/pallas_call | solution.py:51
  2.4 2.3 %collective-permute-start = (bf16[16,2048]{1,0:T(8,128)(2,1)}, bf16[16,2048]{1,0:T(8,128)(2,1)S(1)}, u32[]{:S(2)}, u32[]{:S(2)}) collective-permute-start(bf16[16,2048]{1,0:T(8,128)(2,1)} %get-tuple-element.18), channel_id=1, source_target_pairs={{0,4},{4,8},{8,12},{12,16},{16,20},{20,24},{24,28},{1,5},{5,9},{9,... | collective-permute-start | bytes 196616 | tf_op jit(solution)/shard_map/ppermute | solution.py:557
  4.7 4.4 %collective-permute-start.2 = (bf16[256,512]{1,0:T(8,128)(2,1)}, bf16[256,512]{1,0:T(8,128)(2,1)S(1)}, u32[]{:S(2)}, u32[]{:S(2)}) collective-permute-start(bf16[256,512]{1,0:T(8,128)(2,1)} %get-tuple-element.21), channel_id=1, source_target_pairs={{0,16},{4,20},{8,24},{12,28},{1,17},{5,21},{9,25},{13,29},{2,18},{... | collective-permute-start | bytes 786440 | tf_op jit(solution)/shard_map/ppermute | solution.py:557
  9.2 3.4 %collective-permute-start.1 = (bf16[256,512]{1,0:T(8,128)(2,1)}, bf16[256,512]{1,0:T(8,128)(2,1)S(1)}, u32[]{:S(2)}, u32[]{:S(2)}) collective-permute-start(bf16[256,512]{1,0:T(8,128)(2,1)} %get-tuple-element.21), channel_id=1, source_target_pairs={{0,8},{4,12},{8,16},{12,20},{16,24},{20,28},{1,9},{5,13},{9,17},{1... | collective-permute-start | bytes 786440 | tf_op jit(solution)/shard_map/ppermute | solution.py:557
  12.6 0.6 copy-done.14
  13.2 6.0 %conv_project.1 = (bf16[256,2048]{1,0:T(8,128)(2,1)}, bf16[544,256]{1,0:T(8,128)(2,1)}) custom-call(s32[4]{0:T(128)} %lengths_ref.7, bf16[256,2048]{1,0:T(8,128)(2,1)} %x_ref.3, bf16[16,2048]{1,0:T(8,128)(2,1)} %copy-done.14, f32[4,2048]{1,0:T(4,128)} %w_ref.1, f32[1,2048]{1,0:T(1,128)} %bitcast.31, bf16[544,2048]{1,0:T(8,128)(2,1)} %bitcast.30), custom_call_target="tpu_custom_call" | custom-call | flops 22817013760 | bytes 4194304 | tf_op jit(solution)/shard_map/conv_project/pallas_call | solution.py:109
  19.2 0.0 copy-start
  19.2 0.0 copy-start.1
  19.3 1.9 %collective-permute-done.2 = bf16[256,512]{1,0:T(8,128)(2,1)S(1)} collective-permute-done((bf16[256,512]{1,0:T(8,128)(2,1)}, bf16[256,512]{1,0:T(8,128)(2,1)S(1)}, u32[]{:S(2)}, u32[]{:S(2)}) %collective-permute-start.2) | collective-permute-done | bytes 262176 | tf_op jit(solution)/shard_map/ppermute | solution.py:557
  21.2 0.1 pad_maximum_fusion.mine_ref
  21.3 0.8 collective-permute-start.3
  22.1 4.9 %all-to-all-start = ((bf16[4,136,256]{2,1,0:T(8,128)(2,1)}), bf16[4,136,256]{2,1,0:T(8,128)(2,1)S(1)}, u32[]{:S(2)}, u32[]{:S(2)}) async-start(bf16[4,136,256]{2,1,0:T(8,128)(2,1)} %bitcast.24), calls=%async_computation | async-start | bytes 557056 | tf_op jit(solution)/shard_map/all_to_all | solution.py:602
  27.0 2.9 %attend.2.refs_0_ = bf16[256,2048]{1,0:T(8,128)(2,1)} custom-call(s32[4]{0:T(128)S(1)} %copy-done.1, s32[8,256]{1,0:T(8,128)S(1)} %reshape.30.place_ref, bf16[256,2048]{1,0:T(8,128)(2,1)S(1)} %copy-done, bf16[3,256,512]{2,1,0:T(8,128)(2,1)S(1)} %pad_maximum_fusion.mine_ref, bf16[3,256,512]{2,1,0:T(8,128)(2,1)S(1)} %collective-permute-done.3.theirs_ref), custom_call_target="tpu_custom_call" | custom-call | flops 1073741824 | bytes 2097152 | tf_op jit(solution)/shard_map/attend/pallas_call | solution.py:532
  29.9 6.5 %all-to-all-done = bf16[4,136,256]{2,1,0:T(8,128)(2,1)S(1)} async-done(((bf16[4,136,256]{2,1,0:T(8,128)(2,1)}), bf16[4,136,256]{2,1,0:T(8,128)(2,1)S(1)}, u32[]{:S(2)}, u32[]{:S(2)}) %all-to-all-start) | async-done | bytes 278560 | tf_op jit(solution)/shard_map/all_to_all | solution.py:602
  36.4 0.7 broadcast_in_dim.2
  37.2 3.4 %all-to-all-start.1 = ((bf16[4,136,256]{2,1,0:T(8,128)(2,1)}), bf16[4,136,256]{2,1,0:T(8,128)(2,1)S(1)}, u32[]{:S(2)}, u32[]{:S(2)}) async-start(bf16[4,136,256]{2,1,0:T(8,128)(2,1)} %bitcast.9), calls=%async_computation.1 | async-start | bytes 557056 | tf_op jit(solution)/shard_map/all_to_all | solution.py:610
  40.6 2.9 %attend.3 = bf16[256,2048]{1,0:T(8,128)(2,1)} custom-call(s32[4]{0:T(128)S(1)} %copy-done.1, s32[8,256]{1,0:T(8,128)S(1)} %reshape.30.place_ref, bf16[256,2048]{1,0:T(8,128)(2,1)S(1)} %copy-done, bf16[3,256,512]{2,1,0:T(8,128)(2,1)S(1)} %pad_maximum_fusion.mine_ref, ...), custom_call_target="tpu_custom_call", output_to_operand_aliasing={{}: (5, {})} | custom-call | flops 1073741824 | bytes 2097152 | tf_op jit(solution)/shard_map/attend/pallas_call | solution.py:532
  43.5 4.2 %all-to-all-done.1 = bf16[4,136,256]{2,1,0:T(8,128)(2,1)S(1)} async-done(((bf16[4,136,256]{2,1,0:T(8,128)(2,1)}), bf16[4,136,256]{2,1,0:T(8,128)(2,1)S(1)}, u32[]{:S(2)}, u32[]{:S(2)}) %all-to-all-start.1) | async-done | bytes 278560 | tf_op jit(solution)/shard_map/all_to_all | solution.py:610
  47.7 4.3 %all-to-all-start.2 = ((bf16[8,32,2048]{2,1,0:T(8,128)(2,1)}), bf16[8,32,2048]{2,1,0:T(8,128)(2,1)S(1)}, u32[]{:S(2)}, u32[]{:S(2)}) async-start(bf16[8,32,2048]{2,1,0:T(8,128)(2,1)} %bitcast.13), calls=%async_computation.2 | async-start | bytes 2097152 | tf_op jit(solution)/shard_map/all_to_all | solution.py:614
  52.1 1.6 %copy-done.2 = bf16[512,2048]{1,0:T(8,128)(2,1)S(1)} copy-done((bf16[512,2048]{1,0:T(8,128)(2,1)S(1)}, bf16[512,2048]{1,0:T(8,128)(2,1)}, u32[]{:S(2)}) %copy-start.2) | copy-done | bytes 2097176
  53.7 1.2 %copy-done.11 = bf16[256,2048]{1,0:T(8,128)(2,1)S(1)} copy-done((bf16[256,2048]{1,0:T(8,128)(2,1)S(1)}, bf16[256,2048]{1,0:T(8,128)(2,1)}, u32[]{:S(2)}) %copy-start.11) | copy-done | bytes 1048600
  54.9 15.1 %local_scan.1 = (f32[256,2048]{1,0:T(8,128)S(1)}, f32[32,8,2048]{2,1,0:T(8,128)S(1)}, bf16[18,16,128]{2,1,0:T(8,128)(2,1)S(1)}) custom-call(s32[4]{0:T(128)S(1)} %copy-done.1, bf16[544,256]{1,0:T(8,128)(2,1)S(1)} %bitcast.19, bf16[512,2048]{1,0:T(8,128)(2,1)S(1)} %copy-done.2, f32[1,2048]{1,0:T(1,128)S(1)} %bitcast.22, f32[16,2048]{1,0:T(8,128)S(1)} %copy-done.4, ...), custom_call_target="tpu_custom_call" | custom-call | flops 100663296 | bytes 6291456 | tf_op jit(solution)/shard_map/local_scan/pallas_call | solution.py:271
  70.0 1.3 %copy-done.7 = f32[256,2048]{1,0:T(8,128)} copy-done((f32[256,2048]{1,0:T(8,128)}, f32[256,2048]{1,0:T(8,128)S(1)}, u32[]{:S(2)}) %copy-start.7) | copy-done | bytes 2097176
  71.4 1.3 %copy-done.9 = f32[32,8,2048]{2,1,0:T(8,128)} copy-done((f32[32,8,2048]{2,1,0:T(8,128)}, f32[32,8,2048]{2,1,0:T(8,128)S(1)}, u32[]{:S(2)}) %copy-start.9) | copy-done | bytes 2097176
  72.7 4.1 %collective-permute-start.5 = (bf16[18,16,128]{2,1,0:T(8,128)(2,1)S(1)}, bf16[18,16,128]{2,1,0:T(8,128)(2,1)S(1)}, u32[]{:S(2)}, u32[]{:S(2)}) collective-permute-start(bf16[18,16,128]{2,1,0:T(8,128)(2,1)S(1)} %get-tuple-element.33), channel_id=1, source_target_pairs={{0,16},{4,20},{8,24},{12,28},{1,17},{5,21},{9,25},{13,29},{2,18},{... | collective-permute-start | bytes 221192 | tf_op jit(solution)/shard_map/ppermute | solution.py:557
  76.8 3.1 %collective-permute-start.4 = (bf16[18,16,128]{2,1,0:T(8,128)(2,1)S(1)}, bf16[18,16,128]{2,1,0:T(8,128)(2,1)S(1)}, u32[]{:S(2)}, u32[]{:S(2)}) collective-permute-start(bf16[18,16,128]{2,1,0:T(8,128)(2,1)S(1)} %get-tuple-element.33), channel_id=1, source_target_pairs={{0,8},{4,12},{8,16},{12,20},{16,24},{20,28},{1,9},{5,13},{9,17},{1... | collective-permute-start | bytes 221192 | tf_op jit(solution)/shard_map/ppermute | solution.py:557
  80.0 2.0 %collective-permute-done.4 = bf16[18,16,128]{2,1,0:T(8,128)(2,1)S(1)} collective-permute-done((bf16[18,16,128]{2,1,0:T(8,128)(2,1)S(1)}, bf16[18,16,128]{2,1,0:T(8,128)(2,1)S(1)}, u32[]{:S(2)}, u32[]{:S(2)}) %collective-permute-start.4) | collective-permute-done | bytes 73760 | tf_op jit(solution)/shard_map/ppermute | solution.py:557
  82.0 0.1 collective-permute-start.6
  82.0 1.5 %collective-permute-done.6.theirs_ref = bf16[3,18,16,128]{3,2,1,0:T(8,128)(2,1)S(1)} collective-permute-done((bf16[3,18,16,128]{3,2,1,0:T(8,128)(2,1)S(1)}, bf16[3,18,16,128]{3,2,1,0:T(8,128)(2,1)S(1)}, u32[]{:S(2)}, u32[]{:S(2)}) %collective-permute-start.6) | collective-permute-done | bytes 221216 | tf_op jit(solution)/shard_map/ppermute | solution.py:563
  83.5 1.6 %copy-done.8 = f32[256,2048]{1,0:T(8,128)S(1)} copy-done((f32[256,2048]{1,0:T(8,128)S(1)}, f32[256,2048]{1,0:T(8,128)}, u32[]{:S(2)}) %copy-start.8) | copy-done | bytes 2097176
  85.1 1.6 %copy-done.10 = f32[32,8,2048]{2,1,0:T(8,128)S(1)} copy-done((f32[32,8,2048]{2,1,0:T(8,128)S(1)}, f32[32,8,2048]{2,1,0:T(8,128)}, u32[]{:S(2)}) %copy-start.10) | copy-done | bytes 2097176
  86.7 10.8 %join_states.1 = (bf16[256,2048]{1,0:T(8,128)(2,1)}, bf16[256,2048]{1,0:T(8,128)(2,1)}) custom-call(bf16[544,256]{1,0:T(8,128)(2,1)S(1)} %bitcast.20, f32[256,2048]{1,0:T(8,128)S(1)} %copy-done.8, f32[32,8,2048]{2,1,0:T(8,128)S(1)} %copy-done.10, bf16[256,2048]{1,0:T(8,128)(2,1)S(1)} %copy-done.3, f32[16,2048]{1,0:T(8,128)S(1)} %copy-done.4, ...), custom_call_target="tpu_custom_call" | custom-call | flops 67108864 | bytes 7340032 | tf_op jit(solution)/shard_map/join_states/pallas_call | solution.py:389
  (30 shorter events, 0.1 us)
Async XLA Ops:
  2.4 10.2 %collective-permute-start = (bf16[16,2048]{1,0:T(8,128)(2,1)}, bf16[16,2048]{1,0:T(8,128)(2,1)S(1)}, u32[]{:S(2)}, u32[]{:S(2)}) collective-permute-start(bf16[16,2048]{1,0:T(8,128)(2,1)} %get-tuple-element.18), channel_id=1, source_target_pairs={{0,4},{4,8},{8,12},{12,16},{16,20},{20,24},{24,28},{1,5},{5,9},{9,... | collective-permute-start | bytes 196616 | tf_op jit(solution)/shard_map/ppermute | solution.py:557
  4.7 16.5 %collective-permute-start.2 = (bf16[256,512]{1,0:T(8,128)(2,1)}, bf16[256,512]{1,0:T(8,128)(2,1)S(1)}, u32[]{:S(2)}, u32[]{:S(2)}) collective-permute-start(bf16[256,512]{1,0:T(8,128)(2,1)} %get-tuple-element.21), channel_id=1, source_target_pairs={{0,16},{4,20},{8,24},{12,28},{1,17},{5,21},{9,25},{13,29},{2,18},{... | collective-permute-start | bytes 786440 | tf_op jit(solution)/shard_map/ppermute | solution.py:557
  9.2 12.0 %collective-permute-start.1 = (bf16[256,512]{1,0:T(8,128)(2,1)}, bf16[256,512]{1,0:T(8,128)(2,1)S(1)}, u32[]{:S(2)}, u32[]{:S(2)}) collective-permute-start(bf16[256,512]{1,0:T(8,128)(2,1)} %get-tuple-element.21), channel_id=1, source_target_pairs={{0,8},{4,12},{8,16},{12,20},{16,24},{20,28},{1,9},{5,13},{9,17},{1... | collective-permute-start | bytes 786440 | tf_op jit(solution)/shard_map/ppermute | solution.py:557
  12.6 0.6 copy-start.14
  13.2 8.0 %copy-start.12 = (bf16[256,512]{1,0:T(8,128)(2,1)S(1)}, bf16[256,512]{1,0:T(8,128)(2,1)}, u32[]{:S(2)}) copy-start(bf16[256,512]{1,0:T(8,128)(2,1)} %get-tuple-element.21) | copy-start | bytes 786436
  19.2 7.7 %copy-start.13 = (s32[2048]{0:T(1024)S(1)}, s32[2048]{0:T(1024)}, u32[]{:S(2)}) copy-start(s32[2048]{0:T(1024)} %param.27) | copy-start | bytes 24580
  19.2 7.7 %copy-start = (bf16[256,2048]{1,0:T(8,128)(2,1)S(1)}, bf16[256,2048]{1,0:T(8,128)(2,1)}, u32[]{:S(2)}) copy-start(bf16[256,2048]{1,0:T(8,128)(2,1)} %q_ref.3) | copy-start | bytes 3145732
  19.2 7.7 %copy-start.1 = (s32[4]{0:T(128)S(1)}, s32[4]{0:T(128)}, u32[]{:S(2)}) copy-start(s32[4]{0:T(128)} %lengths_ref.7) | copy-start | bytes 52
  21.3 5.7 %collective-permute-start.3 = (bf16[3,256,512]{2,1,0:T(8,128)(2,1)S(1)}, bf16[3,256,512]{2,1,0:T(8,128)(2,1)S(1)}, u32[]{:S(2)}, u32[]{:S(2)}) collective-permute-start(bf16[3,256,512]{2,1,0:T(8,128)(2,1)S(1)} %pad_maximum_fusion.mine_ref), channel_id=1, source_target_pairs={{0,4},{4,0},{8,12},{12,8},{16,20},{20,16},{24,28},{28,24},{1,5},{5... | collective-permute-start | bytes 2359304 | tf_op jit(solution)/shard_map/ppermute | solution.py:563
  22.1 14.3 %all-to-all-start = ((bf16[4,136,256]{2,1,0:T(8,128)(2,1)}), bf16[4,136,256]{2,1,0:T(8,128)(2,1)S(1)}, u32[]{:S(2)}, u32[]{:S(2)}) async-start(bf16[4,136,256]{2,1,0:T(8,128)(2,1)} %bitcast.24), calls=%async_computation | async-start | bytes 557056 | tf_op jit(solution)/shard_map/all_to_all | solution.py:602
  37.2 10.6 %all-to-all-start.1 = ((bf16[4,136,256]{2,1,0:T(8,128)(2,1)}), bf16[4,136,256]{2,1,0:T(8,128)(2,1)S(1)}, u32[]{:S(2)}, u32[]{:S(2)}) async-start(bf16[4,136,256]{2,1,0:T(8,128)(2,1)} %bitcast.9), calls=%async_computation.1 | async-start | bytes 557056 | tf_op jit(solution)/shard_map/all_to_all | solution.py:610
  43.5 8.5 %copy-start.4 = (f32[16,2048]{1,0:T(8,128)S(1)}, f32[16,2048]{1,0:T(8,128)}, u32[]{:S(2)}) copy-start(f32[16,2048]{1,0:T(8,128)} %rate_ref.3) | copy-start | bytes 393220
  43.5 8.5 %copy-start.5 = (f32[2048]{0:T(1024)S(1)}, f32[2048]{0:T(1024)}, u32[]{:S(2)}) copy-start(f32[2048]{0:T(1024)} %param.20) | copy-start | bytes 24580
  43.5 8.5 %copy-start.6 = (f32[2048]{0:T(1024)S(1)}, f32[2048]{0:T(1024)}, u32[]{:S(2)}) copy-start(f32[2048]{0:T(1024)} %param.22) | copy-start | bytes 24580
  47.7 35.8 %all-to-all-start.2 = ((bf16[8,32,2048]{2,1,0:T(8,128)(2,1)}), bf16[8,32,2048]{2,1,0:T(8,128)(2,1)S(1)}, u32[]{:S(2)}, u32[]{:S(2)}) async-start(bf16[8,32,2048]{2,1,0:T(8,128)(2,1)} %bitcast.13), calls=%async_computation.2 | async-start | bytes 2097152 | tf_op jit(solution)/shard_map/all_to_all | solution.py:614
  52.1 1.6 %copy-start.2 = (bf16[512,2048]{1,0:T(8,128)(2,1)S(1)}, bf16[512,2048]{1,0:T(8,128)(2,1)}, u32[]{:S(2)}) copy-start(bf16[512,2048]{1,0:T(8,128)(2,1)} %dtw_ref.1) | copy-start | bytes 6291460
  53.7 1.2 %copy-start.11 = (bf16[256,2048]{1,0:T(8,128)(2,1)S(1)}, bf16[256,2048]{1,0:T(8,128)(2,1)}, u32[]{:S(2)}) copy-start(bf16[256,2048]{1,0:T(8,128)(2,1)} %get-tuple-element.29.inner_ref) | copy-start | bytes 3145732
  54.9 28.6 %copy-start.3 = (bf16[256,2048]{1,0:T(8,128)(2,1)S(1)}, bf16[256,2048]{1,0:T(8,128)(2,1)}, u32[]{:S(2)}) copy-start(bf16[256,2048]{1,0:T(8,128)(2,1)} %z_ref.1) | copy-start | bytes 3145732
  70.0 1.3 %copy-start.7 = (f32[256,2048]{1,0:T(8,128)}, f32[256,2048]{1,0:T(8,128)S(1)}, u32[]{:S(2)}) copy-start(f32[256,2048]{1,0:T(8,128)S(1)} %get-tuple-element.30.y_ref) | copy-start | bytes 6291460
  71.4 1.3 %copy-start.9 = (f32[32,8,2048]{2,1,0:T(8,128)}, f32[32,8,2048]{2,1,0:T(8,128)S(1)}, u32[]{:S(2)}) copy-start(f32[32,8,2048]{2,1,0:T(8,128)S(1)} %get-tuple-element.31.sum_ref) | copy-start | bytes 6291460
  72.7 7.3 %collective-permute-start.5 = (bf16[18,16,128]{2,1,0:T(8,128)(2,1)S(1)}, bf16[18,16,128]{2,1,0:T(8,128)(2,1)S(1)}, u32[]{:S(2)}, u32[]{:S(2)}) collective-permute-start(bf16[18,16,128]{2,1,0:T(8,128)(2,1)S(1)} %get-tuple-element.33), channel_id=1, source_target_pairs={{0,16},{4,20},{8,24},{12,28},{1,17},{5,21},{9,25},{13,29},{2,18},{... | collective-permute-start | bytes 221192 | tf_op jit(solution)/shard_map/ppermute | solution.py:557
  76.8 5.1 %collective-permute-start.4 = (bf16[18,16,128]{2,1,0:T(8,128)(2,1)S(1)}, bf16[18,16,128]{2,1,0:T(8,128)(2,1)S(1)}, u32[]{:S(2)}, u32[]{:S(2)}) collective-permute-start(bf16[18,16,128]{2,1,0:T(8,128)(2,1)S(1)} %get-tuple-element.33), channel_id=1, source_target_pairs={{0,8},{4,12},{8,16},{12,20},{16,24},{20,28},{1,9},{5,13},{9,17},{1... | collective-permute-start | bytes 221192 | tf_op jit(solution)/shard_map/ppermute | solution.py:557
  82.0 1.5 %collective-permute-start.6 = (bf16[3,18,16,128]{3,2,1,0:T(8,128)(2,1)S(1)}, bf16[3,18,16,128]{3,2,1,0:T(8,128)(2,1)S(1)}, u32[]{:S(2)}, u32[]{:S(2)}) collective-permute-start(bf16[3,18,16,128]{3,2,1,0:T(8,128)(2,1)S(1)} %pad_maximum_fusion.1.mine_ref), channel_id=1, source_target_pairs={{0,4},{4,0},{8,12},{12,8},{16,20},{20,16},{24,28},{28,24},{1,5},{5... | collective-permute-start | bytes 663560 | tf_op jit(solution)/shard_map/ppermute | solution.py:563
  83.5 1.6 %copy-start.8 = (f32[256,2048]{1,0:T(8,128)S(1)}, f32[256,2048]{1,0:T(8,128)}, u32[]{:S(2)}) copy-start(f32[256,2048]{1,0:T(8,128)} %copy-done.7) | copy-start | bytes 6291460
  85.1 1.6 %copy-start.10 = (f32[32,8,2048]{2,1,0:T(8,128)S(1)}, f32[32,8,2048]{2,1,0:T(8,128)}, u32[]{:S(2)}) copy-start(f32[32,8,2048]{2,1,0:T(8,128)} %copy-done.9) | copy-start | bytes 6291460
where the time goes:
time: 98.2 us; the launch traced here: 97.5 us
  Pallas kernels  39.5 us (40%)
  starting transfers between devices  30.9 us (31%)
  waiting for transfers between devices  16.1 us (16%)
  local copies, waits for them, and re-layouts  10 us (10%)
    ppermute x5, starting transfers between devices, shifted(): lax.ppermute(value, 'seq', [(source, source + steps) for source in range(...  17.5 us
    pallas_call x1, Pallas kernels, local_scan(): pl.pallas_call(local_kernel, grid=(channels // chunk,), in_specs=[pl.Bloc...  15.1 us
    pallas_call x1, Pallas kernels, join_states(): pl.pallas_call(functools.partial(join_kernel, low_rank, reach), grid=(cha...  10.8 us
    unnamed x30, local copies, waits for them, and re-layouts  9.27 us
    all_to_all x1, waiting for transfers between devices, local(): lax.all_to_all(partial, 'mp', split_axis=0, concat_axis=0, tiled=True)  6.52 us
    pallas_call x1, Pallas kernels, conv_project(): pl.pallas_call(conv_kernel, grid=(channels // chunk,), in_specs=[pl.Block...  6.01 us
    pallas_call x2, Pallas kernels, attend(): pl.pallas_call(functools.partial(attend_kernel, kv_local, groups[0]), gri...  5.77 us
    all_to_all x1, starting transfers between devices, local(): lax.all_to_all(partial, 'mp', split_axis=0, concat_axis=0, tiled=True)  4.87 us
  transfers between devices with their start and end apart: 10, of which 5 were waited for; matrix products, arithmetic and copies ran while one was open for 0% of the time, Pallas kernels for 28%

commit v1 on v0

--- a/solution.py
+++ b/solution.py
@@ -298,7 +298,7 @@
             pltpu.VMEM((chunk // LANES, UNROLL * ROWS, LANES), jnp.float32),
             pltpu.VMEM((lanes, 1, LANES), jnp.float32),
         ],
-        compiler_params=pltpu.CompilerParams(vmem_limit_bytes=VMEM_LIMIT),
+        compiler_params=pltpu.CompilerParams(vmem_limit_bytes=VMEM_MOST),
         cost_estimate=pl.CostEstimate(
             flops=12 * tok * channels * states,
             bytes_accessed=12 * tok * channels,
@@ -344,16 +344,16 @@
 
     regrouped_ref[...] = moved_ref[...]
 
-    rate2 = lane_tiles(rate_ref[...] * (-LOG2E))
+    rate = lane_tiles(-rate_ref[...])
     row = lax.broadcasted_iota(jnp.int32, (states, LANES), 0)
-    entering = [jnp.zeros_like(r) for r in rate2]
+    entering = [jnp.zeros_like(r) for r in rate]
     odd = lax.rem(lax.axis_index("seq"), 2)
     for back in range(reach, 0, -1):
         ref, which = (mine_ref, back // 2) if back % 2 == 0 else (theirs_ref, (back + 1) // 2 - odd)
         table = ref[which, lanes].astype(jnp.float32) + ref[which, lanes + 1].astype(jnp.float32)
         for i, before in enumerate(entering):
             total = jnp.sum(jnp.where(row == at * tiles + i, table, 0.0), axis=0, keepdims=True)
-            entering[i] = jnp.exp2(rate2[i] * total) * before + ref[which, at * tiles + i].astype(jnp.float32)
+            entering[i] = jnp.exp(rate[i] * total) * before + ref[which, at * tiles + i].astype(jnp.float32)
     entering = [e.astype(jnp.bfloat16) for e in entering]
 
     def body(turn, carry):
@@ -365,8 +365,8 @@
                 tile = turn * (UNROLL // ROWS) + u // ROWS
                 c_rows = c_spread[pl.ds(spread_at + u * states, states), :]
                 for i in range(first, min(first + 2, tiles)):
-                    power = rate2[i] * sum_ref[tile, u % ROWS : u % ROWS + 1, i * LANES : (i + 1) * LANES]
-                    term = jnp.exp2(power.astype(jnp.bfloat16)) * entering[i] * c_rows
+                    power = rate[i] * sum_ref[tile, u % ROWS : u % ROWS + 1, i * LANES : (i + 1) * LANES]
+                    term = jnp.exp(power.astype(jnp.bfloat16)) * entering[i] * c_rows
                     terms[i].append(halves(term.astype(jnp.float32)))
         keep_terms(parts, terms)
         for i in range(tiles):
@@ -405,7 +405,7 @@
             pltpu.VMEM((tok * states, LANES), jnp.bfloat16),
             pltpu.VMEM((chunk // LANES, UNROLL * ROWS, LANES), jnp.float32),
         ],
-        compiler_params=pltpu.CompilerParams(vmem_limit_bytes=VMEM_LIMIT),
+        compiler_params=pltpu.CompilerParams(vmem_limit_bytes=VMEM_MOST),
         cost_estimate=pl.CostEstimate(
             flops=8 * tok * channels * states,
             bytes_accessed=14 * tok * channels,
@@ -423,7 +423,7 @@
     position = lax.axis_index("seq")
     odd = lax.rem(position, 2)
     anchor = position * tok
-    scale = LOG2E * HD**-0.5
+    scale = HD**-0.5
     starts, ends = doc_edges(lengths_ref)
     lane = lax.broadcasted_iota(jnp.int32, (1, LANES), 1)
     first = jnp.full((1, LANES), 2**30, jnp.int32)
@@ -487,7 +487,7 @@
         values = jnp.concatenate([rows_of(back, value_cols), jnp.ones((tok, HD), jnp.bfloat16)], axis=1)
         top = tops[...]
         weights = [
-            jnp.exp2((scores[back, :, at : at + LANES] * scale - top).astype(jnp.bfloat16))
+            jnp.exp((scores[back, :, at : at + LANES] * scale - top).astype(jnp.bfloat16))
             for at in range(0, tok, LANES)
         ]
         return jnp.dot(jnp.concatenate(weights, axis=1), values, preferred_element_type=jnp.float32)
@@ -544,9 +544,7 @@
         input_output_aliases=aliases,
         compiler_params=pltpu.CompilerParams(vmem_limit_bytes=VMEM_LIMIT // 2 + 4 * (reach + 1) * heads * tok * tok),
         cost_estimate=pl.CostEstimate(
-            flops=4 * tok * share * count * tok * 4,
-            bytes_accessed=8 * tok * share * count,
-            transcendentals=tok * tok * 4 * heads * count,
+            flops=tok * share * count, bytes_accessed=tok * share * count, transcendentals=0
         ),
         name="attend",
     )(*operands)

time: 98.2 us -> 94.4 us (0.961)
  local copies, waits for them, and re-layouts: 10 us -> 2.41 us
  Pallas kernels: 39.5 us -> 42 us
    unnamed x30 -> x18, local copies, waits for them, and re-layouts: 9.27 us -> 1.68 us
    pallas_call x1, Pallas kernels: 15.1 us -> 16.5 us  [local_scan(): pl.pallas_call(local_kernel, grid=(channels // chunk,), in_specs=[pl.Bloc...]
    pallas_call x1, Pallas kernels: 10.8 us -> 12 us  [join_states(): pl.pallas_call(functools.partial(join_kernel, low_rank, reach), grid=(cha...]
  transfers between devices with their start and end apart: 10 -> 10, of which waited for: 5 -> 5; matrix products, arithmetic and copies ran while one was open for 0% -> 1% of each run, Pallas kernels for 28% -> 30%
where the time goes in v1:
time: 94.4 us; the launch traced here: 93.8 us
  Pallas kernels  42 us (44%)
  starting transfers between devices  31.2 us (33%)
  waiting for transfers between devices  16.4 us (17%)
  local copies, waits for them, and re-layouts  2.41 us (3%)
  other arithmetic  1.05 us (1%)
    ppermute x5, starting transfers between devices, shifted(): lax.ppermute(value, 'seq', [(source, source + steps) for source in range(...  17.5 us
    pallas_call x1, Pallas kernels, local_scan(): pl.pallas_call(local_kernel, grid=(channels // chunk,), in_specs=[pl.Bloc...  16.5 us
    pallas_call x1, Pallas kernels, join_states(): pl.pallas_call(functools.partial(join_kernel, low_rank, reach), grid=(cha...  12 us
    all_to_all x1, waiting for transfers between devices, local(): lax.all_to_all(partial, 'mp', split_axis=0, concat_axis=0, tiled=True)  6.5 us
    pallas_call x1, Pallas kernels, conv_project(): pl.pallas_call(conv_kernel, grid=(channels // chunk,), in_specs=[pl.Block...  6 us
    pallas_call x2, Pallas kernels, attend(): pl.pallas_call(functools.partial(attend_kernel, kv_local, groups[0]), gri...  5.8 us
    all_to_all x1, starting transfers between devices, local(): lax.all_to_all(partial, 'mp', split_axis=0, concat_axis=0, tiled=True)  4.87 us
    all_to_all x1, starting transfers between devices, local(): lax.all_to_all(attended, 'seq', split_axis=0, concat_axis=0, tiled=True)  4.52 us
  transfers between devices with their start and end apart: 10, of which 5 were waited for; matrix products, arithmetic and copies ran while one was open for 1% of the time, Pallas kernels for 30%

profile of v1, /device:TPU:0, one launch (start us, length us, event | category | flops | bytes accessed | tf_op | source)
XLA Modules:
  0.0 93.8 jit_solution(7584951323706414167)
XLA Ops:
  0.6 1.7 %pack.1 = (bf16[16,2048]{1,0:T(8,128)(2,1)}, bf16[256,512]{1,0:T(8,128)(2,1)}) custom-call(bf16[256,2048]{1,0:T(8,128)(2,1)} %x_ref.3, bf16[256,256]{1,0:T(8,128)(2,1)} %k_ref.1, bf16[256,256]{1,0:T(8,128)(2,1)} %v_ref.1), custom_call_target="tpu_custom_call" | custom-call | bytes 1048576 | tf_op jit(solution)/shard_map/pack/pallas_call | solution.py:51
  2.4 2.3 %collective-permute-start = (bf16[16,2048]{1,0:T(8,128)(2,1)}, bf16[16,2048]{1,0:T(8,128)(2,1)S(1)}, u32[]{:S(2)}, u32[]{:S(2)}) collective-permute-start(bf16[16,2048]{1,0:T(8,128)(2,1)} %get-tuple-element.18), channel_id=1, source_target_pairs={{0,4},{4,8},{8,12},{12,16},{16,20},{20,24},{24,28},{1,5},{5,9},{9,... | collective-permute-start | bytes 196616 | tf_op jit(solution)/shard_map/ppermute | solution.py:555
  4.7 4.4 %collective-permute-start.2 = (bf16[256,512]{1,0:T(8,128)(2,1)}, bf16[256,512]{1,0:T(8,128)(2,1)S(1)}, u32[]{:S(2)}, u32[]{:S(2)}) collective-permute-start(bf16[256,512]{1,0:T(8,128)(2,1)} %get-tuple-element.21), channel_id=1, source_target_pairs={{0,16},{4,20},{8,24},{12,28},{1,17},{5,21},{9,25},{13,29},{2,18},{... | collective-permute-start | bytes 786440 | tf_op jit(solution)/shard_map/ppermute | solution.py:555
  9.2 3.4 %collective-permute-start.1 = (bf16[256,512]{1,0:T(8,128)(2,1)}, bf16[256,512]{1,0:T(8,128)(2,1)S(1)}, u32[]{:S(2)}, u32[]{:S(2)}) collective-permute-start(bf16[256,512]{1,0:T(8,128)(2,1)} %get-tuple-element.21), channel_id=1, source_target_pairs={{0,8},{4,12},{8,16},{12,20},{16,24},{20,28},{1,9},{5,13},{9,17},{1... | collective-permute-start | bytes 786440 | tf_op jit(solution)/shard_map/ppermute | solution.py:555
  12.6 0.0 collective-permute-done.halo_ref
  12.6 0.6 copy-done.8
  13.2 6.0 %conv_project.1 = (bf16[256,2048]{1,0:T(8,128)(2,1)}, bf16[544,256]{1,0:T(8,128)(2,1)}) custom-call(s32[4]{0:T(128)} %lengths_ref.7, bf16[256,2048]{1,0:T(8,128)(2,1)} %x_ref.3, bf16[16,2048]{1,0:T(8,128)(2,1)} %copy-done.8, f32[4,2048]{1,0:T(4,128)} %w_ref.1, f32[1,2048]{1,0:T(1,128)} %bitcast.29, bf16[544,2048]{1,0:T(8,128)(2,1)} %bitcast.28), custom_call_target="tpu_custom_call" | custom-call | flops 22817013760 | bytes 4194304 | tf_op jit(solution)/shard_map/conv_project/pallas_call | solution.py:109
  19.2 0.0 copy-start
  19.2 0.0 copy-start.1
  19.3 1.9 %collective-permute-done.2 = bf16[256,512]{1,0:T(8,128)(2,1)S(1)} collective-permute-done((bf16[256,512]{1,0:T(8,128)(2,1)}, bf16[256,512]{1,0:T(8,128)(2,1)S(1)}, u32[]{:S(2)}, u32[]{:S(2)}) %collective-permute-start.2) | collective-permute-done | bytes 262176 | tf_op jit(solution)/shard_map/ppermute | solution.py:555
  21.2 0.1 pad_maximum_fusion.mine_ref
  21.3 0.8 collective-permute-start.3
  22.1 4.9 %all-to-all-start = ((bf16[4,136,256]{2,1,0:T(8,128)(2,1)}), bf16[4,136,256]{2,1,0:T(8,128)(2,1)S(1)}, u32[]{:S(2)}, u32[]{:S(2)}) async-start(bf16[4,136,256]{2,1,0:T(8,128)(2,1)} %bitcast.21), calls=%async_computation | async-start | bytes 557056 | tf_op jit(solution)/shard_map/all_to_all | solution.py:600
  27.0 0.0 collective-permute-done.3.theirs_ref
  27.0 2.9 %attend.2.refs_0_ = bf16[256,2048]{1,0:T(8,128)(2,1)} custom-call(s32[4]{0:T(128)S(1)} %copy-done.1, s32[8,256]{1,0:T(8,128)S(1)} %reshape.30.place_ref, bf16[256,2048]{1,0:T(8,128)(2,1)S(1)} %copy-done, bf16[3,256,512]{2,1,0:T(8,128)(2,1)S(1)} %pad_maximum_fusion.mine_ref, bf16[3,256,512]{2,1,0:T(8,128)(2,1)S(1)} %collective-permute-done.3.theirs_ref), custom_call_target="tpu_custom_call" | custom-call | flops 262144 | bytes 262144 | tf_op jit(solution)/shard_map/attend/pallas_call | solution.py:532
  29.9 6.5 %all-to-all-done = bf16[4,136,256]{2,1,0:T(8,128)(2,1)S(1)} async-done(((bf16[4,136,256]{2,1,0:T(8,128)(2,1)}), bf16[4,136,256]{2,1,0:T(8,128)(2,1)S(1)}, u32[]{:S(2)}, u32[]{:S(2)}) %all-to-all-start) | async-done | bytes 278560 | tf_op jit(solution)/shard_map/all_to_all | solution.py:600
  36.4 0.7 broadcast_in_dim.2
  37.1 3.4 %all-to-all-start.1 = ((bf16[4,136,256]{2,1,0:T(8,128)(2,1)}), bf16[4,136,256]{2,1,0:T(8,128)(2,1)S(1)}, u32[]{:S(2)}, u32[]{:S(2)}) async-start(bf16[4,136,256]{2,1,0:T(8,128)(2,1)} %bitcast.9), calls=%async_computation.1 | async-start | bytes 557056 | tf_op jit(solution)/shard_map/all_to_all | solution.py:608
  40.6 2.9 %attend.3 = bf16[256,2048]{1,0:T(8,128)(2,1)} custom-call(s32[4]{0:T(128)S(1)} %copy-done.1, s32[8,256]{1,0:T(8,128)S(1)} %reshape.30.place_ref, bf16[256,2048]{1,0:T(8,128)(2,1)S(1)} %copy-done, bf16[3,256,512]{2,1,0:T(8,128)(2,1)S(1)} %pad_maximum_fusion.mine_ref, ...), custom_call_target="tpu_custom_call", output_to_operand_aliasing={{}: (5, {})} | custom-call | flops 262144 | bytes 262144 | tf_op jit(solution)/shard_map/attend/pallas_call | solution.py:532
  43.5 4.2 %all-to-all-done.1 = bf16[4,136,256]{2,1,0:T(8,128)(2,1)S(1)} async-done(((bf16[4,136,256]{2,1,0:T(8,128)(2,1)}), bf16[4,136,256]{2,1,0:T(8,128)(2,1)S(1)}, u32[]{:S(2)}, u32[]{:S(2)}) %all-to-all-start.1) | async-done | bytes 278560 | tf_op jit(solution)/shard_map/all_to_all | solution.py:608
  47.7 4.5 %all-to-all-start.2 = ((bf16[8,32,2048]{2,1,0:T(8,128)(2,1)}), bf16[8,32,2048]{2,1,0:T(8,128)(2,1)S(1)}, u32[]{:S(2)}, u32[]{:S(2)}) async-start(bf16[8,32,2048]{2,1,0:T(8,128)(2,1)} %bitcast.13), calls=%async_computation.2 | async-start | bytes 2097152 | tf_op jit(solution)/shard_map/all_to_all | solution.py:612
  52.2 16.5 %local_scan.1 = (f32[256,2048]{1,0:T(8,128)}, f32[32,8,2048]{2,1,0:T(8,128)}, bf16[18,16,128]{2,1,0:T(8,128)(2,1)}) custom-call(s32[4]{0:T(128)} %lengths_ref.7, bf16[544,256]{1,0:T(8,128)(2,1)} %bitcast.19, bf16[512,2048]{1,0:T(8,128)(2,1)} %dtw_ref.1, f32[1,2048]{1,0:T(1,128)} %bitcast.30, f32[16,2048]{1,0:T(8,128)} %rate_ref.3, f32[1,2048]{1,0:T(1,128)} %bitcast.31, ...), custom_call_target="tpu_custom_call" | custom-call | flops 100663296 | bytes 6291456 | tf_op jit(solution)/shard_map/local_scan/pallas_call | solution.py:271
  68.7 4.2 %collective-permute-start.5 = (bf16[18,16,128]{2,1,0:T(8,128)(2,1)}, bf16[18,16,128]{2,1,0:T(8,128)(2,1)S(1)}, u32[]{:S(2)}, u32[]{:S(2)}) collective-permute-start(bf16[18,16,128]{2,1,0:T(8,128)(2,1)} %get-tuple-element.33), channel_id=1, source_target_pairs={{0,16},{4,20},{8,24},{12,28},{1,17},{5,21},{9,25},{13,29},{2,18},{... | collective-permute-start | bytes 221192 | tf_op jit(solution)/shard_map/ppermute | solution.py:555
  72.9 3.1 %collective-permute-start.4 = (bf16[18,16,128]{2,1,0:T(8,128)(2,1)}, bf16[18,16,128]{2,1,0:T(8,128)(2,1)S(1)}, u32[]{:S(2)}, u32[]{:S(2)}) collective-permute-start(bf16[18,16,128]{2,1,0:T(8,128)(2,1)} %get-tuple-element.33), channel_id=1, source_target_pairs={{0,8},{4,12},{8,16},{12,20},{16,24},{20,28},{1,9},{5,13},{9,17},{1... | collective-permute-start | bytes 221192 | tf_op jit(solution)/shard_map/ppermute | solution.py:555
  76.0 2.3 %collective-permute-done.4 = bf16[18,16,128]{2,1,0:T(8,128)(2,1)S(1)} collective-permute-done((bf16[18,16,128]{2,1,0:T(8,128)(2,1)}, bf16[18,16,128]{2,1,0:T(8,128)(2,1)S(1)}, u32[]{:S(2)}, u32[]{:S(2)}) %collective-permute-start.4) | collective-permute-done | bytes 73760 | tf_op jit(solution)/shard_map/ppermute | solution.py:555
  78.3 0.9 pad_maximum_fusion.1.mine_ref
  79.2 0.1 collective-permute-start.6
  79.3 1.5 %collective-permute-done.6.theirs_ref = bf16[3,18,16,128]{3,2,1,0:T(8,128)(2,1)S(1)} collective-permute-done((bf16[3,18,16,128]{3,2,1,0:T(8,128)(2,1)S(1)}, bf16[3,18,16,128]{3,2,1,0:T(8,128)(2,1)S(1)}, u32[]{:S(2)}, u32[]{:S(2)}) %collective-permute-start.6) | collective-permute-done | bytes 221216 | tf_op jit(solution)/shard_map/ppermute | solution.py:561
  80.8 0.0 all-to-all-done.2
  80.8 0.7 copy-done.7
  81.4 0.4 copy-done.2
  81.8 12.0 %join_states.1 = (bf16[256,2048]{1,0:T(8,128)(2,1)}, bf16[256,2048]{1,0:T(8,128)(2,1)}) custom-call(bf16[544,256]{1,0:T(8,128)(2,1)} %bitcast.20, f32[256,2048]{1,0:T(8,128)} %get-tuple-element.30.y_ref, f32[32,8,2048]{2,1,0:T(8,128)} %get-tuple-element.31.sum_ref, bf16[256,2048]{1,0:T(8,128)(2,1)} %z_ref.1, f32[16,2048]{1,0:T(8,128)} %rate_ref.3, ...), custom_call_target="tpu_custom_call" | custom-call | flops 67108864 | bytes 7340032 | tf_op jit(solution)/shard_map/join_states/pallas_call | solution.py:389
  (18 shorter events, 0.1 us)
Async XLA Ops:
  2.4 10.2 %collective-permute-start = (bf16[16,2048]{1,0:T(8,128)(2,1)}, bf16[16,2048]{1,0:T(8,128)(2,1)S(1)}, u32[]{:S(2)}, u32[]{:S(2)}) collective-permute-start(bf16[16,2048]{1,0:T(8,128)(2,1)} %get-tuple-element.18), channel_id=1, source_target_pairs={{0,4},{4,8},{8,12},{12,16},{16,20},{20,24},{24,28},{1,5},{5,9},{9,... | collective-permute-start | bytes 196616 | tf_op jit(solution)/shard_map/ppermute | solution.py:555
  4.7 16.5 %collective-permute-start.2 = (bf16[256,512]{1,0:T(8,128)(2,1)}, bf16[256,512]{1,0:T(8,128)(2,1)S(1)}, u32[]{:S(2)}, u32[]{:S(2)}) collective-permute-start(bf16[256,512]{1,0:T(8,128)(2,1)} %get-tuple-element.21), channel_id=1, source_target_pairs={{0,16},{4,20},{8,24},{12,28},{1,17},{5,21},{9,25},{13,29},{2,18},{... | collective-permute-start | bytes 786440 | tf_op jit(solution)/shard_map/ppermute | solution.py:555
  9.2 12.0 %collective-permute-start.1 = (bf16[256,512]{1,0:T(8,128)(2,1)}, bf16[256,512]{1,0:T(8,128)(2,1)S(1)}, u32[]{:S(2)}, u32[]{:S(2)}) collective-permute-start(bf16[256,512]{1,0:T(8,128)(2,1)} %get-tuple-element.21), channel_id=1, source_target_pairs={{0,8},{4,12},{8,16},{12,20},{16,24},{20,28},{1,9},{5,13},{9,17},{1... | collective-permute-start | bytes 786440 | tf_op jit(solution)/shard_map/ppermute | solution.py:555
  12.6 0.6 copy-start.8
  13.2 8.0 %copy-start.4 = (bf16[256,512]{1,0:T(8,128)(2,1)S(1)}, bf16[256,512]{1,0:T(8,128)(2,1)}, u32[]{:S(2)}) copy-start(bf16[256,512]{1,0:T(8,128)(2,1)} %get-tuple-element.21) | copy-start | bytes 786436
  19.2 7.7 %copy-start.6 = (s32[2048]{0:T(1024)S(1)}, s32[2048]{0:T(1024)}, u32[]{:S(2)}) copy-start(s32[2048]{0:T(1024)} %param.27) | copy-start | bytes 24580
  19.2 7.7 %copy-start = (bf16[256,2048]{1,0:T(8,128)(2,1)S(1)}, bf16[256,2048]{1,0:T(8,128)(2,1)}, u32[]{:S(2)}) copy-start(bf16[256,2048]{1,0:T(8,128)(2,1)} %q_ref.3) | copy-start | bytes 3145732
  19.2 7.7 %copy-start.1 = (s32[4]{0:T(128)S(1)}, s32[4]{0:T(128)}, u32[]{:S(2)}) copy-start(s32[4]{0:T(128)} %lengths_ref.7) | copy-start | bytes 52
  21.3 5.7 %collective-permute-start.3 = (bf16[3,256,512]{2,1,0:T(8,128)(2,1)S(1)}, bf16[3,256,512]{2,1,0:T(8,128)(2,1)S(1)}, u32[]{:S(2)}, u32[]{:S(2)}) collective-permute-start(bf16[3,256,512]{2,1,0:T(8,128)(2,1)S(1)} %pad_maximum_fusion.mine_ref), channel_id=1, source_target_pairs={{0,4},{4,0},{8,12},{12,8},{16,20},{20,16},{24,28},{28,24},{1,5},{5... | collective-permute-start | bytes 2359304 | tf_op jit(solution)/shard_map/ppermute | solution.py:561
  22.1 14.3 %all-to-all-start = ((bf16[4,136,256]{2,1,0:T(8,128)(2,1)}), bf16[4,136,256]{2,1,0:T(8,128)(2,1)S(1)}, u32[]{:S(2)}, u32[]{:S(2)}) async-start(bf16[4,136,256]{2,1,0:T(8,128)(2,1)} %bitcast.21), calls=%async_computation | async-start | bytes 557056 | tf_op jit(solution)/shard_map/all_to_all | solution.py:600
  37.1 10.6 %all-to-all-start.1 = ((bf16[4,136,256]{2,1,0:T(8,128)(2,1)}), bf16[4,136,256]{2,1,0:T(8,128)(2,1)S(1)}, u32[]{:S(2)}, u32[]{:S(2)}) async-start(bf16[4,136,256]{2,1,0:T(8,128)(2,1)} %bitcast.9), calls=%async_computation.1 | async-start | bytes 557056 | tf_op jit(solution)/shard_map/all_to_all | solution.py:608
  47.7 4.5 %copy-start.3 = (bf16[4,136,256]{2,1,0:T(8,128)(2,1)}, bf16[4,136,256]{2,1,0:T(8,128)(2,1)S(1)}, u32[]{:S(2)}) copy-start(bf16[4,136,256]{2,1,0:T(8,128)(2,1)S(1)} %all-to-all-done.1) | copy-start | bytes 835588
  47.7 33.1 %all-to-all-start.2 = ((bf16[8,32,2048]{2,1,0:T(8,128)(2,1)}), bf16[8,32,2048]{2,1,0:T(8,128)(2,1)S(1)}, u32[]{:S(2)}, u32[]{:S(2)}) async-start(bf16[8,32,2048]{2,1,0:T(8,128)(2,1)} %bitcast.13), calls=%async_computation.2 | async-start | bytes 2097152 | tf_op jit(solution)/shard_map/all_to_all | solution.py:612
  68.7 7.3 %collective-permute-start.5 = (bf16[18,16,128]{2,1,0:T(8,128)(2,1)}, bf16[18,16,128]{2,1,0:T(8,128)(2,1)S(1)}, u32[]{:S(2)}, u32[]{:S(2)}) collective-permute-start(bf16[18,16,128]{2,1,0:T(8,128)(2,1)} %get-tuple-element.33), channel_id=1, source_target_pairs={{0,16},{4,20},{8,24},{12,28},{1,17},{5,21},{9,25},{13,29},{2,18},{... | collective-permute-start | bytes 221192 | tf_op jit(solution)/shard_map/ppermute | solution.py:555
  72.9 5.4 %collective-permute-start.4 = (bf16[18,16,128]{2,1,0:T(8,128)(2,1)}, bf16[18,16,128]{2,1,0:T(8,128)(2,1)S(1)}, u32[]{:S(2)}, u32[]{:S(2)}) collective-permute-start(bf16[18,16,128]{2,1,0:T(8,128)(2,1)} %get-tuple-element.33), channel_id=1, source_target_pairs={{0,8},{4,12},{8,16},{12,20},{16,24},{20,28},{1,9},{5,13},{9,17},{1... | collective-permute-start | bytes 221192 | tf_op jit(solution)/shard_map/ppermute | solution.py:555
  79.2 1.6 %copy-start.5 = (bf16[3,18,16,128]{3,2,1,0:T(8,128)(2,1)}, bf16[3,18,16,128]{3,2,1,0:T(8,128)(2,1)S(1)}, u32[]{:S(2)}) copy-start(bf16[3,18,16,128]{3,2,1,0:T(8,128)(2,1)S(1)} %pad_maximum_fusion.1.mine_ref) | copy-start | bytes 663556
  79.2 1.5 %collective-permute-start.6 = (bf16[3,18,16,128]{3,2,1,0:T(8,128)(2,1)S(1)}, bf16[3,18,16,128]{3,2,1,0:T(8,128)(2,1)S(1)}, u32[]{:S(2)}, u32[]{:S(2)}) collective-permute-start(bf16[3,18,16,128]{3,2,1,0:T(8,128)(2,1)S(1)} %pad_maximum_fusion.1.mine_ref), channel_id=1, source_target_pairs={{0,4},{4,0},{8,12},{12,8},{16,20},{20,16},{24,28},{28,24},{1,5},{5... | collective-permute-start | bytes 663560 | tf_op jit(solution)/shard_map/ppermute | solution.py:561
  80.8 0.7 copy-start.7
  80.8 1.1 %copy-start.2 = (bf16[8,32,2048]{2,1,0:T(8,128)(2,1)}, bf16[8,32,2048]{2,1,0:T(8,128)(2,1)S(1)}, u32[]{:S(2)}) copy-start(bf16[8,32,2048]{2,1,0:T(8,128)(2,1)S(1)} %all-to-all-done.2) | copy-start | bytes 3145732

commit v2 on v1

--- a/solution.py
+++ b/solution.py
@@ -137,40 +137,34 @@
     )(lengths, x_branch, halo, conv_weight, conv_bias.reshape(1, channels), xproj_weight.T)
 
 
+ROWS = 8
+PAIR = 2 * ROWS
+BLOCK = 64
+
+
 def spread(columns):
     tok, k = columns.shape
     own = lax.broadcasted_iota(jnp.int32, (k, k), 0) == lax.broadcasted_iota(jnp.int32, (k, k), 1)
     picked = jnp.where(own[None], columns.astype(jnp.float32)[:, None, :], 0.0).reshape(tok * k, k)
     ones = jnp.ones((k, LANES), jnp.bfloat16)
-    return jnp.dot(picked.astype(jnp.bfloat16), ones, preferred_element_type=jnp.float32)
-
-
-def lane_tiles(value):
-    return [value[:, i : i + LANES] for i in range(0, value.shape[1], LANES)]
-
-
-ROWS = 8
-UNROLL = 2 * ROWS
-
-
-def fold_rows(parts, lane, group):
-    row = parts[lane, pl.ds(group * ROWS, ROWS, stride=ROWS), :]
-    for n in range(1, ROWS):
-        row = row + parts[lane, pl.ds(group * ROWS + n, ROWS, stride=ROWS), :]
-    return row
-
-
-def halves(term):
-    total = term[0:ROWS]
-    for more in range(ROWS, term.shape[0], ROWS):
-        total = total + term[more : more + ROWS]
-    return total
-
-
-def keep_terms(parts, terms):
-    for i, of_lane in enumerate(terms):
-        for u, term in enumerate(of_lane):
-            parts[i, u * ROWS : (u + 1) * ROWS, :] = term
+    return jnp.dot(picked.astype(jnp.bfloat16), ones, preferred_element_type=jnp.float32).reshape(tok, k, LANES)
+
+
+def lane(tile):
+    return slice(tile * LANES, (tile + 1) * LANES)
+
+
+def sublanes(tile):
+    return slice(tile * ROWS, (tile + 1) * ROWS)
+
+
+def by_register(rate_ref, rates):
+    states = rate_ref.shape[0]
+    count = rates.shape[0] // states
+    for n in range(states):
+        for h in range(count):
+            tiles = [rate_ref[n : n + 1, lane(h * ROWS + j)] for j in range(ROWS)]
+            rates[n * count + h] = jnp.concatenate(tiles, axis=0) * (-LOG2E)
 
 
 def local_kernel(
@@ -179,22 +173,24 @@
     dtw_ref,
     bias_ref,
     rate_ref,
-    skip_ref,
     inner_ref,
     y_ref,
     sum_ref,
     state_ref,
     low_cols,
     bc_spread,
-    step_ref,
-    drive_ref,
-    parts,
-    totals,
+    raw,
+    rates,
+    step_tiles,
+    drive_tiles,
+    carry,
 ):
-    tok, chunk = inner_ref.shape
+    tok = proj_ref.shape[1]
+    block, channels = inner_ref.shape
     states = rate_ref.shape[0]
     low_rank = dtw_ref.shape[0]
-    tiles = chunk // LANES
+    tiles = channels // LANES
+    count = tiles // ROWS
     starts, _ = doc_edges(lengths_ref)
     at = pl.program_id(0)
 
@@ -202,101 +198,106 @@
     def _():
         low_cols[...] = proj_ref[:low_rank, :].astype(jnp.float32).T.astype(jnp.bfloat16)
         bc_spread[...] = spread(proj_ref[low_rank:, :].astype(jnp.float32).T)
-
-    anchor = lax.axis_index("seq") * tok
-    places = anchor + lax.broadcasted_iota(jnp.int32, (tok, LANES), 0)
-    at_start = places == doc_start(places, starts)
-    upto = lax.broadcasted_iota(jnp.int32, (tok, tok), 0) >= lax.broadcasted_iota(jnp.int32, (tok, tok), 1)
-    upto = upto.astype(jnp.float32).astype(jnp.bfloat16)
-    raw = jnp.dot(low_cols[...], dtw_ref[...], preferred_element_type=jnp.float32)
-    for i in range(tiles):
-        cols = slice(i * LANES, (i + 1) * LANES)
-        biased = raw[:, cols] + bias_ref[:, cols]
-        step = jnp.maximum(biased, 0.0) + jnp.log(1.0 + jnp.exp(-jnp.abs(biased)))
-        drive = step * inner_ref[:, cols].astype(jnp.float32)
-        drive_ref[:, :, cols] = drive.reshape(tok // ROWS, ROWS, LANES)
-        step = jnp.where(at_start, RESET, step)
-        step_ref[:, :, cols] = step.reshape(tok // ROWS, ROWS, LANES)
-        summed = jnp.dot(upto, step.astype(jnp.bfloat16), preferred_element_type=jnp.float32)
-        sum_ref[:, :, cols] = summed.reshape(tok // ROWS, ROWS, LANES)
-        totals[at * tiles + i] = summed[tok - 1 : tok]
-    rate2 = lane_tiles(rate_ref[...] * (-LOG2E))
-
-    def body(turn, state):
-        base = pl.multiple_of(turn * UNROLL, UNROLL)
-        spread_at = pl.multiple_of(turn * UNROLL * 2 * states, UNROLL * 2 * states)
-        state, terms = list(state), [[] for _ in range(tiles)]
-        for first in range(0, tiles, 2):
-            for u in range(UNROLL):
-                tile = turn * (UNROLL // ROWS) + u // ROWS
-                row = slice(u % ROWS, u % ROWS + 1)
-                b_rows = bc_spread[pl.ds(spread_at + u * 2 * states, states), :]
-                c_rows = bc_spread[pl.ds(spread_at + u * 2 * states + states, states), :]
-                for i in range(first, min(first + 2, tiles)):
-                    cols = slice(i * LANES, (i + 1) * LANES)
-                    decay = jnp.exp2(rate2[i] * step_ref[tile, row, cols])
-                    state[i] = decay * state[i] + b_rows * drive_ref[tile, row, cols]
-                    terms[i].append(halves(c_rows * state[i]))
-        keep_terms(parts, terms)
-        for group in range(0, UNROLL, ROWS):
-            for i in range(tiles):
-                y_ref[pl.ds(base + group, ROWS), i * LANES : (i + 1) * LANES] = fold_rows(parts, i, group)
-        return state
-
-    end = lax.fori_loop(0, tok // UNROLL, body, [jnp.zeros_like(r) for r in rate2])
-    y_ref[...] += skip_ref[...] * inner_ref[...].astype(jnp.float32)
-    for i in range(tiles):
-        state_ref[at * tiles + i] = end[i].astype(jnp.bfloat16)
+        by_register(rate_ref, rates)
+        carry[...] = jnp.zeros_like(carry)
+        for first in range(0, tiles, 4):
+            cols = slice(first * LANES, (first + 4) * LANES)
+            part = jnp.dot(low_cols[...], dtw_ref[:, cols], preferred_element_type=jnp.float32)
+            for i in range(4):
+                raw[:, sublanes(first + i), :] = part[:, lane(i)].reshape(tok // ROWS, ROWS, LANES)
+
+    def steps(pair, unused):
+        rows = pl.ds(pl.multiple_of(pair * PAIR, PAIR), PAIR)
+        places = lax.axis_index("seq") * tok + at * block + pair * PAIR
+        places = places + lax.broadcasted_iota(jnp.int32, (PAIR, LANES), 0)
+        at_start = places == doc_start(places, starts)
+        for tile in range(tiles):
+            inner = inner_ref[rows, lane(tile)].astype(jnp.float32)
+            bias = bias_ref[:, lane(tile)]
+            for k in range(2):
+                biased = raw[at * (block // ROWS) + 2 * pair + k, sublanes(tile), :] + bias
+                step = jnp.maximum(biased, 0.0) + jnp.log(1.0 + jnp.exp(-jnp.abs(biased)))
+                drive_tiles[2 * pair + k, sublanes(tile), :] = step * inner[sublanes(k)]
+                step_tiles[2 * pair + k, sublanes(tile), :] = jnp.where(at_start[sublanes(k)], RESET, step)
+        return unused
+
+    lax.fori_loop(0, block // PAIR, steps, 0)
+
+    def scan(t8, held):
+        held, total = list(held[0]), list(held[1])
+        for first in range(0, ROWS, 4):
+            done = []
+            for r in range(first, first + 4):
+                token = at * block + t8 * ROWS + r
+                picked = [pl.ds(r + h * ROWS * ROWS, ROWS, stride=ROWS) for h in range(count)]
+                step = [step_tiles[t8, rows, :] for rows in picked]
+                drive = [drive_tiles[t8, rows, :] for rows in picked]
+                out = [None] * count
+                for n in range(states):
+                    b_row = bc_spread[token, n : n + 1, :]
+                    c_row = bc_spread[token, states + n : states + n + 1, :]
+                    for h in range(count):
+                        i = n * count + h
+                        held[i] = jnp.exp2(rates[i] * step[h]) * held[i] + b_row * drive[h]
+                        term = c_row * held[i]
+                        out[h] = term if out[h] is None else out[h] + term
+                total = [so_far + more for so_far, more in zip(total, step)]
+                done.append((out, total))
+            for k, (out, so_far) in enumerate(done):
+                for h in range(count):
+                    y_ref[t8 * ROWS + first + k, sublanes(h), :] = out[h]
+                    sum_ref[t8 * ROWS + first + k, sublanes(h), :] = so_far[h]
+        return held, total
+
+    kept = states * count
+    held = ([carry[i] for i in range(kept)], [carry[kept + h] for h in range(count)])
+    held, total = lax.fori_loop(0, block // ROWS, scan, held)
+    for i, value in enumerate(held + total):
+        carry[i] = value
 
     @pl.when(at == pl.num_programs(0) - 1)
     def _():
-        lanes = totals.shape[0]
-        row = lax.broadcasted_iota(jnp.int32, (states, LANES), 0)
-        table = jnp.zeros((states, LANES), jnp.float32)
-        for i in range(lanes):
-            table = jnp.where(row == i, totals[i], table)
-        high = table.astype(jnp.bfloat16)
-        state_ref[lanes] = high
-        state_ref[lanes + 1] = (table - high.astype(jnp.float32)).astype(jnp.bfloat16)
-
-
-def local_scan(lengths, projected, dt_weight, dt_bias, decay_rate, skip_gain, inner_act):
+        state_ref[: states * tiles, :] = jnp.concatenate(held, axis=0).astype(jnp.bfloat16)
+        whole = jnp.concatenate(total, axis=0)
+        high = whole.astype(jnp.bfloat16).astype(jnp.float32)
+        state_ref[states * tiles :, :] = jnp.concatenate([high, whole - high], axis=0).astype(jnp.bfloat16)
+
+
+def local_scan(lengths, projected, dt_weight, dt_bias, decay_rate, inner_act):
     tok, channels = inner_act.shape
     low_rank = dt_weight.shape[0]
     states = decay_rate.shape[0]
-    width = projected.shape[0]
-    chunk = channel_chunk(channels)
-    lanes = channels // LANES
-    by_chunk = lambda rows: pl.BlockSpec((rows, chunk), lambda i: (0, i))
+    tiles = channels // LANES
+    count = tiles // ROWS
+    whole = lambda a: pl.BlockSpec(a.shape, lambda i: (0,) * a.ndim)
+    bias = dt_bias.reshape(1, channels)
+    by_token = pl.BlockSpec((BLOCK, tiles, LANES), lambda i: (i, 0, 0))
+    state_rows = (states + 2) * tiles
     return pl.pallas_call(
         local_kernel,
-        grid=(channels // chunk,),
+        grid=(tok // BLOCK,),
         in_specs=[
             pl.BlockSpec(memory_space=pltpu.SMEM),
-            pl.BlockSpec((width, tok), lambda i: (0, 0)),
-            by_chunk(low_rank),
-            by_chunk(1),
-            by_chunk(states),
-            by_chunk(1),
-            by_chunk(tok),
-        ],
-        out_specs=[
-            by_chunk(tok),
-            pl.BlockSpec((tok // ROWS, ROWS, chunk), lambda i: (0, 0, i)),
-            pl.BlockSpec((lanes + 2, states, LANES), lambda i: (0, 0, 0)),
-        ],
+            whole(projected),
+            whole(dt_weight),
+            whole(bias),
+            whole(decay_rate),
+            pl.BlockSpec((BLOCK, channels), lambda i: (i, 0)),
+        ],
+        out_specs=[by_token, by_token, pl.BlockSpec((state_rows, LANES), lambda i: (0, 0))],
         out_shape=[
-            jax.ShapeDtypeStruct((tok, channels), jnp.float32),
-            jax.ShapeDtypeStruct((tok // ROWS, ROWS, channels), jnp.float32),
-            jax.ShapeDtypeStruct((lanes + 2, states, LANES), jnp.bfloat16),
+            jax.ShapeDtypeStruct((tok, tiles, LANES), jnp.float32),
+            jax.ShapeDtypeStruct((tok, tiles, LANES), jnp.float32),
+            jax.ShapeDtypeStruct((state_rows, LANES), jnp.bfloat16),
         ],
         scratch_shapes=[
             pltpu.VMEM((tok, low_rank), jnp.bfloat16),
-            pltpu.VMEM((tok * 2 * states, LANES), jnp.float32),
-            pltpu.VMEM((tok // ROWS, ROWS, chunk), jnp.float32),
-            pltpu.VMEM((tok // ROWS, ROWS, chunk), jnp.float32),
-            pltpu.VMEM((chunk // LANES, UNROLL * ROWS, LANES), jnp.float32),
-            pltpu.VMEM((lanes, 1, LANES), jnp.float32),
+            pltpu.VMEM((tok, 2 * states, LANES), jnp.float32),
+            pltpu.VMEM((tok // ROWS, tiles * ROWS, LANES), jnp.float32),
+            pltpu.VMEM((states * count, ROWS, LANES), jnp.float32),
+            pltpu.VMEM((BLOCK // ROWS, tiles * ROWS, LANES), jnp.float32),
+            pltpu.VMEM((BLOCK // ROWS, tiles * ROWS, LANES), jnp.float32),
+            pltpu.VMEM(((states + 1) * count, ROWS, LANES), jnp.float32),
         ],
         compiler_params=pltpu.CompilerParams(vmem_limit_bytes=VMEM_MOST),
         cost_estimate=pl.CostEstimate(
@@ -305,15 +306,7 @@
             transcendentals=tok * channels * states,
         ),
         name="local_scan",
-    )(
-        lengths,
-        projected,
-        dt_weight,
-        dt_bias.reshape(1, channels),
-        decay_rate,
-        skip_gain.reshape(1, channels),
-        inner_act,
-    )
+    )(lengths, projected, dt_weight, bias, decay_rate, inner_act)
 
 
 def join_kernel(
@@ -322,88 +315,103 @@
     proj_ref,
     y_ref,
     sum_ref,
+    inner_ref,
     z_ref,
     rate_ref,
+    skip_ref,
     moved_ref,
     mine_ref,
     theirs_ref,
     out_ref,
     regrouped_ref,
     c_spread,
-    parts,
+    rates,
+    entering,
+    rows_tiles,
 ):
-    tok, chunk = y_ref.shape
+    block, channels = z_ref.shape
     states = rate_ref.shape[0]
-    tiles = chunk // LANES
-    lanes = mine_ref.shape[1] - 2
+    tiles = channels // LANES
+    count = tiles // ROWS
+    kept = states * count
     at = pl.program_id(0)
 
     @pl.when(at == 0)
     def _():
-        c_spread[...] = spread(proj_ref[low_rank + states :, :].astype(jnp.float32).T).astype(jnp.bfloat16)
+        c_spread[...] = spread(proj_ref[low_rank + states :, :].astype(jnp.float32).T)
+        by_register(rate_ref, rates)
+        odd = lax.rem(lax.axis_index("seq"), 2)
+        state = [jnp.zeros((ROWS, LANES), jnp.float32)] * kept
+        for back in range(reach, 0, -1):
+            ref, which = (mine_ref, back // 2) if back % 2 == 0 else (theirs_ref, (back + 1) // 2 - odd)
+            sent = ref[which].astype(jnp.float32)
+            totals = sent[states * tiles : (states + 1) * tiles] + sent[(states + 1) * tiles :]
+            state = [
+                jnp.exp2(rates[i] * totals[sublanes(i % count)]) * state[i] + sent[sublanes(i)] for i in range(kept)
+            ]
+        for i in range(kept):
+            entering[i] = state[i]
 
     regrouped_ref[...] = moved_ref[...]
 
-    rate = lane_tiles(-rate_ref[...])
-    row = lax.broadcasted_iota(jnp.int32, (states, LANES), 0)
-    entering = [jnp.zeros_like(r) for r in rate]
-    odd = lax.rem(lax.axis_index("seq"), 2)
-    for back in range(reach, 0, -1):
-        ref, which = (mine_ref, back // 2) if back % 2 == 0 else (theirs_ref, (back + 1) // 2 - odd)
-        table = ref[which, lanes].astype(jnp.float32) + ref[which, lanes + 1].astype(jnp.float32)
-        for i, before in enumerate(entering):
-            total = jnp.sum(jnp.where(row == at * tiles + i, table, 0.0), axis=0, keepdims=True)
-            entering[i] = jnp.exp(rate[i] * total) * before + ref[which, at * tiles + i].astype(jnp.float32)
-    entering = [e.astype(jnp.bfloat16) for e in entering]
-
-    def body(turn, carry):
-        rows = pl.ds(pl.multiple_of(turn * UNROLL, UNROLL), UNROLL)
-        spread_at = pl.multiple_of(turn * UNROLL * states, UNROLL * states)
-        terms = [[] for _ in range(tiles)]
-        for first in range(0, tiles, 2):
-            for u in range(UNROLL):
-                tile = turn * (UNROLL // ROWS) + u // ROWS
-                c_rows = c_spread[pl.ds(spread_at + u * states, states), :]
-                for i in range(first, min(first + 2, tiles)):
-                    power = rate[i] * sum_ref[tile, u % ROWS : u % ROWS + 1, i * LANES : (i + 1) * LANES]
-                    term = jnp.exp(power.astype(jnp.bfloat16)) * entering[i] * c_rows
-                    terms[i].append(halves(term.astype(jnp.float32)))
-        keep_terms(parts, terms)
-        for i in range(tiles):
-            cols = slice(i * LANES, (i + 1) * LANES)
-            more = jnp.concatenate([fold_rows(parts, i, group) for group in range(0, UNROLL, ROWS)], axis=0)
+    def body(pair, unused):
+        rows = pl.ds(pl.multiple_of(pair * PAIR, PAIR), PAIR)
+        for k in range(2):
+            first = pair * PAIR + k * ROWS
+            total = [[sum_ref[first + r, sublanes(h), :] for h in range(count)] for r in range(ROWS)]
+            out = [[y_ref[first + r, sublanes(h), :] for h in range(count)] for r in range(ROWS)]
+            for n in range(states):
+                for r in range(ROWS):
+                    c_row = c_spread[at * block + first + r, n : n + 1, :]
+                    for h in range(count):
+                        i = n * count + h
+                        out[r][h] += jnp.exp2(rates[i] * total[r][h]) * entering[i] * c_row
+            for r in range(ROWS):
+                for h in range(count):
+                    rows_tiles[k, pl.ds(r + h * ROWS * ROWS, ROWS, stride=ROWS), :] = out[r][h]
+        for tile in range(tiles):
+            cols = lane(tile)
             z = z_ref[rows, cols].astype(jnp.float32)
             gate = z * (0.5 + 0.5 * jnp.tanh(0.5 * z))
-            out_ref[rows, cols] = ((y_ref[rows, cols] + more) * gate).astype(jnp.bfloat16)
-        return carry
-
-    lax.fori_loop(0, tok // UNROLL, body, 0)
-
-
-def join_states(projected, y, sums, z_branch, decay_rate, moved, mine, theirs, low_rank, reach):
+            scanned = jnp.concatenate([rows_tiles[k, sublanes(tile), :] for k in range(2)], axis=0)
+            scanned = scanned + skip_ref[:, cols] * inner_ref[rows, cols].astype(jnp.float32)
+            out_ref[rows, cols] = (scanned * gate).astype(jnp.bfloat16)
+        return unused
+
+    lax.fori_loop(0, block // PAIR, body, 0)
+
+
+def join_states(projected, y, sums, inner_act, z_branch, decay_rate, skip_gain, moved, mine, theirs, low_rank, reach):
     tok, channels = z_branch.shape
     states = decay_rate.shape[0]
-    width = projected.shape[0]
-    chunk = channel_chunk(channels)
-    by_chunk = lambda rows: pl.BlockSpec((rows, chunk), lambda i: (0, i))
+    tiles = channels // LANES
+    count = tiles // ROWS
+    whole = lambda a: pl.BlockSpec(a.shape, lambda i: (0,) * a.ndim)
+    by_token = pl.BlockSpec((BLOCK, tiles, LANES), lambda i: (i, 0, 0))
+    by_row = pl.BlockSpec((BLOCK, channels), lambda i: (i, 0))
+    skip = skip_gain.reshape(1, channels)
     return pl.pallas_call(
         functools.partial(join_kernel, low_rank, reach),
-        grid=(channels // chunk,),
+        grid=(tok // BLOCK,),
         in_specs=[
-            pl.BlockSpec((width, tok), lambda i: (0, 0)),
-            by_chunk(tok),
-            pl.BlockSpec((tok // ROWS, ROWS, chunk), lambda i: (0, 0, i)),
-            by_chunk(tok),
-            by_chunk(states),
-            by_chunk(tok),
-            pl.BlockSpec(mine.shape, lambda i: (0, 0, 0, 0)),
-            pl.BlockSpec(theirs.shape, lambda i: (0, 0, 0, 0)),
-        ],
-        out_specs=[by_chunk(tok), by_chunk(tok)],
+            whole(projected),
+            by_token,
+            by_token,
+            by_row,
+            by_row,
+            whole(decay_rate),
+            whole(skip),
+            by_row,
+            whole(mine),
+            whole(theirs),
+        ],
+        out_specs=[by_row, by_row],
         out_shape=[jax.ShapeDtypeStruct((tok, channels), jnp.bfloat16)] * 2,
         scratch_shapes=[
-            pltpu.VMEM((tok * states, LANES), jnp.bfloat16),
-            pltpu.VMEM((chunk // LANES, UNROLL * ROWS, LANES), jnp.float32),
+            pltpu.VMEM((tok, states, LANES), jnp.float32),
+            pltpu.VMEM((states * count, ROWS, LANES), jnp.float32),
+            pltpu.VMEM((states * count, ROWS, LANES), jnp.float32),
+            pltpu.VMEM((2, tiles * ROWS, LANES), jnp.float32),
         ],
         compiler_params=pltpu.CompilerParams(vmem_limit_bytes=VMEM_MOST),
         cost_estimate=pl.CostEstimate(
@@ -412,7 +420,7 @@
             transcendentals=tok * channels * states,
         ),
         name="join_states",
-    )(projected, y, sums, z_branch, decay_rate, moved, mine, theirs)
+    )(projected, y, sums, inner_act, z_branch, decay_rate, skip, moved, mine, theirs)
 
 
 def attend_kernel(kv_local, first_group, lengths_ref, place_ref, q_ref, mine_ref, theirs_ref, *refs):
@@ -611,9 +619,13 @@
     projected, attended = fence((projected, attended))
     regrouped = lax.all_to_all(attended, "seq", split_axis=0, concat_axis=0, tiled=True)
 
-    y, sums, state = local_scan(lengths, projected, dt_weight, dt_bias, decay_rate, skip_gain, inner_act)
+    y, sums, state = local_scan(lengths, projected, dt_weight, dt_bias, decay_rate, inner_act)
     own, other = with_partner(even_back(state, reach))
-    return tuple(join_states(projected, y, sums, z_branch, decay_rate, regrouped, own, other, low_rank, reach))
+    return tuple(
+        join_states(
+            projected, y, sums, inner_act, z_branch, decay_rate, skip_gain, regrouped, own, other, low_rank, reach
+        )
+    )
 
 
 def solution(mesh):

time: 94.4 us -> 89.7 us (0.950)
  Pallas kernels: 42 us -> 37.2 us
    pallas_call x2, Pallas kernels: 28.5 us -> 23.7 us  [the longest x1 13.8 us: local_scan(): pl.pallas_call(local_kernel, grid=(tok // BLOCK,), in_specs=[pl.BlockSpec...]
  transfers between devices with their start and end apart: 10 -> 10, of which waited for: 5 -> 5; matrix products, arithmetic and copies ran while one was open for 1% -> 1% of each run, Pallas kernels for 30% -> 29%
where the time goes in v2:
time: 89.7 us; the launch traced here: 89 us
  Pallas kernels  37.2 us (41%)
  starting transfers between devices  31.2 us (35%)
  waiting for transfers between devices  16.4 us (18%)
  local copies, waits for them, and re-layouts  2.46 us (3%)
  other arithmetic  1.05 us (1%)
    ppermute x5, starting transfers between devices, shifted(): lax.ppermute(value, 'seq', [(source, source + steps) for source in range(...  17.5 us
    pallas_call x1, Pallas kernels, local_scan(): pl.pallas_call(local_kernel, grid=(tok // BLOCK,), in_specs=[pl.BlockSpec...  13.8 us
    pallas_call x1, Pallas kernels, join_states(): pl.pallas_call(functools.partial(join_kernel, low_rank, reach), grid=(tok...  9.86 us
    all_to_all x1, waiting for transfers between devices, local(): lax.all_to_all(partial, 'mp', split_axis=0, concat_axis=0, tiled=True)  6.5 us
    pallas_call x1, Pallas kernels, conv_project(): pl.pallas_call(conv_kernel, grid=(channels // chunk,), in_specs=[pl.Block...  6.01 us
    pallas_call x2, Pallas kernels, attend(): pl.pallas_call(functools.partial(attend_kernel, kv_local, groups[0]), gri...  5.8 us
    all_to_all x1, starting transfers between devices, local(): lax.all_to_all(partial, 'mp', split_axis=0, concat_axis=0, tiled=True)  4.87 us
    all_to_all x1, starting transfers between devices, local(): lax.all_to_all(attended, 'seq', split_axis=0, concat_axis=0, tiled=True)  4.52 us
  transfers between devices with their start and end apart: 10, of which 5 were waited for; matrix products, arithmetic and copies ran while one was open for 1% of the time, Pallas kernels for 29%

profile of v2, /device:TPU:0, one launch (start us, length us, event | category | flops | bytes accessed | tf_op | source)
XLA Modules:
  0.0 89.0 jit_solution(6446330615012991331)
XLA Ops:
  0.6 1.7 %pack.1 = (bf16[16,2048]{1,0:T(8,128)(2,1)}, bf16[256,512]{1,0:T(8,128)(2,1)}) custom-call(bf16[256,2048]{1,0:T(8,128)(2,1)} %x_ref.3, bf16[256,256]{1,0:T(8,128)(2,1)} %k_ref.1, bf16[256,256]{1,0:T(8,128)(2,1)} %v_ref.1), custom_call_target="tpu_custom_call" | custom-call | bytes 1048576 | tf_op jit(solution)/shard_map/pack/pallas_call | solution.py:51
  2.4 2.3 %collective-permute-start = (bf16[16,2048]{1,0:T(8,128)(2,1)}, bf16[16,2048]{1,0:T(8,128)(2,1)S(1)}, u32[]{:S(2)}, u32[]{:S(2)}) collective-permute-start(bf16[16,2048]{1,0:T(8,128)(2,1)} %get-tuple-element.18), channel_id=1, source_target_pairs={{0,4},{4,8},{8,12},{12,16},{16,20},{20,24},{24,28},{1,5},{5,9},{9,... | collective-permute-start | bytes 196616 | tf_op jit(solution)/shard_map/ppermute | solution.py:563
  4.7 4.4 %collective-permute-start.2 = (bf16[256,512]{1,0:T(8,128)(2,1)}, bf16[256,512]{1,0:T(8,128)(2,1)S(1)}, u32[]{:S(2)}, u32[]{:S(2)}) collective-permute-start(bf16[256,512]{1,0:T(8,128)(2,1)} %get-tuple-element.21), channel_id=1, source_target_pairs={{0,16},{4,20},{8,24},{12,28},{1,17},{5,21},{9,25},{13,29},{2,18},{... | collective-permute-start | bytes 786440 | tf_op jit(solution)/shard_map/ppermute | solution.py:563
  9.2 3.4 %collective-permute-start.1 = (bf16[256,512]{1,0:T(8,128)(2,1)}, bf16[256,512]{1,0:T(8,128)(2,1)S(1)}, u32[]{:S(2)}, u32[]{:S(2)}) collective-permute-start(bf16[256,512]{1,0:T(8,128)(2,1)} %get-tuple-element.21), channel_id=1, source_target_pairs={{0,8},{4,12},{8,16},{12,20},{16,24},{20,28},{1,9},{5,13},{9,17},{1... | collective-permute-start | bytes 786440 | tf_op jit(solution)/shard_map/ppermute | solution.py:563
  12.6 0.6 copy-done.8
  13.2 6.0 %conv_project.1 = (bf16[256,2048]{1,0:T(8,128)(2,1)}, bf16[544,256]{1,0:T(8,128)(2,1)}) custom-call(s32[4]{0:T(128)} %lengths_ref.7, bf16[256,2048]{1,0:T(8,128)(2,1)} %x_ref.3, bf16[16,2048]{1,0:T(8,128)(2,1)} %copy-done.8, f32[4,2048]{1,0:T(4,128)} %w_ref.1, f32[1,2048]{1,0:T(1,128)} %bitcast.29, bf16[544,2048]{1,0:T(8,128)(2,1)} %bitcast.28), custom_call_target="tpu_custom_call" | custom-call | flops 22817013760 | bytes 4194304 | tf_op jit(solution)/shard_map/conv_project/pallas_call | solution.py:109
  19.2 0.0 copy-start
  19.3 0.0 copy-start.1
  19.3 1.9 %collective-permute-done.2 = bf16[256,512]{1,0:T(8,128)(2,1)S(1)} collective-permute-done((bf16[256,512]{1,0:T(8,128)(2,1)}, bf16[256,512]{1,0:T(8,128)(2,1)S(1)}, u32[]{:S(2)}, u32[]{:S(2)}) %collective-permute-start.2) | collective-permute-done | bytes 262176 | tf_op jit(solution)/shard_map/ppermute | solution.py:563
  21.2 0.0 collective-permute-done.1
  21.2 0.1 pad_maximum_fusion.mine_ref
  21.3 0.8 collective-permute-start.3
  22.1 4.9 %all-to-all-start = ((bf16[4,136,256]{2,1,0:T(8,128)(2,1)}), bf16[4,136,256]{2,1,0:T(8,128)(2,1)S(1)}, u32[]{:S(2)}, u32[]{:S(2)}) async-start(bf16[4,136,256]{2,1,0:T(8,128)(2,1)} %bitcast.21), calls=%async_computation | async-start | bytes 557056 | tf_op jit(solution)/shard_map/all_to_all | solution.py:608
  27.0 0.0 collective-permute-done.3.theirs_ref
  27.0 2.9 %attend.2.refs_0_ = bf16[256,2048]{1,0:T(8,128)(2,1)} custom-call(s32[4]{0:T(128)S(1)} %copy-done.1, s32[8,256]{1,0:T(8,128)S(1)} %reshape.30.place_ref, bf16[256,2048]{1,0:T(8,128)(2,1)S(1)} %copy-done, bf16[3,256,512]{2,1,0:T(8,128)(2,1)S(1)} %pad_maximum_fusion.mine_ref, bf16[3,256,512]{2,1,0:T(8,128)(2,1)S(1)} %collective-permute-done.3.theirs_ref), custom_call_target="tpu_custom_call" | custom-call | flops 262144 | bytes 262144 | tf_op jit(solution)/shard_map/attend/pallas_call | solution.py:540
  29.9 6.5 %all-to-all-done = bf16[4,136,256]{2,1,0:T(8,128)(2,1)S(1)} async-done(((bf16[4,136,256]{2,1,0:T(8,128)(2,1)}), bf16[4,136,256]{2,1,0:T(8,128)(2,1)S(1)}, u32[]{:S(2)}, u32[]{:S(2)}) %all-to-all-start) | async-done | bytes 278560 | tf_op jit(solution)/shard_map/all_to_all | solution.py:608
  36.4 0.7 broadcast_in_dim.2
  37.2 3.5 %all-to-all-start.1 = ((bf16[4,136,256]{2,1,0:T(8,128)(2,1)}), bf16[4,136,256]{2,1,0:T(8,128)(2,1)S(1)}, u32[]{:S(2)}, u32[]{:S(2)}) async-start(bf16[4,136,256]{2,1,0:T(8,128)(2,1)} %bitcast.9), calls=%async_computation.1 | async-start | bytes 557056 | tf_op jit(solution)/shard_map/all_to_all | solution.py:616
  40.6 2.9 %attend.3 = bf16[256,2048]{1,0:T(8,128)(2,1)} custom-call(s32[4]{0:T(128)S(1)} %copy-done.1, s32[8,256]{1,0:T(8,128)S(1)} %reshape.30.place_ref, bf16[256,2048]{1,0:T(8,128)(2,1)S(1)} %copy-done, bf16[3,256,512]{2,1,0:T(8,128)(2,1)S(1)} %pad_maximum_fusion.mine_ref, ...), custom_call_target="tpu_custom_call", output_to_operand_aliasing={{}: (5, {})} | custom-call | flops 262144 | bytes 262144 | tf_op jit(solution)/shard_map/attend/pallas_call | solution.py:540
  43.5 4.2 %all-to-all-done.1 = bf16[4,136,256]{2,1,0:T(8,128)(2,1)S(1)} async-done(((bf16[4,136,256]{2,1,0:T(8,128)(2,1)}), bf16[4,136,256]{2,1,0:T(8,128)(2,1)S(1)}, u32[]{:S(2)}, u32[]{:S(2)}) %all-to-all-start.1) | async-done | bytes 278560 | tf_op jit(solution)/shard_map/all_to_all | solution.py:616
  47.7 4.5 %all-to-all-start.2 = ((bf16[8,32,2048]{2,1,0:T(8,128)(2,1)}), bf16[8,32,2048]{2,1,0:T(8,128)(2,1)S(1)}, u32[]{:S(2)}, u32[]{:S(2)}) async-start(bf16[8,32,2048]{2,1,0:T(8,128)(2,1)} %bitcast.13), calls=%async_computation.2 | async-start | bytes 2097152 | tf_op jit(solution)/shard_map/all_to_all | solution.py:620
  52.2 13.8 %local_scan.1 = (f32[256,16,128]{2,1,0:T(8,128)}, f32[256,16,128]{2,1,0:T(8,128)}, bf16[288,128]{1,0:T(8,128)(2,1)}) custom-call(s32[4]{0:T(128)} %lengths_ref.7, bf16[544,256]{1,0:T(8,128)(2,1)} %bitcast.19, bf16[512,2048]{1,0:T(8,128)(2,1)} %dtw_ref.1, f32[1,2048]{1,0:T(1,128)} %bitcast.30, f32[16,2048]{1,0:T(8,128)} %rate_ref.3, ...), custom_call_target="tpu_custom_call" | custom-call | flops 100663296 | bytes 6291456 | tf_op jit(solution)/shard_map/local_scan/pallas_call | solution.py:276
  66.0 4.2 %collective-permute-start.5 = (bf16[288,128]{1,0:T(8,128)(2,1)}, bf16[288,128]{1,0:T(8,128)(2,1)S(1)}, u32[]{:S(2)}, u32[]{:S(2)}) collective-permute-start(bf16[288,128]{1,0:T(8,128)(2,1)} %get-tuple-element.33), channel_id=1, source_target_pairs={{0,16},{4,20},{8,24},{12,28},{1,17},{5,21},{9,25},{13,29},{2,18},{... | collective-permute-start | bytes 221192 | tf_op jit(solution)/shard_map/ppermute | solution.py:563
  70.2 3.1 %collective-permute-start.4 = (bf16[288,128]{1,0:T(8,128)(2,1)}, bf16[288,128]{1,0:T(8,128)(2,1)S(1)}, u32[]{:S(2)}, u32[]{:S(2)}) collective-permute-start(bf16[288,128]{1,0:T(8,128)(2,1)} %get-tuple-element.33), channel_id=1, source_target_pairs={{0,8},{4,12},{8,16},{12,20},{16,24},{20,28},{1,9},{5,13},{9,17},{1... | collective-permute-start | bytes 221192 | tf_op jit(solution)/shard_map/ppermute | solution.py:563
  73.3 0.0 collective-permute-done.5
  73.4 2.3 %collective-permute-done.4 = bf16[288,128]{1,0:T(8,128)(2,1)S(1)} collective-permute-done((bf16[288,128]{1,0:T(8,128)(2,1)}, bf16[288,128]{1,0:T(8,128)(2,1)S(1)}, u32[]{:S(2)}, u32[]{:S(2)}) %collective-permute-start.4) | collective-permute-done | bytes 73760 | tf_op jit(solution)/shard_map/ppermute | solution.py:563
  75.6 0.9 %pad_maximum_fusion.1.mine_ref = bf16[3,288,128]{2,1,0:T(8,128)(2,1)S(1)} fusion(bf16[1,288,128]{2,1,0:T(8,128)(2,1)S(1)} %bitcast.26, bf16[1,288,128]{2,1,0:T(8,128)(2,1)S(1)} %bitcast.27, bf16[1,288,128]{2,1,0:T(8,128)(2,1)} %bitcast.25), kind=kLoop, calls=%fused_computation.1 | loop fusion | flops 221184 | bytes 442368 | tf_op jit(solution)/shard_map/stack | solution.py:567
  76.5 0.1 collective-permute-start.6
  76.6 1.5 %collective-permute-done.6.theirs_ref = bf16[3,288,128]{2,1,0:T(8,128)(2,1)S(1)} collective-permute-done((bf16[3,288,128]{2,1,0:T(8,128)(2,1)S(1)}, bf16[3,288,128]{2,1,0:T(8,128)(2,1)S(1)}, u32[]{:S(2)}, u32[]{:S(2)}) %collective-permute-start.6) | collective-permute-done | bytes 221216 | tf_op jit(solution)/shard_map/ppermute | solution.py:569
  78.1 0.7 copy-done.7
  78.8 0.4 copy-done.2
  79.2 9.9 %join_states.1 = (bf16[256,2048]{1,0:T(8,128)(2,1)}, bf16[256,2048]{1,0:T(8,128)(2,1)}) custom-call(bf16[544,256]{1,0:T(8,128)(2,1)} %bitcast.20, f32[256,16,128]{2,1,0:T(8,128)} %get-tuple-element.30.y_ref, f32[256,16,128]{2,1,0:T(8,128)} %get-tuple-element.31.sum_ref, bf16[256,2048]{1,0:T(8,128)(2,1)} %get-tuple-element.29.inner_ref, ...), custom_call_target="tpu_custom_call" | custom-call | flops 67108864 | bytes 7340032 | tf_op jit(solution)/shard_map/join_states/pallas_call | solution.py:393
  (18 shorter events, 0.1 us)
Async XLA Ops:
  2.4 10.2 %collective-permute-start = (bf16[16,2048]{1,0:T(8,128)(2,1)}, bf16[16,2048]{1,0:T(8,128)(2,1)S(1)}, u32[]{:S(2)}, u32[]{:S(2)}) collective-permute-start(bf16[16,2048]{1,0:T(8,128)(2,1)} %get-tuple-element.18), channel_id=1, source_target_pairs={{0,4},{4,8},{8,12},{12,16},{16,20},{20,24},{24,28},{1,5},{5,9},{9,... | collective-permute-start | bytes 196616 | tf_op jit(solution)/shard_map/ppermute | solution.py:563
  4.7 16.5 %collective-permute-start.2 = (bf16[256,512]{1,0:T(8,128)(2,1)}, bf16[256,512]{1,0:T(8,128)(2,1)S(1)}, u32[]{:S(2)}, u32[]{:S(2)}) collective-permute-start(bf16[256,512]{1,0:T(8,128)(2,1)} %get-tuple-element.21), channel_id=1, source_target_pairs={{0,16},{4,20},{8,24},{12,28},{1,17},{5,21},{9,25},{13,29},{2,18},{... | collective-permute-start | bytes 786440 | tf_op jit(solution)/shard_map/ppermute | solution.py:563
  9.2 12.0 %collective-permute-start.1 = (bf16[256,512]{1,0:T(8,128)(2,1)}, bf16[256,512]{1,0:T(8,128)(2,1)S(1)}, u32[]{:S(2)}, u32[]{:S(2)}) collective-permute-start(bf16[256,512]{1,0:T(8,128)(2,1)} %get-tuple-element.21), channel_id=1, source_target_pairs={{0,8},{4,12},{8,16},{12,20},{16,24},{20,28},{1,9},{5,13},{9,17},{1... | collective-permute-start | bytes 786440 | tf_op jit(solution)/shard_map/ppermute | solution.py:563
  12.6 0.6 copy-start.8
  13.2 8.0 %copy-start.4 = (bf16[256,512]{1,0:T(8,128)(2,1)S(1)}, bf16[256,512]{1,0:T(8,128)(2,1)}, u32[]{:S(2)}) copy-start(bf16[256,512]{1,0:T(8,128)(2,1)} %get-tuple-element.21) | copy-start | bytes 786436
  19.2 7.7 %copy-start.6 = (s32[2048]{0:T(1024)S(1)}, s32[2048]{0:T(1024)}, u32[]{:S(2)}) copy-start(s32[2048]{0:T(1024)} %param.27) | copy-start | bytes 24580
  19.2 7.7 %copy-start = (bf16[256,2048]{1,0:T(8,128)(2,1)S(1)}, bf16[256,2048]{1,0:T(8,128)(2,1)}, u32[]{:S(2)}) copy-start(bf16[256,2048]{1,0:T(8,128)(2,1)} %q_ref.3) | copy-start | bytes 3145732
  19.3 7.7 %copy-start.1 = (s32[4]{0:T(128)S(1)}, s32[4]{0:T(128)}, u32[]{:S(2)}) copy-start(s32[4]{0:T(128)} %lengths_ref.7) | copy-start | bytes 52
  21.3 5.7 %collective-permute-start.3 = (bf16[3,256,512]{2,1,0:T(8,128)(2,1)S(1)}, bf16[3,256,512]{2,1,0:T(8,128)(2,1)S(1)}, u32[]{:S(2)}, u32[]{:S(2)}) collective-permute-start(bf16[3,256,512]{2,1,0:T(8,128)(2,1)S(1)} %pad_maximum_fusion.mine_ref), channel_id=1, source_target_pairs={{0,4},{4,0},{8,12},{12,8},{16,20},{20,16},{24,28},{28,24},{1,5},{5... | collective-permute-start | bytes 2359304 | tf_op jit(solution)/shard_map/ppermute | solution.py:569
  22.1 14.3 %all-to-all-start = ((bf16[4,136,256]{2,1,0:T(8,128)(2,1)}), bf16[4,136,256]{2,1,0:T(8,128)(2,1)S(1)}, u32[]{:S(2)}, u32[]{:S(2)}) async-start(bf16[4,136,256]{2,1,0:T(8,128)(2,1)} %bitcast.21), calls=%async_computation | async-start | bytes 557056 | tf_op jit(solution)/shard_map/all_to_all | solution.py:608
  37.2 10.6 %all-to-all-start.1 = ((bf16[4,136,256]{2,1,0:T(8,128)(2,1)}), bf16[4,136,256]{2,1,0:T(8,128)(2,1)S(1)}, u32[]{:S(2)}, u32[]{:S(2)}) async-start(bf16[4,136,256]{2,1,0:T(8,128)(2,1)} %bitcast.9), calls=%async_computation.1 | async-start | bytes 557056 | tf_op jit(solution)/shard_map/all_to_all | solution.py:616
  47.7 4.5 %copy-start.3 = (bf16[4,136,256]{2,1,0:T(8,128)(2,1)}, bf16[4,136,256]{2,1,0:T(8,128)(2,1)S(1)}, u32[]{:S(2)}) copy-start(bf16[4,136,256]{2,1,0:T(8,128)(2,1)S(1)} %all-to-all-done.1) | copy-start | bytes 835588
  47.7 30.4 %all-to-all-start.2 = ((bf16[8,32,2048]{2,1,0:T(8,128)(2,1)}), bf16[8,32,2048]{2,1,0:T(8,128)(2,1)S(1)}, u32[]{:S(2)}, u32[]{:S(2)}) async-start(bf16[8,32,2048]{2,1,0:T(8,128)(2,1)} %bitcast.13), calls=%async_computation.2 | async-start | bytes 2097152 | tf_op jit(solution)/shard_map/all_to_all | solution.py:620
  66.0 7.3 %collective-permute-start.5 = (bf16[288,128]{1,0:T(8,128)(2,1)}, bf16[288,128]{1,0:T(8,128)(2,1)S(1)}, u32[]{:S(2)}, u32[]{:S(2)}) collective-permute-start(bf16[288,128]{1,0:T(8,128)(2,1)} %get-tuple-element.33), channel_id=1, source_target_pairs={{0,16},{4,20},{8,24},{12,28},{1,17},{5,21},{9,25},{13,29},{2,18},{... | collective-permute-start | bytes 221192 | tf_op jit(solution)/shard_map/ppermute | solution.py:563
  70.2 5.4 %collective-permute-start.4 = (bf16[288,128]{1,0:T(8,128)(2,1)}, bf16[288,128]{1,0:T(8,128)(2,1)S(1)}, u32[]{:S(2)}, u32[]{:S(2)}) collective-permute-start(bf16[288,128]{1,0:T(8,128)(2,1)} %get-tuple-element.33), channel_id=1, source_target_pairs={{0,8},{4,12},{8,16},{12,20},{16,24},{20,28},{1,9},{5,13},{9,17},{1... | collective-permute-start | bytes 221192 | tf_op jit(solution)/shard_map/ppermute | solution.py:563
  76.5 1.6 %copy-start.5 = (bf16[3,288,128]{2,1,0:T(8,128)(2,1)}, bf16[3,288,128]{2,1,0:T(8,128)(2,1)S(1)}, u32[]{:S(2)}) copy-start(bf16[3,288,128]{2,1,0:T(8,128)(2,1)S(1)} %pad_maximum_fusion.1.mine_ref) | copy-start | bytes 663556
  76.5 1.5 %collective-permute-start.6 = (bf16[3,288,128]{2,1,0:T(8,128)(2,1)S(1)}, bf16[3,288,128]{2,1,0:T(8,128)(2,1)S(1)}, u32[]{:S(2)}, u32[]{:S(2)}) collective-permute-start(bf16[3,288,128]{2,1,0:T(8,128)(2,1)S(1)} %pad_maximum_fusion.1.mine_ref), channel_id=1, source_target_pairs={{0,4},{4,0},{8,12},{12,8},{16,20},{20,16},{24,28},{28,24},{1,5},{5... | collective-permute-start | bytes 663560 | tf_op jit(solution)/shard_map/ppermute | solution.py:569
  78.1 0.7 copy-start.7
  78.1 1.1 %copy-start.2 = (bf16[8,32,2048]{2,1,0:T(8,128)(2,1)}, bf16[8,32,2048]{2,1,0:T(8,128)(2,1)S(1)}, u32[]{:S(2)}) copy-start(bf16[8,32,2048]{2,1,0:T(8,128)(2,1)S(1)} %all-to-all-done.2) | copy-start | bytes 3145732

commit v3 on v2

--- a/solution.py
+++ b/solution.py
@@ -139,7 +139,8 @@
 
 ROWS = 8
 PAIR = 2 * ROWS
-BLOCK = 64
+BLOCK = 128
+SHARE = ROWS * LANES
 
 
 def spread(columns):
@@ -158,13 +159,8 @@
     return slice(tile * ROWS, (tile + 1) * ROWS)
 
 
-def by_register(rate_ref, rates):
-    states = rate_ref.shape[0]
-    count = rates.shape[0] // states
-    for n in range(states):
-        for h in range(count):
-            tiles = [rate_ref[n : n + 1, lane(h * ROWS + j)] for j in range(ROWS)]
-            rates[n * count + h] = jnp.concatenate(tiles, axis=0) * (-LOG2E)
+def by_register(rate_ref, n):
+    return jnp.concatenate([rate_ref[n : n + 1, lane(j)] for j in range(ROWS)], axis=0) * (-LOG2E)
 
 
 def local_kernel(
@@ -176,6 +172,7 @@
     inner_ref,
     y_ref,
     sum_ref,
+    product_ref,
     state_ref,
     low_cols,
     bc_spread,
@@ -186,24 +183,29 @@
     carry,
 ):
     tok = proj_ref.shape[1]
-    block, channels = inner_ref.shape
+    block = inner_ref.shape[0]
     states = rate_ref.shape[0]
+    stored = product_ref.shape[2] // ROWS
     low_rank = dtw_ref.shape[0]
-    tiles = channels // LANES
-    count = tiles // ROWS
     starts, _ = doc_edges(lengths_ref)
-    at = pl.program_id(0)
-
-    @pl.when(at == 0)
+    at = pl.program_id(1)
+
+    @pl.when((pl.program_id(0) == 0) & (at == 0))
     def _():
         low_cols[...] = proj_ref[:low_rank, :].astype(jnp.float32).T.astype(jnp.bfloat16)
         bc_spread[...] = spread(proj_ref[low_rank:, :].astype(jnp.float32).T)
-        by_register(rate_ref, rates)
-        carry[...] = jnp.zeros_like(carry)
-        for first in range(0, tiles, 4):
-            cols = slice(first * LANES, (first + 4) * LANES)
+
+    @pl.when(at == 0)
+    def _():
+        for n in range(states):
+            rates[n] = by_register(rate_ref, n)
+        for i in range(states + stored + 1):
+            carry[i] = jnp.full((ROWS, LANES), 1.0 if states <= i < states + stored else 0.0, jnp.float32)
+        half = ROWS // 2
+        for first in range(0, ROWS, half):
+            cols = slice(first * LANES, (first + half) * LANES)
             part = jnp.dot(low_cols[...], dtw_ref[:, cols], preferred_element_type=jnp.float32)
-            for i in range(4):
+            for i in range(half):
                 raw[:, sublanes(first + i), :] = part[:, lane(i)].reshape(tok // ROWS, ROWS, LANES)
 
     def steps(pair, unused):
@@ -211,7 +213,7 @@
         places = lax.axis_index("seq") * tok + at * block + pair * PAIR
         places = places + lax.broadcasted_iota(jnp.int32, (PAIR, LANES), 0)
         at_start = places == doc_start(places, starts)
-        for tile in range(tiles):
+        for tile in range(ROWS):
             inner = inner_ref[rows, lane(tile)].astype(jnp.float32)
             bias = bias_ref[:, lane(tile)]
             for k in range(2):
@@ -224,80 +226,90 @@
     lax.fori_loop(0, block // PAIR, steps, 0)
 
     def scan(t8, held):
-        held, total = list(held[0]), list(held[1])
-        for first in range(0, ROWS, 4):
+        held, product, total = list(held[0]), list(held[1]), held[2]
+        for first in range(0, ROWS, 2):
             done = []
-            for r in range(first, first + 4):
+            for r in range(first, first + 2):
                 token = at * block + t8 * ROWS + r
-                picked = [pl.ds(r + h * ROWS * ROWS, ROWS, stride=ROWS) for h in range(count)]
-                step = [step_tiles[t8, rows, :] for rows in picked]
-                drive = [drive_tiles[t8, rows, :] for rows in picked]
-                out = [None] * count
+                picked = pl.ds(r, ROWS, stride=ROWS)
+                step = step_tiles[t8, picked, :]
+                drive = drive_tiles[t8, picked, :]
+                out = None
                 for n in range(states):
-                    b_row = bc_spread[token, n : n + 1, :]
-                    c_row = bc_spread[token, states + n : states + n + 1, :]
-                    for h in range(count):
-                        i = n * count + h
-                        held[i] = jnp.exp2(rates[i] * step[h]) * held[i] + b_row * drive[h]
-                        term = c_row * held[i]
-                        out[h] = term if out[h] is None else out[h] + term
-                total = [so_far + more for so_far, more in zip(total, step)]
-                done.append((out, total))
-            for k, (out, so_far) in enumerate(done):
-                for h in range(count):
-                    y_ref[t8 * ROWS + first + k, sublanes(h), :] = out[h]
-                    sum_ref[t8 * ROWS + first + k, sublanes(h), :] = so_far[h]
-        return held, total
-
-    kept = states * count
-    held = ([carry[i] for i in range(kept)], [carry[kept + h] for h in range(count)])
-    held, total = lax.fori_loop(0, block // ROWS, scan, held)
-    for i, value in enumerate(held + total):
+                    decay = jnp.exp2(rates[n] * step)
+                    held[n] = decay * held[n] + bc_spread[token, n : n + 1, :] * drive
+                    if n < stored:
+                        product[n] = decay * product[n]
+                    term = bc_spread[token, states + n : states + n + 1, :] * held[n]
+                    out = term if out is None else out + term
+                total = total + step
+                done.append((out, total, list(product)))
+            for k, (out, so_far, products) in enumerate(done):
+                row = t8 * ROWS + first + k
+                y_ref[row] = out
+                sum_ref[row] = so_far
+                for n in range(0, stored, 2):
+                    both = jnp.concatenate(products[n : n + 2], axis=0).astype(jnp.bfloat16)
+                    product_ref[0, row, n * ROWS : (n + 2) * ROWS, :] = both
+        return held, product, total
+
+    held = (
+        [carry[n] for n in range(states)],
+        [carry[states + n] for n in range(stored)],
+        carry[states + stored],
+    )
+    held, product, total = lax.fori_loop(0, block // ROWS, scan, held)
+    for i, value in enumerate(held + product + [total]):
         carry[i] = value
 
-    @pl.when(at == pl.num_programs(0) - 1)
-    def _():
-        state_ref[: states * tiles, :] = jnp.concatenate(held, axis=0).astype(jnp.bfloat16)
-        whole = jnp.concatenate(total, axis=0)
-        high = whole.astype(jnp.bfloat16).astype(jnp.float32)
-        state_ref[states * tiles :, :] = jnp.concatenate([high, whole - high], axis=0).astype(jnp.bfloat16)
+    @pl.when(at == pl.num_programs(1) - 1)
+    def _():
+        state_ref[0, : states * ROWS, :] = jnp.concatenate(held, axis=0).astype(jnp.bfloat16)
+        high = total.astype(jnp.bfloat16).astype(jnp.float32)
+        state_ref[0, states * ROWS :, :] = jnp.concatenate([high, total - high], axis=0).astype(jnp.bfloat16)
 
 
 def local_scan(lengths, projected, dt_weight, dt_bias, decay_rate, inner_act):
     tok, channels = inner_act.shape
     low_rank = dt_weight.shape[0]
     states = decay_rate.shape[0]
-    tiles = channels // LANES
-    count = tiles // ROWS
-    whole = lambda a: pl.BlockSpec(a.shape, lambda i: (0,) * a.ndim)
-    bias = dt_bias.reshape(1, channels)
-    by_token = pl.BlockSpec((BLOCK, tiles, LANES), lambda i: (i, 0, 0))
-    state_rows = (states + 2) * tiles
+    shares = channels // SHARE
+    stored = states // 2
+    whole = lambda a: pl.BlockSpec(a.shape, lambda s, t: (0,) * a.ndim)
+    by_share = lambda rows: pl.BlockSpec((rows, SHARE), lambda s, t: (0, s))
+    by_token = pl.BlockSpec((BLOCK, ROWS, LANES), lambda s, t: (t, s, 0))
+    state_rows = (states + 2) * ROWS
     return pl.pallas_call(
         local_kernel,
-        grid=(tok // BLOCK,),
+        grid=(shares, tok // BLOCK),
         in_specs=[
             pl.BlockSpec(memory_space=pltpu.SMEM),
             whole(projected),
-            whole(dt_weight),
-            whole(bias),
-            whole(decay_rate),
-            pl.BlockSpec((BLOCK, channels), lambda i: (i, 0)),
-        ],
-        out_specs=[by_token, by_token, pl.BlockSpec((state_rows, LANES), lambda i: (0, 0))],
+            by_share(low_rank),
+            by_share(1),
+            by_share(states),
+            pl.BlockSpec((BLOCK, SHARE), lambda s, t: (t, s)),
+        ],
+        out_specs=[
+            by_token,
+            by_token,
+            pl.BlockSpec((1, BLOCK, stored * ROWS, LANES), lambda s, t: (s, t, 0, 0)),
+            pl.BlockSpec((1, state_rows, LANES), lambda s, t: (s, 0, 0)),
+        ],
         out_shape=[
-            jax.ShapeDtypeStruct((tok, tiles, LANES), jnp.float32),
-            jax.ShapeDtypeStruct((tok, tiles, LANES), jnp.float32),
-            jax.ShapeDtypeStruct((state_rows, LANES), jnp.bfloat16),
+            jax.ShapeDtypeStruct((tok, shares * ROWS, LANES), jnp.float32),
+            jax.ShapeDtypeStruct((tok, shares * ROWS, LANES), jnp.float32),
+            jax.ShapeDtypeStruct((shares, tok, stored * ROWS, LANES), jnp.bfloat16),
+            jax.ShapeDtypeStruct((shares, state_rows, LANES), jnp.bfloat16),
         ],
         scratch_shapes=[
             pltpu.VMEM((tok, low_rank), jnp.bfloat16),
             pltpu.VMEM((tok, 2 * states, LANES), jnp.float32),
-            pltpu.VMEM((tok // ROWS, tiles * ROWS, LANES), jnp.float32),
-            pltpu.VMEM((states * count, ROWS, LANES), jnp.float32),
-            pltpu.VMEM((BLOCK // ROWS, tiles * ROWS, LANES), jnp.float32),
-            pltpu.VMEM((BLOCK // ROWS, tiles * ROWS, LANES), jnp.float32),
-            pltpu.VMEM(((states + 1) * count, ROWS, LANES), jnp.float32),
+            pltpu.VMEM((tok // ROWS, ROWS * ROWS, LANES), jnp.float32),
+            pltpu.VMEM((states, ROWS, LANES), jnp.float32),
+            pltpu.VMEM((BLOCK // ROWS, ROWS * ROWS, LANES), jnp.float32),
+            pltpu.VMEM((BLOCK // ROWS, ROWS * ROWS, LANES), jnp.float32),
+            pltpu.VMEM((states + stored + 1, ROWS, LANES), jnp.float32),
         ],
         compiler_params=pltpu.CompilerParams(vmem_limit_bytes=VMEM_MOST),
         cost_estimate=pl.CostEstimate(
@@ -306,7 +318,7 @@
             transcendentals=tok * channels * states,
         ),
         name="local_scan",
-    )(lengths, projected, dt_weight, bias, decay_rate, inner_act)
+    )(lengths, projected, dt_weight, dt_bias.reshape(1, channels), decay_rate, inner_act)
 
 
 def join_kernel(
@@ -315,6 +327,7 @@
     proj_ref,
     y_ref,
     sum_ref,
+    product_ref,
     inner_ref,
     z_ref,
     rate_ref,
@@ -329,28 +342,28 @@
     entering,
     rows_tiles,
 ):
-    block, channels = z_ref.shape
+    block = z_ref.shape[0]
     states = rate_ref.shape[0]
-    tiles = channels // LANES
-    count = tiles // ROWS
-    kept = states * count
-    at = pl.program_id(0)
+    stored = product_ref.shape[2] // ROWS
+    at = pl.program_id(1)
+
+    @pl.when((pl.program_id(0) == 0) & (at == 0))
+    def _():
+        c_spread[...] = spread(proj_ref[low_rank + states :, :].astype(jnp.float32).T)
 
     @pl.when(at == 0)
     def _():
-        c_spread[...] = spread(proj_ref[low_rank + states :, :].astype(jnp.float32).T)
-        by_register(rate_ref, rates)
+        rate = [by_register(rate_ref, n) for n in range(states)]
         odd = lax.rem(lax.axis_index("seq"), 2)
-        state = [jnp.zeros((ROWS, LANES), jnp.float32)] * kept
+        state = [jnp.zeros((ROWS, LANES), jnp.float32)] * states
         for back in range(reach, 0, -1):
             ref, which = (mine_ref, back // 2) if back % 2 == 0 else (theirs_ref, (back + 1) // 2 - odd)
-            sent = ref[which].astype(jnp.float32)
-            totals = sent[states * tiles : (states + 1) * tiles] + sent[(states + 1) * tiles :]
-            state = [
-                jnp.exp2(rates[i] * totals[sublanes(i % count)]) * state[i] + sent[sublanes(i)] for i in range(kept)
-            ]
-        for i in range(kept):
-            entering[i] = state[i]
+            sent = ref[which, 0].astype(jnp.float32)
+            total = sent[sublanes(states)] + sent[sublanes(states + 1)]
+            state = [jnp.exp2(rate[n] * total) * state[n] + sent[sublanes(n)] for n in range(states)]
+        for n in range(states):
+            rates[n] = rate[n]
+            entering[n] = state[n]
 
     regrouped_ref[...] = moved_ref[...]
 
@@ -358,18 +371,20 @@
         rows = pl.ds(pl.multiple_of(pair * PAIR, PAIR), PAIR)
         for k in range(2):
             first = pair * PAIR + k * ROWS
-            total = [[sum_ref[first + r, sublanes(h), :] for h in range(count)] for r in range(ROWS)]
-            out = [[y_ref[first + r, sublanes(h), :] for h in range(count)] for r in range(ROWS)]
-            for n in range(states):
+            total = [sum_ref[first + r] for r in range(ROWS)]
+            out = [y_ref[first + r] for r in range(ROWS)]
+            for n in range(states // 2):
                 for r in range(ROWS):
-                    c_row = c_spread[at * block + first + r, n : n + 1, :]
-                    for h in range(count):
-                        i = n * count + h
-                        out[r][h] += jnp.exp2(rates[i] * total[r][h]) * entering[i] * c_row
+                    c_row = lambda m: c_spread[at * block + first + r, m : m + 1, :]
+                    if n % 2 == 0 and n < stored:
+                        both = product_ref[0, first + r, n * ROWS : (n + 2) * ROWS, :].astype(jnp.float32)
+                        for m in range(2):
+                            out[r] += both[sublanes(m)] * entering[n + m] * c_row(n + m)
+                    m = states // 2 + n
+                    out[r] += jnp.exp2(rates[m] * total[r]) * entering[m] * c_row(m)
             for r in range(ROWS):
-                for h in range(count):
-                    rows_tiles[k, pl.ds(r + h * ROWS * ROWS, ROWS, stride=ROWS), :] = out[r][h]
-        for tile in range(tiles):
+                rows_tiles[k, pl.ds(r, ROWS, stride=ROWS), :] = out[r]
+        for tile in range(ROWS):
             cols = lane(tile)
             z = z_ref[rows, cols].astype(jnp.float32)
             gate = z * (0.5 + 0.5 * jnp.tanh(0.5 * z))
@@ -381,37 +396,39 @@
     lax.fori_loop(0, block // PAIR, body, 0)
 
 
-def join_states(projected, y, sums, inner_act, z_branch, decay_rate, skip_gain, moved, mine, theirs, low_rank, reach):
+def join_states(
+    projected, y, sums, products, inner_act, z_branch, decay_rate, skip_gain, moved, mine, theirs, low_rank, reach
+):
     tok, channels = z_branch.shape
     states = decay_rate.shape[0]
-    tiles = channels // LANES
-    count = tiles // ROWS
-    whole = lambda a: pl.BlockSpec(a.shape, lambda i: (0,) * a.ndim)
-    by_token = pl.BlockSpec((BLOCK, tiles, LANES), lambda i: (i, 0, 0))
-    by_row = pl.BlockSpec((BLOCK, channels), lambda i: (i, 0))
-    skip = skip_gain.reshape(1, channels)
+    whole = lambda a: pl.BlockSpec(a.shape, lambda s, t: (0,) * a.ndim)
+    by_share = lambda rows: pl.BlockSpec((rows, SHARE), lambda s, t: (0, s))
+    by_token = pl.BlockSpec((BLOCK, ROWS, LANES), lambda s, t: (t, s, 0))
+    by_row = pl.BlockSpec((BLOCK, SHARE), lambda s, t: (t, s))
+    sent = pl.BlockSpec((mine.shape[0], 1) + mine.shape[2:], lambda s, t: (0, s, 0, 0))
     return pl.pallas_call(
         functools.partial(join_kernel, low_rank, reach),
-        grid=(tok // BLOCK,),
+        grid=(channels // SHARE, tok // BLOCK),
         in_specs=[
             whole(projected),
             by_token,
             by_token,
+            pl.BlockSpec((1, BLOCK) + products.shape[2:], lambda s, t: (s, t, 0, 0)),
             by_row,
             by_row,
-            whole(decay_rate),
-            whole(skip),
+            by_share(states),
+            by_share(1),
             by_row,
-            whole(mine),
-            whole(theirs),
+            sent,
+            sent,
         ],
         out_specs=[by_row, by_row],
         out_shape=[jax.ShapeDtypeStruct((tok, channels), jnp.bfloat16)] * 2,
         scratch_shapes=[
             pltpu.VMEM((tok, states, LANES), jnp.float32),
-            pltpu.VMEM((states * count, ROWS, LANES), jnp.float32),
-            pltpu.VMEM((states * count, ROWS, LANES), jnp.float32),
-            pltpu.VMEM((2, tiles * ROWS, LANES), jnp.float32),
+            pltpu.VMEM((states, ROWS, LANES), jnp.float32),
+            pltpu.VMEM((states, ROWS, LANES), jnp.float32),
+            pltpu.VMEM((2, ROWS * ROWS, LANES), jnp.float32),
         ],
         compiler_params=pltpu.CompilerParams(vmem_limit_bytes=VMEM_MOST),
         cost_estimate=pl.CostEstimate(
@@ -420,7 +437,19 @@
             transcendentals=tok * channels * states,
         ),
         name="join_states",
-    )(projected, y, sums, inner_act, z_branch, decay_rate, skip, moved, mine, theirs)
+    )(
+        projected,
+        y,
+        sums,
+        products,
+        inner_act,
+        z_branch,
+        decay_rate,
+        skip_gain.reshape(1, channels),
+        moved,
+        mine,
+        theirs,
+    )
 
 
 def attend_kernel(kv_local, first_group, lengths_ref, place_ref, q_ref, mine_ref, theirs_ref, *refs):
@@ -619,11 +648,23 @@
     projected, attended = fence((projected, attended))
     regrouped = lax.all_to_all(attended, "seq", split_axis=0, concat_axis=0, tiled=True)
 
-    y, sums, state = local_scan(lengths, projected, dt_weight, dt_bias, decay_rate, inner_act)
+    y, sums, products, state = local_scan(lengths, projected, dt_weight, dt_bias, decay_rate, inner_act)
     own, other = with_partner(even_back(state, reach))
     return tuple(
         join_states(
-            projected, y, sums, inner_act, z_branch, decay_rate, skip_gain, regrouped, own, other, low_rank, reach
+            projected,
+            y,
+            sums,
+            products,
+            inner_act,
+            z_branch,
+            decay_rate,
+            skip_gain,
+            regrouped,
+            own,
+            other,
+            low_rank,
+            reach,
         )
     )
 

time: 89.7 us -> 93.1 us (1.038)
  Pallas kernels: 37.2 us -> 40.7 us
    pallas_call x2, Pallas kernels: 23.7 us -> 27.2 us  [the longest x1 16.4 us: local_scan(): pl.pallas_call(local_kernel, grid=(shares, tok // BLOCK), in_specs=[pl.Bl...]
  transfers between devices with their start and end apart: 10 -> 10, of which waited for: 5 -> 5; matrix products, arithmetic and copies ran while one was open for 1% -> 1% of each run, Pallas kernels for 29% -> 31%
where the time goes in v3:
time: 93.1 us; the launch traced here: 92.5 us
  Pallas kernels  40.7 us (44%)
  starting transfers between devices  31.1 us (33%)
  waiting for transfers between devices  16.4 us (18%)
  local copies, waits for them, and re-layouts  2.42 us (3%)
  other arithmetic  1.05 us (1%)
    ppermute x5, starting transfers between devices, shifted(): lax.ppermute(value, 'seq', [(source, source + steps) for source in range(...  17.5 us
    pallas_call x1, Pallas kernels, local_scan(): pl.pallas_call(local_kernel, grid=(shares, tok // BLOCK), in_specs=[pl.Bl...  16.4 us
    pallas_call x1, Pallas kernels, join_states(): pl.pallas_call(functools.partial(join_kernel, low_rank, reach), grid=(cha...  10.7 us
    all_to_all x1, waiting for transfers between devices, local(): lax.all_to_all(partial, 'mp', split_axis=0, concat_axis=0, tiled=True)  6.5 us
    pallas_call x1, Pallas kernels, conv_project(): pl.pallas_call(conv_kernel, grid=(channels // chunk,), in_specs=[pl.Block...  6.01 us
    pallas_call x2, Pallas kernels, attend(): pl.pallas_call(functools.partial(attend_kernel, kv_local, groups[0]), gri...  5.8 us
    all_to_all x1, starting transfers between devices, local(): lax.all_to_all(partial, 'mp', split_axis=0, concat_axis=0, tiled=True)  4.87 us
    all_to_all x1, starting transfers between devices, local(): lax.all_to_all(attended, 'seq', split_axis=0, concat_axis=0, tiled=True)  4.52 us
  transfers between devices with their start and end apart: 10, of which 5 were waited for; matrix products, arithmetic and copies ran while one was open for 1% of the time, Pallas kernels for 31%

profile of v3, /device:TPU:0, one launch (start us, length us, event | category | flops | bytes accessed | tf_op | source)
XLA Modules:
  0.0 92.5 jit_solution(9736224118856035298)
XLA Ops:
  0.6 1.7 %pack.1 = (bf16[16,2048]{1,0:T(8,128)(2,1)}, bf16[256,512]{1,0:T(8,128)(2,1)}) custom-call(bf16[256,2048]{1,0:T(8,128)(2,1)} %x_ref.3, bf16[256,256]{1,0:T(8,128)(2,1)} %k_ref.1, bf16[256,256]{1,0:T(8,128)(2,1)} %v_ref.1), custom_call_target="tpu_custom_call" | custom-call | bytes 1048576 | tf_op jit(solution)/shard_map/pack/pallas_call | solution.py:51
  2.4 2.3 %collective-permute-start = (bf16[16,2048]{1,0:T(8,128)(2,1)}, bf16[16,2048]{1,0:T(8,128)(2,1)S(1)}, u32[]{:S(2)}, u32[]{:S(2)}) collective-permute-start(bf16[16,2048]{1,0:T(8,128)(2,1)} %get-tuple-element.19), channel_id=1, source_target_pairs={{0,4},{4,8},{8,12},{12,16},{16,20},{20,24},{24,28},{1,5},{5,9},{9,... | collective-permute-start | bytes 196616 | tf_op jit(solution)/shard_map/ppermute | solution.py:592
  4.7 4.4 %collective-permute-start.2 = (bf16[256,512]{1,0:T(8,128)(2,1)}, bf16[256,512]{1,0:T(8,128)(2,1)S(1)}, u32[]{:S(2)}, u32[]{:S(2)}) collective-permute-start(bf16[256,512]{1,0:T(8,128)(2,1)} %get-tuple-element.22), channel_id=1, source_target_pairs={{0,16},{4,20},{8,24},{12,28},{1,17},{5,21},{9,25},{13,29},{2,18},{... | collective-permute-start | bytes 786440 | tf_op jit(solution)/shard_map/ppermute | solution.py:592
  9.2 3.4 %collective-permute-start.1 = (bf16[256,512]{1,0:T(8,128)(2,1)}, bf16[256,512]{1,0:T(8,128)(2,1)S(1)}, u32[]{:S(2)}, u32[]{:S(2)}) collective-permute-start(bf16[256,512]{1,0:T(8,128)(2,1)} %get-tuple-element.22), channel_id=1, source_target_pairs={{0,8},{4,12},{8,16},{12,20},{16,24},{20,28},{1,9},{5,13},{9,17},{1... | collective-permute-start | bytes 786440 | tf_op jit(solution)/shard_map/ppermute | solution.py:592
  12.6 0.6 copy-done.8
  13.2 6.0 %conv_project.1 = (bf16[256,2048]{1,0:T(8,128)(2,1)}, bf16[544,256]{1,0:T(8,128)(2,1)}) custom-call(s32[4]{0:T(128)} %lengths_ref.7, bf16[256,2048]{1,0:T(8,128)(2,1)} %x_ref.3, bf16[16,2048]{1,0:T(8,128)(2,1)} %copy-done.8, f32[4,2048]{1,0:T(4,128)} %w_ref.1, f32[1,2048]{1,0:T(1,128)} %bitcast.30, bf16[544,2048]{1,0:T(8,128)(2,1)} %bitcast.29), custom_call_target="tpu_custom_call" | custom-call | flops 22817013760 | bytes 4194304 | tf_op jit(solution)/shard_map/conv_project/pallas_call | solution.py:109
  19.2 0.0 copy-start
  19.3 0.0 copy-start.1
  19.3 1.9 %collective-permute-done.2 = bf16[256,512]{1,0:T(8,128)(2,1)S(1)} collective-permute-done((bf16[256,512]{1,0:T(8,128)(2,1)}, bf16[256,512]{1,0:T(8,128)(2,1)S(1)}, u32[]{:S(2)}, u32[]{:S(2)}) %collective-permute-start.2) | collective-permute-done | bytes 262176 | tf_op jit(solution)/shard_map/ppermute | solution.py:592
  21.2 0.0 collective-permute-done.1
  21.2 0.1 pad_maximum_fusion.mine_ref
  21.3 0.8 collective-permute-start.3
  22.1 4.9 %all-to-all-start = ((bf16[4,136,256]{2,1,0:T(8,128)(2,1)}), bf16[4,136,256]{2,1,0:T(8,128)(2,1)S(1)}, u32[]{:S(2)}, u32[]{:S(2)}) async-start(bf16[4,136,256]{2,1,0:T(8,128)(2,1)} %bitcast.21), calls=%async_computation | async-start | bytes 557056 | tf_op jit(solution)/shard_map/all_to_all | solution.py:637
  27.0 0.0 collective-permute-done.3.theirs_ref
  27.0 2.9 %attend.2.refs_0_ = bf16[256,2048]{1,0:T(8,128)(2,1)} custom-call(s32[4]{0:T(128)S(1)} %copy-done.1, s32[8,256]{1,0:T(8,128)S(1)} %reshape.30.place_ref, bf16[256,2048]{1,0:T(8,128)(2,1)S(1)} %copy-done, bf16[3,256,512]{2,1,0:T(8,128)(2,1)S(1)} %pad_maximum_fusion.mine_ref, bf16[3,256,512]{2,1,0:T(8,128)(2,1)S(1)} %collective-permute-done.3.theirs_ref), custom_call_target="tpu_custom_call" | custom-call | flops 262144 | bytes 262144 | tf_op jit(solution)/shard_map/attend/pallas_call | solution.py:569
  29.9 6.5 %all-to-all-done = bf16[4,136,256]{2,1,0:T(8,128)(2,1)S(1)} async-done(((bf16[4,136,256]{2,1,0:T(8,128)(2,1)}), bf16[4,136,256]{2,1,0:T(8,128)(2,1)S(1)}, u32[]{:S(2)}, u32[]{:S(2)}) %all-to-all-start) | async-done | bytes 278560 | tf_op jit(solution)/shard_map/all_to_all | solution.py:637
  36.4 0.7 broadcast_in_dim.2
  37.2 3.5 %all-to-all-start.1 = ((bf16[4,136,256]{2,1,0:T(8,128)(2,1)}), bf16[4,136,256]{2,1,0:T(8,128)(2,1)S(1)}, u32[]{:S(2)}, u32[]{:S(2)}) async-start(bf16[4,136,256]{2,1,0:T(8,128)(2,1)} %bitcast.9), calls=%async_computation.1 | async-start | bytes 557056 | tf_op jit(solution)/shard_map/all_to_all | solution.py:645
  40.6 2.9 %attend.3 = bf16[256,2048]{1,0:T(8,128)(2,1)} custom-call(s32[4]{0:T(128)S(1)} %copy-done.1, s32[8,256]{1,0:T(8,128)S(1)} %reshape.30.place_ref, bf16[256,2048]{1,0:T(8,128)(2,1)S(1)} %copy-done, bf16[3,256,512]{2,1,0:T(8,128)(2,1)S(1)} %pad_maximum_fusion.mine_ref, ...), custom_call_target="tpu_custom_call", output_to_operand_aliasing={{}: (5, {})} | custom-call | flops 262144 | bytes 262144 | tf_op jit(solution)/shard_map/attend/pallas_call | solution.py:569
  43.5 4.2 %all-to-all-done.1 = bf16[4,136,256]{2,1,0:T(8,128)(2,1)S(1)} async-done(((bf16[4,136,256]{2,1,0:T(8,128)(2,1)}), bf16[4,136,256]{2,1,0:T(8,128)(2,1)S(1)}, u32[]{:S(2)}, u32[]{:S(2)}) %all-to-all-start.1) | async-done | bytes 278560 | tf_op jit(solution)/shard_map/all_to_all | solution.py:645
  47.7 4.5 %all-to-all-start.2 = ((bf16[8,32,2048]{2,1,0:T(8,128)(2,1)}), bf16[8,32,2048]{2,1,0:T(8,128)(2,1)S(1)}, u32[]{:S(2)}, u32[]{:S(2)}) async-start(bf16[8,32,2048]{2,1,0:T(8,128)(2,1)} %bitcast.13), calls=%async_computation.2 | async-start | bytes 2097152 | tf_op jit(solution)/shard_map/all_to_all | solution.py:649
  52.2 16.4 %local_scan.1 = (f32[256,16,128]{2,1,0:T(8,128)}, f32[256,16,128]{2,1,0:T(8,128)}, bf16[2,256,64,128]{3,2,1,0:T(8,128)(2,1)}, bf16[2,144,128]{2,1,0:T(8,128)(2,1)}) custom-call(s32[4]{0:T(128)} %lengths_ref.7, bf16[544,256]{1,0:T(8,128)(2,1)} %bitcast.19, bf16[512,2048]{1,0:T(8,128)(2,1)} %dtw_ref.1, f32[1,2048]{1,0:T(1,128)} %bitcast.31, ...), custom_call_target="tpu_custom_call" | custom-call | flops 100663296 | bytes 6291456 | tf_op jit(solution)/shard_map/local_scan/pallas_call | solution.py:282
  68.7 4.1 %collective-permute-start.5 = (bf16[2,144,128]{2,1,0:T(8,128)(2,1)}, bf16[2,144,128]{2,1,0:T(8,128)(2,1)S(1)}, u32[]{:S(2)}, u32[]{:S(2)}) collective-permute-start(bf16[2,144,128]{2,1,0:T(8,128)(2,1)} %get-tuple-element.35), channel_id=1, source_target_pairs={{0,16},{4,20},{8,24},{12,28},{1,17},{5,21},{9,25},{13,29},{2,18},{... | collective-permute-start | bytes 221192 | tf_op jit(solution)/shard_map/ppermute | solution.py:592
  72.8 3.1 %collective-permute-start.4 = (bf16[2,144,128]{2,1,0:T(8,128)(2,1)}, bf16[2,144,128]{2,1,0:T(8,128)(2,1)S(1)}, u32[]{:S(2)}, u32[]{:S(2)}) collective-permute-start(bf16[2,144,128]{2,1,0:T(8,128)(2,1)} %get-tuple-element.35), channel_id=1, source_target_pairs={{0,8},{4,12},{8,16},{12,20},{16,24},{20,28},{1,9},{5,13},{9,17},{1... | collective-permute-start | bytes 221192 | tf_op jit(solution)/shard_map/ppermute | solution.py:592
  76.0 2.3 %collective-permute-done.4 = bf16[2,144,128]{2,1,0:T(8,128)(2,1)S(1)} collective-permute-done((bf16[2,144,128]{2,1,0:T(8,128)(2,1)}, bf16[2,144,128]{2,1,0:T(8,128)(2,1)S(1)}, u32[]{:S(2)}, u32[]{:S(2)}) %collective-permute-start.4) | collective-permute-done | bytes 73760 | tf_op jit(solution)/shard_map/ppermute | solution.py:592
  78.2 0.9 pad_maximum_fusion.1.mine_ref
  79.1 0.1 collective-permute-start.6
  79.2 1.5 %collective-permute-done.6.theirs_ref = bf16[3,2,144,128]{3,2,1,0:T(8,128)(2,1)S(1)} collective-permute-done((bf16[3,2,144,128]{3,2,1,0:T(8,128)(2,1)S(1)}, bf16[3,2,144,128]{3,2,1,0:T(8,128)(2,1)S(1)}, u32[]{:S(2)}, u32[]{:S(2)}) %collective-permute-start.6) | collective-permute-done | bytes 221216 | tf_op jit(solution)/shard_map/ppermute | solution.py:598
  80.7 0.0 all-to-all-done.2
  80.7 0.7 copy-done.6
  81.4 0.4 copy-done.2
  81.7 10.7 %join_states.1 = (bf16[256,2048]{1,0:T(8,128)(2,1)}, bf16[256,2048]{1,0:T(8,128)(2,1)}) custom-call(bf16[544,256]{1,0:T(8,128)(2,1)} %bitcast.20, f32[256,16,128]{2,1,0:T(8,128)} %get-tuple-element.31.y_ref, f32[256,16,128]{2,1,0:T(8,128)} %get-tuple-element.32.sum_ref, bf16[2,256,64,128]{3,2,1,0:T(8,128)(2,1)} %get-tuple-element.33.product_ref, ...), custom_call_target="tpu_custom_call" | custom-call | flops 67108864 | bytes 7340032 | tf_op jit(solution)/shard_map/join_states/pallas_call | solution.py:409
  (18 shorter events, 0.1 us)
Async XLA Ops:
  2.4 10.2 %collective-permute-start = (bf16[16,2048]{1,0:T(8,128)(2,1)}, bf16[16,2048]{1,0:T(8,128)(2,1)S(1)}, u32[]{:S(2)}, u32[]{:S(2)}) collective-permute-start(bf16[16,2048]{1,0:T(8,128)(2,1)} %get-tuple-element.19), channel_id=1, source_target_pairs={{0,4},{4,8},{8,12},{12,16},{16,20},{20,24},{24,28},{1,5},{5,9},{9,... | collective-permute-start | bytes 196616 | tf_op jit(solution)/shard_map/ppermute | solution.py:592
  4.7 16.5 %collective-permute-start.2 = (bf16[256,512]{1,0:T(8,128)(2,1)}, bf16[256,512]{1,0:T(8,128)(2,1)S(1)}, u32[]{:S(2)}, u32[]{:S(2)}) collective-permute-start(bf16[256,512]{1,0:T(8,128)(2,1)} %get-tuple-element.22), channel_id=1, source_target_pairs={{0,16},{4,20},{8,24},{12,28},{1,17},{5,21},{9,25},{13,29},{2,18},{... | collective-permute-start | bytes 786440 | tf_op jit(solution)/shard_map/ppermute | solution.py:592
  9.2 12.0 %collective-permute-start.1 = (bf16[256,512]{1,0:T(8,128)(2,1)}, bf16[256,512]{1,0:T(8,128)(2,1)S(1)}, u32[]{:S(2)}, u32[]{:S(2)}) collective-permute-start(bf16[256,512]{1,0:T(8,128)(2,1)} %get-tuple-element.22), channel_id=1, source_target_pairs={{0,8},{4,12},{8,16},{12,20},{16,24},{20,28},{1,9},{5,13},{9,17},{1... | collective-permute-start | bytes 786440 | tf_op jit(solution)/shard_map/ppermute | solution.py:592
  12.6 0.6 copy-start.8
  13.2 8.0 %copy-start.5 = (bf16[256,512]{1,0:T(8,128)(2,1)S(1)}, bf16[256,512]{1,0:T(8,128)(2,1)}, u32[]{:S(2)}) copy-start(bf16[256,512]{1,0:T(8,128)(2,1)} %get-tuple-element.22) | copy-start | bytes 786436
  19.2 7.7 %copy-start.7 = (s32[2048]{0:T(1024)S(1)}, s32[2048]{0:T(1024)}, u32[]{:S(2)}) copy-start(s32[2048]{0:T(1024)} %param.27) | copy-start | bytes 24580
  19.2 7.7 %copy-start = (bf16[256,2048]{1,0:T(8,128)(2,1)S(1)}, bf16[256,2048]{1,0:T(8,128)(2,1)}, u32[]{:S(2)}) copy-start(bf16[256,2048]{1,0:T(8,128)(2,1)} %q_ref.3) | copy-start | bytes 3145732
  19.3 7.7 %copy-start.1 = (s32[4]{0:T(128)S(1)}, s32[4]{0:T(128)}, u32[]{:S(2)}) copy-start(s32[4]{0:T(128)} %lengths_ref.7) | copy-start | bytes 52
  21.3 5.7 %collective-permute-start.3 = (bf16[3,256,512]{2,1,0:T(8,128)(2,1)S(1)}, bf16[3,256,512]{2,1,0:T(8,128)(2,1)S(1)}, u32[]{:S(2)}, u32[]{:S(2)}) collective-permute-start(bf16[3,256,512]{2,1,0:T(8,128)(2,1)S(1)} %pad_maximum_fusion.mine_ref), channel_id=1, source_target_pairs={{0,4},{4,0},{8,12},{12,8},{16,20},{20,16},{24,28},{28,24},{1,5},{5... | collective-permute-start | bytes 2359304 | tf_op jit(solution)/shard_map/ppermute | solution.py:598
  22.1 14.3 %all-to-all-start = ((bf16[4,136,256]{2,1,0:T(8,128)(2,1)}), bf16[4,136,256]{2,1,0:T(8,128)(2,1)S(1)}, u32[]{:S(2)}, u32[]{:S(2)}) async-start(bf16[4,136,256]{2,1,0:T(8,128)(2,1)} %bitcast.21), calls=%async_computation | async-start | bytes 557056 | tf_op jit(solution)/shard_map/all_to_all | solution.py:637
  37.2 10.6 %all-to-all-start.1 = ((bf16[4,136,256]{2,1,0:T(8,128)(2,1)}), bf16[4,136,256]{2,1,0:T(8,128)(2,1)S(1)}, u32[]{:S(2)}, u32[]{:S(2)}) async-start(bf16[4,136,256]{2,1,0:T(8,128)(2,1)} %bitcast.9), calls=%async_computation.1 | async-start | bytes 557056 | tf_op jit(solution)/shard_map/all_to_all | solution.py:645
  47.7 4.5 %copy-start.3 = (bf16[4,136,256]{2,1,0:T(8,128)(2,1)}, bf16[4,136,256]{2,1,0:T(8,128)(2,1)S(1)}, u32[]{:S(2)}) copy-start(bf16[4,136,256]{2,1,0:T(8,128)(2,1)S(1)} %all-to-all-done.1) | copy-start | bytes 835588
  47.7 33.0 %all-to-all-start.2 = ((bf16[8,32,2048]{2,1,0:T(8,128)(2,1)}), bf16[8,32,2048]{2,1,0:T(8,128)(2,1)S(1)}, u32[]{:S(2)}, u32[]{:S(2)}) async-start(bf16[8,32,2048]{2,1,0:T(8,128)(2,1)} %bitcast.13), calls=%async_computation.2 | async-start | bytes 2097152 | tf_op jit(solution)/shard_map/all_to_all | solution.py:649
  68.7 7.3 %collective-permute-start.5 = (bf16[2,144,128]{2,1,0:T(8,128)(2,1)}, bf16[2,144,128]{2,1,0:T(8,128)(2,1)S(1)}, u32[]{:S(2)}, u32[]{:S(2)}) collective-permute-start(bf16[2,144,128]{2,1,0:T(8,128)(2,1)} %get-tuple-element.35), channel_id=1, source_target_pairs={{0,16},{4,20},{8,24},{12,28},{1,17},{5,21},{9,25},{13,29},{2,18},{... | collective-permute-start | bytes 221192 | tf_op jit(solution)/shard_map/ppermute | solution.py:592
  72.8 5.4 %collective-permute-start.4 = (bf16[2,144,128]{2,1,0:T(8,128)(2,1)}, bf16[2,144,128]{2,1,0:T(8,128)(2,1)S(1)}, u32[]{:S(2)}, u32[]{:S(2)}) collective-permute-start(bf16[2,144,128]{2,1,0:T(8,128)(2,1)} %get-tuple-element.35), channel_id=1, source_target_pairs={{0,8},{4,12},{8,16},{12,20},{16,24},{20,28},{1,9},{5,13},{9,17},{1... | collective-permute-start | bytes 221192 | tf_op jit(solution)/shard_map/ppermute | solution.py:592
  79.1 1.6 %copy-start.4 = (bf16[3,2,144,128]{3,2,1,0:T(8,128)(2,1)}, bf16[3,2,144,128]{3,2,1,0:T(8,128)(2,1)S(1)}, u32[]{:S(2)}) copy-start(bf16[3,2,144,128]{3,2,1,0:T(8,128)(2,1)S(1)} %pad_maximum_fusion.1.mine_ref) | copy-start | bytes 663556
  79.1 1.5 %collective-permute-start.6 = (bf16[3,2,144,128]{3,2,1,0:T(8,128)(2,1)S(1)}, bf16[3,2,144,128]{3,2,1,0:T(8,128)(2,1)S(1)}, u32[]{:S(2)}, u32[]{:S(2)}) collective-permute-start(bf16[3,2,144,128]{3,2,1,0:T(8,128)(2,1)S(1)} %pad_maximum_fusion.1.mine_ref), channel_id=1, source_target_pairs={{0,4},{4,0},{8,12},{12,8},{16,20},{20,16},{24,28},{28,24},{1,5},{5... | collective-permute-start | bytes 663560 | tf_op jit(solution)/shard_map/ppermute | solution.py:598
  80.7 0.7 copy-start.6
  80.7 1.0 %copy-start.2 = (bf16[8,32,2048]{2,1,0:T(8,128)(2,1)}, bf16[8,32,2048]{2,1,0:T(8,128)(2,1)S(1)}, u32[]{:S(2)}) copy-start(bf16[8,32,2048]{2,1,0:T(8,128)(2,1)S(1)} %all-to-all-done.2) | copy-start | bytes 3145732

commit v4 on v2

--- a/solution.py
+++ b/solution.py
@@ -15,6 +15,7 @@
 APART = 65536.0
 VMEM_LIMIT = 32 * 1024 * 1024
 VMEM_MOST = 56 * 1024 * 1024
+VMEM_NEARLY = 53 * 1024 * 1024 + 512 * 1024
 
 
 def doc_edges(lengths_ref):
@@ -129,7 +130,7 @@
             pltpu.VMEM((tok + HALO, chunk), jnp.float32),
             pltpu.VMEM((width, tok), jnp.float32),
         ],
-        compiler_params=pltpu.CompilerParams(vmem_limit_bytes=VMEM_MOST),
+        compiler_params=pltpu.CompilerParams(vmem_limit_bytes=VMEM_NEARLY),
         cost_estimate=pl.CostEstimate(
             flops=80 * tok * channels * width, bytes_accessed=8 * tok * channels, transcendentals=tok * channels
         ),
@@ -140,6 +141,7 @@
 ROWS = 8
 PAIR = 2 * ROWS
 BLOCK = 64
+GROUP = 8
 
 
 def spread(columns):
@@ -326,6 +328,7 @@
     regrouped_ref,
     c_spread,
     rates,
+    rates_twice,
     entering,
     rows_tiles,
 ):
@@ -350,7 +353,8 @@
                 jnp.exp2(rates[i] * totals[sublanes(i % count)]) * state[i] + sent[sublanes(i)] for i in range(kept)
             ]
         for i in range(kept):
-            entering[i] = state[i]
+            rates_twice[i] = jnp.concatenate([rates[i]] * 2, axis=0).astype(jnp.bfloat16)
+            entering[i] = jnp.concatenate([state[i]] * 2, axis=0).astype(jnp.bfloat16)
 
     regrouped_ref[...] = moved_ref[...]
 
@@ -358,17 +362,31 @@
         rows = pl.ds(pl.multiple_of(pair * PAIR, PAIR), PAIR)
         for k in range(2):
             first = pair * PAIR + k * ROWS
-            total = [[sum_ref[first + r, sublanes(h), :] for h in range(count)] for r in range(ROWS)]
-            out = [[y_ref[first + r, sublanes(h), :] for h in range(count)] for r in range(ROWS)]
-            for n in range(states):
-                for r in range(ROWS):
-                    c_row = c_spread[at * block + first + r, n : n + 1, :]
-                    for h in range(count):
-                        i = n * count + h
-                        out[r][h] += jnp.exp2(rates[i] * total[r][h]) * entering[i] * c_row
-            for r in range(ROWS):
-                for h in range(count):
-                    rows_tiles[k, pl.ds(r + h * ROWS * ROWS, ROWS, stride=ROWS), :] = out[r][h]
+            twos = [(first + r, first + r + 1) for r in range(0, ROWS, 2)]
+            shares = [(p, h) for p in range(len(twos)) for h in range(count)]
+            total = {
+                (p, h): jnp.concatenate([sum_ref[t, sublanes(h), :] for t in twos[p]], axis=0).astype(jnp.bfloat16)
+                for p, h in shares
+            }
+            out = {(p, h): jnp.concatenate([y_ref[t, sublanes(h), :] for t in twos[p]], axis=0) for p, h in shares}
+            for begin in range(0, states, GROUP):
+                part = {}
+                for n in range(begin, begin + GROUP):
+                    for p, two in enumerate(twos):
+                        c_rows = [
+                            jnp.broadcast_to(c_spread[at * block + t, n : n + 1, :], (ROWS, LANES)) for t in two
+                        ]
+                        c_both = jnp.concatenate(c_rows, axis=0).astype(jnp.bfloat16)
+                        for h in range(count):
+                            i = n * count + h
+                            term = jnp.exp2(rates_twice[i] * total[p, h]) * entering[i] * c_both
+                            part[p, h] = part[p, h] + term if (p, h) in part else term
+                for key in shares:
+                    out[key] = out[key] + part[key].astype(jnp.float32)
+            for p, h in shares:
+                for which in range(2):
+                    place = pl.ds(2 * p + which + h * ROWS * ROWS, ROWS, stride=ROWS)
+                    rows_tiles[k, place, :] = out[p, h][sublanes(which)]
         for tile in range(tiles):
             cols = lane(tile)
             z = z_ref[rows, cols].astype(jnp.float32)
@@ -410,10 +428,11 @@
         scratch_shapes=[
             pltpu.VMEM((tok, states, LANES), jnp.float32),
             pltpu.VMEM((states * count, ROWS, LANES), jnp.float32),
-            pltpu.VMEM((states * count, ROWS, LANES), jnp.float32),
+            pltpu.VMEM((states * count, PAIR, LANES), jnp.bfloat16),
+            pltpu.VMEM((states * count, PAIR, LANES), jnp.bfloat16),
             pltpu.VMEM((2, tiles * ROWS, LANES), jnp.float32),
         ],
-        compiler_params=pltpu.CompilerParams(vmem_limit_bytes=VMEM_MOST),
+        compiler_params=pltpu.CompilerParams(vmem_limit_bytes=VMEM_NEARLY),
         cost_estimate=pl.CostEstimate(
             flops=8 * tok * channels * states,
             bytes_accessed=14 * tok * channels,
@@ -431,7 +450,7 @@
     position = lax.axis_index("seq")
     odd = lax.rem(position, 2)
     anchor = position * tok
-    scale = HD**-0.5
+    scale = jnp.bfloat16(LOG2E * HD**-0.5)
     starts, ends = doc_edges(lengths_ref)
     lane = lax.broadcasted_iota(jnp.int32, (1, LANES), 1)
     first = jnp.full((1, LANES), 2**30, jnp.int32)
@@ -489,13 +508,13 @@
         return carry
 
     lax.fori_loop(1, earlier + 1, look, 0)
-    tops[...] = jnp.broadcast_to(jnp.max(tops[...], axis=1, keepdims=True) * scale, tops.shape)
+    tops[...] = jnp.broadcast_to(jnp.max(tops[...], axis=1, keepdims=True), tops.shape)
 
     def weighted(back):
         values = jnp.concatenate([rows_of(back, value_cols), jnp.ones((tok, HD), jnp.bfloat16)], axis=1)
         top = tops[...]
         weights = [
-            jnp.exp((scores[back, :, at : at + LANES] * scale - top).astype(jnp.bfloat16))
+            jnp.exp2((scores[back, :, at : at + LANES] - top).astype(jnp.bfloat16) * scale)
             for at in range(0, tok, LANES)
         ]
         return jnp.dot(jnp.concatenate(weights, axis=1), values, preferred_element_type=jnp.float32)
@@ -605,17 +624,25 @@
 
     inner_act, partial = conv_project(lengths, x_branch, earlier_rows, conv_weight, conv_bias, xproj_weight)
     _, *held = fence((partial, *held))
-    pieces = lax.all_to_all(partial, "mp", split_axis=0, concat_axis=0, tiled=True)
     mine, theirs = with_partner(held)
-    early = max(kv_local // 2, 1)
-    attended = attend(lengths, send_place, query_rows, mine, theirs, (0, early), None)
-    pieces, attended = fence((pieces, attended))
-    summed = jnp.sum(pieces.reshape(n_mp, -1, tok).astype(jnp.float32), axis=0).astype(jnp.bfloat16)
-    copies = jnp.broadcast_to(summed[None], (n_mp,) + summed.shape).reshape(partial.shape)
-    copies, attended = fence((copies, attended))
-    projected = lax.all_to_all(copies, "mp", split_axis=0, concat_axis=0, tiled=True)
-    if early < kv_local:
-        attended = attend(lengths, send_place, query_rows, mine, theirs, (early, kv_local), attended)
+    middle = max(kv_local // 2, 1)
+    parts = [groups for groups in ((0, middle), (middle, kv_local)) if groups[0] < groups[1]]
+    projected, attended = partial, None
+
+    def attend_next():
+        return attend(lengths, send_place, query_rows, mine, theirs, parts.pop(0), attended)
+
+    steps = [1 << k for k in range((n_mp - 1).bit_length())]
+    for step in steps:
+        other = lax.ppermute(projected, "mp", [(source, source ^ step) for source in range(n_mp)])
+        if parts:
+            attended = attend_next()
+            other, attended = fence((other, attended))
+        projected = (projected.astype(jnp.float32) + other.astype(jnp.float32)).astype(jnp.bfloat16)
+        if attended is not None:
+            projected, attended = fence((projected, attended))
+    while parts:
+        attended = attend_next()
     projected, attended = fence((projected, attended))
     regrouped = lax.all_to_all(attended, "seq", split_axis=0, concat_axis=0, tiled=True)
 

time: 89.7 us -> 91.5 us (1.020)
  starting transfers between devices: 31.2 us -> 27 us
  Pallas kernels: 37.2 us -> 40.4 us
  waiting for transfers between devices: 16.4 us -> 17.7 us
    ppermute x0 -> x2, waiting for transfers between devices: none -> 13.1 us  [local(): lax.ppermute(projected, 'mp', [(source, source ^ step) for source in rang...]
    all_to_all x2 -> x0, waiting for transfers between devices: 10.7 us -> none  [the longest x1 6.5 us: local(): lax.all_to_all(partial, 'mp', split_axis=0, concat_axis=0, tiled=True)]
    all_to_all x2 -> x0, starting transfers between devices: 8.32 us -> none  [the longest x1 4.87 us: local(): lax.all_to_all(partial, 'mp', split_axis=0, concat_axis=0, tiled=True)]
    ppermute x0 -> x2, starting transfers between devices: none -> 4.23 us  [local(): lax.ppermute(projected, 'mp', [(source, source ^ step) for source in rang...]
    pallas_call x1, Pallas kernels: 9.86 us -> 13.3 us  [join_states(): pl.pallas_call(functools.partial(join_kernel, low_rank, reach), grid=(tok...]
    unnamed x18 -> x22, local copies, waits for them, and re-layouts: 1.73 us -> 3.18 us
    ppermute x5, waiting for transfers between devices: 4.21 us -> 2.91 us  [shifted(): lax.ppermute(value, 'seq', [(source, source + steps) for source in range(...]
  transfers between devices with their start and end apart: 10 -> 10, of which waited for: 5 -> 6; matrix products, arithmetic and copies ran while one was open for 1% -> 1% of each run, Pallas kernels for 29% -> 28%
where the time goes in v4:
time: 91.5 us; the launch traced here: 91 us
  Pallas kernels  40.4 us (44%)
  starting transfers between devices  27 us (30%)
  waiting for transfers between devices  17.7 us (19%)
  local copies, waits for them, and re-layouts  3.19 us (3%)
  other arithmetic  1.87 us (2%)
    ppermute x5, starting transfers between devices, shifted(): lax.ppermute(value, 'seq', [(source, source + steps) for source in range(...  17.5 us
    pallas_call x1, Pallas kernels, local_scan(): pl.pallas_call(local_kernel, grid=(tok // BLOCK,), in_specs=[pl.BlockSpec...  13.8 us
    pallas_call x1, Pallas kernels, join_states(): pl.pallas_call(functools.partial(join_kernel, low_rank, reach), grid=(tok...  13.3 us
    ppermute x2, waiting for transfers between devices, local(): lax.ppermute(projected, 'mp', [(source, source ^ step) for source in rang...  13.1 us
    pallas_call x1, Pallas kernels, conv_project(): pl.pallas_call(conv_kernel, grid=(channels // chunk,), in_specs=[pl.Block...  5.84 us
    pallas_call x2, Pallas kernels, attend(): pl.pallas_call(functools.partial(attend_kernel, kv_local, groups[0]), gri...  5.74 us
    all_to_all x1, starting transfers between devices, local(): lax.all_to_all(attended, 'seq', split_axis=0, concat_axis=0, tiled=True)  4.46 us
    ppermute x2, starting transfers between devices, local(): lax.ppermute(projected, 'mp', [(source, source ^ step) for source in rang...  4.23 us
  transfers between devices with their start and end apart: 10, of which 6 were waited for; matrix products, arithmetic and copies ran while one was open for 1% of the time, Pallas kernels for 28%

profile of v4, /device:TPU:0, one launch (start us, length us, event | category | flops | bytes accessed | tf_op | source)
XLA Modules:
  0.0 91.0 jit_solution(3463112461466980883)
XLA Ops:
  0.6 1.7 %pack.1 = (bf16[16,2048]{1,0:T(8,128)(2,1)}, bf16[256,512]{1,0:T(8,128)(2,1)}) custom-call(bf16[256,2048]{1,0:T(8,128)(2,1)} %x_ref.3, bf16[256,256]{1,0:T(8,128)(2,1)} %k_ref.1, bf16[256,256]{1,0:T(8,128)(2,1)} %v_ref.1), custom_call_target="tpu_custom_call" | custom-call | bytes 1048576 | tf_op jit(solution)/shard_map/pack/pallas_call | solution.py:52
  2.4 2.3 %collective-permute-start = (bf16[16,2048]{1,0:T(8,128)(2,1)}, bf16[16,2048]{1,0:T(8,128)(2,1)S(1)}, u32[]{:S(2)}, u32[]{:S(2)}) collective-permute-start(bf16[16,2048]{1,0:T(8,128)(2,1)} %get-tuple-element.20), channel_id=1, source_target_pairs={{0,4},{4,8},{8,12},{12,16},{16,20},{20,24},{24,28},{1,5},{5,9},{9,... | collective-permute-start | bytes 196616 | tf_op jit(solution)/shard_map/ppermute | solution.py:582
  4.7 4.4 %collective-permute-start.3 = (bf16[256,512]{1,0:T(8,128)(2,1)}, bf16[256,512]{1,0:T(8,128)(2,1)S(1)}, u32[]{:S(2)}, u32[]{:S(2)}) collective-permute-start(bf16[256,512]{1,0:T(8,128)(2,1)} %get-tuple-element.23), channel_id=1, source_target_pairs={{0,16},{4,20},{8,24},{12,28},{1,17},{5,21},{9,25},{13,29},{2,18},{... | collective-permute-start | bytes 786440 | tf_op jit(solution)/shard_map/ppermute | solution.py:582
  9.2 3.4 %collective-permute-start.2 = (bf16[256,512]{1,0:T(8,128)(2,1)}, bf16[256,512]{1,0:T(8,128)(2,1)S(1)}, u32[]{:S(2)}, u32[]{:S(2)}) collective-permute-start(bf16[256,512]{1,0:T(8,128)(2,1)} %get-tuple-element.23), channel_id=1, source_target_pairs={{0,8},{4,12},{8,16},{12,20},{16,24},{20,28},{1,9},{5,13},{9,17},{1... | collective-permute-start | bytes 786440 | tf_op jit(solution)/shard_map/ppermute | solution.py:582
  12.6 0.0 copy-start.1
  12.6 0.6 copy-done.1
  13.3 0.8 copy-done.4
  14.0 0.7 copy-done.5
  14.7 5.8 %conv_project.1 = (bf16[256,2048]{1,0:T(8,128)(2,1)}, bf16[544,256]{1,0:T(8,128)(2,1)S(1)}) custom-call(s32[4]{0:T(128)S(1)} %copy-done.1, bf16[256,2048]{1,0:T(8,128)(2,1)} %x_ref.3, bf16[16,2048]{1,0:T(8,128)(2,1)S(1)} %collective-permute-done.halo_ref, f32[4,2048]{1,0:T(4,128)S(1)} %copy-done.4, f32[1,2048]{1,0:T(1,128)S(1)} %bitcast.12, ...), custom_call_target="tpu_custom_call" | custom-call | flops 22817013760 | bytes 4194304 | tf_op jit(solution)/shard_map/conv_project/pallas_call | solution.py:110
  20.6 0.6 collective-permute-done.3
  21.2 0.1 pad_maximum_fusion.mine_ref
  21.3 0.8 collective-permute-start.4
  22.1 1.6 %collective-permute-start.1 = (bf16[544,256]{1,0:T(8,128)(2,1)S(1)}, bf16[544,256]{1,0:T(8,128)(2,1)S(1)}, u32[]{:S(2)}, u32[]{:S(2)}) collective-permute-start(bf16[544,256]{1,0:T(8,128)(2,1)S(1)} %get-tuple-element.21), channel_id=1, source_target_pairs={{0,1},{1,0},{2,3},{3,2},{4,5},{5,4},{6,7},{7,6},{8,9},{9,8},{10,11... | collective-permute-start | bytes 835592 | tf_op jit(solution)/shard_map/ppermute | solution.py:637
  23.7 0.3 collective-permute-done.4.theirs_ref
  24.0 2.9 %attend.2.refs_0_ = bf16[256,2048]{1,0:T(8,128)(2,1)} custom-call(s32[4]{0:T(128)S(1)} %copy-done.2, s32[8,256]{1,0:T(8,128)S(1)} %reshape.19.place_ref, bf16[256,2048]{1,0:T(8,128)(2,1)S(1)} %copy-done, bf16[3,256,512]{2,1,0:T(8,128)(2,1)S(1)} %pad_maximum_fusion.mine_ref, bf16[3,256,512]{2,1,0:T(8,128)(2,1)S(1)} %collective-permute-done.4.theirs_ref), custom_call_target="tpu_custom_call" | custom-call | flops 262144 | bytes 262144 | tf_op jit(solution)/shard_map/attend/pallas_call | solution.py:559
  26.8 3.9 %collective-permute-done.1 = bf16[544,256]{1,0:T(8,128)(2,1)S(1)} collective-permute-done((bf16[544,256]{1,0:T(8,128)(2,1)S(1)}, bf16[544,256]{1,0:T(8,128)(2,1)S(1)}, u32[]{:S(2)}, u32[]{:S(2)}) %collective-permute-start.1) | collective-permute-done | bytes 278560 | tf_op jit(solution)/shard_map/ppermute | solution.py:637
  30.7 0.1 add_convert_fusion.1
  30.8 2.7 %collective-permute-start.5 = (bf16[544,256]{1,0:T(8,128)(2,1)S(1)}, bf16[544,256]{1,0:T(8,128)(2,1)S(1)}, u32[]{:S(2)}, u32[]{:S(2)}) collective-permute-start(bf16[544,256]{1,0:T(8,128)(2,1)S(1)} %add_convert_fusion.1), channel_id=1, source_target_pairs={{0,2},{1,3},{2,0},{3,1},{4,6},{5,7},{6,4},{7,5},{8,10},{9,11},{10,... | collective-permute-start | bytes 835592 | tf_op jit(solution)/shard_map/ppermute | solution.py:637
  33.4 2.9 %attend.3 = bf16[256,2048]{1,0:T(8,128)(2,1)} custom-call(s32[4]{0:T(128)S(1)} %copy-done.2, s32[8,256]{1,0:T(8,128)S(1)} %reshape.19.place_ref, bf16[256,2048]{1,0:T(8,128)(2,1)S(1)} %copy-done, bf16[3,256,512]{2,1,0:T(8,128)(2,1)S(1)} %pad_maximum_fusion.mine_ref, ...), custom_call_target="tpu_custom_call", output_to_operand_aliasing={{}: (5, {})} | custom-call | flops 262144 | bytes 262144 | tf_op jit(solution)/shard_map/attend/pallas_call | solution.py:559
  36.3 9.2 %collective-permute-done.5 = bf16[544,256]{1,0:T(8,128)(2,1)S(1)} collective-permute-done((bf16[544,256]{1,0:T(8,128)(2,1)S(1)}, bf16[544,256]{1,0:T(8,128)(2,1)S(1)}, u32[]{:S(2)}, u32[]{:S(2)}) %collective-permute-start.5) | collective-permute-done | bytes 278560 | tf_op jit(solution)/shard_map/ppermute | solution.py:637
  45.5 0.8 add_convert_fusion.proj_ref
  46.3 4.5 %all-to-all-start = ((bf16[8,32,2048]{2,1,0:T(8,128)(2,1)}), bf16[8,32,2048]{2,1,0:T(8,128)(2,1)S(1)}, u32[]{:S(2)}, u32[]{:S(2)}) async-start(bf16[8,32,2048]{2,1,0:T(8,128)(2,1)} %bitcast.7), calls=%async_computation | async-start | bytes 2097152 | tf_op jit(solution)/shard_map/all_to_all | solution.py:647
  50.8 13.8 %local_scan.1 = (f32[256,16,128]{2,1,0:T(8,128)}, f32[256,16,128]{2,1,0:T(8,128)}, bf16[288,128]{1,0:T(8,128)(2,1)}) custom-call(s32[4]{0:T(128)} %lengths_ref.7, bf16[544,256]{1,0:T(8,128)(2,1)} %add_convert_fusion.proj_ref, bf16[512,2048]{1,0:T(8,128)(2,1)} %dtw_ref.1, f32[1,2048]{1,0:T(1,128)} %bitcast.22, f32[16,2048]{1,0:T(8,128)} %rate_ref.3, ...), custom_call_target="tpu_custom_call" | custom-call | flops 100663296 | bytes 6291456 | tf_op jit(solution)/shard_map/local_scan/pallas_call | solution.py:278
  64.6 4.2 %collective-permute-start.7 = (bf16[288,128]{1,0:T(8,128)(2,1)}, bf16[288,128]{1,0:T(8,128)(2,1)S(1)}, u32[]{:S(2)}, u32[]{:S(2)}) collective-permute-start(bf16[288,128]{1,0:T(8,128)(2,1)} %get-tuple-element.37), channel_id=1, source_target_pairs={{0,16},{4,20},{8,24},{12,28},{1,17},{5,21},{9,25},{13,29},{2,18},{... | collective-permute-start | bytes 221192 | tf_op jit(solution)/shard_map/ppermute | solution.py:582
  68.8 3.1 %collective-permute-start.6 = (bf16[288,128]{1,0:T(8,128)(2,1)}, bf16[288,128]{1,0:T(8,128)(2,1)S(1)}, u32[]{:S(2)}, u32[]{:S(2)}) collective-permute-start(bf16[288,128]{1,0:T(8,128)(2,1)} %get-tuple-element.37), channel_id=1, source_target_pairs={{0,8},{4,12},{8,16},{12,20},{16,24},{20,28},{1,9},{5,13},{9,17},{1... | collective-permute-start | bytes 221192 | tf_op jit(solution)/shard_map/ppermute | solution.py:582
  71.9 2.3 %collective-permute-done.6 = bf16[288,128]{1,0:T(8,128)(2,1)S(1)} collective-permute-done((bf16[288,128]{1,0:T(8,128)(2,1)}, bf16[288,128]{1,0:T(8,128)(2,1)S(1)}, u32[]{:S(2)}, u32[]{:S(2)}) %collective-permute-start.6) | collective-permute-done | bytes 73760 | tf_op jit(solution)/shard_map/ppermute | solution.py:582
  74.2 0.9 %pad_maximum_fusion.1.mine_ref = bf16[3,288,128]{2,1,0:T(8,128)(2,1)S(1)} fusion(bf16[1,288,128]{2,1,0:T(8,128)(2,1)S(1)} %bitcast.19, bf16[1,288,128]{2,1,0:T(8,128)(2,1)S(1)} %bitcast.20, bf16[1,288,128]{2,1,0:T(8,128)(2,1)} %bitcast.18), kind=kLoop, calls=%fused_computation.3 | loop fusion | flops 221184 | bytes 442368 | tf_op jit(solution)/shard_map/stack | solution.py:586
  75.1 0.1 collective-permute-start.8
  75.2 1.5 %collective-permute-done.8.theirs_ref = bf16[3,288,128]{2,1,0:T(8,128)(2,1)S(1)} collective-permute-done((bf16[3,288,128]{2,1,0:T(8,128)(2,1)S(1)}, bf16[3,288,128]{2,1,0:T(8,128)(2,1)S(1)}, u32[]{:S(2)}, u32[]{:S(2)}) %collective-permute-start.8) | collective-permute-done | bytes 221216 | tf_op jit(solution)/shard_map/ppermute | solution.py:588
  76.6 0.7 copy-done.10
  77.3 0.4 copy-done.7
  77.7 13.3 %join_states.1 = (bf16[256,2048]{1,0:T(8,128)(2,1)}, bf16[256,2048]{1,0:T(8,128)(2,1)}) custom-call(bf16[544,256]{1,0:T(8,128)(2,1)} %add_convert_fusion.proj_ref, f32[256,16,128]{2,1,0:T(8,128)} %get-tuple-element.34.y_ref, f32[256,16,128]{2,1,0:T(8,128)} %get-tuple-element.35.sum_ref, bf16[256,2048]{1,0:T(8,128)(2,1)} %get-tuple-element.33.inner_ref, ...), custom_call_target="tpu_custom_call" | custom-call | flops 67108864 | bytes 7340032 | tf_op jit(solution)/shard_map/join_states/pallas_call | solution.py:411
  (22 shorter events, 0.1 us)
Async XLA Ops:
  2.4 10.2 %collective-permute-start = (bf16[16,2048]{1,0:T(8,128)(2,1)}, bf16[16,2048]{1,0:T(8,128)(2,1)S(1)}, u32[]{:S(2)}, u32[]{:S(2)}) collective-permute-start(bf16[16,2048]{1,0:T(8,128)(2,1)} %get-tuple-element.20), channel_id=1, source_target_pairs={{0,4},{4,8},{8,12},{12,16},{16,20},{20,24},{24,28},{1,5},{5,9},{9,... | collective-permute-start | bytes 196616 | tf_op jit(solution)/shard_map/ppermute | solution.py:582
  4.7 16.5 %collective-permute-start.3 = (bf16[256,512]{1,0:T(8,128)(2,1)}, bf16[256,512]{1,0:T(8,128)(2,1)S(1)}, u32[]{:S(2)}, u32[]{:S(2)}) collective-permute-start(bf16[256,512]{1,0:T(8,128)(2,1)} %get-tuple-element.23), channel_id=1, source_target_pairs={{0,16},{4,20},{8,24},{12,28},{1,17},{5,21},{9,25},{13,29},{2,18},{... | collective-permute-start | bytes 786440 | tf_op jit(solution)/shard_map/ppermute | solution.py:582
  9.2 12.0 %collective-permute-start.2 = (bf16[256,512]{1,0:T(8,128)(2,1)}, bf16[256,512]{1,0:T(8,128)(2,1)S(1)}, u32[]{:S(2)}, u32[]{:S(2)}) collective-permute-start(bf16[256,512]{1,0:T(8,128)(2,1)} %get-tuple-element.23), channel_id=1, source_target_pairs={{0,8},{4,12},{8,16},{12,20},{16,24},{20,28},{1,9},{5,13},{9,17},{1... | collective-permute-start | bytes 786440 | tf_op jit(solution)/shard_map/ppermute | solution.py:582
  12.6 0.7 copy-start.1
  13.3 0.8 copy-start.4
  14.0 0.7 copy-start.5
  14.7 6.5 %copy-start.8 = (bf16[256,512]{1,0:T(8,128)(2,1)S(1)}, bf16[256,512]{1,0:T(8,128)(2,1)}, u32[]{:S(2)}) copy-start(bf16[256,512]{1,0:T(8,128)(2,1)} %get-tuple-element.23) | copy-start | bytes 786436
  14.7 8.9 %copy-start.9 = (s32[2048]{0:T(1024)S(1)}, s32[2048]{0:T(1024)}, u32[]{:S(2)}) copy-start(s32[2048]{0:T(1024)} %param.27) | copy-start | bytes 24580
  14.7 9.2 %copy-start.2 = (s32[4]{0:T(128)S(1)}, s32[4]{0:T(128)}, u32[]{:S(2)}) copy-start(s32[4]{0:T(128)} %lengths_ref.7) | copy-start | bytes 52
  20.6 3.4 %copy-start = (bf16[256,2048]{1,0:T(8,128)(2,1)S(1)}, bf16[256,2048]{1,0:T(8,128)(2,1)}, u32[]{:S(2)}) copy-start(bf16[256,2048]{1,0:T(8,128)(2,1)} %q_ref.3) | copy-start | bytes 3145732
  21.3 2.7 %collective-permute-start.4 = (bf16[3,256,512]{2,1,0:T(8,128)(2,1)S(1)}, bf16[3,256,512]{2,1,0:T(8,128)(2,1)S(1)}, u32[]{:S(2)}, u32[]{:S(2)}) collective-permute-start(bf16[3,256,512]{2,1,0:T(8,128)(2,1)S(1)} %pad_maximum_fusion.mine_ref), channel_id=1, source_target_pairs={{0,4},{4,0},{8,12},{12,8},{16,20},{20,16},{24,28},{28,24},{1,5},{5... | collective-permute-start | bytes 2359304 | tf_op jit(solution)/shard_map/ppermute | solution.py:588
  22.1 8.6 %collective-permute-start.1 = (bf16[544,256]{1,0:T(8,128)(2,1)S(1)}, bf16[544,256]{1,0:T(8,128)(2,1)S(1)}, u32[]{:S(2)}, u32[]{:S(2)}) collective-permute-start(bf16[544,256]{1,0:T(8,128)(2,1)S(1)} %get-tuple-element.21), channel_id=1, source_target_pairs={{0,1},{1,0},{2,3},{3,2},{4,5},{5,4},{6,7},{7,6},{8,9},{9,8},{10,11... | collective-permute-start | bytes 835592 | tf_op jit(solution)/shard_map/ppermute | solution.py:637
  30.8 14.7 %collective-permute-start.5 = (bf16[544,256]{1,0:T(8,128)(2,1)S(1)}, bf16[544,256]{1,0:T(8,128)(2,1)S(1)}, u32[]{:S(2)}, u32[]{:S(2)}) collective-permute-start(bf16[544,256]{1,0:T(8,128)(2,1)S(1)} %add_convert_fusion.1), channel_id=1, source_target_pairs={{0,2},{1,3},{2,0},{3,1},{4,6},{5,7},{6,4},{7,5},{8,10},{9,11},{10,... | collective-permute-start | bytes 835592 | tf_op jit(solution)/shard_map/ppermute | solution.py:637
  46.3 30.3 %all-to-all-start = ((bf16[8,32,2048]{2,1,0:T(8,128)(2,1)}), bf16[8,32,2048]{2,1,0:T(8,128)(2,1)S(1)}, u32[]{:S(2)}, u32[]{:S(2)}) async-start(bf16[8,32,2048]{2,1,0:T(8,128)(2,1)} %bitcast.7), calls=%async_computation | async-start | bytes 2097152 | tf_op jit(solution)/shard_map/all_to_all | solution.py:647
  50.8 26.9 %copy-start.3 = (f32[16,2048]{1,0:T(8,128)S(1)}, f32[16,2048]{1,0:T(8,128)}, u32[]{:S(2)}) copy-start(f32[16,2048]{1,0:T(8,128)} %rate_ref.3) | copy-start | bytes 393220
  50.8 26.9 %copy-start.6 = (f32[2048]{0:T(1024)S(1)}, f32[2048]{0:T(1024)}, u32[]{:S(2)}) copy-start(f32[2048]{0:T(1024)} %param.22) | copy-start | bytes 24580
  64.6 7.3 %collective-permute-start.7 = (bf16[288,128]{1,0:T(8,128)(2,1)}, bf16[288,128]{1,0:T(8,128)(2,1)S(1)}, u32[]{:S(2)}, u32[]{:S(2)}) collective-permute-start(bf16[288,128]{1,0:T(8,128)(2,1)} %get-tuple-element.37), channel_id=1, source_target_pairs={{0,16},{4,20},{8,24},{12,28},{1,17},{5,21},{9,25},{13,29},{2,18},{... | collective-permute-start | bytes 221192 | tf_op jit(solution)/shard_map/ppermute | solution.py:582
  68.8 5.4 %collective-permute-start.6 = (bf16[288,128]{1,0:T(8,128)(2,1)}, bf16[288,128]{1,0:T(8,128)(2,1)S(1)}, u32[]{:S(2)}, u32[]{:S(2)}) collective-permute-start(bf16[288,128]{1,0:T(8,128)(2,1)} %get-tuple-element.37), channel_id=1, source_target_pairs={{0,8},{4,12},{8,16},{12,20},{16,24},{20,28},{1,9},{5,13},{9,17},{1... | collective-permute-start | bytes 221192 | tf_op jit(solution)/shard_map/ppermute | solution.py:582
  75.1 1.5 %collective-permute-start.8 = (bf16[3,288,128]{2,1,0:T(8,128)(2,1)S(1)}, bf16[3,288,128]{2,1,0:T(8,128)(2,1)S(1)}, u32[]{:S(2)}, u32[]{:S(2)}) collective-permute-start(bf16[3,288,128]{2,1,0:T(8,128)(2,1)S(1)} %pad_maximum_fusion.1.mine_ref), channel_id=1, source_target_pairs={{0,4},{4,0},{8,12},{12,8},{16,20},{20,16},{24,28},{28,24},{1,5},{5... | collective-permute-start | bytes 663560 | tf_op jit(solution)/shard_map/ppermute | solution.py:588
  76.6 0.7 copy-start.10
  76.6 1.1 %copy-start.7 = (bf16[8,32,2048]{2,1,0:T(8,128)(2,1)}, bf16[8,32,2048]{2,1,0:T(8,128)(2,1)S(1)}, u32[]{:S(2)}) copy-start(bf16[8,32,2048]{2,1,0:T(8,128)(2,1)S(1)} %all-to-all-done) | copy-start | bytes 3145732

commit v5 on v2

--- a/solution.py
+++ b/solution.py
@@ -37,30 +37,31 @@
     return 512 if channels % 512 == 0 else channels
 
 
-def pack_kernel(x_ref, k_ref, v_ref, halo_ref, kv_ref):
-    width = k_ref.shape[1]
-    halo_ref[...] = x_ref[...]
-    kv_ref[:, :width] = k_ref[...]
-    kv_ref[:, width:] = v_ref[...]
+def pack_kernel(x_ref, k_ref, v_ref, halo_ref, kv_ref, sems):
+    tok, width = k_ref.shape
+    copies = [
+        pltpu.make_async_copy(x_ref.at[pl.ds(tok - HALO, HALO), :], halo_ref, sems.at[0]),
+        pltpu.make_async_copy(k_ref, kv_ref.at[:, pl.ds(0, width)], sems.at[1]),
+        pltpu.make_async_copy(v_ref, kv_ref.at[:, pl.ds(width, width)], sems.at[2]),
+    ]
+    for copy in copies:
+        copy.start()
+    for copy in copies:
+        copy.wait()
 
 
 def pack(x_branch, key_rows, value_rows):
     tok, channels = x_branch.shape
     width = key_rows.shape[1]
-    whole = lambda rows, columns: pl.BlockSpec((rows, columns), lambda i: (0, 0))
     return pl.pallas_call(
         pack_kernel,
-        grid=(1,),
-        in_specs=[
-            pl.BlockSpec((HALO, channels), lambda i: (tok // HALO - 1, 0)),
-            whole(tok, width),
-            whole(tok, width),
-        ],
-        out_specs=[whole(HALO, channels), whole(tok, 2 * width)],
+        in_specs=[pl.BlockSpec(memory_space=pl.ANY)] * 3,
+        out_specs=[pl.BlockSpec(memory_space=pl.ANY)] * 2,
         out_shape=[
             jax.ShapeDtypeStruct((HALO, channels), x_branch.dtype),
             jax.ShapeDtypeStruct((tok, 2 * width), key_rows.dtype),
         ],
+        scratch_shapes=[pltpu.SemaphoreType.DMA((3,))],
         compiler_params=pltpu.CompilerParams(vmem_limit_bytes=VMEM_MOST),
         cost_estimate=pl.CostEstimate(flops=0, bytes_accessed=16 * tok * width, transcendentals=0),
         name="pack",
@@ -225,28 +226,29 @@
 
     def scan(t8, held):
         held, total = list(held[0]), list(held[1])
-        for first in range(0, ROWS, 4):
-            done = []
-            for r in range(first, first + 4):
-                token = at * block + t8 * ROWS + r
-                picked = [pl.ds(r + h * ROWS * ROWS, ROWS, stride=ROWS) for h in range(count)]
-                step = [step_tiles[t8, rows, :] for rows in picked]
-                drive = [drive_tiles[t8, rows, :] for rows in picked]
-                out = [None] * count
-                for n in range(states):
-                    b_row = bc_spread[token, n : n + 1, :]
-                    c_row = bc_spread[token, states + n : states + n + 1, :]
-                    for h in range(count):
-                        i = n * count + h
-                        held[i] = jnp.exp2(rates[i] * step[h]) * held[i] + b_row * drive[h]
-                        term = c_row * held[i]
-                        out[h] = term if out[h] is None else out[h] + term
-                total = [so_far + more for so_far, more in zip(total, step)]
-                done.append((out, total))
-            for k, (out, so_far) in enumerate(done):
+        for first in range(0, ROWS, 2):
+            tokens = range(first, first + 2)
+            picked = [[pl.ds(r + h * ROWS * ROWS, ROWS, stride=ROWS) for h in range(count)] for r in tokens]
+            step = [[step_tiles[t8, rows, :] for rows in of_token] for of_token in picked]
+            drive = [[drive_tiles[t8, rows, :] for rows in of_token] for of_token in picked]
+            out = [[None] * count for _ in tokens]
+            for n in range(states):
+                where = [at * block + t8 * ROWS + r for r in tokens]
+                b_row = [bc_spread[token, n : n + 1, :] for token in where]
+                c_row = [bc_spread[token, states + n : states + n + 1, :] for token in where]
                 for h in range(count):
-                    y_ref[t8 * ROWS + first + k, sublanes(h), :] = out[h]
-                    sum_ref[t8 * ROWS + first + k, sublanes(h), :] = so_far[h]
+                    i = n * count + h
+                    rate = rates[i]
+                    decay = [jnp.exp2(rate * step[k][h]) for k in range(2)]
+                    for k in range(2):
+                        held[i] = decay[k] * held[i] + b_row[k] * drive[k][h]
+                        term = c_row[k] * held[i]
+                        out[k][h] = term if out[k][h] is None else out[k][h] + term
+            for k, r in enumerate(tokens):
+                for h in range(count):
+                    total[h] = total[h] + step[k][h]
+                    y_ref[t8 * ROWS + r, sublanes(h), :] = out[k][h]
+                    sum_ref[t8 * ROWS + r, sublanes(h), :] = total[h]
         return held, total
 
     kept = states * count
@@ -361,11 +363,11 @@
             total = [[sum_ref[first + r, sublanes(h), :] for h in range(count)] for r in range(ROWS)]
             out = [[y_ref[first + r, sublanes(h), :] for h in range(count)] for r in range(ROWS)]
             for n in range(states):
-                for r in range(ROWS):
-                    c_row = c_spread[at * block + first + r, n : n + 1, :]
-                    for h in range(count):
-                        i = n * count + h
-                        out[r][h] += jnp.exp2(rates[i] * total[r][h]) * entering[i] * c_row
+                c_row = [c_spread[at * block + first + r, n : n + 1, :] for r in range(ROWS)]
+                for h in range(count):
+                    rate, state = rates[n * count + h], entering[n * count + h]
+                    for r in range(ROWS):
+                        out[r][h] += jnp.exp2(rate * total[r][h]) * state * c_row[r]
             for r in range(ROWS):
                 for h in range(count):
                     rows_tiles[k, pl.ds(r + h * ROWS * ROWS, ROWS, stride=ROWS), :] = out[r][h]
@@ -431,7 +433,7 @@
     position = lax.axis_index("seq")
     odd = lax.rem(position, 2)
     anchor = position * tok
-    scale = HD**-0.5
+    scale = jnp.bfloat16(LOG2E * HD**-0.5)
     starts, ends = doc_edges(lengths_ref)
     lane = lax.broadcasted_iota(jnp.int32, (1, LANES), 1)
     first = jnp.full((1, LANES), 2**30, jnp.int32)
@@ -489,13 +491,13 @@
         return carry
 
     lax.fori_loop(1, earlier + 1, look, 0)
-    tops[...] = jnp.broadcast_to(jnp.max(tops[...], axis=1, keepdims=True) * scale, tops.shape)
+    tops[...] = jnp.broadcast_to(jnp.max(tops[...], axis=1, keepdims=True), tops.shape)
 
     def weighted(back):
         values = jnp.concatenate([rows_of(back, value_cols), jnp.ones((tok, HD), jnp.bfloat16)], axis=1)
         top = tops[...]
         weights = [
-            jnp.exp((scores[back, :, at : at + LANES] * scale - top).astype(jnp.bfloat16))
+            jnp.exp2((scores[back, :, at : at + LANES] - top).astype(jnp.bfloat16) * scale)
             for at in range(0, tok, LANES)
         ]
         return jnp.dot(jnp.concatenate(weights, axis=1), values, preferred_element_type=jnp.float32)
@@ -605,19 +607,27 @@
 
     inner_act, partial = conv_project(lengths, x_branch, earlier_rows, conv_weight, conv_bias, xproj_weight)
     _, *held = fence((partial, *held))
-    pieces = lax.all_to_all(partial, "mp", split_axis=0, concat_axis=0, tiled=True)
     mine, theirs = with_partner(held)
-    early = max(kv_local // 2, 1)
-    attended = attend(lengths, send_place, query_rows, mine, theirs, (0, early), None)
-    pieces, attended = fence((pieces, attended))
-    summed = jnp.sum(pieces.reshape(n_mp, -1, tok).astype(jnp.float32), axis=0).astype(jnp.bfloat16)
-    copies = jnp.broadcast_to(summed[None], (n_mp,) + summed.shape).reshape(partial.shape)
-    copies, attended = fence((copies, attended))
-    projected = lax.all_to_all(copies, "mp", split_axis=0, concat_axis=0, tiled=True)
-    if early < kv_local:
-        attended = attend(lengths, send_place, query_rows, mine, theirs, (early, kv_local), attended)
-    projected, attended = fence((projected, attended))
+    middle = max(kv_local // 2, 1)
+    parts = [groups for groups in ((0, middle), (middle, kv_local)) if groups[0] < groups[1]]
+    projected, attended = partial, None
+
+    def attend_next():
+        return attend(lengths, send_place, query_rows, mine, theirs, parts.pop(0), attended)
+
+    steps = [1 << k for k in range((n_mp - 1).bit_length())]
+    for step in steps:
+        other = lax.ppermute(projected, "mp", [(source, source ^ step) for source in range(n_mp)])
+        if parts:
+            attended = attend_next()
+            other, attended = fence((other, attended))
+        projected = (projected.astype(jnp.float32) + other.astype(jnp.float32)).astype(jnp.bfloat16)
+        if parts:
+            projected, attended = fence((projected, attended))
+    while parts:
+        attended = attend_next()
     regrouped = lax.all_to_all(attended, "seq", split_axis=0, concat_axis=0, tiled=True)
+    projected, _ = fence((projected, attended))
 
     y, sums, state = local_scan(lengths, projected, dt_weight, dt_bias, decay_rate, inner_act)
     own, other = with_partner(even_back(state, reach))

time: 89.7 us -> 97.3 us (1.085)
  Pallas kernels: 37.2 us -> 46.4 us
  starting transfers between devices: 31.2 us -> 26.8 us
  waiting for transfers between devices: 16.4 us -> 19.3 us
    ppermute x0 -> x2, waiting for transfers between devices: none -> 13.3 us  [local(): lax.ppermute(projected, 'mp', [(source, source ^ step) for source in rang...]
    all_to_all x2 -> x0, waiting for transfers between devices: 10.7 us -> none  [the longest x1 6.5 us: local(): lax.all_to_all(partial, 'mp', split_axis=0, concat_axis=0, tiled=True)]
    pallas_call x1, Pallas kernels: 1.73 us -> 11.1 us  [pack(): pl.pallas_call(pack_kernel, in_specs=[pl.BlockSpec(memory_space=pl.ANY)]...]
    all_to_all x2 -> x0, starting transfers between devices: 8.32 us -> none  [the longest x1 4.87 us: local(): lax.all_to_all(partial, 'mp', split_axis=0, concat_axis=0, tiled=True)]
    ppermute x0 -> x2, starting transfers between devices: none -> 4.23 us  [local(): lax.ppermute(projected, 'mp', [(source, source ^ step) for source in rang...]
  transfers between devices with their start and end apart: 10 -> 10, of which waited for: 5 -> 6; matrix products, arithmetic and copies ran while one was open for 1% -> 2% of each run, Pallas kernels for 29% -> 26%
where the time goes in v5:
time: 97.3 us; the launch traced here: 96.9 us
  Pallas kernels  46.4 us (48%)
  starting transfers between devices  26.8 us (28%)
  waiting for transfers between devices  19.3 us (20%)
  other arithmetic  1.87 us (2%)
  local copies, waits for them, and re-layouts  1.73 us (2%)
    ppermute x5, starting transfers between devices, shifted(): lax.ppermute(value, 'seq', [(source, source + steps) for source in range(...  17.5 us
    pallas_call x1, Pallas kernels, local_scan(): pl.pallas_call(local_kernel, grid=(tok // BLOCK,), in_specs=[pl.BlockSpec...  13.8 us
    ppermute x2, waiting for transfers between devices, local(): lax.ppermute(projected, 'mp', [(source, source ^ step) for source in rang...  13.3 us
    pallas_call x1, Pallas kernels, pack(): pl.pallas_call(pack_kernel, in_specs=[pl.BlockSpec(memory_space=pl.ANY)]...  11.1 us
    pallas_call x1, Pallas kernels, join_states(): pl.pallas_call(functools.partial(join_kernel, low_rank, reach), grid=(tok...  9.82 us
    pallas_call x1, Pallas kernels, conv_project(): pl.pallas_call(conv_kernel, grid=(channels // chunk,), in_specs=[pl.Block...  6.01 us
    pallas_call x2, Pallas kernels, attend(): pl.pallas_call(functools.partial(attend_kernel, kv_local, groups[0]), gri...  5.72 us
    all_to_all x1, starting transfers between devices, local(): lax.all_to_all(attended, 'seq', split_axis=0, concat_axis=0, tiled=True)  4.26 us
  transfers between devices with their start and end apart: 10, of which 6 were waited for; matrix products, arithmetic and copies ran while one was open for 2% of the time, Pallas kernels for 26%

profile of v5, /device:TPU:0, one launch (start us, length us, event | category | flops | bytes accessed | tf_op | source)
XLA Modules:
  0.0 96.9 jit_solution(2176243776282190182)
XLA Ops:
  0.6 11.1 %pack.1 = (bf16[16,2048]{1,0:T(8,128)(2,1)}, bf16[256,512]{1,0:T(8,128)(2,1)}) custom-call(bf16[256,2048]{1,0:T(8,128)(2,1)} %x_ref.3, bf16[256,256]{1,0:T(8,128)(2,1)} %k_ref.1, bf16[256,256]{1,0:T(8,128)(2,1)} %v_ref.1), custom_call_target="tpu_custom_call" | custom-call | bytes 1048576 | tf_op jit(solution)/shard_map/pack/pallas_call | solution.py:56
  11.7 2.4 %collective-permute-start = (bf16[16,2048]{1,0:T(8,128)(2,1)}, bf16[16,2048]{1,0:T(8,128)(2,1)S(1)}, u32[]{:S(2)}, u32[]{:S(2)}) collective-permute-start(bf16[16,2048]{1,0:T(8,128)(2,1)} %get-tuple-element.19), channel_id=1, source_target_pairs={{0,4},{4,8},{8,12},{12,16},{16,20},{20,24},{24,28},{1,5},{5,9},{9,... | collective-permute-start | bytes 196616 | tf_op jit(solution)/shard_map/ppermute | solution.py:565
  14.1 4.4 %collective-permute-start.3 = (bf16[256,512]{1,0:T(8,128)(2,1)}, bf16[256,512]{1,0:T(8,128)(2,1)S(1)}, u32[]{:S(2)}, u32[]{:S(2)}) collective-permute-start(bf16[256,512]{1,0:T(8,128)(2,1)} %get-tuple-element.22), channel_id=1, source_target_pairs={{0,16},{4,20},{8,24},{12,28},{1,17},{5,21},{9,25},{13,29},{2,18},{... | collective-permute-start | bytes 786440 | tf_op jit(solution)/shard_map/ppermute | solution.py:565
  18.5 3.4 %collective-permute-start.2 = (bf16[256,512]{1,0:T(8,128)(2,1)}, bf16[256,512]{1,0:T(8,128)(2,1)S(1)}, u32[]{:S(2)}, u32[]{:S(2)}) collective-permute-start(bf16[256,512]{1,0:T(8,128)(2,1)} %get-tuple-element.22), channel_id=1, source_target_pairs={{0,8},{4,12},{8,16},{12,20},{16,24},{20,28},{1,9},{5,13},{9,17},{1... | collective-permute-start | bytes 786440 | tf_op jit(solution)/shard_map/ppermute | solution.py:565
  22.0 0.6 copy-done.8
  22.6 6.0 %conv_project.1 = (bf16[256,2048]{1,0:T(8,128)(2,1)}, bf16[544,256]{1,0:T(8,128)(2,1)}) custom-call(s32[4]{0:T(128)} %lengths_ref.7, bf16[256,2048]{1,0:T(8,128)(2,1)} %x_ref.3, bf16[16,2048]{1,0:T(8,128)(2,1)} %copy-done.8, f32[4,2048]{1,0:T(4,128)} %w_ref.1, f32[1,2048]{1,0:T(1,128)} %bitcast.20, bf16[544,2048]{1,0:T(8,128)(2,1)} %bitcast.19), custom_call_target="tpu_custom_call" | custom-call | flops 22817013760 | bytes 4194304 | tf_op jit(solution)/shard_map/conv_project/pallas_call | solution.py:110
  28.6 2.0 %collective-permute-done.3 = bf16[256,512]{1,0:T(8,128)(2,1)S(1)} collective-permute-done((bf16[256,512]{1,0:T(8,128)(2,1)}, bf16[256,512]{1,0:T(8,128)(2,1)S(1)}, u32[]{:S(2)}, u32[]{:S(2)}) %collective-permute-start.3) | collective-permute-done | bytes 262176 | tf_op jit(solution)/shard_map/ppermute | solution.py:565
  30.5 0.0 collective-permute-done.2
  30.6 0.1 pad_maximum_fusion.mine_ref
  30.6 0.0 copy-start.3
  30.7 0.8 collective-permute-start.4
  31.4 1.6 %collective-permute-start.1 = (bf16[544,256]{1,0:T(8,128)(2,1)}, bf16[544,256]{1,0:T(8,128)(2,1)S(1)}, u32[]{:S(2)}, u32[]{:S(2)}) collective-permute-start(bf16[544,256]{1,0:T(8,128)(2,1)} %get-tuple-element.20), channel_id=1, source_target_pairs={{0,1},{1,0},{2,3},{3,2},{4,5},{5,4},{6,7},{7,6},{8,9},{9,8},{10,11... | collective-permute-start | bytes 835592 | tf_op jit(solution)/shard_map/ppermute | solution.py:620
  33.0 0.3 collective-permute-done.4.theirs_ref
  33.3 2.9 %attend.2.refs_0_ = bf16[256,2048]{1,0:T(8,128)(2,1)} custom-call(s32[4]{0:T(128)S(1)} %copy-done.1, s32[8,256]{1,0:T(8,128)S(1)} %reshape.19.place_ref, bf16[256,2048]{1,0:T(8,128)(2,1)S(1)} %copy-done, bf16[3,256,512]{2,1,0:T(8,128)(2,1)S(1)} %pad_maximum_fusion.mine_ref, bf16[3,256,512]{2,1,0:T(8,128)(2,1)S(1)} %collective-permute-done.4.theirs_ref), custom_call_target="tpu_custom_call" | custom-call | flops 262144 | bytes 262144 | tf_op jit(solution)/shard_map/attend/pallas_call | solution.py:542
  36.2 4.1 %collective-permute-done.1 = bf16[544,256]{1,0:T(8,128)(2,1)S(1)} collective-permute-done((bf16[544,256]{1,0:T(8,128)(2,1)}, bf16[544,256]{1,0:T(8,128)(2,1)S(1)}, u32[]{:S(2)}, u32[]{:S(2)}) %collective-permute-start.1) | collective-permute-done | bytes 278560 | tf_op jit(solution)/shard_map/ppermute | solution.py:620
  40.3 0.1 add_convert_fusion.1
  40.3 2.7 %collective-permute-start.5 = (bf16[544,256]{1,0:T(8,128)(2,1)S(1)}, bf16[544,256]{1,0:T(8,128)(2,1)S(1)}, u32[]{:S(2)}, u32[]{:S(2)}) collective-permute-start(bf16[544,256]{1,0:T(8,128)(2,1)S(1)} %add_convert_fusion.1), channel_id=1, source_target_pairs={{0,2},{1,3},{2,0},{3,1},{4,6},{5,7},{6,4},{7,5},{8,10},{9,11},{10,... | collective-permute-start | bytes 835592 | tf_op jit(solution)/shard_map/ppermute | solution.py:620
  43.0 2.9 %attend.3 = bf16[256,2048]{1,0:T(8,128)(2,1)} custom-call(s32[4]{0:T(128)S(1)} %copy-done.1, s32[8,256]{1,0:T(8,128)S(1)} %reshape.19.place_ref, bf16[256,2048]{1,0:T(8,128)(2,1)S(1)} %copy-done, bf16[3,256,512]{2,1,0:T(8,128)(2,1)S(1)} %pad_maximum_fusion.mine_ref, ...), custom_call_target="tpu_custom_call", output_to_operand_aliasing={{}: (5, {})} | custom-call | flops 262144 | bytes 262144 | tf_op jit(solution)/shard_map/attend/pallas_call | solution.py:542
  45.8 9.2 %collective-permute-done.5 = bf16[544,256]{1,0:T(8,128)(2,1)S(1)} collective-permute-done((bf16[544,256]{1,0:T(8,128)(2,1)S(1)}, bf16[544,256]{1,0:T(8,128)(2,1)S(1)}, u32[]{:S(2)}, u32[]{:S(2)}) %collective-permute-start.5) | collective-permute-done | bytes 278560 | tf_op jit(solution)/shard_map/ppermute | solution.py:620
  55.1 4.3 %all-to-all-start = ((bf16[8,32,2048]{2,1,0:T(8,128)(2,1)}), bf16[8,32,2048]{2,1,0:T(8,128)(2,1)S(1)}, u32[]{:S(2)}, u32[]{:S(2)}) async-start(bf16[8,32,2048]{2,1,0:T(8,128)(2,1)} %bitcast.7), calls=%async_computation | async-start | bytes 2097152 | tf_op jit(solution)/shard_map/all_to_all | solution.py:629
  59.3 0.8 add_convert_fusion.proj_ref
  60.1 13.8 %local_scan.1 = (f32[256,16,128]{2,1,0:T(8,128)}, f32[256,16,128]{2,1,0:T(8,128)}, bf16[288,128]{1,0:T(8,128)(2,1)}) custom-call(s32[4]{0:T(128)} %lengths_ref.7, bf16[544,256]{1,0:T(8,128)(2,1)} %add_convert_fusion.proj_ref, bf16[512,2048]{1,0:T(8,128)(2,1)} %dtw_ref.1, f32[1,2048]{1,0:T(1,128)} %bitcast.21, f32[16,2048]{1,0:T(8,128)} %rate_ref.3, ...), custom_call_target="tpu_custom_call" | custom-call | flops 100663296 | bytes 6291456 | tf_op jit(solution)/shard_map/local_scan/pallas_call | solution.py:278
  73.9 4.1 %collective-permute-start.7 = (bf16[288,128]{1,0:T(8,128)(2,1)}, bf16[288,128]{1,0:T(8,128)(2,1)S(1)}, u32[]{:S(2)}, u32[]{:S(2)}) collective-permute-start(bf16[288,128]{1,0:T(8,128)(2,1)} %get-tuple-element.35), channel_id=1, source_target_pairs={{0,16},{4,20},{8,24},{12,28},{1,17},{5,21},{9,25},{13,29},{2,18},{... | collective-permute-start | bytes 221192 | tf_op jit(solution)/shard_map/ppermute | solution.py:565
  78.0 3.2 %collective-permute-start.6 = (bf16[288,128]{1,0:T(8,128)(2,1)}, bf16[288,128]{1,0:T(8,128)(2,1)S(1)}, u32[]{:S(2)}, u32[]{:S(2)}) collective-permute-start(bf16[288,128]{1,0:T(8,128)(2,1)} %get-tuple-element.35), channel_id=1, source_target_pairs={{0,8},{4,12},{8,16},{12,20},{16,24},{20,28},{1,9},{5,13},{9,17},{1... | collective-permute-start | bytes 221192 | tf_op jit(solution)/shard_map/ppermute | solution.py:565
  81.2 2.3 %collective-permute-done.6 = bf16[288,128]{1,0:T(8,128)(2,1)S(1)} collective-permute-done((bf16[288,128]{1,0:T(8,128)(2,1)}, bf16[288,128]{1,0:T(8,128)(2,1)S(1)}, u32[]{:S(2)}, u32[]{:S(2)}) %collective-permute-start.6) | collective-permute-done | bytes 73760 | tf_op jit(solution)/shard_map/ppermute | solution.py:565
  83.5 0.9 pad_maximum_fusion.1.mine_ref
  84.4 0.1 collective-permute-start.8
  84.5 1.5 %collective-permute-done.8.theirs_ref = bf16[3,288,128]{2,1,0:T(8,128)(2,1)S(1)} collective-permute-done((bf16[3,288,128]{2,1,0:T(8,128)(2,1)S(1)}, bf16[3,288,128]{2,1,0:T(8,128)(2,1)S(1)}, u32[]{:S(2)}, u32[]{:S(2)}) %collective-permute-start.8) | collective-permute-done | bytes 221216 | tf_op jit(solution)/shard_map/ppermute | solution.py:571
  86.0 0.0 all-to-all-done
  86.0 0.7 copy-done.7
  86.6 0.4 copy-done.2
  87.0 9.8 %join_states.1 = (bf16[256,2048]{1,0:T(8,128)(2,1)}, bf16[256,2048]{1,0:T(8,128)(2,1)}) custom-call(bf16[544,256]{1,0:T(8,128)(2,1)} %add_convert_fusion.proj_ref, f32[256,16,128]{2,1,0:T(8,128)} %get-tuple-element.33.y_ref, f32[256,16,128]{2,1,0:T(8,128)} %get-tuple-element.34.sum_ref, bf16[256,2048]{1,0:T(8,128)(2,1)} %get-tuple-element.32.inner_ref, ...), custom_call_target="tpu_custom_call" | custom-call | flops 67108864 | bytes 7340032 | tf_op jit(solution)/shard_map/join_states/pallas_call | solution.py:395
  (18 shorter events, 0.0 us)
Async XLA Ops:
  11.7 10.2 %collective-permute-start = (bf16[16,2048]{1,0:T(8,128)(2,1)}, bf16[16,2048]{1,0:T(8,128)(2,1)S(1)}, u32[]{:S(2)}, u32[]{:S(2)}) collective-permute-start(bf16[16,2048]{1,0:T(8,128)(2,1)} %get-tuple-element.19), channel_id=1, source_target_pairs={{0,4},{4,8},{8,12},{12,16},{16,20},{20,24},{24,28},{1,5},{5,9},{9,... | collective-permute-start | bytes 196616 | tf_op jit(solution)/shard_map/ppermute | solution.py:565
  14.1 16.5 %collective-permute-start.3 = (bf16[256,512]{1,0:T(8,128)(2,1)}, bf16[256,512]{1,0:T(8,128)(2,1)S(1)}, u32[]{:S(2)}, u32[]{:S(2)}) collective-permute-start(bf16[256,512]{1,0:T(8,128)(2,1)} %get-tuple-element.22), channel_id=1, source_target_pairs={{0,16},{4,20},{8,24},{12,28},{1,17},{5,21},{9,25},{13,29},{2,18},{... | collective-permute-start | bytes 786440 | tf_op jit(solution)/shard_map/ppermute | solution.py:565
  18.5 12.0 %collective-permute-start.2 = (bf16[256,512]{1,0:T(8,128)(2,1)}, bf16[256,512]{1,0:T(8,128)(2,1)S(1)}, u32[]{:S(2)}, u32[]{:S(2)}) collective-permute-start(bf16[256,512]{1,0:T(8,128)(2,1)} %get-tuple-element.22), channel_id=1, source_target_pairs={{0,8},{4,12},{8,16},{12,20},{16,24},{20,28},{1,9},{5,13},{9,17},{1... | collective-permute-start | bytes 786440 | tf_op jit(solution)/shard_map/ppermute | solution.py:565
  21.9 0.6 copy-start.8
  22.6 8.0 %copy-start.4 = (bf16[256,512]{1,0:T(8,128)(2,1)S(1)}, bf16[256,512]{1,0:T(8,128)(2,1)}, u32[]{:S(2)}) copy-start(bf16[256,512]{1,0:T(8,128)(2,1)} %get-tuple-element.22) | copy-start | bytes 786436
  22.6 10.4 %copy-start.6 = (s32[2048]{0:T(1024)S(1)}, s32[2048]{0:T(1024)}, u32[]{:S(2)}) copy-start(s32[2048]{0:T(1024)} %param.27) | copy-start | bytes 24580
  22.6 10.7 %copy-start.1 = (s32[4]{0:T(128)S(1)}, s32[4]{0:T(128)}, u32[]{:S(2)}) copy-start(s32[4]{0:T(128)} %lengths_ref.7) | copy-start | bytes 52
  28.6 4.7 %copy-start = (bf16[256,2048]{1,0:T(8,128)(2,1)S(1)}, bf16[256,2048]{1,0:T(8,128)(2,1)}, u32[]{:S(2)}) copy-start(bf16[256,2048]{1,0:T(8,128)(2,1)} %q_ref.3) | copy-start | bytes 3145732
  30.6 9.6 %copy-start.3 = (bf16[544,256]{1,0:T(8,128)(2,1)S(1)}, bf16[544,256]{1,0:T(8,128)(2,1)}, u32[]{:S(2)}) copy-start(bf16[544,256]{1,0:T(8,128)(2,1)} %get-tuple-element.20) | copy-start | bytes 835588
  30.7 2.7 %collective-permute-start.4 = (bf16[3,256,512]{2,1,0:T(8,128)(2,1)S(1)}, bf16[3,256,512]{2,1,0:T(8,128)(2,1)S(1)}, u32[]{:S(2)}, u32[]{:S(2)}) collective-permute-start(bf16[3,256,512]{2,1,0:T(8,128)(2,1)S(1)} %pad_maximum_fusion.mine_ref), channel_id=1, source_target_pairs={{0,4},{4,0},{8,12},{12,8},{16,20},{20,16},{24,28},{28,24},{1,5},{5... | collective-permute-start | bytes 2359304 | tf_op jit(solution)/shard_map/ppermute | solution.py:571
  31.4 8.9 %collective-permute-start.1 = (bf16[544,256]{1,0:T(8,128)(2,1)}, bf16[544,256]{1,0:T(8,128)(2,1)S(1)}, u32[]{:S(2)}, u32[]{:S(2)}) collective-permute-start(bf16[544,256]{1,0:T(8,128)(2,1)} %get-tuple-element.20), channel_id=1, source_target_pairs={{0,1},{1,0},{2,3},{3,2},{4,5},{5,4},{6,7},{7,6},{8,9},{9,8},{10,11... | collective-permute-start | bytes 835592 | tf_op jit(solution)/shard_map/ppermute | solution.py:620
  40.3 14.7 %collective-permute-start.5 = (bf16[544,256]{1,0:T(8,128)(2,1)S(1)}, bf16[544,256]{1,0:T(8,128)(2,1)S(1)}, u32[]{:S(2)}, u32[]{:S(2)}) collective-permute-start(bf16[544,256]{1,0:T(8,128)(2,1)S(1)} %add_convert_fusion.1), channel_id=1, source_target_pairs={{0,2},{1,3},{2,0},{3,1},{4,6},{5,7},{6,4},{7,5},{8,10},{9,11},{10,... | collective-permute-start | bytes 835592 | tf_op jit(solution)/shard_map/ppermute | solution.py:620
  55.1 30.9 %all-to-all-start = ((bf16[8,32,2048]{2,1,0:T(8,128)(2,1)}), bf16[8,32,2048]{2,1,0:T(8,128)(2,1)S(1)}, u32[]{:S(2)}, u32[]{:S(2)}) async-start(bf16[8,32,2048]{2,1,0:T(8,128)(2,1)} %bitcast.7), calls=%async_computation | async-start | bytes 2097152 | tf_op jit(solution)/shard_map/all_to_all | solution.py:629
  73.9 7.3 %collective-permute-start.7 = (bf16[288,128]{1,0:T(8,128)(2,1)}, bf16[288,128]{1,0:T(8,128)(2,1)S(1)}, u32[]{:S(2)}, u32[]{:S(2)}) collective-permute-start(bf16[288,128]{1,0:T(8,128)(2,1)} %get-tuple-element.35), channel_id=1, source_target_pairs={{0,16},{4,20},{8,24},{12,28},{1,17},{5,21},{9,25},{13,29},{2,18},{... | collective-permute-start | bytes 221192 | tf_op jit(solution)/shard_map/ppermute | solution.py:565
  78.0 5.4 %collective-permute-start.6 = (bf16[288,128]{1,0:T(8,128)(2,1)}, bf16[288,128]{1,0:T(8,128)(2,1)S(1)}, u32[]{:S(2)}, u32[]{:S(2)}) collective-permute-start(bf16[288,128]{1,0:T(8,128)(2,1)} %get-tuple-element.35), channel_id=1, source_target_pairs={{0,8},{4,12},{8,16},{12,20},{16,24},{20,28},{1,9},{5,13},{9,17},{1... | collective-permute-start | bytes 221192 | tf_op jit(solution)/shard_map/ppermute | solution.py:565
  84.4 1.6 %copy-start.5 = (bf16[3,288,128]{2,1,0:T(8,128)(2,1)}, bf16[3,288,128]{2,1,0:T(8,128)(2,1)S(1)}, u32[]{:S(2)}) copy-start(bf16[3,288,128]{2,1,0:T(8,128)(2,1)S(1)} %pad_maximum_fusion.1.mine_ref) | copy-start | bytes 663556
  84.4 1.5 %collective-permute-start.8 = (bf16[3,288,128]{2,1,0:T(8,128)(2,1)S(1)}, bf16[3,288,128]{2,1,0:T(8,128)(2,1)S(1)}, u32[]{:S(2)}, u32[]{:S(2)}) collective-permute-start(bf16[3,288,128]{2,1,0:T(8,128)(2,1)S(1)} %pad_maximum_fusion.1.mine_ref), channel_id=1, source_target_pairs={{0,4},{4,0},{8,12},{12,8},{16,20},{20,16},{24,28},{28,24},{1,5},{5... | collective-permute-start | bytes 663560 | tf_op jit(solution)/shard_map/ppermute | solution.py:571
  85.9 0.7 copy-start.7
  86.0 1.1 %copy-start.2 = (bf16[8,32,2048]{2,1,0:T(8,128)(2,1)}, bf16[8,32,2048]{2,1,0:T(8,128)(2,1)S(1)}, u32[]{:S(2)}) copy-start(bf16[8,32,2048]{2,1,0:T(8,128)(2,1)S(1)} %all-to-all-done) | copy-start | bytes 3145732

commit v6 on v5

--- a/solution.py
+++ b/solution.py
@@ -37,31 +37,30 @@
     return 512 if channels % 512 == 0 else channels
 
 
-def pack_kernel(x_ref, k_ref, v_ref, halo_ref, kv_ref, sems):
-    tok, width = k_ref.shape
-    copies = [
-        pltpu.make_async_copy(x_ref.at[pl.ds(tok - HALO, HALO), :], halo_ref, sems.at[0]),
-        pltpu.make_async_copy(k_ref, kv_ref.at[:, pl.ds(0, width)], sems.at[1]),
-        pltpu.make_async_copy(v_ref, kv_ref.at[:, pl.ds(width, width)], sems.at[2]),
-    ]
-    for copy in copies:
-        copy.start()
-    for copy in copies:
-        copy.wait()
+def pack_kernel(x_ref, k_ref, v_ref, halo_ref, kv_ref):
+    width = k_ref.shape[1]
+    halo_ref[...] = x_ref[...]
+    kv_ref[:, :width] = k_ref[...]
+    kv_ref[:, width:] = v_ref[...]
 
 
 def pack(x_branch, key_rows, value_rows):
     tok, channels = x_branch.shape
     width = key_rows.shape[1]
+    whole = lambda rows, columns: pl.BlockSpec((rows, columns), lambda i: (0, 0))
     return pl.pallas_call(
         pack_kernel,
-        in_specs=[pl.BlockSpec(memory_space=pl.ANY)] * 3,
-        out_specs=[pl.BlockSpec(memory_space=pl.ANY)] * 2,
+        grid=(1,),
+        in_specs=[
+            pl.BlockSpec((HALO, channels), lambda i: (tok // HALO - 1, 0)),
+            whole(tok, width),
+            whole(tok, width),
+        ],
+        out_specs=[whole(HALO, channels), whole(tok, 2 * width)],
         out_shape=[
             jax.ShapeDtypeStruct((HALO, channels), x_branch.dtype),
             jax.ShapeDtypeStruct((tok, 2 * width), key_rows.dtype),
         ],
-        scratch_shapes=[pltpu.SemaphoreType.DMA((3,))],
         compiler_params=pltpu.CompilerParams(vmem_limit_bytes=VMEM_MOST),
         cost_estimate=pl.CostEstimate(flops=0, bytes_accessed=16 * tok * width, transcendentals=0),
         name="pack",
@@ -159,18 +158,24 @@
     return slice(tile * ROWS, (tile + 1) * ROWS)
 
 
+def added(one_ref, other_ref, rows):
+    total = one_ref[rows, :].astype(jnp.float32) + other_ref[rows, :].astype(jnp.float32)
+    return total.astype(jnp.bfloat16).astype(jnp.float32)
+
+
 def by_register(rate_ref, rates):
     states = rate_ref.shape[0]
     count = rates.shape[0] // states
     for n in range(states):
         for h in range(count):
             tiles = [rate_ref[n : n + 1, lane(h * ROWS + j)] for j in range(ROWS)]
-            rates[n * count + h] = jnp.concatenate(tiles, axis=0) * (-LOG2E)
+            rates[n * count + h] = -jnp.concatenate(tiles, axis=0)
 
 
 def local_kernel(
     lengths_ref,
     proj_ref,
+    other_ref,
     dtw_ref,
     bias_ref,
     rate_ref,
@@ -197,8 +202,8 @@
 
     @pl.when(at == 0)
     def _():
-        low_cols[...] = proj_ref[:low_rank, :].astype(jnp.float32).T.astype(jnp.bfloat16)
-        bc_spread[...] = spread(proj_ref[low_rank:, :].astype(jnp.float32).T)
+        low_cols[...] = added(proj_ref, other_ref, slice(0, low_rank)).T.astype(jnp.bfloat16)
+        bc_spread[...] = spread(added(proj_ref, other_ref, slice(low_rank, None)).T)
         by_register(rate_ref, rates)
         carry[...] = jnp.zeros_like(carry)
         for first in range(0, tiles, 4):
@@ -239,7 +244,7 @@
                 for h in range(count):
                     i = n * count + h
                     rate = rates[i]
-                    decay = [jnp.exp2(rate * step[k][h]) for k in range(2)]
+                    decay = [jnp.exp(rate * step[k][h]) for k in range(2)]
                     for k in range(2):
                         held[i] = decay[k] * held[i] + b_row[k] * drive[k][h]
                         term = c_row[k] * held[i]
@@ -265,7 +270,7 @@
         state_ref[states * tiles :, :] = jnp.concatenate([high, whole - high], axis=0).astype(jnp.bfloat16)
 
 
-def local_scan(lengths, projected, dt_weight, dt_bias, decay_rate, inner_act):
+def local_scan(lengths, projected, other, dt_weight, dt_bias, decay_rate, inner_act):
     tok, channels = inner_act.shape
     low_rank = dt_weight.shape[0]
     states = decay_rate.shape[0]
@@ -281,6 +286,7 @@
         in_specs=[
             pl.BlockSpec(memory_space=pltpu.SMEM),
             whole(projected),
+            whole(other),
             whole(dt_weight),
             whole(bias),
             whole(decay_rate),
@@ -308,13 +314,14 @@
             transcendentals=tok * channels * states,
         ),
         name="local_scan",
-    )(lengths, projected, dt_weight, bias, decay_rate, inner_act)
+    )(lengths, projected, other, dt_weight, bias, decay_rate, inner_act)
 
 
 def join_kernel(
     low_rank,
     reach,
     proj_ref,
+    other_ref,
     y_ref,
     sum_ref,
     inner_ref,
@@ -340,7 +347,7 @@
 
     @pl.when(at == 0)
     def _():
-        c_spread[...] = spread(proj_ref[low_rank + states :, :].astype(jnp.float32).T)
+        c_spread[...] = spread(added(proj_ref, other_ref, slice(low_rank + states, None)).T)
         by_register(rate_ref, rates)
         odd = lax.rem(lax.axis_index("seq"), 2)
         state = [jnp.zeros((ROWS, LANES), jnp.float32)] * kept
@@ -349,7 +356,7 @@
             sent = ref[which].astype(jnp.float32)
             totals = sent[states * tiles : (states + 1) * tiles] + sent[(states + 1) * tiles :]
             state = [
-                jnp.exp2(rates[i] * totals[sublanes(i % count)]) * state[i] + sent[sublanes(i)] for i in range(kept)
+                jnp.exp(rates[i] * totals[sublanes(i % count)]) * state[i] + sent[sublanes(i)] for i in range(kept)
             ]
         for i in range(kept):
             entering[i] = state[i]
@@ -367,7 +374,7 @@
                 for h in range(count):
                     rate, state = rates[n * count + h], entering[n * count + h]
                     for r in range(ROWS):
-                        out[r][h] += jnp.exp2(rate * total[r][h]) * state * c_row[r]
+                        out[r][h] += jnp.exp(rate * total[r][h]) * state * c_row[r]
             for r in range(ROWS):
                 for h in range(count):
                     rows_tiles[k, pl.ds(r + h * ROWS * ROWS, ROWS, stride=ROWS), :] = out[r][h]
@@ -383,7 +390,7 @@
     lax.fori_loop(0, block // PAIR, body, 0)
 
 
-def join_states(projected, y, sums, inner_act, z_branch, decay_rate, skip_gain, moved, mine, theirs, low_rank, reach):
+def join_states(projected, other, y, sums, inner_act, z_branch, decay_rate, skip_gain, moved, mine, theirs, low_rank, reach):
     tok, channels = z_branch.shape
     states = decay_rate.shape[0]
     tiles = channels // LANES
@@ -397,6 +404,7 @@
         grid=(tok // BLOCK,),
         in_specs=[
             whole(projected),
+            whole(other),
             by_token,
             by_token,
             by_row,
@@ -422,7 +430,7 @@
             transcendentals=tok * channels * states,
         ),
         name="join_states",
-    )(projected, y, sums, inner_act, z_branch, decay_rate, skip, moved, mine, theirs)
+    )(projected, other, y, sums, inner_act, z_branch, decay_rate, skip, moved, mine, theirs)
 
 
 def attend_kernel(kv_local, first_group, lengths_ref, place_ref, q_ref, mine_ref, theirs_ref, *refs):
@@ -616,24 +624,38 @@
         return attend(lengths, send_place, query_rows, mine, theirs, parts.pop(0), attended)
 
     steps = [1 << k for k in range((n_mp - 1).bit_length())]
+    other = jnp.zeros_like(projected)
     for step in steps:
+        if step > 1:
+            projected = (projected.astype(jnp.float32) + other.astype(jnp.float32)).astype(jnp.bfloat16)
+            if parts:
+                projected, attended = fence((projected, attended))
         other = lax.ppermute(projected, "mp", [(source, source ^ step) for source in range(n_mp)])
         if parts:
             attended = attend_next()
-            other, attended = fence((other, attended))
-        projected = (projected.astype(jnp.float32) + other.astype(jnp.float32)).astype(jnp.bfloat16)
-        if parts:
-            projected, attended = fence((projected, attended))
+            if step < steps[-1]:
+                other, attended = fence((other, attended))
     while parts:
         attended = attend_next()
     regrouped = lax.all_to_all(attended, "seq", split_axis=0, concat_axis=0, tiled=True)
-    projected, _ = fence((projected, attended))
-
-    y, sums, state = local_scan(lengths, projected, dt_weight, dt_bias, decay_rate, inner_act)
-    own, other = with_partner(even_back(state, reach))
+    projected, other, _ = fence((projected, other, attended))
+
+    y, sums, state = local_scan(lengths, projected, other, dt_weight, dt_bias, decay_rate, inner_act)
+    states = with_partner(even_back(state, reach))
     return tuple(
         join_states(
-            projected, y, sums, inner_act, z_branch, decay_rate, skip_gain, regrouped, own, other, low_rank, reach
+            projected,
+            other,
+            y,
+            sums,
+            inner_act,
+            z_branch,
+            decay_rate,
+            skip_gain,
+            regrouped,
+            *states,
+            low_rank,
+            reach,
         )
     )
 

time: 97.3 us -> 96.7 us (level)
  Pallas kernels: 46.4 us -> 39.5 us
  waiting for transfers between devices: 19.3 us -> 23.3 us
  starting transfers between devices: 26.8 us -> 29.1 us
    pallas_call x1, Pallas kernels: 11.1 us -> 1.73 us  [pack(): pl.pallas_call(pack_kernel, grid=(1,), in_specs=[pl.BlockSpec((HALO, chan...]
    ppermute x2, waiting for transfers between devices: 13.3 us -> 17.3 us  [local(): lax.ppermute(projected, 'mp', [(source, source ^ step) for source in rang...]
    all_to_all x1, starting transfers between devices: 4.26 us -> 6.94 us  [local(): lax.all_to_all(attended, 'seq', split_axis=0, concat_axis=0, tiled=True)]
    pallas_call x1, Pallas kernels: 13.8 us -> 15 us  [local_scan(): pl.pallas_call(local_kernel, grid=(tok // BLOCK,), in_specs=[pl.BlockSpec...]
    pallas_call x1, Pallas kernels: 9.82 us -> 11.1 us  [join_states(): pl.pallas_call(functools.partial(join_kernel, low_rank, reach), grid=(tok...]
    unnamed x18 -> x22, local copies, waits for them, and re-layouts: 1.72 us -> 2.42 us
  transfers between devices with their start and end apart: 10 -> 10, of which waited for: 6 -> 6; matrix products, arithmetic and copies ran while one was open for 2% -> 1% of each run, Pallas kernels for 26% -> 25%
where the time goes in v6:
time: 96.7 us; the launch traced here: 96.3 us
  Pallas kernels  39.5 us (41%)
  starting transfers between devices  29.1 us (30%)
  waiting for transfers between devices  23.3 us (24%)
  local copies, waits for them, and re-layouts  2.42 us (3%)
  other arithmetic  1.08 us (1%)
    ppermute x2, waiting for transfers between devices, local(): lax.ppermute(projected, 'mp', [(source, source ^ step) for source in rang...  17.3 us
    ppermute x5, starting transfers between devices, shifted(): lax.ppermute(value, 'seq', [(source, source + steps) for source in range(...  17.2 us
    pallas_call x1, Pallas kernels, local_scan(): pl.pallas_call(local_kernel, grid=(tok // BLOCK,), in_specs=[pl.BlockSpec...  15 us
    pallas_call x1, Pallas kernels, join_states(): pl.pallas_call(functools.partial(join_kernel, low_rank, reach), grid=(tok...  11.1 us
    all_to_all x1, starting transfers between devices, local(): lax.all_to_all(attended, 'seq', split_axis=0, concat_axis=0, tiled=True)  6.94 us
    pallas_call x1, Pallas kernels, conv_project(): pl.pallas_call(conv_kernel, grid=(channels // chunk,), in_specs=[pl.Block...  6.01 us
    pallas_call x2, Pallas kernels, attend(): pl.pallas_call(functools.partial(attend_kernel, kv_local, groups[0]), gri...  5.74 us
    ppermute x2, starting transfers between devices, local(): lax.ppermute(projected, 'mp', [(source, source ^ step) for source in rang...  4.23 us
  transfers between devices with their start and end apart: 10, of which 6 were waited for; matrix products, arithmetic and copies ran while one was open for 1% of the time, Pallas kernels for 25%

profile of v6, /device:TPU:0, one launch (start us, length us, event | category | flops | bytes accessed | tf_op | source)
XLA Modules:
  0.0 96.3 jit_solution(3013349368661903064)
XLA Ops:
  0.6 1.7 %pack.1 = (bf16[16,2048]{1,0:T(8,128)(2,1)}, bf16[256,512]{1,0:T(8,128)(2,1)}) custom-call(bf16[256,2048]{1,0:T(8,128)(2,1)} %x_ref.3, bf16[256,256]{1,0:T(8,128)(2,1)} %k_ref.1, bf16[256,256]{1,0:T(8,128)(2,1)} %v_ref.1), custom_call_target="tpu_custom_call" | custom-call | bytes 1048576 | tf_op jit(solution)/shard_map/pack/pallas_call | solution.py:51
  2.4 2.3 %collective-permute-start = (bf16[16,2048]{1,0:T(8,128)(2,1)}, bf16[16,2048]{1,0:T(8,128)(2,1)S(1)}, u32[]{:S(2)}, u32[]{:S(2)}) collective-permute-start(bf16[16,2048]{1,0:T(8,128)(2,1)} %get-tuple-element.18), channel_id=1, source_target_pairs={{0,4},{4,8},{8,12},{12,16},{16,20},{20,24},{24,28},{1,5},{5,9},{9,... | collective-permute-start | bytes 196616 | tf_op jit(solution)/shard_map/ppermute | solution.py:573
  4.7 4.4 %collective-permute-start.3 = (bf16[256,512]{1,0:T(8,128)(2,1)}, bf16[256,512]{1,0:T(8,128)(2,1)S(1)}, u32[]{:S(2)}, u32[]{:S(2)}) collective-permute-start(bf16[256,512]{1,0:T(8,128)(2,1)} %get-tuple-element.21), channel_id=1, source_target_pairs={{0,16},{4,20},{8,24},{12,28},{1,17},{5,21},{9,25},{13,29},{2,18},{... | collective-permute-start | bytes 786440 | tf_op jit(solution)/shard_map/ppermute | solution.py:573
  9.2 3.4 %collective-permute-start.2 = (bf16[256,512]{1,0:T(8,128)(2,1)}, bf16[256,512]{1,0:T(8,128)(2,1)S(1)}, u32[]{:S(2)}, u32[]{:S(2)}) collective-permute-start(bf16[256,512]{1,0:T(8,128)(2,1)} %get-tuple-element.21), channel_id=1, source_target_pairs={{0,8},{4,12},{8,16},{12,20},{16,24},{20,28},{1,9},{5,13},{9,17},{1... | collective-permute-start | bytes 786440 | tf_op jit(solution)/shard_map/ppermute | solution.py:573
  12.6 0.0 collective-permute-done.halo_ref
  12.6 0.6 copy-done.10
  13.2 6.0 %conv_project.1 = (bf16[256,2048]{1,0:T(8,128)(2,1)}, bf16[544,256]{1,0:T(8,128)(2,1)}) custom-call(s32[4]{0:T(128)} %lengths_ref.7, bf16[256,2048]{1,0:T(8,128)(2,1)} %x_ref.3, bf16[16,2048]{1,0:T(8,128)(2,1)} %copy-done.10, f32[4,2048]{1,0:T(4,128)} %w_ref.1, f32[1,2048]{1,0:T(1,128)} %bitcast.20, bf16[544,2048]{1,0:T(8,128)(2,1)} %bitcast.19), custom_call_target="tpu_custom_call" | custom-call | flops 22817013760 | bytes 4194304 | tf_op jit(solution)/shard_map/conv_project/pallas_call | solution.py:109
  19.2 2.0 %collective-permute-done.3 = bf16[256,512]{1,0:T(8,128)(2,1)S(1)} collective-permute-done((bf16[256,512]{1,0:T(8,128)(2,1)}, bf16[256,512]{1,0:T(8,128)(2,1)S(1)}, u32[]{:S(2)}, u32[]{:S(2)}) %collective-permute-start.3) | collective-permute-done | bytes 262176 | tf_op jit(solution)/shard_map/ppermute | solution.py:573
  21.2 0.0 collective-permute-done.2
  21.2 0.1 pad_maximum_fusion.mine_ref
  21.3 0.0 copy-start.4
  21.3 0.8 collective-permute-start.4
  22.1 1.6 %collective-permute-start.1 = (bf16[544,256]{1,0:T(8,128)(2,1)}, bf16[544,256]{1,0:T(8,128)(2,1)S(1)}, u32[]{:S(2)}, u32[]{:S(2)}) collective-permute-start(bf16[544,256]{1,0:T(8,128)(2,1)} %get-tuple-element.19), channel_id=1, source_target_pairs={{0,1},{1,0},{2,3},{3,2},{4,5},{5,4},{6,7},{7,6},{8,9},{9,8},{10,11... | collective-permute-start | bytes 835592 | tf_op jit(solution)/shard_map/ppermute | solution.py:633
  23.7 0.3 collective-permute-done.4.theirs_ref
  24.0 2.9 %attend.2.refs_0_ = bf16[256,2048]{1,0:T(8,128)(2,1)} custom-call(s32[4]{0:T(128)S(1)} %copy-done.1, s32[8,256]{1,0:T(8,128)S(1)} %reshape.19.place_ref, bf16[256,2048]{1,0:T(8,128)(2,1)S(1)} %copy-done, bf16[3,256,512]{2,1,0:T(8,128)(2,1)S(1)} %pad_maximum_fusion.mine_ref, bf16[3,256,512]{2,1,0:T(8,128)(2,1)S(1)} %collective-permute-done.4.theirs_ref), custom_call_target="tpu_custom_call" | custom-call | flops 262144 | bytes 262144 | tf_op jit(solution)/shard_map/attend/pallas_call | solution.py:550
  26.8 4.1 %collective-permute-done.1 = bf16[544,256]{1,0:T(8,128)(2,1)S(1)} collective-permute-done((bf16[544,256]{1,0:T(8,128)(2,1)}, bf16[544,256]{1,0:T(8,128)(2,1)S(1)}, u32[]{:S(2)}, u32[]{:S(2)}) %collective-permute-start.1) | collective-permute-done | bytes 278560 | tf_op jit(solution)/shard_map/ppermute | solution.py:633
  30.9 0.1 add_convert_fusion.proj_ref
  31.0 2.9 %attend.3 = bf16[256,2048]{1,0:T(8,128)(2,1)} custom-call(s32[4]{0:T(128)S(1)} %copy-done.1, s32[8,256]{1,0:T(8,128)S(1)} %reshape.19.place_ref, bf16[256,2048]{1,0:T(8,128)(2,1)S(1)} %copy-done, bf16[3,256,512]{2,1,0:T(8,128)(2,1)S(1)} %pad_maximum_fusion.mine_ref, ...), custom_call_target="tpu_custom_call", output_to_operand_aliasing={{}: (5, {})} | custom-call | flops 262144 | bytes 262144 | tf_op jit(solution)/shard_map/attend/pallas_call | solution.py:550
  33.9 6.9 %all-to-all-start = ((bf16[8,32,2048]{2,1,0:T(8,128)(2,1)}), bf16[8,32,2048]{2,1,0:T(8,128)(2,1)S(1)}, u32[]{:S(2)}, u32[]{:S(2)}) async-start(bf16[8,32,2048]{2,1,0:T(8,128)(2,1)} %bitcast.7), calls=%async_computation | async-start | bytes 2097152 | tf_op jit(solution)/shard_map/all_to_all | solution.py:640
  40.8 2.7 %collective-permute-start.5 = (bf16[544,256]{1,0:T(8,128)(2,1)S(1)}, bf16[544,256]{1,0:T(8,128)(2,1)S(1)}, u32[]{:S(2)}, u32[]{:S(2)}) collective-permute-start(bf16[544,256]{1,0:T(8,128)(2,1)S(1)} %add_convert_fusion.proj_ref), channel_id=1, source_target_pairs={{0,2},{1,3},{2,0},{3,1},{4,6},{5,7},{6,4},{7,5},{8,10},{9,11},{10,... | collective-permute-start | bytes 835592 | tf_op jit(solution)/shard_map/ppermute | solution.py:633
  43.5 13.3 %collective-permute-done.5.other_ref = bf16[544,256]{1,0:T(8,128)(2,1)S(1)} collective-permute-done((bf16[544,256]{1,0:T(8,128)(2,1)S(1)}, bf16[544,256]{1,0:T(8,128)(2,1)S(1)}, u32[]{:S(2)}, u32[]{:S(2)}) %collective-permute-start.5) | collective-permute-done | bytes 278560 | tf_op jit(solution)/shard_map/ppermute | solution.py:633
  56.7 0.7 copy-done.8
  57.5 15.0 %local_scan.1 = (f32[256,16,128]{2,1,0:T(8,128)}, f32[256,16,128]{2,1,0:T(8,128)}, bf16[288,128]{1,0:T(8,128)(2,1)}) custom-call(s32[4]{0:T(128)} %lengths_ref.7, bf16[544,256]{1,0:T(8,128)(2,1)} %copy-done.3, bf16[544,256]{1,0:T(8,128)(2,1)} %copy-done.8, bf16[512,2048]{1,0:T(8,128)(2,1)} %dtw_ref.1, f32[1,2048]{1,0:T(1,128)} %bitcast.21, ...), custom_call_target="tpu_custom_call" | custom-call | flops 100663296 | bytes 6291456 | tf_op jit(solution)/shard_map/local_scan/pallas_call | solution.py:283
  72.5 4.1 %collective-permute-start.7 = (bf16[288,128]{1,0:T(8,128)(2,1)}, bf16[288,128]{1,0:T(8,128)(2,1)S(1)}, u32[]{:S(2)}, u32[]{:S(2)}) collective-permute-start(bf16[288,128]{1,0:T(8,128)(2,1)} %get-tuple-element.33), channel_id=1, source_target_pairs={{0,16},{4,20},{8,24},{12,28},{1,17},{5,21},{9,25},{13,29},{2,18},{... | collective-permute-start | bytes 221192 | tf_op jit(solution)/shard_map/ppermute | solution.py:573
  76.6 2.8 %collective-permute-start.6 = (bf16[288,128]{1,0:T(8,128)(2,1)}, bf16[288,128]{1,0:T(8,128)(2,1)S(1)}, u32[]{:S(2)}, u32[]{:S(2)}) collective-permute-start(bf16[288,128]{1,0:T(8,128)(2,1)} %get-tuple-element.33), channel_id=1, source_target_pairs={{0,8},{4,12},{8,16},{12,20},{16,24},{20,28},{1,9},{5,13},{9,17},{1... | collective-permute-start | bytes 221192 | tf_op jit(solution)/shard_map/ppermute | solution.py:573
  79.4 2.3 %collective-permute-done.6 = bf16[288,128]{1,0:T(8,128)(2,1)S(1)} collective-permute-done((bf16[288,128]{1,0:T(8,128)(2,1)}, bf16[288,128]{1,0:T(8,128)(2,1)S(1)}, u32[]{:S(2)}, u32[]{:S(2)}) %collective-permute-start.6) | collective-permute-done | bytes 73760 | tf_op jit(solution)/shard_map/ppermute | solution.py:573
  81.7 0.9 pad_maximum_fusion.1.mine_ref
  82.6 0.1 collective-permute-start.8
  82.7 1.5 %collective-permute-done.8.theirs_ref = bf16[3,288,128]{2,1,0:T(8,128)(2,1)S(1)} collective-permute-done((bf16[3,288,128]{2,1,0:T(8,128)(2,1)S(1)}, bf16[3,288,128]{2,1,0:T(8,128)(2,1)S(1)}, u32[]{:S(2)}, u32[]{:S(2)}) %collective-permute-start.8) | collective-permute-done | bytes 221216 | tf_op jit(solution)/shard_map/ppermute | solution.py:579
  84.2 0.7 copy-done.9
  84.9 0.4 copy-done.2
  85.3 11.1 %join_states.1 = (bf16[256,2048]{1,0:T(8,128)(2,1)}, bf16[256,2048]{1,0:T(8,128)(2,1)}) custom-call(bf16[544,256]{1,0:T(8,128)(2,1)} %copy-done.3, bf16[544,256]{1,0:T(8,128)(2,1)} %copy-done.8, f32[256,16,128]{2,1,0:T(8,128)} %get-tuple-element.31.y_ref, f32[256,16,128]{2,1,0:T(8,128)} %get-tuple-element.32.sum_ref, ...), custom_call_target="tpu_custom_call" | custom-call | flops 67108864 | bytes 7340032 | tf_op jit(solution)/shard_map/join_states/pallas_call | solution.py:402
  (21 shorter events, 0.1 us)
Async XLA Ops:
  2.4 10.2 %collective-permute-start = (bf16[16,2048]{1,0:T(8,128)(2,1)}, bf16[16,2048]{1,0:T(8,128)(2,1)S(1)}, u32[]{:S(2)}, u32[]{:S(2)}) collective-permute-start(bf16[16,2048]{1,0:T(8,128)(2,1)} %get-tuple-element.18), channel_id=1, source_target_pairs={{0,4},{4,8},{8,12},{12,16},{16,20},{20,24},{24,28},{1,5},{5,9},{9,... | collective-permute-start | bytes 196616 | tf_op jit(solution)/shard_map/ppermute | solution.py:573
  4.7 16.5 %collective-permute-start.3 = (bf16[256,512]{1,0:T(8,128)(2,1)}, bf16[256,512]{1,0:T(8,128)(2,1)S(1)}, u32[]{:S(2)}, u32[]{:S(2)}) collective-permute-start(bf16[256,512]{1,0:T(8,128)(2,1)} %get-tuple-element.21), channel_id=1, source_target_pairs={{0,16},{4,20},{8,24},{12,28},{1,17},{5,21},{9,25},{13,29},{2,18},{... | collective-permute-start | bytes 786440 | tf_op jit(solution)/shard_map/ppermute | solution.py:573
  9.2 12.0 %collective-permute-start.2 = (bf16[256,512]{1,0:T(8,128)(2,1)}, bf16[256,512]{1,0:T(8,128)(2,1)S(1)}, u32[]{:S(2)}, u32[]{:S(2)}) collective-permute-start(bf16[256,512]{1,0:T(8,128)(2,1)} %get-tuple-element.21), channel_id=1, source_target_pairs={{0,8},{4,12},{8,16},{12,20},{16,24},{20,28},{1,9},{5,13},{9,17},{1... | collective-permute-start | bytes 786440 | tf_op jit(solution)/shard_map/ppermute | solution.py:573
  12.6 0.6 copy-start.10
  13.2 8.0 %copy-start.5 = (bf16[256,512]{1,0:T(8,128)(2,1)S(1)}, bf16[256,512]{1,0:T(8,128)(2,1)}, u32[]{:S(2)}) copy-start(bf16[256,512]{1,0:T(8,128)(2,1)} %get-tuple-element.21) | copy-start | bytes 786436
  13.2 10.4 %copy-start.7 = (s32[2048]{0:T(1024)S(1)}, s32[2048]{0:T(1024)}, u32[]{:S(2)}) copy-start(s32[2048]{0:T(1024)} %param.27) | copy-start | bytes 24580
  13.2 10.8 %copy-start.1 = (s32[4]{0:T(128)S(1)}, s32[4]{0:T(128)}, u32[]{:S(2)}) copy-start(s32[4]{0:T(128)} %lengths_ref.7) | copy-start | bytes 52
  19.2 4.7 %copy-start = (bf16[256,2048]{1,0:T(8,128)(2,1)S(1)}, bf16[256,2048]{1,0:T(8,128)(2,1)}, u32[]{:S(2)}) copy-start(bf16[256,2048]{1,0:T(8,128)(2,1)} %q_ref.3) | copy-start | bytes 3145732
  21.3 9.6 %copy-start.4 = (bf16[544,256]{1,0:T(8,128)(2,1)S(1)}, bf16[544,256]{1,0:T(8,128)(2,1)}, u32[]{:S(2)}) copy-start(bf16[544,256]{1,0:T(8,128)(2,1)} %get-tuple-element.19) | copy-start | bytes 835588
  21.3 2.7 %collective-permute-start.4 = (bf16[3,256,512]{2,1,0:T(8,128)(2,1)S(1)}, bf16[3,256,512]{2,1,0:T(8,128)(2,1)S(1)}, u32[]{:S(2)}, u32[]{:S(2)}) collective-permute-start(bf16[3,256,512]{2,1,0:T(8,128)(2,1)S(1)} %pad_maximum_fusion.mine_ref), channel_id=1, source_target_pairs={{0,4},{4,0},{8,12},{12,8},{16,20},{20,16},{24,28},{28,24},{1,5},{5... | collective-permute-start | bytes 2359304 | tf_op jit(solution)/shard_map/ppermute | solution.py:579
  22.1 8.9 %collective-permute-start.1 = (bf16[544,256]{1,0:T(8,128)(2,1)}, bf16[544,256]{1,0:T(8,128)(2,1)S(1)}, u32[]{:S(2)}, u32[]{:S(2)}) collective-permute-start(bf16[544,256]{1,0:T(8,128)(2,1)} %get-tuple-element.19), channel_id=1, source_target_pairs={{0,1},{1,0},{2,3},{3,2},{4,5},{5,4},{6,7},{7,6},{8,9},{9,8},{10,11... | collective-permute-start | bytes 835592 | tf_op jit(solution)/shard_map/ppermute | solution.py:633
  31.0 9.8 %copy-start.3 = (bf16[544,256]{1,0:T(8,128)(2,1)}, bf16[544,256]{1,0:T(8,128)(2,1)S(1)}, u32[]{:S(2)}) copy-start(bf16[544,256]{1,0:T(8,128)(2,1)S(1)} %add_convert_fusion.proj_ref) | copy-start | bytes 835588
  33.9 50.3 %all-to-all-start = ((bf16[8,32,2048]{2,1,0:T(8,128)(2,1)}), bf16[8,32,2048]{2,1,0:T(8,128)(2,1)S(1)}, u32[]{:S(2)}, u32[]{:S(2)}) async-start(bf16[8,32,2048]{2,1,0:T(8,128)(2,1)} %bitcast.7), calls=%async_computation | async-start | bytes 2097152 | tf_op jit(solution)/shard_map/all_to_all | solution.py:640
  40.8 15.9 %collective-permute-start.5 = (bf16[544,256]{1,0:T(8,128)(2,1)S(1)}, bf16[544,256]{1,0:T(8,128)(2,1)S(1)}, u32[]{:S(2)}, u32[]{:S(2)}) collective-permute-start(bf16[544,256]{1,0:T(8,128)(2,1)S(1)} %add_convert_fusion.proj_ref), channel_id=1, source_target_pairs={{0,2},{1,3},{2,0},{3,1},{4,6},{5,7},{6,4},{7,5},{8,10},{9,11},{10,... | collective-permute-start | bytes 835592 | tf_op jit(solution)/shard_map/ppermute | solution.py:633
  56.7 0.7 copy-start.8
  72.5 7.0 %collective-permute-start.7 = (bf16[288,128]{1,0:T(8,128)(2,1)}, bf16[288,128]{1,0:T(8,128)(2,1)S(1)}, u32[]{:S(2)}, u32[]{:S(2)}) collective-permute-start(bf16[288,128]{1,0:T(8,128)(2,1)} %get-tuple-element.33), channel_id=1, source_target_pairs={{0,16},{4,20},{8,24},{12,28},{1,17},{5,21},{9,25},{13,29},{2,18},{... | collective-permute-start | bytes 221192 | tf_op jit(solution)/shard_map/ppermute | solution.py:573
  76.6 5.1 %collective-permute-start.6 = (bf16[288,128]{1,0:T(8,128)(2,1)}, bf16[288,128]{1,0:T(8,128)(2,1)S(1)}, u32[]{:S(2)}, u32[]{:S(2)}) collective-permute-start(bf16[288,128]{1,0:T(8,128)(2,1)} %get-tuple-element.33), channel_id=1, source_target_pairs={{0,8},{4,12},{8,16},{12,20},{16,24},{20,28},{1,9},{5,13},{9,17},{1... | collective-permute-start | bytes 221192 | tf_op jit(solution)/shard_map/ppermute | solution.py:573
  82.6 1.6 %copy-start.6 = (bf16[3,288,128]{2,1,0:T(8,128)(2,1)}, bf16[3,288,128]{2,1,0:T(8,128)(2,1)S(1)}, u32[]{:S(2)}) copy-start(bf16[3,288,128]{2,1,0:T(8,128)(2,1)S(1)} %pad_maximum_fusion.1.mine_ref) | copy-start | bytes 663556
  82.6 1.5 %collective-permute-start.8 = (bf16[3,288,128]{2,1,0:T(8,128)(2,1)S(1)}, bf16[3,288,128]{2,1,0:T(8,128)(2,1)S(1)}, u32[]{:S(2)}, u32[]{:S(2)}) collective-permute-start(bf16[3,288,128]{2,1,0:T(8,128)(2,1)S(1)} %pad_maximum_fusion.1.mine_ref), channel_id=1, source_target_pairs={{0,4},{4,0},{8,12},{12,8},{16,20},{20,16},{24,28},{28,24},{1,5},{5... | collective-permute-start | bytes 663560 | tf_op jit(solution)/shard_map/ppermute | solution.py:579
  84.2 0.7 copy-start.9
  84.2 1.1 %copy-start.2 = (bf16[8,32,2048]{2,1,0:T(8,128)(2,1)}, bf16[8,32,2048]{2,1,0:T(8,128)(2,1)S(1)}, u32[]{:S(2)}) copy-start(bf16[8,32,2048]{2,1,0:T(8,128)(2,1)S(1)} %all-to-all-done) | copy-start | bytes 3145732

commit v7 on v6

--- a/solution.py
+++ b/solution.py
@@ -169,7 +169,7 @@
     for n in range(states):
         for h in range(count):
             tiles = [rate_ref[n : n + 1, lane(h * ROWS + j)] for j in range(ROWS)]
-            rates[n * count + h] = -jnp.concatenate(tiles, axis=0)
+            rates[n * count + h] = jnp.concatenate(tiles, axis=0) * (-LOG2E)
 
 
 def local_kernel(
@@ -244,7 +244,7 @@
                 for h in range(count):
                     i = n * count + h
                     rate = rates[i]
-                    decay = [jnp.exp(rate * step[k][h]) for k in range(2)]
+                    decay = [jnp.exp2(rate * step[k][h]) for k in range(2)]
                     for k in range(2):
                         held[i] = decay[k] * held[i] + b_row[k] * drive[k][h]
                         term = c_row[k] * held[i]
@@ -356,7 +356,7 @@
             sent = ref[which].astype(jnp.float32)
             totals = sent[states * tiles : (states + 1) * tiles] + sent[(states + 1) * tiles :]
             state = [
-                jnp.exp(rates[i] * totals[sublanes(i % count)]) * state[i] + sent[sublanes(i)] for i in range(kept)
+                jnp.exp2(rates[i] * totals[sublanes(i % count)]) * state[i] + sent[sublanes(i)] for i in range(kept)
             ]
         for i in range(kept):
             entering[i] = state[i]
@@ -374,7 +374,7 @@
                 for h in range(count):
                     rate, state = rates[n * count + h], entering[n * count + h]
                     for r in range(ROWS):
-                        out[r][h] += jnp.exp(rate * total[r][h]) * state * c_row[r]
+                        out[r][h] += jnp.exp2(rate * total[r][h]) * state * c_row[r]
             for r in range(ROWS):
                 for h in range(count):
                     rows_tiles[k, pl.ds(r + h * ROWS * ROWS, ROWS, stride=ROWS), :] = out[r][h]
@@ -433,11 +433,22 @@
     )(projected, other, y, sums, inner_act, z_branch, decay_rate, skip, moved, mine, theirs)
 
 
-def attend_kernel(kv_local, first_group, lengths_ref, place_ref, q_ref, mine_ref, theirs_ref, *refs):
-    out_ref, queries, scores, tops, acc = refs[-5:]
+def attend_kernel(
+    lengths_ref,
+    place_ref,
+    q_ref,
+    keys_mine,
+    keys_theirs,
+    values_mine,
+    values_theirs,
+    out_ref,
+    queries,
+    scores,
+    tops,
+    acc,
+):
     tok = q_ref.shape[0]
     heads = q_ref.shape[1] // HD
-    group = pl.program_id(0) + first_group
     position = lax.axis_index("seq")
     odd = lax.rem(position, 2)
     anchor = position * tok
@@ -458,19 +469,15 @@
     for head in range(heads):
         queries[head * tok : (head + 1) * tok, :HD] = q_ref[:, head * HD : (head + 1) * HD]
         queries[head * tok : (head + 1) * tok, HD:] = apart
-    key_cols = pl.ds(pl.multiple_of(group * HD, HD), HD)
-    value_cols = pl.ds(pl.multiple_of((group + kv_local) * HD, HD), HD)
-
-    def rows_of(back, cols):
+
+    def rows_of(mine_ref, theirs_ref, back):
         if isinstance(back, int) and back == 0:
-            return mine_ref[0, :, cols]
-        ours = mine_ref[back // 2, :, cols]
-        other = theirs_ref[(back + 1) // 2 - odd, :, cols]
-        return jnp.where(lax.rem(back, 2) == 0, ours, other)
+            return mine_ref[0]
+        return jnp.where(lax.rem(back, 2) == 0, mine_ref[back // 2], theirs_ref[(back + 1) // 2 - odd])
 
     def score(back):
         marks = jnp.where(in_doc(anchor - back * tok), 1.0, 0.0).astype(jnp.bfloat16)
-        keys = jnp.concatenate([rows_of(back, key_cols), marks], axis=1)
+        keys = jnp.concatenate([rows_of(keys_mine, keys_theirs, back), marks], axis=1)
         return lax.dot_general(queries[...], keys, (((1,), (1,)), ((), ())), preferred_element_type=jnp.float32)
 
     def widest(s):
@@ -502,7 +509,7 @@
     tops[...] = jnp.broadcast_to(jnp.max(tops[...], axis=1, keepdims=True), tops.shape)
 
     def weighted(back):
-        values = jnp.concatenate([rows_of(back, value_cols), jnp.ones((tok, HD), jnp.bfloat16)], axis=1)
+        values = jnp.concatenate([rows_of(values_mine, values_theirs, back), jnp.ones((tok, HD), jnp.bfloat16)], axis=1)
         top = tops[...]
         weights = [
             jnp.exp2((scores[back, :, at : at + LANES] - top).astype(jnp.bfloat16) * scale)
@@ -526,32 +533,28 @@
         out_ref[:, head * HD : (head + 1) * HD] = moved.astype(jnp.bfloat16)
 
 
-def attend(lengths, send_place, query_rows, mine, theirs, groups, so_far):
+def attend(lengths, send_place, query_rows, mine, theirs):
     tok, width = query_rows.shape
     kv_local = mine.shape[2] // (2 * HD)
     share = width // kv_local
     heads = share // HD
     reach = 2 * (mine.shape[0] - 1)
-    count = groups[1] - groups[0]
-    whole = lambda a: pl.BlockSpec(a.shape, lambda i: (0,) * a.ndim)
-    in_specs = [
-        pl.BlockSpec(memory_space=pltpu.SMEM),
-        whole(send_place),
-        pl.BlockSpec((tok, share), lambda i: (0, i + groups[0])),
-        whole(mine),
-        whole(theirs),
-    ]
-    operands = [lengths, send_place, query_rows, mine, theirs]
-    aliases = {}
-    if so_far is not None:
-        aliases = {len(operands): 0}
-        in_specs.append(pl.BlockSpec(memory_space=pl.ANY))
-        operands.append(so_far)
+    by_group = pl.BlockSpec((tok, share), lambda i: (0, i))
+    keys = pl.BlockSpec(mine.shape[:2] + (HD,), lambda i: (0, 0, i))
+    values = pl.BlockSpec(mine.shape[:2] + (HD,), lambda i: (0, 0, i + kv_local))
     return pl.pallas_call(
-        functools.partial(attend_kernel, kv_local, groups[0]),
-        grid=(count,),
-        in_specs=in_specs,
-        out_specs=pl.BlockSpec((tok, share), lambda i: (0, i + groups[0])),
+        attend_kernel,
+        grid=(kv_local,),
+        in_specs=[
+            pl.BlockSpec(memory_space=pltpu.SMEM),
+            pl.BlockSpec(send_place.shape, lambda i: (0, 0)),
+            by_group,
+            keys,
+            keys,
+            values,
+            values,
+        ],
+        out_specs=by_group,
         out_shape=jax.ShapeDtypeStruct((tok, width), jnp.bfloat16),
         scratch_shapes=[
             pltpu.VMEM((heads * tok, 2 * HD), jnp.bfloat16),
@@ -559,13 +562,10 @@
             pltpu.VMEM((heads * tok, LANES), jnp.float32),
             pltpu.VMEM((heads * tok, 2 * HD), jnp.float32),
         ],
-        input_output_aliases=aliases,
         compiler_params=pltpu.CompilerParams(vmem_limit_bytes=VMEM_LIMIT // 2 + 4 * (reach + 1) * heads * tok * tok),
-        cost_estimate=pl.CostEstimate(
-            flops=tok * share * count, bytes_accessed=tok * share * count, transcendentals=0
-        ),
+        cost_estimate=pl.CostEstimate(flops=tok * width, bytes_accessed=tok * width, transcendentals=0),
         name="attend",
-    )(*operands)
+    )(lengths, send_place, query_rows, mine, theirs, mine, theirs)
 
 
 def shifted(value, steps):
@@ -605,7 +605,6 @@
     low_rank = dt_weight.shape[0]
     reach = n_seq // 2
     run_rows = tok // n_seq
-    kv_local = key_rows.shape[1] // HD
     fence = lax.optimization_barrier
 
     halo, kv = pack(x_branch, key_rows, value_rows)
@@ -616,35 +615,23 @@
     inner_act, partial = conv_project(lengths, x_branch, earlier_rows, conv_weight, conv_bias, xproj_weight)
     _, *held = fence((partial, *held))
     mine, theirs = with_partner(held)
-    middle = max(kv_local // 2, 1)
-    parts = [groups for groups in ((0, middle), (middle, kv_local)) if groups[0] < groups[1]]
-    projected, attended = partial, None
-
-    def attend_next():
-        return attend(lengths, send_place, query_rows, mine, theirs, parts.pop(0), attended)
-
+    total, other = partial, jnp.zeros_like(partial)
     steps = [1 << k for k in range((n_mp - 1).bit_length())]
-    other = jnp.zeros_like(projected)
     for step in steps:
         if step > 1:
-            projected = (projected.astype(jnp.float32) + other.astype(jnp.float32)).astype(jnp.bfloat16)
-            if parts:
-                projected, attended = fence((projected, attended))
-        other = lax.ppermute(projected, "mp", [(source, source ^ step) for source in range(n_mp)])
-        if parts:
-            attended = attend_next()
-            if step < steps[-1]:
-                other, attended = fence((other, attended))
-    while parts:
-        attended = attend_next()
+            total = (total.astype(jnp.float32) + other.astype(jnp.float32)).astype(jnp.bfloat16)
+        if step == steps[-1]:
+            total, send_place = fence((total, send_place))
+        other = lax.ppermute(total, "mp", [(source, source ^ step) for source in range(n_mp)])
+    attended = attend(lengths, send_place, query_rows, mine, theirs)
+    total, other, attended = fence((total, other, attended))
     regrouped = lax.all_to_all(attended, "seq", split_axis=0, concat_axis=0, tiled=True)
-    projected, other, _ = fence((projected, other, attended))
-
-    y, sums, state = local_scan(lengths, projected, other, dt_weight, dt_bias, decay_rate, inner_act)
+
+    y, sums, state = local_scan(lengths, total, other, dt_weight, dt_bias, decay_rate, inner_act)
     states = with_partner(even_back(state, reach))
     return tuple(
         join_states(
-            projected,
+            total,
             other,
             y,
             sums,

time: 96.7 us -> 83.9 us (0.87)
  waiting for transfers between devices: 23.3 us -> 15.7 us
  Pallas kernels: 39.5 us -> 36.3 us
  starting transfers between devices: 29.1 us -> 26.8 us
    ppermute x2, waiting for transfers between devices: 17.3 us -> 11.7 us  [local(): lax.ppermute(total, 'mp', [(source, source ^ step) for source in range(n_...]
    all_to_all x1, starting transfers between devices: 6.94 us -> 4.22 us  [local(): lax.all_to_all(attended, 'seq', split_axis=0, concat_axis=0, tiled=True)]
    ppermute x5, waiting for transfers between devices: 4.23 us -> 2.58 us  [shifted(): lax.ppermute(value, 'seq', [(source, source + steps) for source in range(...]
    pallas_call x1, Pallas kernels: 11.1 us -> 9.9 us  [join_states(): pl.pallas_call(functools.partial(join_kernel, low_rank, reach), grid=(tok...]
    pallas_call x2 -> x1, Pallas kernels: 5.74 us -> 4.67 us  [attend(): pl.pallas_call(attend_kernel, grid=(kv_local,), in_specs=[pl.BlockSpec(me...]
    pallas_call x1, Pallas kernels: 15 us -> 14 us  [local_scan(): pl.pallas_call(local_kernel, grid=(tok // BLOCK,), in_specs=[pl.BlockSpec...]
    unnamed x22 -> x20, local copies, waits for them, and re-layouts: 2.42 us -> 1.72 us
  transfers between devices with their start and end apart: 10 -> 10, of which waited for: 6 -> 5; matrix products, arithmetic and copies ran while one was open for 1% -> 2% of each run, Pallas kernels for 25% -> 30%
where the time goes in v7:
time: 83.9 us; the launch traced here: 83.4 us
  Pallas kernels  36.3 us (43%)
  starting transfers between devices  26.8 us (32%)
  waiting for transfers between devices  15.7 us (19%)
  other arithmetic  2.04 us (2%)
  local copies, waits for them, and re-layouts  1.72 us (2%)
    ppermute x5, starting transfers between devices, shifted(): lax.ppermute(value, 'seq', [(source, source + steps) for source in range(...  17.5 us
    pallas_call x1, Pallas kernels, local_scan(): pl.pallas_call(local_kernel, grid=(tok // BLOCK,), in_specs=[pl.BlockSpec...  14 us
    ppermute x2, waiting for transfers between devices, local(): lax.ppermute(total, 'mp', [(source, source ^ step) for source in range(n_...  11.7 us
    pallas_call x1, Pallas kernels, join_states(): pl.pallas_call(functools.partial(join_kernel, low_rank, reach), grid=(tok...  9.9 us
    pallas_call x1, Pallas kernels, conv_project(): pl.pallas_call(conv_kernel, grid=(channels // chunk,), in_specs=[pl.Block...  6.01 us
    pallas_call x1, Pallas kernels, attend(): pl.pallas_call(attend_kernel, grid=(kv_local,), in_specs=[pl.BlockSpec(me...  4.67 us
    ppermute x2, starting transfers between devices, local(): lax.ppermute(total, 'mp', [(source, source ^ step) for source in range(n_...  4.3 us
    all_to_all x1, starting transfers between devices, local(): lax.all_to_all(attended, 'seq', split_axis=0, concat_axis=0, tiled=True)  4.22 us
  transfers between devices with their start and end apart: 10, of which 5 were waited for; matrix products, arithmetic and copies ran while one was open for 2% of the time, Pallas kernels for 30%

profile of v7, /device:TPU:0, one launch (start us, length us, event | category | flops | bytes accessed | tf_op | source)
XLA Modules:
  0.0 83.4 jit_solution(552780465633443333)
XLA Ops:
  0.6 1.7 %pack.1 = (bf16[16,2048]{1,0:T(8,128)(2,1)}, bf16[256,512]{1,0:T(8,128)(2,1)}) custom-call(bf16[256,2048]{1,0:T(8,128)(2,1)} %x_ref.3, bf16[256,256]{1,0:T(8,128)(2,1)} %k_ref.1, bf16[256,256]{1,0:T(8,128)(2,1)} %v_ref.1), custom_call_target="tpu_custom_call" | custom-call | bytes 1048576 | tf_op jit(solution)/shard_map/pack/pallas_call | solution.py:51
  2.4 2.3 %collective-permute-start = (bf16[16,2048]{1,0:T(8,128)(2,1)}, bf16[16,2048]{1,0:T(8,128)(2,1)S(1)}, u32[]{:S(2)}, u32[]{:S(2)}) collective-permute-start(bf16[16,2048]{1,0:T(8,128)(2,1)} %get-tuple-element.17), channel_id=1, source_target_pairs={{0,4},{4,8},{8,12},{12,16},{16,20},{20,24},{24,28},{1,5},{5,9},{9,... | collective-permute-start | bytes 196616 | tf_op jit(solution)/shard_map/ppermute | solution.py:573
  4.7 4.4 %collective-permute-start.4 = (bf16[256,512]{1,0:T(8,128)(2,1)}, bf16[256,512]{1,0:T(8,128)(2,1)S(1)}, u32[]{:S(2)}, u32[]{:S(2)}) collective-permute-start(bf16[256,512]{1,0:T(8,128)(2,1)} %get-tuple-element.22), channel_id=1, source_target_pairs={{0,16},{4,20},{8,24},{12,28},{1,17},{5,21},{9,25},{13,29},{2,18},{... | collective-permute-start | bytes 786440 | tf_op jit(solution)/shard_map/ppermute | solution.py:573
  9.2 3.4 %collective-permute-start.3 = (bf16[256,512]{1,0:T(8,128)(2,1)}, bf16[256,512]{1,0:T(8,128)(2,1)S(1)}, u32[]{:S(2)}, u32[]{:S(2)}) collective-permute-start(bf16[256,512]{1,0:T(8,128)(2,1)} %get-tuple-element.22), channel_id=1, source_target_pairs={{0,8},{4,12},{8,16},{12,20},{16,24},{20,28},{1,9},{5,13},{9,17},{1... | collective-permute-start | bytes 786440 | tf_op jit(solution)/shard_map/ppermute | solution.py:573
  12.6 0.0 collective-permute-done.halo_ref
  12.6 0.6 copy-done.9
  13.2 6.0 %conv_project.1 = (bf16[256,2048]{1,0:T(8,128)(2,1)}, bf16[544,256]{1,0:T(8,128)(2,1)}) custom-call(s32[4]{0:T(128)} %lengths_ref.5, bf16[256,2048]{1,0:T(8,128)(2,1)} %x_ref.3, bf16[16,2048]{1,0:T(8,128)(2,1)} %copy-done.9, f32[4,2048]{1,0:T(4,128)} %w_ref.1, f32[1,2048]{1,0:T(1,128)} %bitcast.20, bf16[544,2048]{1,0:T(8,128)(2,1)} %bitcast.19), custom_call_target="tpu_custom_call" | custom-call | flops 22817013760 | bytes 4194304 | tf_op jit(solution)/shard_map/conv_project/pallas_call | solution.py:109
  19.2 0.0 copy-start.1
  19.3 1.6 %collective-permute-start.1 = (bf16[544,256]{1,0:T(8,128)(2,1)}, bf16[544,256]{1,0:T(8,128)(2,1)S(1)}, u32[]{:S(2)}, u32[]{:S(2)}) collective-permute-start(bf16[544,256]{1,0:T(8,128)(2,1)} %get-tuple-element.18), channel_id=1, source_target_pairs={{0,1},{1,0},{2,3},{3,2},{4,5},{5,4},{6,7},{7,6},{8,9},{9,8},{10,11... | collective-permute-start | bytes 835592 | tf_op jit(solution)/shard_map/ppermute | solution.py:625
  20.9 0.3 collective-permute-done.4
  21.2 0.0 collective-permute-done.3
  21.2 0.1 pad_maximum_fusion.keys_mine.values_mine
  21.3 0.8 collective-permute-start.5
  22.1 5.2 %collective-permute-done.1 = bf16[544,256]{1,0:T(8,128)(2,1)S(1)} collective-permute-done((bf16[544,256]{1,0:T(8,128)(2,1)}, bf16[544,256]{1,0:T(8,128)(2,1)S(1)}, u32[]{:S(2)}, u32[]{:S(2)}) %collective-permute-start.1) | collective-permute-done | bytes 278560 | tf_op jit(solution)/shard_map/ppermute | solution.py:625
  27.3 1.0 %add_convert_fusion.proj_ref = bf16[544,256]{1,0:T(8,128)(2,1)S(1)} fusion(bf16[544,256]{1,0:T(8,128)(2,1)S(1)} %collective-permute-done.1, bf16[544,256]{1,0:T(8,128)(2,1)} %get-tuple-element.18), kind=kLoop, calls=%fused_computation.1 | loop fusion | flops 557056 | bytes 835584 | tf_op jit(solution)/shard_map/convert_element_type | solution.py:622
  28.3 2.7 %collective-permute-start.2 = (bf16[544,256]{1,0:T(8,128)(2,1)S(1)}, bf16[544,256]{1,0:T(8,128)(2,1)S(1)}, u32[]{:S(2)}, u32[]{:S(2)}) collective-permute-start(bf16[544,256]{1,0:T(8,128)(2,1)S(1)} %add_convert_fusion.proj_ref), channel_id=1, source_target_pairs={{0,2},{1,3},{2,0},{3,1},{4,6},{5,7},{6,4},{7,5},{8,10},{9,11},{10,... | collective-permute-start | bytes 835592 | tf_op jit(solution)/shard_map/ppermute | solution.py:625
  31.0 0.0 collective-permute-done.5.keys_theirs.values_theirs
  31.0 4.7 %attend.1 = bf16[256,2048]{1,0:T(8,128)(2,1)} custom-call(s32[4]{0:T(128)S(1)} %copy-done.1, s32[8,256]{1,0:T(8,128)S(1)} %reshape.19.place_ref, bf16[256,2048]{1,0:T(8,128)(2,1)S(1)} %copy-done, bf16[3,256,512]{2,1,0:T(8,128)(2,1)S(1)} %pad_maximum_fusion.keys_mine.values_mine, bf16[3,256,512]{2,1,0:T(8,128)(2,1)S(1)} %collective-permute-done.5.keys_theirs.values_theirs, ...), custom_call_target="tpu_custom_call" | custom-call | flops 524288 | bytes 524288 | tf_op jit(solution)/shard_map/attend/pallas_call | solution.py:545
  35.7 6.4 %collective-permute-done.2.other_ref = bf16[544,256]{1,0:T(8,128)(2,1)S(1)} collective-permute-done((bf16[544,256]{1,0:T(8,128)(2,1)S(1)}, bf16[544,256]{1,0:T(8,128)(2,1)S(1)}, u32[]{:S(2)}, u32[]{:S(2)}) %collective-permute-start.2) | collective-permute-done | bytes 278560 | tf_op jit(solution)/shard_map/ppermute | solution.py:625
  42.1 4.2 %all-to-all-start = ((bf16[8,32,2048]{2,1,0:T(8,128)(2,1)}), bf16[8,32,2048]{2,1,0:T(8,128)(2,1)S(1)}, u32[]{:S(2)}, u32[]{:S(2)}) async-start(bf16[8,32,2048]{2,1,0:T(8,128)(2,1)} %bitcast.7), calls=%async_computation | async-start | bytes 2097152 | tf_op jit(solution)/shard_map/all_to_all | solution.py:628
  46.3 14.0 %local_scan.1 = (f32[256,16,128]{2,1,0:T(8,128)}, f32[256,16,128]{2,1,0:T(8,128)}, bf16[288,128]{1,0:T(8,128)(2,1)}) custom-call(s32[4]{0:T(128)} %lengths_ref.5, bf16[544,256]{1,0:T(8,128)(2,1)} %copy-done.3, bf16[544,256]{1,0:T(8,128)(2,1)} %copy-done.7, bf16[512,2048]{1,0:T(8,128)(2,1)} %dtw_ref.1, f32[1,2048]{1,0:T(1,128)} %bitcast.21, ...), custom_call_target="tpu_custom_call" | custom-call | flops 100663296 | bytes 6291456 | tf_op jit(solution)/shard_map/local_scan/pallas_call | solution.py:283
  60.4 3.9 %collective-permute-start.7 = (bf16[288,128]{1,0:T(8,128)(2,1)}, bf16[288,128]{1,0:T(8,128)(2,1)S(1)}, u32[]{:S(2)}, u32[]{:S(2)}) collective-permute-start(bf16[288,128]{1,0:T(8,128)(2,1)} %get-tuple-element.31), channel_id=1, source_target_pairs={{0,16},{4,20},{8,24},{12,28},{1,17},{5,21},{9,25},{13,29},{2,18},{... | collective-permute-start | bytes 221192 | tf_op jit(solution)/shard_map/ppermute | solution.py:573
  64.3 3.4 %collective-permute-start.6 = (bf16[288,128]{1,0:T(8,128)(2,1)}, bf16[288,128]{1,0:T(8,128)(2,1)S(1)}, u32[]{:S(2)}, u32[]{:S(2)}) collective-permute-start(bf16[288,128]{1,0:T(8,128)(2,1)} %get-tuple-element.31), channel_id=1, source_target_pairs={{0,8},{4,12},{8,16},{12,20},{16,24},{20,28},{1,9},{5,13},{9,17},{1... | collective-permute-start | bytes 221192 | tf_op jit(solution)/shard_map/ppermute | solution.py:573
  67.6 0.0 collective-permute-done.7
  67.7 2.3 %collective-permute-done.6 = bf16[288,128]{1,0:T(8,128)(2,1)S(1)} collective-permute-done((bf16[288,128]{1,0:T(8,128)(2,1)}, bf16[288,128]{1,0:T(8,128)(2,1)S(1)}, u32[]{:S(2)}, u32[]{:S(2)}) %collective-permute-start.6) | collective-permute-done | bytes 73760 | tf_op jit(solution)/shard_map/ppermute | solution.py:573
  69.9 0.9 %pad_maximum_fusion.1.mine_ref = bf16[3,288,128]{2,1,0:T(8,128)(2,1)S(1)} fusion(bf16[1,288,128]{2,1,0:T(8,128)(2,1)S(1)} %bitcast.17, bf16[1,288,128]{2,1,0:T(8,128)(2,1)S(1)} %bitcast.18, bf16[1,288,128]{2,1,0:T(8,128)(2,1)} %bitcast.16), kind=kLoop, calls=%fused_computation.2 | loop fusion | flops 221184 | bytes 442368 | tf_op jit(solution)/shard_map/stack | solution.py:577
  70.8 0.1 collective-permute-start.8
  70.9 1.5 %collective-permute-done.8.theirs_ref = bf16[3,288,128]{2,1,0:T(8,128)(2,1)S(1)} collective-permute-done((bf16[3,288,128]{2,1,0:T(8,128)(2,1)S(1)}, bf16[3,288,128]{2,1,0:T(8,128)(2,1)S(1)}, u32[]{:S(2)}, u32[]{:S(2)}) %collective-permute-start.8) | collective-permute-done | bytes 221216 | tf_op jit(solution)/shard_map/ppermute | solution.py:579
  72.4 0.0 all-to-all-done
  72.4 0.7 copy-done.8
  73.1 0.4 copy-done.2
  73.5 9.9 %join_states.1 = (bf16[256,2048]{1,0:T(8,128)(2,1)}, bf16[256,2048]{1,0:T(8,128)(2,1)}) custom-call(bf16[544,256]{1,0:T(8,128)(2,1)} %copy-done.3, bf16[544,256]{1,0:T(8,128)(2,1)} %copy-done.7, f32[256,16,128]{2,1,0:T(8,128)} %get-tuple-element.28.y_ref, f32[256,16,128]{2,1,0:T(8,128)} %get-tuple-element.29.sum_ref, ...), custom_call_target="tpu_custom_call" | custom-call | flops 67108864 | bytes 7340032 | tf_op jit(solution)/shard_map/join_states/pallas_call | solution.py:402
  (18 shorter events, 0.0 us)
Async XLA Ops:
  2.4 10.2 %collective-permute-start = (bf16[16,2048]{1,0:T(8,128)(2,1)}, bf16[16,2048]{1,0:T(8,128)(2,1)S(1)}, u32[]{:S(2)}, u32[]{:S(2)}) collective-permute-start(bf16[16,2048]{1,0:T(8,128)(2,1)} %get-tuple-element.17), channel_id=1, source_target_pairs={{0,4},{4,8},{8,12},{12,16},{16,20},{20,24},{24,28},{1,5},{5,9},{9,... | collective-permute-start | bytes 196616 | tf_op jit(solution)/shard_map/ppermute | solution.py:573
  4.7 16.5 %collective-permute-start.4 = (bf16[256,512]{1,0:T(8,128)(2,1)}, bf16[256,512]{1,0:T(8,128)(2,1)S(1)}, u32[]{:S(2)}, u32[]{:S(2)}) collective-permute-start(bf16[256,512]{1,0:T(8,128)(2,1)} %get-tuple-element.22), channel_id=1, source_target_pairs={{0,16},{4,20},{8,24},{12,28},{1,17},{5,21},{9,25},{13,29},{2,18},{... | collective-permute-start | bytes 786440 | tf_op jit(solution)/shard_map/ppermute | solution.py:573
  9.2 12.0 %collective-permute-start.3 = (bf16[256,512]{1,0:T(8,128)(2,1)}, bf16[256,512]{1,0:T(8,128)(2,1)S(1)}, u32[]{:S(2)}, u32[]{:S(2)}) collective-permute-start(bf16[256,512]{1,0:T(8,128)(2,1)} %get-tuple-element.22), channel_id=1, source_target_pairs={{0,8},{4,12},{8,16},{12,20},{16,24},{20,28},{1,9},{5,13},{9,17},{1... | collective-permute-start | bytes 786440 | tf_op jit(solution)/shard_map/ppermute | solution.py:573
  12.6 0.6 copy-start.9
  13.2 8.0 %copy-start.4 = (bf16[256,512]{1,0:T(8,128)(2,1)S(1)}, bf16[256,512]{1,0:T(8,128)(2,1)}, u32[]{:S(2)}) copy-start(bf16[256,512]{1,0:T(8,128)(2,1)} %get-tuple-element.22) | copy-start | bytes 786436
  13.2 8.8 %copy-start.6 = (s32[2048]{0:T(1024)S(1)}, s32[2048]{0:T(1024)}, u32[]{:S(2)}) copy-start(s32[2048]{0:T(1024)} %param.27) | copy-start | bytes 24580
  19.2 11.8 %copy-start = (bf16[256,2048]{1,0:T(8,128)(2,1)S(1)}, bf16[256,2048]{1,0:T(8,128)(2,1)}, u32[]{:S(2)}) copy-start(bf16[256,2048]{1,0:T(8,128)(2,1)} %q_ref.1) | copy-start | bytes 3145732
  19.2 11.8 %copy-start.1 = (s32[4]{0:T(128)S(1)}, s32[4]{0:T(128)}, u32[]{:S(2)}) copy-start(s32[4]{0:T(128)} %lengths_ref.5) | copy-start | bytes 52
  19.3 8.0 %collective-permute-start.1 = (bf16[544,256]{1,0:T(8,128)(2,1)}, bf16[544,256]{1,0:T(8,128)(2,1)S(1)}, u32[]{:S(2)}, u32[]{:S(2)}) collective-permute-start(bf16[544,256]{1,0:T(8,128)(2,1)} %get-tuple-element.18), channel_id=1, source_target_pairs={{0,1},{1,0},{2,3},{3,2},{4,5},{5,4},{6,7},{7,6},{8,9},{9,8},{10,11... | collective-permute-start | bytes 835592 | tf_op jit(solution)/shard_map/ppermute | solution.py:625
  21.3 9.7 %collective-permute-start.5 = (bf16[3,256,512]{2,1,0:T(8,128)(2,1)S(1)}, bf16[3,256,512]{2,1,0:T(8,128)(2,1)S(1)}, u32[]{:S(2)}, u32[]{:S(2)}) collective-permute-start(bf16[3,256,512]{2,1,0:T(8,128)(2,1)S(1)} %pad_maximum_fusion.keys_mine.values_mine), channel_id=1, source_target_pairs={{0,4},{4,0},{8,12},{12,8},{16,20},{20,16},{24,28},{28,24},{1,5},{5... | collective-permute-start | bytes 2359304 | tf_op jit(solution)/shard_map/ppermute | solution.py:579
  28.3 7.3 %copy-start.3 = (bf16[544,256]{1,0:T(8,128)(2,1)}, bf16[544,256]{1,0:T(8,128)(2,1)S(1)}, u32[]{:S(2)}) copy-start(bf16[544,256]{1,0:T(8,128)(2,1)S(1)} %add_convert_fusion.proj_ref) | copy-start | bytes 835588
  28.3 13.8 %collective-permute-start.2 = (bf16[544,256]{1,0:T(8,128)(2,1)S(1)}, bf16[544,256]{1,0:T(8,128)(2,1)S(1)}, u32[]{:S(2)}, u32[]{:S(2)}) collective-permute-start(bf16[544,256]{1,0:T(8,128)(2,1)S(1)} %add_convert_fusion.proj_ref), channel_id=1, source_target_pairs={{0,2},{1,3},{2,0},{3,1},{4,6},{5,7},{6,4},{7,5},{8,10},{9,11},{10,... | collective-permute-start | bytes 835592 | tf_op jit(solution)/shard_map/ppermute | solution.py:625
  42.1 4.2 %copy-start.7 = (bf16[544,256]{1,0:T(8,128)(2,1)}, bf16[544,256]{1,0:T(8,128)(2,1)S(1)}, u32[]{:S(2)}) copy-start(bf16[544,256]{1,0:T(8,128)(2,1)S(1)} %collective-permute-done.2.other_ref) | copy-start | bytes 835588
  42.1 30.3 %all-to-all-start = ((bf16[8,32,2048]{2,1,0:T(8,128)(2,1)}), bf16[8,32,2048]{2,1,0:T(8,128)(2,1)S(1)}, u32[]{:S(2)}, u32[]{:S(2)}) async-start(bf16[8,32,2048]{2,1,0:T(8,128)(2,1)} %bitcast.7), calls=%async_computation | async-start | bytes 2097152 | tf_op jit(solution)/shard_map/all_to_all | solution.py:628
  60.4 7.3 %collective-permute-start.7 = (bf16[288,128]{1,0:T(8,128)(2,1)}, bf16[288,128]{1,0:T(8,128)(2,1)S(1)}, u32[]{:S(2)}, u32[]{:S(2)}) collective-permute-start(bf16[288,128]{1,0:T(8,128)(2,1)} %get-tuple-element.31), channel_id=1, source_target_pairs={{0,16},{4,20},{8,24},{12,28},{1,17},{5,21},{9,25},{13,29},{2,18},{... | collective-permute-start | bytes 221192 | tf_op jit(solution)/shard_map/ppermute | solution.py:573
  64.3 5.7 %collective-permute-start.6 = (bf16[288,128]{1,0:T(8,128)(2,1)}, bf16[288,128]{1,0:T(8,128)(2,1)S(1)}, u32[]{:S(2)}, u32[]{:S(2)}) collective-permute-start(bf16[288,128]{1,0:T(8,128)(2,1)} %get-tuple-element.31), channel_id=1, source_target_pairs={{0,8},{4,12},{8,16},{12,20},{16,24},{20,28},{1,9},{5,13},{9,17},{1... | collective-permute-start | bytes 221192 | tf_op jit(solution)/shard_map/ppermute | solution.py:573
  70.8 1.6 %copy-start.5 = (bf16[3,288,128]{2,1,0:T(8,128)(2,1)}, bf16[3,288,128]{2,1,0:T(8,128)(2,1)S(1)}, u32[]{:S(2)}) copy-start(bf16[3,288,128]{2,1,0:T(8,128)(2,1)S(1)} %pad_maximum_fusion.1.mine_ref) | copy-start | bytes 663556
  70.8 1.5 %collective-permute-start.8 = (bf16[3,288,128]{2,1,0:T(8,128)(2,1)S(1)}, bf16[3,288,128]{2,1,0:T(8,128)(2,1)S(1)}, u32[]{:S(2)}, u32[]{:S(2)}) collective-permute-start(bf16[3,288,128]{2,1,0:T(8,128)(2,1)S(1)} %pad_maximum_fusion.1.mine_ref), channel_id=1, source_target_pairs={{0,4},{4,0},{8,12},{12,8},{16,20},{20,16},{24,28},{28,24},{1,5},{5... | collective-permute-start | bytes 663560 | tf_op jit(solution)/shard_map/ppermute | solution.py:579
  72.4 0.7 copy-start.8
  72.4 1.1 %copy-start.2 = (bf16[8,32,2048]{2,1,0:T(8,128)(2,1)}, bf16[8,32,2048]{2,1,0:T(8,128)(2,1)S(1)}, u32[]{:S(2)}) copy-start(bf16[8,32,2048]{2,1,0:T(8,128)(2,1)S(1)} %all-to-all-done) | copy-start | bytes 3145732

commit v8 on v7

--- a/solution.py
+++ b/solution.py
@@ -34,7 +34,7 @@
 
 
 def channel_chunk(channels):
-    return 512 if channels % 512 == 0 else channels
+    return 1024 if channels % 1024 == 0 else channels
 
 
 def pack_kernel(x_ref, k_ref, v_ref, halo_ref, kv_ref):
@@ -176,13 +176,15 @@
     lengths_ref,
     proj_ref,
     other_ref,
-    dtw_ref,
+    dtw_hbm,
     bias_ref,
     rate_ref,
     inner_ref,
     y_ref,
     sum_ref,
     state_ref,
+    dtw_ref,
+    fetched,
     low_cols,
     bc_spread,
     raw,
@@ -202,10 +204,13 @@
 
     @pl.when(at == 0)
     def _():
+        fetch = pltpu.make_async_copy(dtw_hbm, dtw_ref, fetched)
+        fetch.start()
         low_cols[...] = added(proj_ref, other_ref, slice(0, low_rank)).T.astype(jnp.bfloat16)
         bc_spread[...] = spread(added(proj_ref, other_ref, slice(low_rank, None)).T)
         by_register(rate_ref, rates)
         carry[...] = jnp.zeros_like(carry)
+        fetch.wait()
         for first in range(0, tiles, 4):
             cols = slice(first * LANES, (first + 4) * LANES)
             part = jnp.dot(low_cols[...], dtw_ref[:, cols], preferred_element_type=jnp.float32)
@@ -287,7 +292,7 @@
             pl.BlockSpec(memory_space=pltpu.SMEM),
             whole(projected),
             whole(other),
-            whole(dt_weight),
+            pl.BlockSpec(memory_space=pl.ANY),
             whole(bias),
             whole(decay_rate),
             pl.BlockSpec((BLOCK, channels), lambda i: (i, 0)),
@@ -299,6 +304,8 @@
             jax.ShapeDtypeStruct((state_rows, LANES), jnp.bfloat16),
         ],
         scratch_shapes=[
+            pltpu.VMEM(dt_weight.shape, dt_weight.dtype),
+            pltpu.SemaphoreType.DMA,
             pltpu.VMEM((tok, low_rank), jnp.bfloat16),
             pltpu.VMEM((tok, 2 * states, LANES), jnp.float32),
             pltpu.VMEM((tok // ROWS, tiles * ROWS, LANES), jnp.float32),
@@ -318,7 +325,6 @@
 
 
 def join_kernel(
-    low_rank,
     reach,
     proj_ref,
     other_ref,
@@ -333,7 +339,7 @@
     theirs_ref,
     out_ref,
     regrouped_ref,
-    c_spread,
+    c_cols,
     rates,
     entering,
     rows_tiles,
@@ -347,7 +353,7 @@
 
     @pl.when(at == 0)
     def _():
-        c_spread[...] = spread(added(proj_ref, other_ref, slice(low_rank + states, None)).T)
+        c_cols[:, :, :states] = added(proj_ref, other_ref, slice(None)).T.reshape(-1, ROWS, states)
         by_register(rate_ref, rates)
         odd = lax.rem(lax.axis_index("seq"), 2)
         state = [jnp.zeros((ROWS, LANES), jnp.float32)] * kept
@@ -367,10 +373,12 @@
         rows = pl.ds(pl.multiple_of(pair * PAIR, PAIR), PAIR)
         for k in range(2):
             first = pair * PAIR + k * ROWS
+            t8 = at * (block // ROWS) + 2 * pair + k
+            c_rows = [c_cols[t8, r : r + 1, :] for r in range(ROWS)]
             total = [[sum_ref[first + r, sublanes(h), :] for h in range(count)] for r in range(ROWS)]
             out = [[y_ref[first + r, sublanes(h), :] for h in range(count)] for r in range(ROWS)]
             for n in range(states):
-                c_row = [c_spread[at * block + first + r, n : n + 1, :] for r in range(ROWS)]
+                c_row = [jnp.broadcast_to(row[:, n : n + 1], (ROWS, LANES)) for row in c_rows]
                 for h in range(count):
                     rate, state = rates[n * count + h], entering[n * count + h]
                     for r in range(ROWS):
@@ -399,12 +407,13 @@
     by_token = pl.BlockSpec((BLOCK, tiles, LANES), lambda i: (i, 0, 0))
     by_row = pl.BlockSpec((BLOCK, channels), lambda i: (i, 0))
     skip = skip_gain.reshape(1, channels)
+    c_part = pl.BlockSpec((states, tok), lambda i: (low_rank // states + 1, 0))
     return pl.pallas_call(
-        functools.partial(join_kernel, low_rank, reach),
+        functools.partial(join_kernel, reach),
         grid=(tok // BLOCK,),
         in_specs=[
-            whole(projected),
-            whole(other),
+            c_part,
+            c_part,
             by_token,
             by_token,
             by_row,
@@ -418,7 +427,7 @@
         out_specs=[by_row, by_row],
         out_shape=[jax.ShapeDtypeStruct((tok, channels), jnp.bfloat16)] * 2,
         scratch_shapes=[
-            pltpu.VMEM((tok, states, LANES), jnp.float32),
+            pltpu.VMEM((tok // ROWS, ROWS, LANES), jnp.float32),
             pltpu.VMEM((states * count, ROWS, LANES), jnp.float32),
             pltpu.VMEM((states * count, ROWS, LANES), jnp.float32),
             pltpu.VMEM((2, tiles * ROWS, LANES), jnp.float32),

time: 83.9 us -> 85.6 us (1.020)
  Pallas kernels: 36.3 us -> 38.1 us
    pallas_call x1, Pallas kernels: 9.9 us -> 11.5 us  [join_states(): pl.pallas_call(functools.partial(join_kernel, reach), grid=(tok // BLOCK,...]
  transfers between devices with their start and end apart: 10 -> 10, of which waited for: 5 -> 5; matrix products, arithmetic and copies ran while one was open for 2% -> 2% of each run, Pallas kernels for 30% -> 29%
where the time goes in v8:
time: 85.6 us; the launch traced here: 85.2 us
  Pallas kernels  38.1 us (45%)
  starting transfers between devices  26.8 us (31%)
  waiting for transfers between devices  15.7 us (18%)
  other arithmetic  2.04 us (2%)
  local copies, waits for them, and re-layouts  1.72 us (2%)
    ppermute x5, starting transfers between devices, shifted(): lax.ppermute(value, 'seq', [(source, source + steps) for source in range(...  17.5 us
    pallas_call x1, Pallas kernels, local_scan(): pl.pallas_call(local_kernel, grid=(tok // BLOCK,), in_specs=[pl.BlockSpec...  14.7 us
    pallas_call x1, Pallas kernels, join_states(): pl.pallas_call(functools.partial(join_kernel, reach), grid=(tok // BLOCK,...  11.5 us
    ppermute x2, waiting for transfers between devices, local(): lax.ppermute(total, 'mp', [(source, source ^ step) for source in range(n_...  11.1 us
    pallas_call x1, Pallas kernels, conv_project(): pl.pallas_call(conv_kernel, grid=(channels // chunk,), in_specs=[pl.Block...  5.47 us
    pallas_call x1, Pallas kernels, attend(): pl.pallas_call(attend_kernel, grid=(kv_local,), in_specs=[pl.BlockSpec(me...  4.67 us
    ppermute x2, starting transfers between devices, local(): lax.ppermute(total, 'mp', [(source, source ^ step) for source in range(n_...  4.3 us
    all_to_all x1, starting transfers between devices, local(): lax.all_to_all(attended, 'seq', split_axis=0, concat_axis=0, tiled=True)  4.21 us
  transfers between devices with their start and end apart: 10, of which 5 were waited for; matrix products, arithmetic and copies ran while one was open for 2% of the time, Pallas kernels for 29%

profile of v8, /device:TPU:0, one launch (start us, length us, event | category | flops | bytes accessed | tf_op | source)
XLA Modules:
  0.0 85.2 jit_solution(2972256957166689084)
XLA Ops:
  0.6 1.7 %pack.1 = (bf16[16,2048]{1,0:T(8,128)(2,1)}, bf16[256,512]{1,0:T(8,128)(2,1)}) custom-call(bf16[256,2048]{1,0:T(8,128)(2,1)} %x_ref.3, bf16[256,256]{1,0:T(8,128)(2,1)} %k_ref.1, bf16[256,256]{1,0:T(8,128)(2,1)} %v_ref.1), custom_call_target="tpu_custom_call" | custom-call | bytes 1048576 | tf_op jit(solution)/shard_map/pack/pallas_call | solution.py:51
  2.4 2.3 %collective-permute-start = (bf16[16,2048]{1,0:T(8,128)(2,1)}, bf16[16,2048]{1,0:T(8,128)(2,1)S(1)}, u32[]{:S(2)}, u32[]{:S(2)}) collective-permute-start(bf16[16,2048]{1,0:T(8,128)(2,1)} %get-tuple-element.17), channel_id=1, source_target_pairs={{0,4},{4,8},{8,12},{12,16},{16,20},{20,24},{24,28},{1,5},{5,9},{9,... | collective-permute-start | bytes 196616 | tf_op jit(solution)/shard_map/ppermute | solution.py:582
  4.7 4.4 %collective-permute-start.4 = (bf16[256,512]{1,0:T(8,128)(2,1)}, bf16[256,512]{1,0:T(8,128)(2,1)S(1)}, u32[]{:S(2)}, u32[]{:S(2)}) collective-permute-start(bf16[256,512]{1,0:T(8,128)(2,1)} %get-tuple-element.22), channel_id=1, source_target_pairs={{0,16},{4,20},{8,24},{12,28},{1,17},{5,21},{9,25},{13,29},{2,18},{... | collective-permute-start | bytes 786440 | tf_op jit(solution)/shard_map/ppermute | solution.py:582
  9.2 3.4 %collective-permute-start.3 = (bf16[256,512]{1,0:T(8,128)(2,1)}, bf16[256,512]{1,0:T(8,128)(2,1)S(1)}, u32[]{:S(2)}, u32[]{:S(2)}) collective-permute-start(bf16[256,512]{1,0:T(8,128)(2,1)} %get-tuple-element.22), channel_id=1, source_target_pairs={{0,8},{4,12},{8,16},{12,20},{16,24},{20,28},{1,9},{5,13},{9,17},{1... | collective-permute-start | bytes 786440 | tf_op jit(solution)/shard_map/ppermute | solution.py:582
  12.6 0.0 collective-permute-done.halo_ref
  12.6 0.6 copy-done.9
  13.2 5.5 %conv_project.1 = (bf16[256,2048]{1,0:T(8,128)(2,1)}, bf16[544,256]{1,0:T(8,128)(2,1)}) custom-call(s32[4]{0:T(128)} %lengths_ref.5, bf16[256,2048]{1,0:T(8,128)(2,1)} %x_ref.3, bf16[16,2048]{1,0:T(8,128)(2,1)} %copy-done.9, f32[4,2048]{1,0:T(4,128)} %w_ref.1, f32[1,2048]{1,0:T(1,128)} %bitcast.20, bf16[544,2048]{1,0:T(8,128)(2,1)} %bitcast.19), custom_call_target="tpu_custom_call" | custom-call | flops 22817013760 | bytes 4194304 | tf_op jit(solution)/shard_map/conv_project/pallas_call | solution.py:109
  18.7 0.0 copy-start.1
  18.7 1.6 %collective-permute-start.1 = (bf16[544,256]{1,0:T(8,128)(2,1)}, bf16[544,256]{1,0:T(8,128)(2,1)S(1)}, u32[]{:S(2)}, u32[]{:S(2)}) collective-permute-start(bf16[544,256]{1,0:T(8,128)(2,1)} %get-tuple-element.18), channel_id=1, source_target_pairs={{0,1},{1,0},{2,3},{3,2},{4,5},{5,4},{6,7},{7,6},{8,9},{9,8},{10,11... | collective-permute-start | bytes 835592 | tf_op jit(solution)/shard_map/ppermute | solution.py:634
  20.4 0.8 collective-permute-done.4
  21.2 0.0 collective-permute-done.3
  21.2 0.1 pad_maximum_fusion.keys_mine.values_mine
  21.3 0.8 collective-permute-start.5
  22.1 4.7 %collective-permute-done.1 = bf16[544,256]{1,0:T(8,128)(2,1)S(1)} collective-permute-done((bf16[544,256]{1,0:T(8,128)(2,1)}, bf16[544,256]{1,0:T(8,128)(2,1)S(1)}, u32[]{:S(2)}, u32[]{:S(2)}) %collective-permute-start.1) | collective-permute-done | bytes 278560 | tf_op jit(solution)/shard_map/ppermute | solution.py:634
  26.8 1.0 %add_convert_fusion.proj_ref = bf16[544,256]{1,0:T(8,128)(2,1)S(1)} fusion(bf16[544,256]{1,0:T(8,128)(2,1)S(1)} %collective-permute-done.1, bf16[544,256]{1,0:T(8,128)(2,1)} %get-tuple-element.18), kind=kLoop, calls=%fused_computation.1 | loop fusion | flops 557056 | bytes 835584 | tf_op jit(solution)/shard_map/convert_element_type | solution.py:631
  27.8 2.7 %collective-permute-start.2 = (bf16[544,256]{1,0:T(8,128)(2,1)S(1)}, bf16[544,256]{1,0:T(8,128)(2,1)S(1)}, u32[]{:S(2)}, u32[]{:S(2)}) collective-permute-start(bf16[544,256]{1,0:T(8,128)(2,1)S(1)} %add_convert_fusion.proj_ref), channel_id=1, source_target_pairs={{0,2},{1,3},{2,0},{3,1},{4,6},{5,7},{6,4},{7,5},{8,10},{9,11},{10,... | collective-permute-start | bytes 835592 | tf_op jit(solution)/shard_map/ppermute | solution.py:634
  30.5 0.0 collective-permute-done.5.keys_theirs.values_theirs
  30.5 4.7 %attend.1 = bf16[256,2048]{1,0:T(8,128)(2,1)} custom-call(s32[4]{0:T(128)S(1)} %copy-done.1, s32[8,256]{1,0:T(8,128)S(1)} %reshape.19.place_ref, bf16[256,2048]{1,0:T(8,128)(2,1)S(1)} %copy-done, bf16[3,256,512]{2,1,0:T(8,128)(2,1)S(1)} %pad_maximum_fusion.keys_mine.values_mine, bf16[3,256,512]{2,1,0:T(8,128)(2,1)S(1)} %collective-permute-done.5.keys_theirs.values_theirs, ...), custom_call_target="tpu_custom_call" | custom-call | flops 524288 | bytes 524288 | tf_op jit(solution)/shard_map/attend/pallas_call | solution.py:554
  35.1 6.4 %collective-permute-done.2.other_ref = bf16[544,256]{1,0:T(8,128)(2,1)S(1)} collective-permute-done((bf16[544,256]{1,0:T(8,128)(2,1)S(1)}, bf16[544,256]{1,0:T(8,128)(2,1)S(1)}, u32[]{:S(2)}, u32[]{:S(2)}) %collective-permute-start.2) | collective-permute-done | bytes 278560 | tf_op jit(solution)/shard_map/ppermute | solution.py:634
  41.6 4.2 %all-to-all-start = ((bf16[8,32,2048]{2,1,0:T(8,128)(2,1)}), bf16[8,32,2048]{2,1,0:T(8,128)(2,1)S(1)}, u32[]{:S(2)}, u32[]{:S(2)}) async-start(bf16[8,32,2048]{2,1,0:T(8,128)(2,1)} %bitcast.7), calls=%async_computation | async-start | bytes 2097152 | tf_op jit(solution)/shard_map/all_to_all | solution.py:637
  45.8 14.7 %local_scan.1 = (f32[256,16,128]{2,1,0:T(8,128)}, f32[256,16,128]{2,1,0:T(8,128)}, bf16[288,128]{1,0:T(8,128)(2,1)}) custom-call(s32[4]{0:T(128)} %lengths_ref.5, bf16[544,256]{1,0:T(8,128)(2,1)} %copy-done.3, bf16[544,256]{1,0:T(8,128)(2,1)} %copy-done.7, bf16[512,2048]{1,0:T(8,128)(2,1)} %dtw_hbm.1, f32[1,2048]{1,0:T(1,128)} %bitcast.21, ...), custom_call_target="tpu_custom_call" | custom-call | flops 100663296 | bytes 6291456 | tf_op jit(solution)/shard_map/local_scan/pallas_call | solution.py:288
  60.5 3.9 %collective-permute-start.7 = (bf16[288,128]{1,0:T(8,128)(2,1)}, bf16[288,128]{1,0:T(8,128)(2,1)S(1)}, u32[]{:S(2)}, u32[]{:S(2)}) collective-permute-start(bf16[288,128]{1,0:T(8,128)(2,1)} %get-tuple-element.31), channel_id=1, source_target_pairs={{0,16},{4,20},{8,24},{12,28},{1,17},{5,21},{9,25},{13,29},{2,18},{... | collective-permute-start | bytes 221192 | tf_op jit(solution)/shard_map/ppermute | solution.py:582
  64.5 3.4 %collective-permute-start.6 = (bf16[288,128]{1,0:T(8,128)(2,1)}, bf16[288,128]{1,0:T(8,128)(2,1)S(1)}, u32[]{:S(2)}, u32[]{:S(2)}) collective-permute-start(bf16[288,128]{1,0:T(8,128)(2,1)} %get-tuple-element.31), channel_id=1, source_target_pairs={{0,8},{4,12},{8,16},{12,20},{16,24},{20,28},{1,9},{5,13},{9,17},{1... | collective-permute-start | bytes 221192 | tf_op jit(solution)/shard_map/ppermute | solution.py:582
  67.8 0.0 collective-permute-done.7
  67.8 2.3 %collective-permute-done.6 = bf16[288,128]{1,0:T(8,128)(2,1)S(1)} collective-permute-done((bf16[288,128]{1,0:T(8,128)(2,1)}, bf16[288,128]{1,0:T(8,128)(2,1)S(1)}, u32[]{:S(2)}, u32[]{:S(2)}) %collective-permute-start.6) | collective-permute-done | bytes 73760 | tf_op jit(solution)/shard_map/ppermute | solution.py:582
  70.1 0.9 %pad_maximum_fusion.1.mine_ref = bf16[3,288,128]{2,1,0:T(8,128)(2,1)S(1)} fusion(bf16[1,288,128]{2,1,0:T(8,128)(2,1)S(1)} %bitcast.17, bf16[1,288,128]{2,1,0:T(8,128)(2,1)S(1)} %bitcast.18, bf16[1,288,128]{2,1,0:T(8,128)(2,1)} %bitcast.16), kind=kLoop, calls=%fused_computation.2 | loop fusion | flops 221184 | bytes 442368 | tf_op jit(solution)/shard_map/stack | solution.py:586
  71.0 0.1 collective-permute-start.8
  71.1 1.5 %collective-permute-done.8.theirs_ref = bf16[3,288,128]{2,1,0:T(8,128)(2,1)S(1)} collective-permute-done((bf16[3,288,128]{2,1,0:T(8,128)(2,1)S(1)}, bf16[3,288,128]{2,1,0:T(8,128)(2,1)S(1)}, u32[]{:S(2)}, u32[]{:S(2)}) %collective-permute-start.8) | collective-permute-done | bytes 221216 | tf_op jit(solution)/shard_map/ppermute | solution.py:588
  72.6 0.0 all-to-all-done
  72.6 0.7 copy-done.8
  73.3 0.4 copy-done.2
  73.7 11.5 %join_states.1 = (bf16[256,2048]{1,0:T(8,128)(2,1)}, bf16[256,2048]{1,0:T(8,128)(2,1)}) custom-call(bf16[544,256]{1,0:T(8,128)(2,1)} %copy-done.3, bf16[544,256]{1,0:T(8,128)(2,1)} %copy-done.7, f32[256,16,128]{2,1,0:T(8,128)} %get-tuple-element.28.y_ref, f32[256,16,128]{2,1,0:T(8,128)} %get-tuple-element.29.sum_ref, ...), custom_call_target="tpu_custom_call" | custom-call | flops 67108864 | bytes 7340032 | tf_op jit(solution)/shard_map/join_states/pallas_call | solution.py:411
  (18 shorter events, 0.0 us)
Async XLA Ops:
  2.4 10.2 %collective-permute-start = (bf16[16,2048]{1,0:T(8,128)(2,1)}, bf16[16,2048]{1,0:T(8,128)(2,1)S(1)}, u32[]{:S(2)}, u32[]{:S(2)}) collective-permute-start(bf16[16,2048]{1,0:T(8,128)(2,1)} %get-tuple-element.17), channel_id=1, source_target_pairs={{0,4},{4,8},{8,12},{12,16},{16,20},{20,24},{24,28},{1,5},{5,9},{9,... | collective-permute-start | bytes 196616 | tf_op jit(solution)/shard_map/ppermute | solution.py:582
  4.7 16.5 %collective-permute-start.4 = (bf16[256,512]{1,0:T(8,128)(2,1)}, bf16[256,512]{1,0:T(8,128)(2,1)S(1)}, u32[]{:S(2)}, u32[]{:S(2)}) collective-permute-start(bf16[256,512]{1,0:T(8,128)(2,1)} %get-tuple-element.22), channel_id=1, source_target_pairs={{0,16},{4,20},{8,24},{12,28},{1,17},{5,21},{9,25},{13,29},{2,18},{... | collective-permute-start | bytes 786440 | tf_op jit(solution)/shard_map/ppermute | solution.py:582
  9.2 12.0 %collective-permute-start.3 = (bf16[256,512]{1,0:T(8,128)(2,1)}, bf16[256,512]{1,0:T(8,128)(2,1)S(1)}, u32[]{:S(2)}, u32[]{:S(2)}) collective-permute-start(bf16[256,512]{1,0:T(8,128)(2,1)} %get-tuple-element.22), channel_id=1, source_target_pairs={{0,8},{4,12},{8,16},{12,20},{16,24},{20,28},{1,9},{5,13},{9,17},{1... | collective-permute-start | bytes 786440 | tf_op jit(solution)/shard_map/ppermute | solution.py:582
  12.6 0.6 copy-start.9
  13.2 8.0 %copy-start.4 = (bf16[256,512]{1,0:T(8,128)(2,1)S(1)}, bf16[256,512]{1,0:T(8,128)(2,1)}, u32[]{:S(2)}) copy-start(bf16[256,512]{1,0:T(8,128)(2,1)} %get-tuple-element.22) | copy-start | bytes 786436
  13.2 8.8 %copy-start.6 = (s32[2048]{0:T(1024)S(1)}, s32[2048]{0:T(1024)}, u32[]{:S(2)}) copy-start(s32[2048]{0:T(1024)} %param.27) | copy-start | bytes 24580
  18.7 11.8 %copy-start = (bf16[256,2048]{1,0:T(8,128)(2,1)S(1)}, bf16[256,2048]{1,0:T(8,128)(2,1)}, u32[]{:S(2)}) copy-start(bf16[256,2048]{1,0:T(8,128)(2,1)} %q_ref.1) | copy-start | bytes 3145732
  18.7 11.8 %copy-start.1 = (s32[4]{0:T(128)S(1)}, s32[4]{0:T(128)}, u32[]{:S(2)}) copy-start(s32[4]{0:T(128)} %lengths_ref.5) | copy-start | bytes 52
  18.7 8.0 %collective-permute-start.1 = (bf16[544,256]{1,0:T(8,128)(2,1)}, bf16[544,256]{1,0:T(8,128)(2,1)S(1)}, u32[]{:S(2)}, u32[]{:S(2)}) collective-permute-start(bf16[544,256]{1,0:T(8,128)(2,1)} %get-tuple-element.18), channel_id=1, source_target_pairs={{0,1},{1,0},{2,3},{3,2},{4,5},{5,4},{6,7},{7,6},{8,9},{9,8},{10,11... | collective-permute-start | bytes 835592 | tf_op jit(solution)/shard_map/ppermute | solution.py:634
  21.3 9.2 %collective-permute-start.5 = (bf16[3,256,512]{2,1,0:T(8,128)(2,1)S(1)}, bf16[3,256,512]{2,1,0:T(8,128)(2,1)S(1)}, u32[]{:S(2)}, u32[]{:S(2)}) collective-permute-start(bf16[3,256,512]{2,1,0:T(8,128)(2,1)S(1)} %pad_maximum_fusion.keys_mine.values_mine), channel_id=1, source_target_pairs={{0,4},{4,0},{8,12},{12,8},{16,20},{20,16},{24,28},{28,24},{1,5},{5... | collective-permute-start | bytes 2359304 | tf_op jit(solution)/shard_map/ppermute | solution.py:588
  27.8 7.3 %copy-start.3 = (bf16[544,256]{1,0:T(8,128)(2,1)}, bf16[544,256]{1,0:T(8,128)(2,1)S(1)}, u32[]{:S(2)}) copy-start(bf16[544,256]{1,0:T(8,128)(2,1)S(1)} %add_convert_fusion.proj_ref) | copy-start | bytes 835588
  27.8 13.8 %collective-permute-start.2 = (bf16[544,256]{1,0:T(8,128)(2,1)S(1)}, bf16[544,256]{1,0:T(8,128)(2,1)S(1)}, u32[]{:S(2)}, u32[]{:S(2)}) collective-permute-start(bf16[544,256]{1,0:T(8,128)(2,1)S(1)} %add_convert_fusion.proj_ref), channel_id=1, source_target_pairs={{0,2},{1,3},{2,0},{3,1},{4,6},{5,7},{6,4},{7,5},{8,10},{9,11},{10,... | collective-permute-start | bytes 835592 | tf_op jit(solution)/shard_map/ppermute | solution.py:634
  41.6 4.2 %copy-start.7 = (bf16[544,256]{1,0:T(8,128)(2,1)}, bf16[544,256]{1,0:T(8,128)(2,1)S(1)}, u32[]{:S(2)}) copy-start(bf16[544,256]{1,0:T(8,128)(2,1)S(1)} %collective-permute-done.2.other_ref) | copy-start | bytes 835588
  41.6 31.0 %all-to-all-start = ((bf16[8,32,2048]{2,1,0:T(8,128)(2,1)}), bf16[8,32,2048]{2,1,0:T(8,128)(2,1)S(1)}, u32[]{:S(2)}, u32[]{:S(2)}) async-start(bf16[8,32,2048]{2,1,0:T(8,128)(2,1)} %bitcast.7), calls=%async_computation | async-start | bytes 2097152 | tf_op jit(solution)/shard_map/all_to_all | solution.py:637
  60.5 7.3 %collective-permute-start.7 = (bf16[288,128]{1,0:T(8,128)(2,1)}, bf16[288,128]{1,0:T(8,128)(2,1)S(1)}, u32[]{:S(2)}, u32[]{:S(2)}) collective-permute-start(bf16[288,128]{1,0:T(8,128)(2,1)} %get-tuple-element.31), channel_id=1, source_target_pairs={{0,16},{4,20},{8,24},{12,28},{1,17},{5,21},{9,25},{13,29},{2,18},{... | collective-permute-start | bytes 221192 | tf_op jit(solution)/shard_map/ppermute | solution.py:582
  64.5 5.7 %collective-permute-start.6 = (bf16[288,128]{1,0:T(8,128)(2,1)}, bf16[288,128]{1,0:T(8,128)(2,1)S(1)}, u32[]{:S(2)}, u32[]{:S(2)}) collective-permute-start(bf16[288,128]{1,0:T(8,128)(2,1)} %get-tuple-element.31), channel_id=1, source_target_pairs={{0,8},{4,12},{8,16},{12,20},{16,24},{20,28},{1,9},{5,13},{9,17},{1... | collective-permute-start | bytes 221192 | tf_op jit(solution)/shard_map/ppermute | solution.py:582
  71.0 1.6 %copy-start.5 = (bf16[3,288,128]{2,1,0:T(8,128)(2,1)}, bf16[3,288,128]{2,1,0:T(8,128)(2,1)S(1)}, u32[]{:S(2)}) copy-start(bf16[3,288,128]{2,1,0:T(8,128)(2,1)S(1)} %pad_maximum_fusion.1.mine_ref) | copy-start | bytes 663556
  71.0 1.5 %collective-permute-start.8 = (bf16[3,288,128]{2,1,0:T(8,128)(2,1)S(1)}, bf16[3,288,128]{2,1,0:T(8,128)(2,1)S(1)}, u32[]{:S(2)}, u32[]{:S(2)}) collective-permute-start(bf16[3,288,128]{2,1,0:T(8,128)(2,1)S(1)} %pad_maximum_fusion.1.mine_ref), channel_id=1, source_target_pairs={{0,4},{4,0},{8,12},{12,8},{16,20},{20,16},{24,28},{28,24},{1,5},{5... | collective-permute-start | bytes 663560 | tf_op jit(solution)/shard_map/ppermute | solution.py:588
  72.6 0.7 copy-start.8
  72.6 1.1 %copy-start.2 = (bf16[8,32,2048]{2,1,0:T(8,128)(2,1)}, bf16[8,32,2048]{2,1,0:T(8,128)(2,1)S(1)}, u32[]{:S(2)}) copy-start(bf16[8,32,2048]{2,1,0:T(8,128)(2,1)S(1)} %all-to-all-done) | copy-start | bytes 3145732

commit v9 on v7

--- a/solution.py
+++ b/solution.py
@@ -13,6 +13,7 @@
 LOG2E = 1.4426950408889634
 RESET = 1e30
 APART = 65536.0
+MARKS = 16
 VMEM_LIMIT = 32 * 1024 * 1024
 VMEM_MOST = 56 * 1024 * 1024
 
@@ -34,7 +35,7 @@
 
 
 def channel_chunk(channels):
-    return 512 if channels % 512 == 0 else channels
+    return 1024 if channels % 1024 == 0 else channels
 
 
 def pack_kernel(x_ref, k_ref, v_ref, halo_ref, kv_ref):
@@ -318,7 +319,6 @@
 
 
 def join_kernel(
-    low_rank,
     reach,
     proj_ref,
     other_ref,
@@ -347,7 +347,7 @@
 
     @pl.when(at == 0)
     def _():
-        c_spread[...] = spread(added(proj_ref, other_ref, slice(low_rank + states, None)).T)
+        c_spread[...] = spread(added(proj_ref, other_ref, slice(None)).T)
         by_register(rate_ref, rates)
         odd = lax.rem(lax.axis_index("seq"), 2)
         state = [jnp.zeros((ROWS, LANES), jnp.float32)] * kept
@@ -399,12 +399,13 @@
     by_token = pl.BlockSpec((BLOCK, tiles, LANES), lambda i: (i, 0, 0))
     by_row = pl.BlockSpec((BLOCK, channels), lambda i: (i, 0))
     skip = skip_gain.reshape(1, channels)
+    c_part = pl.BlockSpec((states, tok), lambda i: (low_rank // states + 1, 0))
     return pl.pallas_call(
-        functools.partial(join_kernel, low_rank, reach),
+        functools.partial(join_kernel, reach),
         grid=(tok // BLOCK,),
         in_specs=[
-            whole(projected),
-            whole(other),
+            c_part,
+            c_part,
             by_token,
             by_token,
             by_row,
@@ -434,6 +435,7 @@
 
 
 def attend_kernel(
+    turn_heads,
     lengths_ref,
     place_ref,
     q_ref,
@@ -442,95 +444,85 @@
     values_mine,
     values_theirs,
     out_ref,
-    queries,
-    scores,
-    tops,
-    acc,
+    keys_across,
+    values_wide,
 ):
     tok = q_ref.shape[0]
     heads = q_ref.shape[1] // HD
+    reach = values_wide.shape[0] // tok - 1
     position = lax.axis_index("seq")
     odd = lax.rem(position, 2)
     anchor = position * tok
     scale = jnp.bfloat16(LOG2E * HD**-0.5)
     starts, ends = doc_edges(lengths_ref)
-    lane = lax.broadcasted_iota(jnp.int32, (1, LANES), 1)
-    first = jnp.full((1, LANES), 2**30, jnp.int32)
-    last = jnp.zeros((1, LANES), jnp.int32)
-    for i, (start, end) in enumerate(zip(starts, ends)):
-        first = jnp.where(lane == i, start, first)
-        last = jnp.where(lane == i, end, last)
-    rows = lax.broadcasted_iota(jnp.int32, (tok, LANES), 0)
-
-    def in_doc(base):
-        return (rows + base >= first) & (rows + base < last)
-
-    apart = jnp.where(in_doc(anchor) | (lane >= len(starts)), 0.0, -APART).astype(jnp.bfloat16)
-    for head in range(heads):
-        queries[head * tok : (head + 1) * tok, :HD] = q_ref[:, head * HD : (head + 1) * HD]
-        queries[head * tok : (head + 1) * tok, HD:] = apart
-
-    def rows_of(mine_ref, theirs_ref, back):
-        if isinstance(back, int) and back == 0:
-            return mine_ref[0]
-        return jnp.where(lax.rem(back, 2) == 0, mine_ref[back // 2], theirs_ref[(back + 1) // 2 - odd])
-
-    def score(back):
-        marks = jnp.where(in_doc(anchor - back * tok), 1.0, 0.0).astype(jnp.bfloat16)
-        keys = jnp.concatenate([rows_of(keys_mine, keys_theirs, back), marks], axis=1)
-        return lax.dot_general(queries[...], keys, (((1,), (1,)), ((), ())), preferred_element_type=jnp.float32)
-
-    def widest(s):
-        top = s[:, :LANES]
-        for at in range(LANES, tok, LANES):
-            top = jnp.maximum(top, s[:, at : at + LANES])
-        return top
-
-    own = score(0)
-    causal = lax.broadcasted_iota(jnp.int32, (tok, tok), 1) <= lax.broadcasted_iota(jnp.int32, (tok, tok), 0)
-    for head in range(heads):
-        part = slice(head * tok, (head + 1) * tok)
-        s = jnp.where(causal, own[part], -APART)
-        scores[0, part, :] = s
-        tops[part, :] = widest(s)
+    edges = list(zip(starts, ends)) + [(jnp.int32(-(2**30)), jnp.int32(0))]
+    lane_at = lax.broadcasted_iota(jnp.int32, (1, LANES), 1)
+    places = anchor + lax.broadcasted_iota(jnp.int32, (tok, LANES), 0)
+    apart = jnp.where(lane_at < len(edges), -APART, 0.0) + jnp.zeros((tok, LANES), jnp.float32)
+    for i, (start, end) in enumerate(edges):
+        apart = jnp.where((lane_at == i) & (places >= start) & (places < end), 0.0, apart)
+    apart = apart.astype(jnp.bfloat16)
+
+    def stage(back, keys, values):
+        at = pl.ds(pl.multiple_of(back * tok, tok), tok)
+        place = anchor - back * tok + lax.broadcasted_iota(jnp.int32, (MARKS, tok), 1)
+        row = lax.broadcasted_iota(jnp.int32, (MARKS, tok), 0)
+        marks = jnp.zeros((MARKS, tok), jnp.float32)
+        for i, (start, end) in enumerate(edges):
+            marks = jnp.where((row == i) & (place >= start) & (place < end), 1.0, marks)
+        keys_across[:HD, at] = keys.astype(jnp.float32).T.astype(jnp.bfloat16)
+        keys_across[HD : HD + MARKS, at] = marks.astype(jnp.bfloat16)
+        values_wide[at, :HD] = values
+
+    keys_across[HD + MARKS :, :] = jnp.zeros((HD - MARKS, keys_across.shape[1]), jnp.bfloat16)
+    values_wide[:, HD:] = jnp.ones((values_wide.shape[0], HD), jnp.bfloat16)
+    stage(0, keys_mine[0], values_mine[0])
+
+    def stage_earlier(back, unused):
+        even = lax.rem(back, 2) == 0
+        ours, other = back // 2, (back + 1) // 2 - odd
+        stage(
+            back,
+            jnp.where(even, keys_mine[ours], keys_theirs[other]),
+            jnp.where(even, values_mine[ours], values_theirs[other]),
+        )
+        return unused
 
     begin = jnp.int32(0)
     for start in starts[1:]:
         begin = jnp.where(anchor >= start, start, begin)
-    earlier = (anchor - begin + tok - 1) // tok
-
-    def look(back, carry):
-        s = score(back)
-        scores[back] = s
-        tops[...] = jnp.maximum(tops[...], widest(s))
-        return carry
-
-    lax.fori_loop(1, earlier + 1, look, 0)
-    tops[...] = jnp.broadcast_to(jnp.max(tops[...], axis=1, keepdims=True), tops.shape)
-
-    def weighted(back):
-        values = jnp.concatenate([rows_of(values_mine, values_theirs, back), jnp.ones((tok, HD), jnp.bfloat16)], axis=1)
-        top = tops[...]
-        weights = [
-            jnp.exp2((scores[back, :, at : at + LANES] - top).astype(jnp.bfloat16) * scale)
-            for at in range(0, tok, LANES)
-        ]
-        return jnp.dot(jnp.concatenate(weights, axis=1), values, preferred_element_type=jnp.float32)
-
-    acc[...] = weighted(0)
-
-    def absorb(back, carry):
-        acc[...] += weighted(back)
-        return carry
-
-    lax.fori_loop(1, earlier + 1, absorb, 0)
+    pairs = ((anchor - begin + tok - 1) // tok + 1) // 2
+    lax.fori_loop(1, 2 * pairs + 1, stage_earlier, 0)
+
     order = place_ref[pl.ds(position, 1), :]
     move = (lax.broadcasted_iota(jnp.int32, (tok, tok), 0) == order).astype(jnp.float32).astype(jnp.bfloat16)
-    for head in range(heads):
-        part = slice(head * tok, (head + 1) * tok)
-        result = (acc[part, :HD] / acc[part, HD:]).astype(jnp.bfloat16)
-        moved = jnp.dot(move, result, preferred_element_type=jnp.float32)
-        out_ref[:, head * HD : (head + 1) * HD] = moved.astype(jnp.bfloat16)
+    causal = lax.broadcasted_iota(jnp.int32, (tok, tok), 1) <= lax.broadcasted_iota(jnp.int32, (tok, tok), 0)
+
+    def one_head(head, blocks):
+        cols = pl.ds(pl.multiple_of(head * HD, HD), HD)
+        query = jnp.concatenate([q_ref[:, cols], apart], axis=1)
+        s = jnp.dot(query, keys_across[:, : blocks * tok], preferred_element_type=jnp.float32)
+        parts = [jnp.where(causal, s[:, :tok], -APART)] + ([s[:, tok:]] if blocks > 1 else [])
+        pieces = [part[:, at : at + LANES] for part in parts for at in range(0, part.shape[1], LANES)]
+        top = functools.reduce(jnp.maximum, pieces)
+        top = jnp.broadcast_to(jnp.max(top, axis=1, keepdims=True), top.shape)
+        weights = [jnp.exp2((piece - top).astype(jnp.bfloat16) * scale) for piece in pieces]
+        both = jnp.dot(
+            jnp.concatenate(weights, axis=1), values_wide[: blocks * tok, :], preferred_element_type=jnp.float32
+        )
+        result = (both[:, :HD] / both[:, HD:]).astype(jnp.bfloat16)
+        out_ref[:, cols] = jnp.dot(move, result, preferred_element_type=jnp.float32).astype(jnp.bfloat16)
+
+    def all_heads(blocks):
+        def some(turn, unused):
+            for k in range(turn_heads):
+                one_head(turn * turn_heads + k, blocks)
+            return unused
+
+        lax.fori_loop(0, heads // turn_heads, some, 0)
+
+    for case in range(reach // 2 + 1):
+        pl.when(pairs == case)(functools.partial(all_heads, 1 + 2 * case))
 
 
 def attend(lengths, send_place, query_rows, mine, theirs):
@@ -542,8 +534,9 @@
     by_group = pl.BlockSpec((tok, share), lambda i: (0, i))
     keys = pl.BlockSpec(mine.shape[:2] + (HD,), lambda i: (0, 0, i))
     values = pl.BlockSpec(mine.shape[:2] + (HD,), lambda i: (0, 0, i + kv_local))
+    turn_heads = next(n for n in (4, 2, 1) if heads % n == 0 and n * (reach + 1) <= 24)
     return pl.pallas_call(
-        attend_kernel,
+        functools.partial(attend_kernel, turn_heads),
         grid=(kv_local,),
         in_specs=[
             pl.BlockSpec(memory_space=pltpu.SMEM),
@@ -557,12 +550,10 @@
         out_specs=by_group,
         out_shape=jax.ShapeDtypeStruct((tok, width), jnp.bfloat16),
         scratch_shapes=[
-            pltpu.VMEM((heads * tok, 2 * HD), jnp.bfloat16),
-            pltpu.VMEM((reach + 1, heads * tok, tok), jnp.float32),
-            pltpu.VMEM((heads * tok, LANES), jnp.float32),
-            pltpu.VMEM((heads * tok, 2 * HD), jnp.float32),
-        ],
-        compiler_params=pltpu.CompilerParams(vmem_limit_bytes=VMEM_LIMIT // 2 + 4 * (reach + 1) * heads * tok * tok),
+            pltpu.VMEM((2 * HD, (reach + 1) * tok), jnp.bfloat16),
+            pltpu.VMEM(((reach + 1) * tok, 2 * HD), jnp.bfloat16),
+        ],
+        compiler_params=pltpu.CompilerParams(vmem_limit_bytes=VMEM_LIMIT),
         cost_estimate=pl.CostEstimate(flops=tok * width, bytes_accessed=tok * width, transcendentals=0),
         name="attend",
     )(lengths, send_place, query_rows, mine, theirs, mine, theirs)

time: 83.9 us -> 88.2 us (1.051)
  starting transfers between devices: 26.8 us -> 31.9 us
  waiting for transfers between devices: 15.7 us -> 12.4 us
  Pallas kernels: 36.3 us -> 38.9 us
    all_to_all x1, starting transfers between devices: 4.22 us -> 9.31 us  [local(): lax.all_to_all(attended, 'seq', split_axis=0, concat_axis=0, tiled=True)]
    ppermute x2, waiting for transfers between devices: 11.7 us -> 7.82 us  [local(): lax.ppermute(total, 'mp', [(source, source ^ step) for source in range(n_...]
    pallas_call x2, Pallas kernels: 14.6 us -> 17.7 us  [the longest x1 9.77 us: join_states(): pl.pallas_call(functools.partial(join_kernel, reach), grid=(tok // BLOCK,...]
  transfers between devices with their start and end apart: 10 -> 10, of which waited for: 5 -> 5; matrix products, arithmetic and copies ran while one was open for 2% -> 2% of each run, Pallas kernels for 30% -> 31%
where the time goes in v9:
time: 88.2 us; the launch traced here: 87.8 us
  Pallas kernels  38.9 us (44%)
  starting transfers between devices  31.9 us (36%)
  waiting for transfers between devices  12.4 us (14%)
  other arithmetic  2.04 us (2%)
  local copies, waits for them, and re-layouts  1.72 us (2%)
    ppermute x5, starting transfers between devices, shifted(): lax.ppermute(value, 'seq', [(source, source + steps) for source in range(...  17.5 us
    pallas_call x1, Pallas kernels, local_scan(): pl.pallas_call(local_kernel, grid=(tok // BLOCK,), in_specs=[pl.BlockSpec...  14 us
    pallas_call x1, Pallas kernels, join_states(): pl.pallas_call(functools.partial(join_kernel, reach), grid=(tok // BLOCK,...  9.77 us
    all_to_all x1, starting transfers between devices, local(): lax.all_to_all(attended, 'seq', split_axis=0, concat_axis=0, tiled=True)  9.31 us
    pallas_call x1, Pallas kernels, attend(): pl.pallas_call(functools.partial(attend_kernel, turn_heads), grid=(kv_loc...  7.97 us
    ppermute x2, waiting for transfers between devices, local(): lax.ppermute(total, 'mp', [(source, source ^ step) for source in range(n_...  7.82 us
    pallas_call x1, Pallas kernels, conv_project(): pl.pallas_call(conv_kernel, grid=(channels // chunk,), in_specs=[pl.Block...  5.47 us
    ppermute x2, starting transfers between devices, local(): lax.ppermute(total, 'mp', [(source, source ^ step) for source in range(n_...  4.3 us
  transfers between devices with their start and end apart: 10, of which 5 were waited for; matrix products, arithmetic and copies ran while one was open for 2% of the time, Pallas kernels for 31%

profile of v9, /device:TPU:0, one launch (start us, length us, event | category | flops | bytes accessed | tf_op | source)
XLA Modules:
  0.0 87.8 jit_solution(261109764528915827)
XLA Ops:
  0.6 1.7 %pack.1 = (bf16[16,2048]{1,0:T(8,128)(2,1)}, bf16[256,512]{1,0:T(8,128)(2,1)}) custom-call(bf16[256,2048]{1,0:T(8,128)(2,1)} %x_ref.3, bf16[256,256]{1,0:T(8,128)(2,1)} %k_ref.1, bf16[256,256]{1,0:T(8,128)(2,1)} %v_ref.1), custom_call_target="tpu_custom_call" | custom-call | bytes 1048576 | tf_op jit(solution)/shard_map/pack/pallas_call | solution.py:52
  2.4 2.3 %collective-permute-start = (bf16[16,2048]{1,0:T(8,128)(2,1)}, bf16[16,2048]{1,0:T(8,128)(2,1)S(1)}, u32[]{:S(2)}, u32[]{:S(2)}) collective-permute-start(bf16[16,2048]{1,0:T(8,128)(2,1)} %get-tuple-element.17), channel_id=1, source_target_pairs={{0,4},{4,8},{8,12},{12,16},{16,20},{20,24},{24,28},{1,5},{5,9},{9,... | collective-permute-start | bytes 196616 | tf_op jit(solution)/shard_map/ppermute | solution.py:564
  4.7 4.4 %collective-permute-start.4 = (bf16[256,512]{1,0:T(8,128)(2,1)}, bf16[256,512]{1,0:T(8,128)(2,1)S(1)}, u32[]{:S(2)}, u32[]{:S(2)}) collective-permute-start(bf16[256,512]{1,0:T(8,128)(2,1)} %get-tuple-element.22), channel_id=1, source_target_pairs={{0,16},{4,20},{8,24},{12,28},{1,17},{5,21},{9,25},{13,29},{2,18},{... | collective-permute-start | bytes 786440 | tf_op jit(solution)/shard_map/ppermute | solution.py:564
  9.2 3.4 %collective-permute-start.3 = (bf16[256,512]{1,0:T(8,128)(2,1)}, bf16[256,512]{1,0:T(8,128)(2,1)S(1)}, u32[]{:S(2)}, u32[]{:S(2)}) collective-permute-start(bf16[256,512]{1,0:T(8,128)(2,1)} %get-tuple-element.22), channel_id=1, source_target_pairs={{0,8},{4,12},{8,16},{12,20},{16,24},{20,28},{1,9},{5,13},{9,17},{1... | collective-permute-start | bytes 786440 | tf_op jit(solution)/shard_map/ppermute | solution.py:564
  12.6 0.0 collective-permute-done.halo_ref
  12.6 0.6 copy-done.9
  13.2 5.5 %conv_project.1 = (bf16[256,2048]{1,0:T(8,128)(2,1)}, bf16[544,256]{1,0:T(8,128)(2,1)}) custom-call(s32[4]{0:T(128)} %lengths_ref.5, bf16[256,2048]{1,0:T(8,128)(2,1)} %x_ref.3, bf16[16,2048]{1,0:T(8,128)(2,1)} %copy-done.9, f32[4,2048]{1,0:T(4,128)} %w_ref.1, f32[1,2048]{1,0:T(1,128)} %bitcast.20, bf16[544,2048]{1,0:T(8,128)(2,1)} %bitcast.19), custom_call_target="tpu_custom_call" | custom-call | flops 22817013760 | bytes 4194304 | tf_op jit(solution)/shard_map/conv_project/pallas_call | solution.py:110
  18.7 0.0 copy-start.1
  18.7 1.6 %collective-permute-start.1 = (bf16[544,256]{1,0:T(8,128)(2,1)}, bf16[544,256]{1,0:T(8,128)(2,1)S(1)}, u32[]{:S(2)}, u32[]{:S(2)}) collective-permute-start(bf16[544,256]{1,0:T(8,128)(2,1)} %get-tuple-element.18), channel_id=1, source_target_pairs={{0,1},{1,0},{2,3},{3,2},{4,5},{5,4},{6,7},{7,6},{8,9},{9,8},{10,11... | collective-permute-start | bytes 835592 | tf_op jit(solution)/shard_map/ppermute | solution.py:616
  20.4 0.8 collective-permute-done.4
  21.2 0.0 collective-permute-done.3
  21.2 0.1 pad_maximum_fusion.keys_mine.values_mine
  21.3 0.8 collective-permute-start.5
  22.1 4.7 %collective-permute-done.1 = bf16[544,256]{1,0:T(8,128)(2,1)S(1)} collective-permute-done((bf16[544,256]{1,0:T(8,128)(2,1)}, bf16[544,256]{1,0:T(8,128)(2,1)S(1)}, u32[]{:S(2)}, u32[]{:S(2)}) %collective-permute-start.1) | collective-permute-done | bytes 278560 | tf_op jit(solution)/shard_map/ppermute | solution.py:616
  26.8 1.0 %add_convert_fusion.proj_ref = bf16[544,256]{1,0:T(8,128)(2,1)S(1)} fusion(bf16[544,256]{1,0:T(8,128)(2,1)S(1)} %collective-permute-done.1, bf16[544,256]{1,0:T(8,128)(2,1)} %get-tuple-element.18), kind=kLoop, calls=%fused_computation.1 | loop fusion | flops 557056 | bytes 835584 | tf_op jit(solution)/shard_map/convert_element_type | solution.py:613
  27.8 2.7 %collective-permute-start.2 = (bf16[544,256]{1,0:T(8,128)(2,1)S(1)}, bf16[544,256]{1,0:T(8,128)(2,1)S(1)}, u32[]{:S(2)}, u32[]{:S(2)}) collective-permute-start(bf16[544,256]{1,0:T(8,128)(2,1)S(1)} %add_convert_fusion.proj_ref), channel_id=1, source_target_pairs={{0,2},{1,3},{2,0},{3,1},{4,6},{5,7},{6,4},{7,5},{8,10},{9,11},{10,... | collective-permute-start | bytes 835592 | tf_op jit(solution)/shard_map/ppermute | solution.py:616
  30.5 0.0 collective-permute-done.5.keys_theirs.values_theirs
  30.5 8.0 %attend.1 = bf16[256,2048]{1,0:T(8,128)(2,1)} custom-call(s32[4]{0:T(128)S(1)} %copy-done.1, s32[8,256]{1,0:T(8,128)S(1)} %reshape.19.place_ref, bf16[256,2048]{1,0:T(8,128)(2,1)S(1)} %copy-done, bf16[3,256,512]{2,1,0:T(8,128)(2,1)S(1)} %pad_maximum_fusion.keys_mine.values_mine, bf16[3,256,512]{2,1,0:T(8,128)(2,1)S(1)} %collective-permute-done.5.keys_theirs.values_theirs, ...), custom_call_target="tpu_custom_call" | custom-call | flops 524288 | bytes 524288 | tf_op jit(solution)/shard_map/attend/pallas_call | solution.py:538
  38.4 3.1 %collective-permute-done.2.other_ref = bf16[544,256]{1,0:T(8,128)(2,1)S(1)} collective-permute-done((bf16[544,256]{1,0:T(8,128)(2,1)S(1)}, bf16[544,256]{1,0:T(8,128)(2,1)S(1)}, u32[]{:S(2)}, u32[]{:S(2)}) %collective-permute-start.2) | collective-permute-done | bytes 278560 | tf_op jit(solution)/shard_map/ppermute | solution.py:616
  41.6 9.3 %all-to-all-start = ((bf16[8,32,2048]{2,1,0:T(8,128)(2,1)}), bf16[8,32,2048]{2,1,0:T(8,128)(2,1)S(1)}, u32[]{:S(2)}, u32[]{:S(2)}) async-start(bf16[8,32,2048]{2,1,0:T(8,128)(2,1)} %bitcast.7), calls=%async_computation | async-start | bytes 2097152 | tf_op jit(solution)/shard_map/all_to_all | solution.py:619
  50.9 14.0 %local_scan.1 = (f32[256,16,128]{2,1,0:T(8,128)}, f32[256,16,128]{2,1,0:T(8,128)}, bf16[288,128]{1,0:T(8,128)(2,1)}) custom-call(s32[4]{0:T(128)} %lengths_ref.5, bf16[544,256]{1,0:T(8,128)(2,1)} %copy-done.3, bf16[544,256]{1,0:T(8,128)(2,1)} %copy-done.7, bf16[512,2048]{1,0:T(8,128)(2,1)} %dtw_ref.1, f32[1,2048]{1,0:T(1,128)} %bitcast.21, ...), custom_call_target="tpu_custom_call" | custom-call | flops 100663296 | bytes 6291456 | tf_op jit(solution)/shard_map/local_scan/pallas_call | solution.py:284
  64.9 4.2 %collective-permute-start.7 = (bf16[288,128]{1,0:T(8,128)(2,1)}, bf16[288,128]{1,0:T(8,128)(2,1)S(1)}, u32[]{:S(2)}, u32[]{:S(2)}) collective-permute-start(bf16[288,128]{1,0:T(8,128)(2,1)} %get-tuple-element.31), channel_id=1, source_target_pairs={{0,16},{4,20},{8,24},{12,28},{1,17},{5,21},{9,25},{13,29},{2,18},{... | collective-permute-start | bytes 221192 | tf_op jit(solution)/shard_map/ppermute | solution.py:564
  69.1 3.1 %collective-permute-start.6 = (bf16[288,128]{1,0:T(8,128)(2,1)}, bf16[288,128]{1,0:T(8,128)(2,1)S(1)}, u32[]{:S(2)}, u32[]{:S(2)}) collective-permute-start(bf16[288,128]{1,0:T(8,128)(2,1)} %get-tuple-element.31), channel_id=1, source_target_pairs={{0,8},{4,12},{8,16},{12,20},{16,24},{20,28},{1,9},{5,13},{9,17},{1... | collective-permute-start | bytes 221192 | tf_op jit(solution)/shard_map/ppermute | solution.py:564
  72.2 0.0 collective-permute-done.7
  72.2 2.3 %collective-permute-done.6 = bf16[288,128]{1,0:T(8,128)(2,1)S(1)} collective-permute-done((bf16[288,128]{1,0:T(8,128)(2,1)}, bf16[288,128]{1,0:T(8,128)(2,1)S(1)}, u32[]{:S(2)}, u32[]{:S(2)}) %collective-permute-start.6) | collective-permute-done | bytes 73760 | tf_op jit(solution)/shard_map/ppermute | solution.py:564
  74.5 0.9 %pad_maximum_fusion.1.mine_ref = bf16[3,288,128]{2,1,0:T(8,128)(2,1)S(1)} fusion(bf16[1,288,128]{2,1,0:T(8,128)(2,1)S(1)} %bitcast.17, bf16[1,288,128]{2,1,0:T(8,128)(2,1)S(1)} %bitcast.18, bf16[1,288,128]{2,1,0:T(8,128)(2,1)} %bitcast.16), kind=kLoop, calls=%fused_computation.2 | loop fusion | flops 221184 | bytes 442368 | tf_op jit(solution)/shard_map/stack | solution.py:568
  75.4 0.1 collective-permute-start.8
  75.5 1.5 %collective-permute-done.8.theirs_ref = bf16[3,288,128]{2,1,0:T(8,128)(2,1)S(1)} collective-permute-done((bf16[3,288,128]{2,1,0:T(8,128)(2,1)S(1)}, bf16[3,288,128]{2,1,0:T(8,128)(2,1)S(1)}, u32[]{:S(2)}, u32[]{:S(2)}) %collective-permute-start.8) | collective-permute-done | bytes 221216 | tf_op jit(solution)/shard_map/ppermute | solution.py:570
  77.0 0.0 all-to-all-done
  77.0 0.7 copy-done.8
  77.6 0.4 copy-done.2
  78.0 9.8 %join_states.1 = (bf16[256,2048]{1,0:T(8,128)(2,1)}, bf16[256,2048]{1,0:T(8,128)(2,1)}) custom-call(bf16[544,256]{1,0:T(8,128)(2,1)} %copy-done.3, bf16[544,256]{1,0:T(8,128)(2,1)} %copy-done.7, f32[256,16,128]{2,1,0:T(8,128)} %get-tuple-element.28.y_ref, f32[256,16,128]{2,1,0:T(8,128)} %get-tuple-element.29.sum_ref, ...), custom_call_target="tpu_custom_call" | custom-call | flops 67108864 | bytes 7340032 | tf_op jit(solution)/shard_map/join_states/pallas_call | solution.py:403
  (18 shorter events, 0.0 us)
Async XLA Ops:
  2.4 10.2 %collective-permute-start = (bf16[16,2048]{1,0:T(8,128)(2,1)}, bf16[16,2048]{1,0:T(8,128)(2,1)S(1)}, u32[]{:S(2)}, u32[]{:S(2)}) collective-permute-start(bf16[16,2048]{1,0:T(8,128)(2,1)} %get-tuple-element.17), channel_id=1, source_target_pairs={{0,4},{4,8},{8,12},{12,16},{16,20},{20,24},{24,28},{1,5},{5,9},{9,... | collective-permute-start | bytes 196616 | tf_op jit(solution)/shard_map/ppermute | solution.py:564
  4.7 16.5 %collective-permute-start.4 = (bf16[256,512]{1,0:T(8,128)(2,1)}, bf16[256,512]{1,0:T(8,128)(2,1)S(1)}, u32[]{:S(2)}, u32[]{:S(2)}) collective-permute-start(bf16[256,512]{1,0:T(8,128)(2,1)} %get-tuple-element.22), channel_id=1, source_target_pairs={{0,16},{4,20},{8,24},{12,28},{1,17},{5,21},{9,25},{13,29},{2,18},{... | collective-permute-start | bytes 786440 | tf_op jit(solution)/shard_map/ppermute | solution.py:564
  9.2 12.0 %collective-permute-start.3 = (bf16[256,512]{1,0:T(8,128)(2,1)}, bf16[256,512]{1,0:T(8,128)(2,1)S(1)}, u32[]{:S(2)}, u32[]{:S(2)}) collective-permute-start(bf16[256,512]{1,0:T(8,128)(2,1)} %get-tuple-element.22), channel_id=1, source_target_pairs={{0,8},{4,12},{8,16},{12,20},{16,24},{20,28},{1,9},{5,13},{9,17},{1... | collective-permute-start | bytes 786440 | tf_op jit(solution)/shard_map/ppermute | solution.py:564
  12.6 0.6 copy-start.9
  13.2 8.0 %copy-start.4 = (bf16[256,512]{1,0:T(8,128)(2,1)S(1)}, bf16[256,512]{1,0:T(8,128)(2,1)}, u32[]{:S(2)}) copy-start(bf16[256,512]{1,0:T(8,128)(2,1)} %get-tuple-element.22) | copy-start | bytes 786436
  13.2 8.8 %copy-start.6 = (s32[2048]{0:T(1024)S(1)}, s32[2048]{0:T(1024)}, u32[]{:S(2)}) copy-start(s32[2048]{0:T(1024)} %param.27) | copy-start | bytes 24580
  18.7 11.8 %copy-start = (bf16[256,2048]{1,0:T(8,128)(2,1)S(1)}, bf16[256,2048]{1,0:T(8,128)(2,1)}, u32[]{:S(2)}) copy-start(bf16[256,2048]{1,0:T(8,128)(2,1)} %q_ref.1) | copy-start | bytes 3145732
  18.7 11.8 %copy-start.1 = (s32[4]{0:T(128)S(1)}, s32[4]{0:T(128)}, u32[]{:S(2)}) copy-start(s32[4]{0:T(128)} %lengths_ref.5) | copy-start | bytes 52
  18.7 8.0 %collective-permute-start.1 = (bf16[544,256]{1,0:T(8,128)(2,1)}, bf16[544,256]{1,0:T(8,128)(2,1)S(1)}, u32[]{:S(2)}, u32[]{:S(2)}) collective-permute-start(bf16[544,256]{1,0:T(8,128)(2,1)} %get-tuple-element.18), channel_id=1, source_target_pairs={{0,1},{1,0},{2,3},{3,2},{4,5},{5,4},{6,7},{7,6},{8,9},{9,8},{10,11... | collective-permute-start | bytes 835592 | tf_op jit(solution)/shard_map/ppermute | solution.py:616
  21.3 9.2 %collective-permute-start.5 = (bf16[3,256,512]{2,1,0:T(8,128)(2,1)S(1)}, bf16[3,256,512]{2,1,0:T(8,128)(2,1)S(1)}, u32[]{:S(2)}, u32[]{:S(2)}) collective-permute-start(bf16[3,256,512]{2,1,0:T(8,128)(2,1)S(1)} %pad_maximum_fusion.keys_mine.values_mine), channel_id=1, source_target_pairs={{0,4},{4,0},{8,12},{12,8},{16,20},{20,16},{24,28},{28,24},{1,5},{5... | collective-permute-start | bytes 2359304 | tf_op jit(solution)/shard_map/ppermute | solution.py:570
  27.8 10.7 %copy-start.3 = (bf16[544,256]{1,0:T(8,128)(2,1)}, bf16[544,256]{1,0:T(8,128)(2,1)S(1)}, u32[]{:S(2)}) copy-start(bf16[544,256]{1,0:T(8,128)(2,1)S(1)} %add_convert_fusion.proj_ref) | copy-start | bytes 835588
  27.8 13.8 %collective-permute-start.2 = (bf16[544,256]{1,0:T(8,128)(2,1)S(1)}, bf16[544,256]{1,0:T(8,128)(2,1)S(1)}, u32[]{:S(2)}, u32[]{:S(2)}) collective-permute-start(bf16[544,256]{1,0:T(8,128)(2,1)S(1)} %add_convert_fusion.proj_ref), channel_id=1, source_target_pairs={{0,2},{1,3},{2,0},{3,1},{4,6},{5,7},{6,4},{7,5},{8,10},{9,11},{10,... | collective-permute-start | bytes 835592 | tf_op jit(solution)/shard_map/ppermute | solution.py:616
  41.6 9.3 %copy-start.7 = (bf16[544,256]{1,0:T(8,128)(2,1)}, bf16[544,256]{1,0:T(8,128)(2,1)S(1)}, u32[]{:S(2)}) copy-start(bf16[544,256]{1,0:T(8,128)(2,1)S(1)} %collective-permute-done.2.other_ref) | copy-start | bytes 835588
  41.6 35.4 %all-to-all-start = ((bf16[8,32,2048]{2,1,0:T(8,128)(2,1)}), bf16[8,32,2048]{2,1,0:T(8,128)(2,1)S(1)}, u32[]{:S(2)}, u32[]{:S(2)}) async-start(bf16[8,32,2048]{2,1,0:T(8,128)(2,1)} %bitcast.7), calls=%async_computation | async-start | bytes 2097152 | tf_op jit(solution)/shard_map/all_to_all | solution.py:619
  64.9 7.3 %collective-permute-start.7 = (bf16[288,128]{1,0:T(8,128)(2,1)}, bf16[288,128]{1,0:T(8,128)(2,1)S(1)}, u32[]{:S(2)}, u32[]{:S(2)}) collective-permute-start(bf16[288,128]{1,0:T(8,128)(2,1)} %get-tuple-element.31), channel_id=1, source_target_pairs={{0,16},{4,20},{8,24},{12,28},{1,17},{5,21},{9,25},{13,29},{2,18},{... | collective-permute-start | bytes 221192 | tf_op jit(solution)/shard_map/ppermute | solution.py:564
  69.1 5.4 %collective-permute-start.6 = (bf16[288,128]{1,0:T(8,128)(2,1)}, bf16[288,128]{1,0:T(8,128)(2,1)S(1)}, u32[]{:S(2)}, u32[]{:S(2)}) collective-permute-start(bf16[288,128]{1,0:T(8,128)(2,1)} %get-tuple-element.31), channel_id=1, source_target_pairs={{0,8},{4,12},{8,16},{12,20},{16,24},{20,28},{1,9},{5,13},{9,17},{1... | collective-permute-start | bytes 221192 | tf_op jit(solution)/shard_map/ppermute | solution.py:564
  75.4 1.6 %copy-start.5 = (bf16[3,288,128]{2,1,0:T(8,128)(2,1)}, bf16[3,288,128]{2,1,0:T(8,128)(2,1)S(1)}, u32[]{:S(2)}) copy-start(bf16[3,288,128]{2,1,0:T(8,128)(2,1)S(1)} %pad_maximum_fusion.1.mine_ref) | copy-start | bytes 663556
  75.4 1.5 %collective-permute-start.8 = (bf16[3,288,128]{2,1,0:T(8,128)(2,1)S(1)}, bf16[3,288,128]{2,1,0:T(8,128)(2,1)S(1)}, u32[]{:S(2)}, u32[]{:S(2)}) collective-permute-start(bf16[3,288,128]{2,1,0:T(8,128)(2,1)S(1)} %pad_maximum_fusion.1.mine_ref), channel_id=1, source_target_pairs={{0,4},{4,0},{8,12},{12,8},{16,20},{20,16},{24,28},{28,24},{1,5},{5... | collective-permute-start | bytes 663560 | tf_op jit(solution)/shard_map/ppermute | solution.py:570
  76.9 0.7 copy-start.8
  77.0 1.1 %copy-start.2 = (bf16[8,32,2048]{2,1,0:T(8,128)(2,1)}, bf16[8,32,2048]{2,1,0:T(8,128)(2,1)S(1)}, u32[]{:S(2)}) copy-start(bf16[8,32,2048]{2,1,0:T(8,128)(2,1)S(1)} %all-to-all-done) | copy-start | bytes 3145732

commit v10 on v7

--- a/solution.py
+++ b/solution.py
@@ -34,7 +34,7 @@
 
 
 def channel_chunk(channels):
-    return 512 if channels % 512 == 0 else channels
+    return 1024 if channels % 1024 == 0 else channels
 
 
 def pack_kernel(x_ref, k_ref, v_ref, halo_ref, kv_ref):
@@ -318,7 +318,6 @@
 
 
 def join_kernel(
-    low_rank,
     reach,
     proj_ref,
     other_ref,
@@ -347,7 +346,7 @@
 
     @pl.when(at == 0)
     def _():
-        c_spread[...] = spread(added(proj_ref, other_ref, slice(low_rank + states, None)).T)
+        c_spread[...] = spread(added(proj_ref, other_ref, slice(None)).T)
         by_register(rate_ref, rates)
         odd = lax.rem(lax.axis_index("seq"), 2)
         state = [jnp.zeros((ROWS, LANES), jnp.float32)] * kept
@@ -399,12 +398,13 @@
     by_token = pl.BlockSpec((BLOCK, tiles, LANES), lambda i: (i, 0, 0))
     by_row = pl.BlockSpec((BLOCK, channels), lambda i: (i, 0))
     skip = skip_gain.reshape(1, channels)
+    c_part = pl.BlockSpec((states, tok), lambda i: (low_rank // states + 1, 0))
     return pl.pallas_call(
-        functools.partial(join_kernel, low_rank, reach),
+        functools.partial(join_kernel, reach),
         grid=(tok // BLOCK,),
         in_specs=[
-            whole(projected),
-            whole(other),
+            c_part,
+            c_part,
             by_token,
             by_token,
             by_row,
@@ -454,10 +454,11 @@
     anchor = position * tok
     scale = jnp.bfloat16(LOG2E * HD**-0.5)
     starts, ends = doc_edges(lengths_ref)
+    edges = list(zip(starts, ends)) + [(jnp.int32(-(2**30)), jnp.int32(0))]
     lane = lax.broadcasted_iota(jnp.int32, (1, LANES), 1)
     first = jnp.full((1, LANES), 2**30, jnp.int32)
     last = jnp.zeros((1, LANES), jnp.int32)
-    for i, (start, end) in enumerate(zip(starts, ends)):
+    for i, (start, end) in enumerate(edges):
         first = jnp.where(lane == i, start, first)
         last = jnp.where(lane == i, end, last)
     rows = lax.broadcasted_iota(jnp.int32, (tok, LANES), 0)
@@ -465,7 +466,7 @@
     def in_doc(base):
         return (rows + base >= first) & (rows + base < last)
 
-    apart = jnp.where(in_doc(anchor) | (lane >= len(starts)), 0.0, -APART).astype(jnp.bfloat16)
+    apart = jnp.where(in_doc(anchor) | (lane >= len(edges)), 0.0, -APART).astype(jnp.bfloat16)
     for head in range(heads):
         queries[head * tok : (head + 1) * tok, :HD] = q_ref[:, head * HD : (head + 1) * HD]
         queries[head * tok : (head + 1) * tok, HD:] = apart
@@ -480,50 +481,64 @@
         keys = jnp.concatenate([rows_of(keys_mine, keys_theirs, back), marks], axis=1)
         return lax.dot_general(queries[...], keys, (((1,), (1,)), ((), ())), preferred_element_type=jnp.float32)
 
-    def widest(s):
-        top = s[:, :LANES]
-        for at in range(LANES, tok, LANES):
-            top = jnp.maximum(top, s[:, at : at + LANES])
+    causal = lax.broadcasted_iota(jnp.int32, (tok, tok), 1) <= lax.broadcasted_iota(jnp.int32, (tok, tok), 0)
+
+    def highest(backs):
+        top = None
+        for back in backs:
+            s = score(back)
+            if isinstance(back, int) and back == 0:
+                s = jnp.concatenate(
+                    [jnp.where(causal, s[h * tok : (h + 1) * tok], -APART) for h in range(heads)], axis=0
+                )
+            scores[back] = s
+            for at in range(0, tok, LANES):
+                piece = s[:, at : at + LANES]
+                top = piece if top is None else jnp.maximum(top, piece)
         return top
-
-    own = score(0)
-    causal = lax.broadcasted_iota(jnp.int32, (tok, tok), 1) <= lax.broadcasted_iota(jnp.int32, (tok, tok), 0)
-    for head in range(heads):
-        part = slice(head * tok, (head + 1) * tok)
-        s = jnp.where(causal, own[part], -APART)
-        scores[0, part, :] = s
-        tops[part, :] = widest(s)
 
     begin = jnp.int32(0)
     for start in starts[1:]:
         begin = jnp.where(anchor >= start, start, begin)
-    earlier = (anchor - begin + tok - 1) // tok
-
-    def look(back, carry):
-        s = score(back)
-        scores[back] = s
-        tops[...] = jnp.maximum(tops[...], widest(s))
+    pairs = ((anchor - begin + tok - 1) // tok + 1) // 2
+
+    def start_with(alone, together):
+        pl.when(pairs == 0)(alone)
+        pl.when(pairs > 0)(together)
+
+    def set_tops(backs):
+        tops[...] = highest(backs)
+
+    start_with(lambda: set_tops([0]), lambda: set_tops([0, 1, 2]))
+
+    def look(pair, carry):
+        tops[...] = jnp.maximum(tops[...], highest([2 * pair - 1, 2 * pair]))
         return carry
 
-    lax.fori_loop(1, earlier + 1, look, 0)
+    lax.fori_loop(2, pairs + 1, look, 0)
     tops[...] = jnp.broadcast_to(jnp.max(tops[...], axis=1, keepdims=True), tops.shape)
 
-    def weighted(back):
-        values = jnp.concatenate([rows_of(values_mine, values_theirs, back), jnp.ones((tok, HD), jnp.bfloat16)], axis=1)
+    def weighted(backs):
+        values = jnp.concatenate([rows_of(values_mine, values_theirs, back) for back in backs], axis=0)
+        values = jnp.concatenate([values, jnp.ones(values.shape, jnp.bfloat16)], axis=1)
         top = tops[...]
         weights = [
             jnp.exp2((scores[back, :, at : at + LANES] - top).astype(jnp.bfloat16) * scale)
+            for back in backs
             for at in range(0, tok, LANES)
         ]
         return jnp.dot(jnp.concatenate(weights, axis=1), values, preferred_element_type=jnp.float32)
 
-    acc[...] = weighted(0)
-
-    def absorb(back, carry):
-        acc[...] += weighted(back)
+    def set_acc(backs):
+        acc[...] = weighted(backs)
+
+    start_with(lambda: set_acc([0]), lambda: set_acc([0, 1, 2]))
+
+    def absorb(pair, carry):
+        acc[...] += weighted([2 * pair - 1, 2 * pair])
         return carry
 
-    lax.fori_loop(1, earlier + 1, absorb, 0)
+    lax.fori_loop(2, pairs + 1, absorb, 0)
     order = place_ref[pl.ds(position, 1), :]
     move = (lax.broadcasted_iota(jnp.int32, (tok, tok), 0) == order).astype(jnp.float32).astype(jnp.bfloat16)
     for head in range(heads):

time: 83.9 us -> 83.1 us (level)
    ppermute x2, waiting for transfers between devices: 11.7 us -> 10.4 us  [local(): lax.ppermute(total, 'mp', [(source, source ^ step) for source in range(n_...]
where the time goes in v10:
time: 83.1 us; the launch traced here: 82.7 us
  Pallas kernels  36.3 us (44%)
  starting transfers between devices  26.8 us (32%)
  waiting for transfers between devices  15 us (18%)
  other arithmetic  2.04 us (2%)
  local copies, waits for them, and re-layouts  1.72 us (2%)
    ppermute x5, starting transfers between devices, shifted(): lax.ppermute(value, 'seq', [(source, source + steps) for source in range(...  17.5 us
    pallas_call x1, Pallas kernels, local_scan(): pl.pallas_call(local_kernel, grid=(tok // BLOCK,), in_specs=[pl.BlockSpec...  14 us
    ppermute x2, waiting for transfers between devices, local(): lax.ppermute(total, 'mp', [(source, source ^ step) for source in range(n_...  10.4 us
    pallas_call x1, Pallas kernels, join_states(): pl.pallas_call(functools.partial(join_kernel, reach), grid=(tok // BLOCK,...  9.77 us
    pallas_call x1, Pallas kernels, conv_project(): pl.pallas_call(conv_kernel, grid=(channels // chunk,), in_specs=[pl.Block...  5.47 us
    pallas_call x1, Pallas kernels, attend(): pl.pallas_call(attend_kernel, grid=(kv_local,), in_specs=[pl.BlockSpec(me...  5.38 us
    ppermute x2, starting transfers between devices, local(): lax.ppermute(total, 'mp', [(source, source ^ step) for source in range(n_...  4.3 us
    all_to_all x1, starting transfers between devices, local(): lax.all_to_all(attended, 'seq', split_axis=0, concat_axis=0, tiled=True)  4.21 us
  transfers between devices with their start and end apart: 10, of which 5 were waited for; matrix products, arithmetic and copies ran while one was open for 2% of the time, Pallas kernels for 30%

profile of v10, /device:TPU:0, one launch (start us, length us, event | category | flops | bytes accessed | tf_op | source)
XLA Modules:
  0.0 82.7 jit_solution(10901173953325534425)
XLA Ops:
  0.6 1.7 %pack.1 = (bf16[16,2048]{1,0:T(8,128)(2,1)}, bf16[256,512]{1,0:T(8,128)(2,1)}) custom-call(bf16[256,2048]{1,0:T(8,128)(2,1)} %x_ref.3, bf16[256,256]{1,0:T(8,128)(2,1)} %k_ref.1, bf16[256,256]{1,0:T(8,128)(2,1)} %v_ref.1), custom_call_target="tpu_custom_call" | custom-call | bytes 1048576 | tf_op jit(solution)/shard_map/pack/pallas_call | solution.py:51
  2.4 2.3 %collective-permute-start = (bf16[16,2048]{1,0:T(8,128)(2,1)}, bf16[16,2048]{1,0:T(8,128)(2,1)S(1)}, u32[]{:S(2)}, u32[]{:S(2)}) collective-permute-start(bf16[16,2048]{1,0:T(8,128)(2,1)} %get-tuple-element.17), channel_id=1, source_target_pairs={{0,4},{4,8},{8,12},{12,16},{16,20},{20,24},{24,28},{1,5},{5,9},{9,... | collective-permute-start | bytes 196616 | tf_op jit(solution)/shard_map/ppermute | solution.py:588
  4.7 4.4 %collective-permute-start.4 = (bf16[256,512]{1,0:T(8,128)(2,1)}, bf16[256,512]{1,0:T(8,128)(2,1)S(1)}, u32[]{:S(2)}, u32[]{:S(2)}) collective-permute-start(bf16[256,512]{1,0:T(8,128)(2,1)} %get-tuple-element.22), channel_id=1, source_target_pairs={{0,16},{4,20},{8,24},{12,28},{1,17},{5,21},{9,25},{13,29},{2,18},{... | collective-permute-start | bytes 786440 | tf_op jit(solution)/shard_map/ppermute | solution.py:588
  9.2 3.4 %collective-permute-start.3 = (bf16[256,512]{1,0:T(8,128)(2,1)}, bf16[256,512]{1,0:T(8,128)(2,1)S(1)}, u32[]{:S(2)}, u32[]{:S(2)}) collective-permute-start(bf16[256,512]{1,0:T(8,128)(2,1)} %get-tuple-element.22), channel_id=1, source_target_pairs={{0,8},{4,12},{8,16},{12,20},{16,24},{20,28},{1,9},{5,13},{9,17},{1... | collective-permute-start | bytes 786440 | tf_op jit(solution)/shard_map/ppermute | solution.py:588
  12.6 0.0 collective-permute-done.halo_ref
  12.6 0.6 copy-done.9
  13.2 5.5 %conv_project.1 = (bf16[256,2048]{1,0:T(8,128)(2,1)}, bf16[544,256]{1,0:T(8,128)(2,1)}) custom-call(s32[4]{0:T(128)} %lengths_ref.5, bf16[256,2048]{1,0:T(8,128)(2,1)} %x_ref.3, bf16[16,2048]{1,0:T(8,128)(2,1)} %copy-done.9, f32[4,2048]{1,0:T(4,128)} %w_ref.1, f32[1,2048]{1,0:T(1,128)} %bitcast.20, bf16[544,2048]{1,0:T(8,128)(2,1)} %bitcast.19), custom_call_target="tpu_custom_call" | custom-call | flops 22817013760 | bytes 4194304 | tf_op jit(solution)/shard_map/conv_project/pallas_call | solution.py:109
  18.7 0.0 copy-start.1
  18.7 1.6 %collective-permute-start.1 = (bf16[544,256]{1,0:T(8,128)(2,1)}, bf16[544,256]{1,0:T(8,128)(2,1)S(1)}, u32[]{:S(2)}, u32[]{:S(2)}) collective-permute-start(bf16[544,256]{1,0:T(8,128)(2,1)} %get-tuple-element.18), channel_id=1, source_target_pairs={{0,1},{1,0},{2,3},{3,2},{4,5},{5,4},{6,7},{7,6},{8,9},{9,8},{10,11... | collective-permute-start | bytes 835592 | tf_op jit(solution)/shard_map/ppermute | solution.py:640
  20.4 0.8 %collective-permute-done.4 = bf16[256,512]{1,0:T(8,128)(2,1)S(1)} collective-permute-done((bf16[256,512]{1,0:T(8,128)(2,1)}, bf16[256,512]{1,0:T(8,128)(2,1)S(1)}, u32[]{:S(2)}, u32[]{:S(2)}) %collective-permute-start.4) | collective-permute-done | bytes 262176 | tf_op jit(solution)/shard_map/ppermute | solution.py:588
  21.2 0.0 collective-permute-done.3
  21.2 0.1 pad_maximum_fusion.keys_mine.values_mine
  21.3 0.8 collective-permute-start.5
  22.1 4.7 %collective-permute-done.1 = bf16[544,256]{1,0:T(8,128)(2,1)S(1)} collective-permute-done((bf16[544,256]{1,0:T(8,128)(2,1)}, bf16[544,256]{1,0:T(8,128)(2,1)S(1)}, u32[]{:S(2)}, u32[]{:S(2)}) %collective-permute-start.1) | collective-permute-done | bytes 278560 | tf_op jit(solution)/shard_map/ppermute | solution.py:640
  26.8 1.0 %add_convert_fusion.proj_ref = bf16[544,256]{1,0:T(8,128)(2,1)S(1)} fusion(bf16[544,256]{1,0:T(8,128)(2,1)S(1)} %collective-permute-done.1, bf16[544,256]{1,0:T(8,128)(2,1)} %get-tuple-element.18), kind=kLoop, calls=%fused_computation.1 | loop fusion | flops 557056 | bytes 835584 | tf_op jit(solution)/shard_map/convert_element_type | solution.py:637
  27.8 2.7 %collective-permute-start.2 = (bf16[544,256]{1,0:T(8,128)(2,1)S(1)}, bf16[544,256]{1,0:T(8,128)(2,1)S(1)}, u32[]{:S(2)}, u32[]{:S(2)}) collective-permute-start(bf16[544,256]{1,0:T(8,128)(2,1)S(1)} %add_convert_fusion.proj_ref), channel_id=1, source_target_pairs={{0,2},{1,3},{2,0},{3,1},{4,6},{5,7},{6,4},{7,5},{8,10},{9,11},{10,... | collective-permute-start | bytes 835592 | tf_op jit(solution)/shard_map/ppermute | solution.py:640
  30.5 0.0 collective-permute-done.5.keys_theirs.values_theirs
  30.5 5.4 %attend.1 = bf16[256,2048]{1,0:T(8,128)(2,1)} custom-call(s32[4]{0:T(128)S(1)} %copy-done.1, s32[8,256]{1,0:T(8,128)S(1)} %reshape.19.place_ref, bf16[256,2048]{1,0:T(8,128)(2,1)S(1)} %copy-done, bf16[3,256,512]{2,1,0:T(8,128)(2,1)S(1)} %pad_maximum_fusion.keys_mine.values_mine, bf16[3,256,512]{2,1,0:T(8,128)(2,1)S(1)} %collective-permute-done.5.keys_theirs.values_theirs, ...), custom_call_target="tpu_custom_call" | custom-call | flops 524288 | bytes 524288 | tf_op jit(solution)/shard_map/attend/pallas_call | solution.py:560
  35.8 5.7 %collective-permute-done.2.other_ref = bf16[544,256]{1,0:T(8,128)(2,1)S(1)} collective-permute-done((bf16[544,256]{1,0:T(8,128)(2,1)S(1)}, bf16[544,256]{1,0:T(8,128)(2,1)S(1)}, u32[]{:S(2)}, u32[]{:S(2)}) %collective-permute-start.2) | collective-permute-done | bytes 278560 | tf_op jit(solution)/shard_map/ppermute | solution.py:640
  41.6 4.2 %all-to-all-start = ((bf16[8,32,2048]{2,1,0:T(8,128)(2,1)}), bf16[8,32,2048]{2,1,0:T(8,128)(2,1)S(1)}, u32[]{:S(2)}, u32[]{:S(2)}) async-start(bf16[8,32,2048]{2,1,0:T(8,128)(2,1)} %bitcast.7), calls=%async_computation | async-start | bytes 2097152 | tf_op jit(solution)/shard_map/all_to_all | solution.py:643
  45.8 14.0 %local_scan.1 = (f32[256,16,128]{2,1,0:T(8,128)}, f32[256,16,128]{2,1,0:T(8,128)}, bf16[288,128]{1,0:T(8,128)(2,1)}) custom-call(s32[4]{0:T(128)} %lengths_ref.5, bf16[544,256]{1,0:T(8,128)(2,1)} %copy-done.3, bf16[544,256]{1,0:T(8,128)(2,1)} %copy-done.7, bf16[512,2048]{1,0:T(8,128)(2,1)} %dtw_ref.1, f32[1,2048]{1,0:T(1,128)} %bitcast.21, ...), custom_call_target="tpu_custom_call" | custom-call | flops 100663296 | bytes 6291456 | tf_op jit(solution)/shard_map/local_scan/pallas_call | solution.py:283
  59.8 3.9 %collective-permute-start.7 = (bf16[288,128]{1,0:T(8,128)(2,1)}, bf16[288,128]{1,0:T(8,128)(2,1)S(1)}, u32[]{:S(2)}, u32[]{:S(2)}) collective-permute-start(bf16[288,128]{1,0:T(8,128)(2,1)} %get-tuple-element.31), channel_id=1, source_target_pairs={{0,16},{4,20},{8,24},{12,28},{1,17},{5,21},{9,25},{13,29},{2,18},{... | collective-permute-start | bytes 221192 | tf_op jit(solution)/shard_map/ppermute | solution.py:588
  63.7 3.4 %collective-permute-start.6 = (bf16[288,128]{1,0:T(8,128)(2,1)}, bf16[288,128]{1,0:T(8,128)(2,1)S(1)}, u32[]{:S(2)}, u32[]{:S(2)}) collective-permute-start(bf16[288,128]{1,0:T(8,128)(2,1)} %get-tuple-element.31), channel_id=1, source_target_pairs={{0,8},{4,12},{8,16},{12,20},{16,24},{20,28},{1,9},{5,13},{9,17},{1... | collective-permute-start | bytes 221192 | tf_op jit(solution)/shard_map/ppermute | solution.py:588
  67.1 0.0 collective-permute-done.7
  67.1 2.3 %collective-permute-done.6 = bf16[288,128]{1,0:T(8,128)(2,1)S(1)} collective-permute-done((bf16[288,128]{1,0:T(8,128)(2,1)}, bf16[288,128]{1,0:T(8,128)(2,1)S(1)}, u32[]{:S(2)}, u32[]{:S(2)}) %collective-permute-start.6) | collective-permute-done | bytes 73760 | tf_op jit(solution)/shard_map/ppermute | solution.py:588
  69.4 0.9 %pad_maximum_fusion.1.mine_ref = bf16[3,288,128]{2,1,0:T(8,128)(2,1)S(1)} fusion(bf16[1,288,128]{2,1,0:T(8,128)(2,1)S(1)} %bitcast.17, bf16[1,288,128]{2,1,0:T(8,128)(2,1)S(1)} %bitcast.18, bf16[1,288,128]{2,1,0:T(8,128)(2,1)} %bitcast.16), kind=kLoop, calls=%fused_computation.2 | loop fusion | flops 221184 | bytes 442368 | tf_op jit(solution)/shard_map/stack | solution.py:592
  70.3 0.1 collective-permute-start.8
  70.4 1.5 %collective-permute-done.8.theirs_ref = bf16[3,288,128]{2,1,0:T(8,128)(2,1)S(1)} collective-permute-done((bf16[3,288,128]{2,1,0:T(8,128)(2,1)S(1)}, bf16[3,288,128]{2,1,0:T(8,128)(2,1)S(1)}, u32[]{:S(2)}, u32[]{:S(2)}) %collective-permute-start.8) | collective-permute-done | bytes 221216 | tf_op jit(solution)/shard_map/ppermute | solution.py:594
  71.9 0.0 all-to-all-done
  71.9 0.7 copy-done.8
  72.5 0.4 copy-done.2
  72.9 9.8 %join_states.1 = (bf16[256,2048]{1,0:T(8,128)(2,1)}, bf16[256,2048]{1,0:T(8,128)(2,1)}) custom-call(bf16[544,256]{1,0:T(8,128)(2,1)} %copy-done.3, bf16[544,256]{1,0:T(8,128)(2,1)} %copy-done.7, f32[256,16,128]{2,1,0:T(8,128)} %get-tuple-element.28.y_ref, f32[256,16,128]{2,1,0:T(8,128)} %get-tuple-element.29.sum_ref, ...), custom_call_target="tpu_custom_call" | custom-call | flops 67108864 | bytes 7340032 | tf_op jit(solution)/shard_map/join_states/pallas_call | solution.py:402
  (18 shorter events, 0.0 us)
Async XLA Ops:
  2.4 10.2 %collective-permute-start = (bf16[16,2048]{1,0:T(8,128)(2,1)}, bf16[16,2048]{1,0:T(8,128)(2,1)S(1)}, u32[]{:S(2)}, u32[]{:S(2)}) collective-permute-start(bf16[16,2048]{1,0:T(8,128)(2,1)} %get-tuple-element.17), channel_id=1, source_target_pairs={{0,4},{4,8},{8,12},{12,16},{16,20},{20,24},{24,28},{1,5},{5,9},{9,... | collective-permute-start | bytes 196616 | tf_op jit(solution)/shard_map/ppermute | solution.py:588
  4.7 16.5 %collective-permute-start.4 = (bf16[256,512]{1,0:T(8,128)(2,1)}, bf16[256,512]{1,0:T(8,128)(2,1)S(1)}, u32[]{:S(2)}, u32[]{:S(2)}) collective-permute-start(bf16[256,512]{1,0:T(8,128)(2,1)} %get-tuple-element.22), channel_id=1, source_target_pairs={{0,16},{4,20},{8,24},{12,28},{1,17},{5,21},{9,25},{13,29},{2,18},{... | collective-permute-start | bytes 786440 | tf_op jit(solution)/shard_map/ppermute | solution.py:588
  9.2 12.0 %collective-permute-start.3 = (bf16[256,512]{1,0:T(8,128)(2,1)}, bf16[256,512]{1,0:T(8,128)(2,1)S(1)}, u32[]{:S(2)}, u32[]{:S(2)}) collective-permute-start(bf16[256,512]{1,0:T(8,128)(2,1)} %get-tuple-element.22), channel_id=1, source_target_pairs={{0,8},{4,12},{8,16},{12,20},{16,24},{20,28},{1,9},{5,13},{9,17},{1... | collective-permute-start | bytes 786440 | tf_op jit(solution)/shard_map/ppermute | solution.py:588
  12.6 0.6 copy-start.9
  13.2 8.0 %copy-start.4 = (bf16[256,512]{1,0:T(8,128)(2,1)S(1)}, bf16[256,512]{1,0:T(8,128)(2,1)}, u32[]{:S(2)}) copy-start(bf16[256,512]{1,0:T(8,128)(2,1)} %get-tuple-element.22) | copy-start | bytes 786436
  13.2 8.8 %copy-start.6 = (s32[2048]{0:T(1024)S(1)}, s32[2048]{0:T(1024)}, u32[]{:S(2)}) copy-start(s32[2048]{0:T(1024)} %param.27) | copy-start | bytes 24580
  18.7 11.8 %copy-start = (bf16[256,2048]{1,0:T(8,128)(2,1)S(1)}, bf16[256,2048]{1,0:T(8,128)(2,1)}, u32[]{:S(2)}) copy-start(bf16[256,2048]{1,0:T(8,128)(2,1)} %q_ref.1) | copy-start | bytes 3145732
  18.7 11.8 %copy-start.1 = (s32[4]{0:T(128)S(1)}, s32[4]{0:T(128)}, u32[]{:S(2)}) copy-start(s32[4]{0:T(128)} %lengths_ref.5) | copy-start | bytes 52
  18.7 8.0 %collective-permute-start.1 = (bf16[544,256]{1,0:T(8,128)(2,1)}, bf16[544,256]{1,0:T(8,128)(2,1)S(1)}, u32[]{:S(2)}, u32[]{:S(2)}) collective-permute-start(bf16[544,256]{1,0:T(8,128)(2,1)} %get-tuple-element.18), channel_id=1, source_target_pairs={{0,1},{1,0},{2,3},{3,2},{4,5},{5,4},{6,7},{7,6},{8,9},{9,8},{10,11... | collective-permute-start | bytes 835592 | tf_op jit(solution)/shard_map/ppermute | solution.py:640
  21.3 9.2 %collective-permute-start.5 = (bf16[3,256,512]{2,1,0:T(8,128)(2,1)S(1)}, bf16[3,256,512]{2,1,0:T(8,128)(2,1)S(1)}, u32[]{:S(2)}, u32[]{:S(2)}) collective-permute-start(bf16[3,256,512]{2,1,0:T(8,128)(2,1)S(1)} %pad_maximum_fusion.keys_mine.values_mine), channel_id=1, source_target_pairs={{0,4},{4,0},{8,12},{12,8},{16,20},{20,16},{24,28},{28,24},{1,5},{5... | collective-permute-start | bytes 2359304 | tf_op jit(solution)/shard_map/ppermute | solution.py:594
  27.8 8.1 %copy-start.3 = (bf16[544,256]{1,0:T(8,128)(2,1)}, bf16[544,256]{1,0:T(8,128)(2,1)S(1)}, u32[]{:S(2)}) copy-start(bf16[544,256]{1,0:T(8,128)(2,1)S(1)} %add_convert_fusion.proj_ref) | copy-start | bytes 835588
  27.8 13.8 %collective-permute-start.2 = (bf16[544,256]{1,0:T(8,128)(2,1)S(1)}, bf16[544,256]{1,0:T(8,128)(2,1)S(1)}, u32[]{:S(2)}, u32[]{:S(2)}) collective-permute-start(bf16[544,256]{1,0:T(8,128)(2,1)S(1)} %add_convert_fusion.proj_ref), channel_id=1, source_target_pairs={{0,2},{1,3},{2,0},{3,1},{4,6},{5,7},{6,4},{7,5},{8,10},{9,11},{10,... | collective-permute-start | bytes 835592 | tf_op jit(solution)/shard_map/ppermute | solution.py:640
  41.6 4.2 %copy-start.7 = (bf16[544,256]{1,0:T(8,128)(2,1)}, bf16[544,256]{1,0:T(8,128)(2,1)S(1)}, u32[]{:S(2)}) copy-start(bf16[544,256]{1,0:T(8,128)(2,1)S(1)} %collective-permute-done.2.other_ref) | copy-start | bytes 835588
  41.6 30.3 %all-to-all-start = ((bf16[8,32,2048]{2,1,0:T(8,128)(2,1)}), bf16[8,32,2048]{2,1,0:T(8,128)(2,1)S(1)}, u32[]{:S(2)}, u32[]{:S(2)}) async-start(bf16[8,32,2048]{2,1,0:T(8,128)(2,1)} %bitcast.7), calls=%async_computation | async-start | bytes 2097152 | tf_op jit(solution)/shard_map/all_to_all | solution.py:643
  59.8 7.3 %collective-permute-start.7 = (bf16[288,128]{1,0:T(8,128)(2,1)}, bf16[288,128]{1,0:T(8,128)(2,1)S(1)}, u32[]{:S(2)}, u32[]{:S(2)}) collective-permute-start(bf16[288,128]{1,0:T(8,128)(2,1)} %get-tuple-element.31), channel_id=1, source_target_pairs={{0,16},{4,20},{8,24},{12,28},{1,17},{5,21},{9,25},{13,29},{2,18},{... | collective-permute-start | bytes 221192 | tf_op jit(solution)/shard_map/ppermute | solution.py:588
  63.7 5.7 %collective-permute-start.6 = (bf16[288,128]{1,0:T(8,128)(2,1)}, bf16[288,128]{1,0:T(8,128)(2,1)S(1)}, u32[]{:S(2)}, u32[]{:S(2)}) collective-permute-start(bf16[288,128]{1,0:T(8,128)(2,1)} %get-tuple-element.31), channel_id=1, source_target_pairs={{0,8},{4,12},{8,16},{12,20},{16,24},{20,28},{1,9},{5,13},{9,17},{1... | collective-permute-start | bytes 221192 | tf_op jit(solution)/shard_map/ppermute | solution.py:588
  70.3 1.6 %copy-start.5 = (bf16[3,288,128]{2,1,0:T(8,128)(2,1)}, bf16[3,288,128]{2,1,0:T(8,128)(2,1)S(1)}, u32[]{:S(2)}) copy-start(bf16[3,288,128]{2,1,0:T(8,128)(2,1)S(1)} %pad_maximum_fusion.1.mine_ref) | copy-start | bytes 663556
  70.3 1.5 %collective-permute-start.8 = (bf16[3,288,128]{2,1,0:T(8,128)(2,1)S(1)}, bf16[3,288,128]{2,1,0:T(8,128)(2,1)S(1)}, u32[]{:S(2)}, u32[]{:S(2)}) collective-permute-start(bf16[3,288,128]{2,1,0:T(8,128)(2,1)S(1)} %pad_maximum_fusion.1.mine_ref), channel_id=1, source_target_pairs={{0,4},{4,0},{8,12},{12,8},{16,20},{20,16},{24,28},{28,24},{1,5},{5... | collective-permute-start | bytes 663560 | tf_op jit(solution)/shard_map/ppermute | solution.py:594
  71.9 0.7 copy-start.8
  71.9 1.1 %copy-start.2 = (bf16[8,32,2048]{2,1,0:T(8,128)(2,1)}, bf16[8,32,2048]{2,1,0:T(8,128)(2,1)S(1)}, u32[]{:S(2)}) copy-start(bf16[8,32,2048]{2,1,0:T(8,128)(2,1)S(1)} %all-to-all-done) | copy-start | bytes 3145732

commit v11 on v10

--- a/solution.py
+++ b/solution.py
@@ -15,6 +15,7 @@
 APART = 65536.0
 VMEM_LIMIT = 32 * 1024 * 1024
 VMEM_MOST = 56 * 1024 * 1024
+VMEM_NEARLY = 53 * 1024 * 1024
 
 
 def doc_edges(lengths_ref):
@@ -67,26 +68,45 @@
     )(x_branch, key_rows, value_rows)
 
 
-def conv_kernel(lengths_ref, x_ref, halo_ref, w_ref, b_ref, xp_ref, inner_ref, part_ref, ext, acc):
+def conv_kernel(
+    lengths_ref, x_ref, halo_ref, w_hbm, b_hbm, xp_ref, inner_ref, part_ref, ext, acc, w_ref, b_ref, fetched
+):
     tok, chunk = x_ref.shape
     starts, _ = doc_edges(lengths_ref)
     anchor = lax.axis_index("seq") * tok
     places = anchor + lax.broadcasted_iota(jnp.int32, (tok, LANES), 0)
     depth = places - doc_start(places, starts)
+    at = pl.program_id(0)
+    fetches = [
+        pltpu.make_async_copy(w_hbm, w_ref, fetched.at[0]),
+        pltpu.make_async_copy(b_hbm, b_ref, fetched.at[1]),
+    ]
+
+    @pl.when(at == 0)
+    def _():
+        for fetch in fetches:
+            fetch.start()
+
     ext[0:HALO, :] = halo_ref[...].astype(jnp.float32)
     ext[HALO:, :] = x_ref[...].astype(jnp.float32)
+
+    @pl.when(at == 0)
+    def _():
+        for fetch in fetches:
+            fetch.wait()
+
     for lane in range(0, chunk, LANES):
         cols = slice(lane, lane + LANES)
-        total = b_ref[:, cols] + w_ref[0:1, cols] * ext[HALO:, cols]
+        here = pl.ds(pl.multiple_of(at * chunk + lane, LANES), LANES)
+        total = b_ref[:, here] + w_ref[0:1, here] * ext[HALO:, cols]
         for lag in range(1, w_ref.shape[0]):
             window = ext[HALO - lag : HALO - lag + tok, cols]
-            total += w_ref[lag : lag + 1, cols] * jnp.where(depth >= lag, window, 0.0)
+            total += w_ref[lag : lag + 1, here] * jnp.where(depth >= lag, window, 0.0)
         act = total * (0.5 + 0.5 * jnp.tanh(0.5 * total))
         inner_ref[:, cols] = act.astype(jnp.bfloat16)
     product = lax.dot_general(
         xp_ref[...], inner_ref[...], (((1,), (1,)), ((), ())), preferred_element_type=jnp.float32
     )
-    at = pl.program_id(0)
 
     @pl.when(at == 0)
     def _():
@@ -113,8 +133,8 @@
             pl.BlockSpec(memory_space=pltpu.SMEM),
             pl.BlockSpec((tok, chunk), lambda i: (0, i)),
             pl.BlockSpec((HALO, chunk), lambda i: (0, i)),
-            pl.BlockSpec((taps, chunk), lambda i: (0, i)),
-            pl.BlockSpec((1, chunk), lambda i: (0, i)),
+            pl.BlockSpec(memory_space=pltpu.HBM),
+            pl.BlockSpec(memory_space=pltpu.HBM),
             pl.BlockSpec((width, chunk), lambda i: (0, i)),
         ],
         out_specs=[
@@ -128,8 +148,11 @@
         scratch_shapes=[
             pltpu.VMEM((tok + HALO, chunk), jnp.float32),
             pltpu.VMEM((width, tok), jnp.float32),
-        ],
-        compiler_params=pltpu.CompilerParams(vmem_limit_bytes=VMEM_MOST),
+            pltpu.VMEM((taps, channels), jnp.float32),
+            pltpu.VMEM((1, channels), jnp.float32),
+            pltpu.SemaphoreType.DMA((2,)),
+        ],
+        compiler_params=pltpu.CompilerParams(vmem_limit_bytes=VMEM_NEARLY),
         cost_estimate=pl.CostEstimate(
             flops=80 * tok * channels * width, bytes_accessed=8 * tok * channels, transcendentals=tok * channels
         ),
@@ -423,7 +446,7 @@
             pltpu.VMEM((states * count, ROWS, LANES), jnp.float32),
             pltpu.VMEM((2, tiles * ROWS, LANES), jnp.float32),
         ],
-        compiler_params=pltpu.CompilerParams(vmem_limit_bytes=VMEM_MOST),
+        compiler_params=pltpu.CompilerParams(vmem_limit_bytes=VMEM_NEARLY),
         cost_estimate=pl.CostEstimate(
             flops=8 * tok * channels * states,
             bytes_accessed=14 * tok * channels,

time: 83.1 us -> 83.3 us (level)
  local copies, waits for them, and re-layouts: 1.72 us -> 3.14 us
  other arithmetic: 2.04 us -> 1.09 us
    unnamed x20 -> x26, local copies, waits for them, and re-layouts: 1.72 us -> 3.13 us
    ppermute x2, waiting for transfers between devices: 10.4 us -> 11.7 us  [local(): lax.ppermute(total, 'mp', [(source, source ^ step) for source in range(n_...]
    convert_element_type x1, other arithmetic: 1.03 us -> 0.08 us  [local(): (total.astype(jnp.float32) + other.astype(jnp.float32)).astype(jnp.bfloat16)]
    ppermute x5, waiting for transfers between devices: 3.12 us -> 2.28 us  [shifted(): lax.ppermute(value, 'seq', [(source, source + steps) for source in range(...]
  transfers between devices with their start and end apart: 10 -> 10, of which waited for: 5 -> 4; matrix products, arithmetic and copies ran while one was open for 2% -> 1% of each run, Pallas kernels for 30% -> 30%
where the time goes in v11:
time: 83.3 us; the launch traced here: 82.8 us
  Pallas kernels  36.2 us (43%)
  starting transfers between devices  26.2 us (31%)
  waiting for transfers between devices  15.4 us (18%)
  local copies, waits for them, and re-layouts  3.14 us (4%)
  other arithmetic  1.09 us (1%)
    ppermute x5, starting transfers between devices, shifted(): lax.ppermute(value, 'seq', [(source, source + steps) for source in range(...  17.5 us
    pallas_call x1, Pallas kernels, local_scan(): pl.pallas_call(local_kernel, grid=(tok // BLOCK,), in_specs=[pl.BlockSpec...  14 us
    ppermute x2, waiting for transfers between devices, local(): lax.ppermute(total, 'mp', [(source, source ^ step) for source in range(n_...  11.7 us
    pallas_call x1, Pallas kernels, join_states(): pl.pallas_call(functools.partial(join_kernel, reach), grid=(tok // BLOCK,...  9.59 us
    pallas_call x1, Pallas kernels, conv_project(): pl.pallas_call(conv_kernel, grid=(channels // chunk,), in_specs=[pl.Block...  5.46 us
    pallas_call x1, Pallas kernels, attend(): pl.pallas_call(attend_kernel, grid=(kv_local,), in_specs=[pl.BlockSpec(me...  5.38 us
    ppermute x2, starting transfers between devices, local(): lax.ppermute(total, 'mp', [(source, source ^ step) for source in range(n_...  4.29 us
    all_to_all x1, starting transfers between devices, local(): lax.all_to_all(attended, 'seq', split_axis=0, concat_axis=0, tiled=True)  4.22 us
  transfers between devices with their start and end apart: 10, of which 4 were waited for; matrix products, arithmetic and copies ran while one was open for 1% of the time, Pallas kernels for 30%

profile of v11, /device:TPU:0, one launch (start us, length us, event | category | flops | bytes accessed | tf_op | source)
XLA Modules:
  0.0 82.8 jit_solution(855380591903823020)
XLA Ops:
  0.6 1.7 %pack.1 = (bf16[16,2048]{1,0:T(8,128)(2,1)}, bf16[256,512]{1,0:T(8,128)(2,1)}) custom-call(bf16[256,2048]{1,0:T(8,128)(2,1)} %x_ref.3, bf16[256,256]{1,0:T(8,128)(2,1)} %k_ref.1, bf16[256,256]{1,0:T(8,128)(2,1)} %v_ref.1), custom_call_target="tpu_custom_call" | custom-call | bytes 1048576 | tf_op jit(solution)/shard_map/pack/pallas_call | solution.py:52
  2.4 2.3 %collective-permute-start = (bf16[16,2048]{1,0:T(8,128)(2,1)}, bf16[16,2048]{1,0:T(8,128)(2,1)S(1)}, u32[]{:S(2)}, u32[]{:S(2)}) collective-permute-start(bf16[16,2048]{1,0:T(8,128)(2,1)} %get-tuple-element.17), channel_id=1, source_target_pairs={{0,4},{4,8},{8,12},{12,16},{16,20},{20,24},{24,28},{1,5},{5,9},{9,... | collective-permute-start | bytes 196616 | tf_op jit(solution)/shard_map/ppermute | solution.py:611
  4.7 4.4 %collective-permute-start.4 = (bf16[256,512]{1,0:T(8,128)(2,1)}, bf16[256,512]{1,0:T(8,128)(2,1)S(1)}, u32[]{:S(2)}, u32[]{:S(2)}) collective-permute-start(bf16[256,512]{1,0:T(8,128)(2,1)} %get-tuple-element.22), channel_id=1, source_target_pairs={{0,16},{4,20},{8,24},{12,28},{1,17},{5,21},{9,25},{13,29},{2,18},{... | collective-permute-start | bytes 786440 | tf_op jit(solution)/shard_map/ppermute | solution.py:611
  9.2 3.4 %collective-permute-start.3 = (bf16[256,512]{1,0:T(8,128)(2,1)}, bf16[256,512]{1,0:T(8,128)(2,1)S(1)}, u32[]{:S(2)}, u32[]{:S(2)}) collective-permute-start(bf16[256,512]{1,0:T(8,128)(2,1)} %get-tuple-element.22), channel_id=1, source_target_pairs={{0,8},{4,12},{8,16},{12,20},{16,24},{20,28},{1,9},{5,13},{9,17},{1... | collective-permute-start | bytes 786440 | tf_op jit(solution)/shard_map/ppermute | solution.py:611
  12.6 0.0 copy-start.3
  12.6 0.6 copy-done.3
  13.3 0.8 copy-done.6
  14.0 0.7 copy-done.7
  14.7 5.5 %conv_project.1 = (bf16[256,2048]{1,0:T(8,128)(2,1)}, bf16[544,256]{1,0:T(8,128)(2,1)S(1)}) custom-call(s32[4]{0:T(128)S(1)} %copy-done.3, bf16[256,2048]{1,0:T(8,128)(2,1)} %x_ref.3, bf16[16,2048]{1,0:T(8,128)(2,1)S(1)} %collective-permute-done.halo_ref, f32[4,2048]{1,0:T(4,128)S(1)} %copy-done.6, f32[1,2048]{1,0:T(1,128)S(1)} %bitcast.12, ...), custom_call_target="tpu_custom_call" | custom-call | flops 22817013760 | bytes 4194304 | tf_op jit(solution)/shard_map/conv_project/pallas_call | solution.py:129
  20.2 0.0 copy-start
  20.2 0.0 copy-start.4
  20.2 1.6 %collective-permute-start.1 = (bf16[544,256]{1,0:T(8,128)(2,1)S(1)}, bf16[544,256]{1,0:T(8,128)(2,1)S(1)}, u32[]{:S(2)}, u32[]{:S(2)}) collective-permute-start(bf16[544,256]{1,0:T(8,128)(2,1)S(1)} %get-tuple-element.18), channel_id=1, source_target_pairs={{0,1},{1,0},{2,3},{3,2},{4,5},{5,4},{6,7},{7,6},{8,9},{9,8},{10,11... | collective-permute-start | bytes 835592 | tf_op jit(solution)/shard_map/ppermute | solution.py:663
  21.9 0.1 pad_maximum_fusion.keys_mine.values_mine
  22.0 0.1 collective-permute-start.5
  22.1 6.0 %collective-permute-done.1 = bf16[544,256]{1,0:T(8,128)(2,1)S(1)} collective-permute-done((bf16[544,256]{1,0:T(8,128)(2,1)S(1)}, bf16[544,256]{1,0:T(8,128)(2,1)S(1)}, u32[]{:S(2)}, u32[]{:S(2)}) %collective-permute-start.1) | collective-permute-done | bytes 278560 | tf_op jit(solution)/shard_map/ppermute | solution.py:663
  28.0 0.1 add_convert_fusion.proj_ref
  28.1 0.0 copy-start.1
  28.1 2.7 %collective-permute-start.2 = (bf16[544,256]{1,0:T(8,128)(2,1)S(1)}, bf16[544,256]{1,0:T(8,128)(2,1)S(1)}, u32[]{:S(2)}, u32[]{:S(2)}) collective-permute-start(bf16[544,256]{1,0:T(8,128)(2,1)S(1)} %add_convert_fusion.proj_ref), channel_id=1, source_target_pairs={{0,2},{1,3},{2,0},{3,1},{4,6},{5,7},{6,4},{7,5},{8,10},{9,11},{10,... | collective-permute-start | bytes 835592 | tf_op jit(solution)/shard_map/ppermute | solution.py:663
  30.8 5.4 %attend.1 = bf16[256,2048]{1,0:T(8,128)(2,1)} custom-call(s32[4]{0:T(128)S(1)} %copy-done.4, s32[8,256]{1,0:T(8,128)S(1)} %reshape.19.place_ref, bf16[256,2048]{1,0:T(8,128)(2,1)S(1)} %copy-done, bf16[3,256,512]{2,1,0:T(8,128)(2,1)S(1)} %pad_maximum_fusion.keys_mine.values_mine, bf16[3,256,512]{2,1,0:T(8,128)(2,1)S(1)} %collective-permute-done.5.keys_theirs.values_theirs, ...), custom_call_target="tpu_custom_call" | custom-call | flops 524288 | bytes 524288 | tf_op jit(solution)/shard_map/attend/pallas_call | solution.py:583
  36.2 5.7 %collective-permute-done.2.other_ref = bf16[544,256]{1,0:T(8,128)(2,1)S(1)} collective-permute-done((bf16[544,256]{1,0:T(8,128)(2,1)S(1)}, bf16[544,256]{1,0:T(8,128)(2,1)S(1)}, u32[]{:S(2)}, u32[]{:S(2)}) %collective-permute-start.2) | collective-permute-done | bytes 278560 | tf_op jit(solution)/shard_map/ppermute | solution.py:663
  41.9 4.2 %all-to-all-start = ((bf16[8,32,2048]{2,1,0:T(8,128)(2,1)}), bf16[8,32,2048]{2,1,0:T(8,128)(2,1)S(1)}, u32[]{:S(2)}, u32[]{:S(2)}) async-start(bf16[8,32,2048]{2,1,0:T(8,128)(2,1)} %bitcast.7), calls=%async_computation | async-start | bytes 2097152 | tf_op jit(solution)/shard_map/all_to_all | solution.py:666
  46.2 0.0 copy-start.5
  46.2 0.0 copy-start.8
  46.2 14.0 %local_scan.1 = (f32[256,16,128]{2,1,0:T(8,128)}, f32[256,16,128]{2,1,0:T(8,128)}, bf16[288,128]{1,0:T(8,128)(2,1)}) custom-call(s32[4]{0:T(128)} %lengths_ref.5, bf16[544,256]{1,0:T(8,128)(2,1)} %copy-done.1, bf16[544,256]{1,0:T(8,128)(2,1)} %copy-done.12, bf16[512,2048]{1,0:T(8,128)(2,1)} %dtw_ref.1, f32[1,2048]{1,0:T(1,128)} %bitcast.22, ...), custom_call_target="tpu_custom_call" | custom-call | flops 100663296 | bytes 6291456 | tf_op jit(solution)/shard_map/local_scan/pallas_call | solution.py:306
  60.2 3.9 %collective-permute-start.7 = (bf16[288,128]{1,0:T(8,128)(2,1)}, bf16[288,128]{1,0:T(8,128)(2,1)S(1)}, u32[]{:S(2)}, u32[]{:S(2)}) collective-permute-start(bf16[288,128]{1,0:T(8,128)(2,1)} %get-tuple-element.31), channel_id=1, source_target_pairs={{0,16},{4,20},{8,24},{12,28},{1,17},{5,21},{9,25},{13,29},{2,18},{... | collective-permute-start | bytes 221192 | tf_op jit(solution)/shard_map/ppermute | solution.py:611
  64.1 3.4 %collective-permute-start.6 = (bf16[288,128]{1,0:T(8,128)(2,1)}, bf16[288,128]{1,0:T(8,128)(2,1)S(1)}, u32[]{:S(2)}, u32[]{:S(2)}) collective-permute-start(bf16[288,128]{1,0:T(8,128)(2,1)} %get-tuple-element.31), channel_id=1, source_target_pairs={{0,8},{4,12},{8,16},{12,20},{16,24},{20,28},{1,9},{5,13},{9,17},{1... | collective-permute-start | bytes 221192 | tf_op jit(solution)/shard_map/ppermute | solution.py:611
  67.5 2.3 %collective-permute-done.6 = bf16[288,128]{1,0:T(8,128)(2,1)S(1)} collective-permute-done((bf16[288,128]{1,0:T(8,128)(2,1)}, bf16[288,128]{1,0:T(8,128)(2,1)S(1)}, u32[]{:S(2)}, u32[]{:S(2)}) %collective-permute-start.6) | collective-permute-done | bytes 73760 | tf_op jit(solution)/shard_map/ppermute | solution.py:611
  69.8 0.9 %pad_maximum_fusion.1.mine_ref = bf16[3,288,128]{2,1,0:T(8,128)(2,1)S(1)} fusion(bf16[1,288,128]{2,1,0:T(8,128)(2,1)S(1)} %bitcast.19, bf16[1,288,128]{2,1,0:T(8,128)(2,1)S(1)} %bitcast.20, bf16[1,288,128]{2,1,0:T(8,128)(2,1)} %bitcast.18), kind=kLoop, calls=%fused_computation.2 | loop fusion | flops 221184 | bytes 442368 | tf_op jit(solution)/shard_map/stack | solution.py:615
  70.7 0.1 collective-permute-start.8
  70.8 1.5 %collective-permute-done.8.theirs_ref = bf16[3,288,128]{2,1,0:T(8,128)(2,1)S(1)} collective-permute-done((bf16[3,288,128]{2,1,0:T(8,128)(2,1)S(1)}, bf16[3,288,128]{2,1,0:T(8,128)(2,1)S(1)}, u32[]{:S(2)}, u32[]{:S(2)}) %collective-permute-start.8) | collective-permute-done | bytes 221216 | tf_op jit(solution)/shard_map/ppermute | solution.py:617
  72.3 1.0 %copy-done.9 = bf16[8,32,2048]{2,1,0:T(8,128)(2,1)} copy-done((bf16[8,32,2048]{2,1,0:T(8,128)(2,1)}, bf16[8,32,2048]{2,1,0:T(8,128)(2,1)S(1)}, u32[]{:S(2)}) %copy-start.9) | copy-done | bytes 1048600
  73.2 9.6 %join_states.1 = (bf16[256,2048]{1,0:T(8,128)(2,1)}, bf16[256,2048]{1,0:T(8,128)(2,1)}) custom-call(bf16[544,256]{1,0:T(8,128)(2,1)S(1)} %copy-done.2, bf16[544,256]{1,0:T(8,128)(2,1)} %copy-done.12, f32[256,16,128]{2,1,0:T(8,128)} %get-tuple-element.28.y_ref, f32[256,16,128]{2,1,0:T(8,128)} %get-tuple-element.29.sum_ref, ...), custom_call_target="tpu_custom_call" | custom-call | flops 67108864 | bytes 7340032 | tf_op jit(solution)/shard_map/join_states/pallas_call | solution.py:425
  (24 shorter events, 0.1 us)
Async XLA Ops:
  2.4 10.2 %collective-permute-start = (bf16[16,2048]{1,0:T(8,128)(2,1)}, bf16[16,2048]{1,0:T(8,128)(2,1)S(1)}, u32[]{:S(2)}, u32[]{:S(2)}) collective-permute-start(bf16[16,2048]{1,0:T(8,128)(2,1)} %get-tuple-element.17), channel_id=1, source_target_pairs={{0,4},{4,8},{8,12},{12,16},{16,20},{20,24},{24,28},{1,5},{5,9},{9,... | collective-permute-start | bytes 196616 | tf_op jit(solution)/shard_map/ppermute | solution.py:611
  4.7 17.1 %collective-permute-start.4 = (bf16[256,512]{1,0:T(8,128)(2,1)}, bf16[256,512]{1,0:T(8,128)(2,1)S(1)}, u32[]{:S(2)}, u32[]{:S(2)}) collective-permute-start(bf16[256,512]{1,0:T(8,128)(2,1)} %get-tuple-element.22), channel_id=1, source_target_pairs={{0,16},{4,20},{8,24},{12,28},{1,17},{5,21},{9,25},{13,29},{2,18},{... | collective-permute-start | bytes 786440 | tf_op jit(solution)/shard_map/ppermute | solution.py:611
  9.2 12.7 %collective-permute-start.3 = (bf16[256,512]{1,0:T(8,128)(2,1)}, bf16[256,512]{1,0:T(8,128)(2,1)S(1)}, u32[]{:S(2)}, u32[]{:S(2)}) collective-permute-start(bf16[256,512]{1,0:T(8,128)(2,1)} %get-tuple-element.22), channel_id=1, source_target_pairs={{0,8},{4,12},{8,16},{12,20},{16,24},{20,28},{1,9},{5,13},{9,17},{1... | collective-permute-start | bytes 786440 | tf_op jit(solution)/shard_map/ppermute | solution.py:611
  12.6 0.7 copy-start.3
  13.3 0.8 copy-start.6
  14.0 0.7 copy-start.7
  14.7 7.1 %copy-start.10 = (bf16[256,512]{1,0:T(8,128)(2,1)S(1)}, bf16[256,512]{1,0:T(8,128)(2,1)}, u32[]{:S(2)}) copy-start(bf16[256,512]{1,0:T(8,128)(2,1)} %get-tuple-element.22) | copy-start | bytes 786436
  14.7 7.3 %copy-start.11 = (s32[2048]{0:T(1024)S(1)}, s32[2048]{0:T(1024)}, u32[]{:S(2)}) copy-start(s32[2048]{0:T(1024)} %param.27) | copy-start | bytes 24580
  20.2 10.6 %copy-start = (bf16[256,2048]{1,0:T(8,128)(2,1)S(1)}, bf16[256,2048]{1,0:T(8,128)(2,1)}, u32[]{:S(2)}) copy-start(bf16[256,2048]{1,0:T(8,128)(2,1)} %q_ref.1) | copy-start | bytes 3145732
  20.2 10.6 %copy-start.4 = (s32[4]{0:T(128)S(1)}, s32[4]{0:T(128)}, u32[]{:S(2)}) copy-start(s32[4]{0:T(128)} %lengths_ref.5) | copy-start | bytes 52
  20.2 7.8 %collective-permute-start.1 = (bf16[544,256]{1,0:T(8,128)(2,1)S(1)}, bf16[544,256]{1,0:T(8,128)(2,1)S(1)}, u32[]{:S(2)}, u32[]{:S(2)}) collective-permute-start(bf16[544,256]{1,0:T(8,128)(2,1)S(1)} %get-tuple-element.18), channel_id=1, source_target_pairs={{0,1},{1,0},{2,3},{3,2},{4,5},{5,4},{6,7},{7,6},{8,9},{9,8},{10,11... | collective-permute-start | bytes 835592 | tf_op jit(solution)/shard_map/ppermute | solution.py:663
  22.0 8.8 %collective-permute-start.5 = (bf16[3,256,512]{2,1,0:T(8,128)(2,1)S(1)}, bf16[3,256,512]{2,1,0:T(8,128)(2,1)S(1)}, u32[]{:S(2)}, u32[]{:S(2)}) collective-permute-start(bf16[3,256,512]{2,1,0:T(8,128)(2,1)S(1)} %pad_maximum_fusion.keys_mine.values_mine), channel_id=1, source_target_pairs={{0,4},{4,0},{8,12},{12,8},{16,20},{20,16},{24,28},{28,24},{1,5},{5... | collective-permute-start | bytes 2359304 | tf_op jit(solution)/shard_map/ppermute | solution.py:617
  28.1 8.1 %copy-start.1 = (bf16[544,256]{1,0:T(8,128)(2,1)}, bf16[544,256]{1,0:T(8,128)(2,1)S(1)}, u32[]{:S(2)}) copy-start(bf16[544,256]{1,0:T(8,128)(2,1)S(1)} %add_convert_fusion.proj_ref) | copy-start | bytes 835588
  28.1 13.8 %collective-permute-start.2 = (bf16[544,256]{1,0:T(8,128)(2,1)S(1)}, bf16[544,256]{1,0:T(8,128)(2,1)S(1)}, u32[]{:S(2)}, u32[]{:S(2)}) collective-permute-start(bf16[544,256]{1,0:T(8,128)(2,1)S(1)} %add_convert_fusion.proj_ref), channel_id=1, source_target_pairs={{0,2},{1,3},{2,0},{3,1},{4,6},{5,7},{6,4},{7,5},{8,10},{9,11},{10,... | collective-permute-start | bytes 835592 | tf_op jit(solution)/shard_map/ppermute | solution.py:663
  41.9 4.2 %copy-start.12 = (bf16[544,256]{1,0:T(8,128)(2,1)}, bf16[544,256]{1,0:T(8,128)(2,1)S(1)}, u32[]{:S(2)}) copy-start(bf16[544,256]{1,0:T(8,128)(2,1)S(1)} %collective-permute-done.2.other_ref) | copy-start | bytes 835588
  41.9 30.3 %all-to-all-start = ((bf16[8,32,2048]{2,1,0:T(8,128)(2,1)}), bf16[8,32,2048]{2,1,0:T(8,128)(2,1)S(1)}, u32[]{:S(2)}, u32[]{:S(2)}) async-start(bf16[8,32,2048]{2,1,0:T(8,128)(2,1)} %bitcast.7), calls=%async_computation | async-start | bytes 2097152 | tf_op jit(solution)/shard_map/all_to_all | solution.py:666
  46.1 27.1 %copy-start.2 = (bf16[544,256]{1,0:T(8,128)(2,1)S(1)}, bf16[544,256]{1,0:T(8,128)(2,1)}, u32[]{:S(2)}) copy-start(bf16[544,256]{1,0:T(8,128)(2,1)} %copy-done.1) | copy-start | bytes 835588
  46.2 27.1 %copy-start.5 = (f32[16,2048]{1,0:T(8,128)S(1)}, f32[16,2048]{1,0:T(8,128)}, u32[]{:S(2)}) copy-start(f32[16,2048]{1,0:T(8,128)} %rate_ref.3) | copy-start | bytes 393220
  46.2 27.1 %copy-start.8 = (f32[2048]{0:T(1024)S(1)}, f32[2048]{0:T(1024)}, u32[]{:S(2)}) copy-start(f32[2048]{0:T(1024)} %param.22) | copy-start | bytes 24580
  60.2 7.3 %collective-permute-start.7 = (bf16[288,128]{1,0:T(8,128)(2,1)}, bf16[288,128]{1,0:T(8,128)(2,1)S(1)}, u32[]{:S(2)}, u32[]{:S(2)}) collective-permute-start(bf16[288,128]{1,0:T(8,128)(2,1)} %get-tuple-element.31), channel_id=1, source_target_pairs={{0,16},{4,20},{8,24},{12,28},{1,17},{5,21},{9,25},{13,29},{2,18},{... | collective-permute-start | bytes 221192 | tf_op jit(solution)/shard_map/ppermute | solution.py:611
  64.1 5.7 %collective-permute-start.6 = (bf16[288,128]{1,0:T(8,128)(2,1)}, bf16[288,128]{1,0:T(8,128)(2,1)S(1)}, u32[]{:S(2)}, u32[]{:S(2)}) collective-permute-start(bf16[288,128]{1,0:T(8,128)(2,1)} %get-tuple-element.31), channel_id=1, source_target_pairs={{0,8},{4,12},{8,16},{12,20},{16,24},{20,28},{1,9},{5,13},{9,17},{1... | collective-permute-start | bytes 221192 | tf_op jit(solution)/shard_map/ppermute | solution.py:611
  70.7 1.5 %collective-permute-start.8 = (bf16[3,288,128]{2,1,0:T(8,128)(2,1)S(1)}, bf16[3,288,128]{2,1,0:T(8,128)(2,1)S(1)}, u32[]{:S(2)}, u32[]{:S(2)}) collective-permute-start(bf16[3,288,128]{2,1,0:T(8,128)(2,1)S(1)} %pad_maximum_fusion.1.mine_ref), channel_id=1, source_target_pairs={{0,4},{4,0},{8,12},{12,8},{16,20},{20,16},{24,28},{28,24},{1,5},{5... | collective-permute-start | bytes 663560 | tf_op jit(solution)/shard_map/ppermute | solution.py:617
  72.3 1.0 %copy-start.9 = (bf16[8,32,2048]{2,1,0:T(8,128)(2,1)}, bf16[8,32,2048]{2,1,0:T(8,128)(2,1)S(1)}, u32[]{:S(2)}) copy-start(bf16[8,32,2048]{2,1,0:T(8,128)(2,1)S(1)} %all-to-all-done) | copy-start | bytes 3145732

commit v12 on v11

--- a/solution.py
+++ b/solution.py
@@ -15,7 +15,8 @@
 APART = 65536.0
 VMEM_LIMIT = 32 * 1024 * 1024
 VMEM_MOST = 56 * 1024 * 1024
-VMEM_NEARLY = 53 * 1024 * 1024
+VMEM_NEARLY = 52 * 1024 * 1024 + 512 * 1024
+VMEM_SOME = 50 * 1024 * 1024
 
 
 def doc_edges(lengths_ref):
@@ -32,6 +33,10 @@
     for start in starts[1:]:
         found = jnp.where(places >= start, start, found)
     return found
+
+
+def in_hbm(value):
+    return pltpu.with_memory_space_constraint(value, pltpu.HBM)
 
 
 def channel_chunk(channels):
@@ -157,7 +162,14 @@
             flops=80 * tok * channels * width, bytes_accessed=8 * tok * channels, transcendentals=tok * channels
         ),
         name="conv_project",
-    )(lengths, x_branch, halo, conv_weight, conv_bias.reshape(1, channels), xproj_weight.T)
+    )(
+        lengths,
+        in_hbm(x_branch),
+        halo,
+        in_hbm(conv_weight),
+        in_hbm(conv_bias.reshape(1, channels)),
+        in_hbm(xproj_weight.T),
+    )
 
 
 ROWS = 8
@@ -330,14 +342,16 @@
             pltpu.VMEM((BLOCK // ROWS, tiles * ROWS, LANES), jnp.float32),
             pltpu.VMEM(((states + 1) * count, ROWS, LANES), jnp.float32),
         ],
-        compiler_params=pltpu.CompilerParams(vmem_limit_bytes=VMEM_MOST),
+        compiler_params=pltpu.CompilerParams(vmem_limit_bytes=VMEM_NEARLY),
         cost_estimate=pl.CostEstimate(
             flops=12 * tok * channels * states,
             bytes_accessed=12 * tok * channels,
             transcendentals=tok * channels * states,
         ),
         name="local_scan",
-    )(lengths, projected, other, dt_weight, bias, decay_rate, inner_act)
+    )(
+        lengths, projected, other, in_hbm(dt_weight), in_hbm(bias), in_hbm(decay_rate), in_hbm(inner_act)
+    )
 
 
 def join_kernel(
@@ -446,14 +460,26 @@
             pltpu.VMEM((states * count, ROWS, LANES), jnp.float32),
             pltpu.VMEM((2, tiles * ROWS, LANES), jnp.float32),
         ],
-        compiler_params=pltpu.CompilerParams(vmem_limit_bytes=VMEM_NEARLY),
+        compiler_params=pltpu.CompilerParams(vmem_limit_bytes=VMEM_SOME),
         cost_estimate=pl.CostEstimate(
             flops=8 * tok * channels * states,
             bytes_accessed=14 * tok * channels,
             transcendentals=tok * channels * states,
         ),
         name="join_states",
-    )(projected, other, y, sums, inner_act, z_branch, decay_rate, skip, moved, mine, theirs)
+    )(
+        projected,
+        other,
+        in_hbm(y),
+        in_hbm(sums),
+        in_hbm(inner_act),
+        in_hbm(z_branch),
+        in_hbm(decay_rate),
+        in_hbm(skip),
+        moved,
+        mine,
+        theirs,
+    )
 
 
 def attend_kernel(
@@ -645,6 +671,7 @@
     run_rows = tok // n_seq
     fence = lax.optimization_barrier
 
+    lengths = in_hbm(lengths)
     halo, kv = pack(x_branch, key_rows, value_rows)
     earlier_rows = shifted(halo, 1)
     held = even_back(kv, reach)

time: 83.3 us -> 78.6 us (0.944)
  local copies, waits for them, and re-layouts: 3.14 us -> 0.03 us
  waiting for transfers between devices: 15.4 us -> 14.4 us
  other arithmetic: 1.09 us -> 0.2 us
    unnamed x26 -> x8, local copies, waits for them, and re-layouts: 3.13 us -> 0.02 us
    ppermute x2, waiting for transfers between devices: 11.7 us -> 9.5 us  [local(): lax.ppermute(total, 'mp', [(source, source ^ step) for source in range(n_...]
    ppermute x5, waiting for transfers between devices: 2.28 us -> 3.43 us  [shifted(): lax.ppermute(value, 'seq', [(source, source + steps) for source in range(...]
    another operation x2, other arithmetic: 1 us -> 0.12 us  [with_partner(): mine = jnp.stack(held)]
  transfers between devices with their start and end apart: 10 -> 10, of which waited for: 4 -> 5; matrix products, arithmetic and copies ran while one was open for 1% -> 0% of each run, Pallas kernels for 30% -> 32%
where the time goes in v12:
time: 78.6 us; the launch traced here: 78.2 us
  Pallas kernels  36 us (46%)
  starting transfers between devices  26.8 us (34%)
  waiting for transfers between devices  14.4 us (18%)
    ppermute x5, starting transfers between devices, shifted(): lax.ppermute(value, 'seq', [(source, source + steps) for source in range(...  17.5 us
    pallas_call x1, Pallas kernels, local_scan(): pl.pallas_call(local_kernel, grid=(tok // BLOCK,), in_specs=[pl.BlockSpec...  13.8 us
    pallas_call x1, Pallas kernels, join_states(): pl.pallas_call(functools.partial(join_kernel, reach), grid=(tok // BLOCK,...  9.56 us
    ppermute x2, waiting for transfers between devices, local(): lax.ppermute(total, 'mp', [(source, source ^ step) for source in range(n_...  9.5 us
    pallas_call x1, Pallas kernels, attend(): pl.pallas_call(attend_kernel, grid=(kv_local,), in_specs=[pl.BlockSpec(me...  5.46 us
    pallas_call x1, Pallas kernels, conv_project(): pl.pallas_call(conv_kernel, grid=(channels // chunk,), in_specs=[pl.Block...  5.44 us
    ppermute x2, starting transfers between devices, local(): lax.ppermute(total, 'mp', [(source, source ^ step) for source in range(n_...  4.29 us
    all_to_all x1, starting transfers between devices, local(): lax.all_to_all(attended, 'seq', split_axis=0, concat_axis=0, tiled=True)  4.22 us
  transfers between devices with their start and end apart: 10, of which 5 were waited for; matrix products, arithmetic and copies ran while one was open for 0% of the time, Pallas kernels for 32%

profile of v12, /device:TPU:0, one launch (start us, length us, event | category | flops | bytes accessed | tf_op | source)
XLA Modules:
  0.0 78.2 jit_solution(1161064802517518983)
XLA Ops:
  0.6 1.7 %pack.1 = (bf16[16,2048]{1,0:T(8,128)(2,1)}, bf16[256,512]{1,0:T(8,128)(2,1)}) custom-call(bf16[256,2048]{1,0:T(8,128)(2,1)} %x_ref.3, bf16[256,256]{1,0:T(8,128)(2,1)} %k_ref.1, bf16[256,256]{1,0:T(8,128)(2,1)} %v_ref.1), custom_call_target="tpu_custom_call" | custom-call | bytes 1048576 | tf_op jit(solution)/shard_map/pack/pallas_call | solution.py:57
  2.4 2.3 %collective-permute-start = (bf16[16,2048]{1,0:T(8,128)(2,1)}, bf16[16,2048]{1,0:T(8,128)(2,1)S(1)}, u32[]{:S(2)}, u32[]{:S(2)}) collective-permute-start(bf16[16,2048]{1,0:T(8,128)(2,1)} %get-tuple-element.17), channel_id=1, source_target_pairs={{0,4},{4,8},{8,12},{12,16},{16,20},{20,24},{24,28},{1,5},{5,9},{9,... | collective-permute-start | bytes 196616 | tf_op jit(solution)/shard_map/ppermute | solution.py:637
  4.7 4.4 %collective-permute-start.4 = (bf16[256,512]{1,0:T(8,128)(2,1)}, bf16[256,512]{1,0:T(8,128)(2,1)S(1)}, u32[]{:S(2)}, u32[]{:S(2)}) collective-permute-start(bf16[256,512]{1,0:T(8,128)(2,1)} %get-tuple-element.22), channel_id=1, source_target_pairs={{0,16},{4,20},{8,24},{12,28},{1,17},{5,21},{9,25},{13,29},{2,18},{... | collective-permute-start | bytes 786440 | tf_op jit(solution)/shard_map/ppermute | solution.py:637
  9.2 3.4 %collective-permute-start.3 = (bf16[256,512]{1,0:T(8,128)(2,1)}, bf16[256,512]{1,0:T(8,128)(2,1)S(1)}, u32[]{:S(2)}, u32[]{:S(2)}) collective-permute-start(bf16[256,512]{1,0:T(8,128)(2,1)} %get-tuple-element.22), channel_id=1, source_target_pairs={{0,8},{4,12},{8,16},{12,20},{16,24},{20,28},{1,9},{5,13},{9,17},{1... | collective-permute-start | bytes 786440 | tf_op jit(solution)/shard_map/ppermute | solution.py:637
  12.6 0.0 collective-permute-done.halo_ref
  12.6 0.0 copy-start.2
  12.6 0.0 copy-start.3
  12.6 5.4 %conv_project.1 = (bf16[256,2048]{1,0:T(8,128)(2,1)S(1)}, bf16[544,256]{1,0:T(8,128)(2,1)S(1)}) custom-call(s32[4]{0:T(128)} %lengths_ref.5, bf16[256,2048]{1,0:T(8,128)(2,1)} %x_ref.3, bf16[16,2048]{1,0:T(8,128)(2,1)S(1)} %collective-permute-done.halo_ref, f32[4,2048]{1,0:T(4,128)} %w_hbm.1, f32[1,2048]{1,0:T(1,128)} %bitcast.20, bf16[544,2048]{1,0:T(8,128)(2,1)} %bitcast.19), custom_call_target="tpu_custom_call" | custom-call | flops 22817013760 | bytes 4194304 | tf_op jit(solution)/shard_map/conv_project/pallas_call | solution.py:134
  18.1 0.0 copy-start.1
  18.1 0.0 copy-start
  18.1 1.6 %collective-permute-start.1 = (bf16[544,256]{1,0:T(8,128)(2,1)S(1)}, bf16[544,256]{1,0:T(8,128)(2,1)S(1)}, u32[]{:S(2)}, u32[]{:S(2)}) collective-permute-start(bf16[544,256]{1,0:T(8,128)(2,1)S(1)} %get-tuple-element.18), channel_id=1, source_target_pairs={{0,1},{1,0},{2,3},{3,2},{4,5},{5,4},{6,7},{7,6},{8,9},{9,8},{10,11... | collective-permute-start | bytes 835592 | tf_op jit(solution)/shard_map/ppermute | solution.py:690
  19.7 1.5 %collective-permute-done.4 = bf16[256,512]{1,0:T(8,128)(2,1)S(1)} collective-permute-done((bf16[256,512]{1,0:T(8,128)(2,1)}, bf16[256,512]{1,0:T(8,128)(2,1)S(1)}, u32[]{:S(2)}, u32[]{:S(2)}) %collective-permute-start.4) | collective-permute-done | bytes 262176 | tf_op jit(solution)/shard_map/ppermute | solution.py:637
  21.2 0.0 collective-permute-done.3
  21.2 0.0 copy-done.2
  21.2 0.1 pad_maximum_fusion.keys_mine.values_mine
  21.3 0.8 collective-permute-start.5
  22.1 3.8 %collective-permute-done.1 = bf16[544,256]{1,0:T(8,128)(2,1)S(1)} collective-permute-done((bf16[544,256]{1,0:T(8,128)(2,1)S(1)}, bf16[544,256]{1,0:T(8,128)(2,1)S(1)}, u32[]{:S(2)}, u32[]{:S(2)}) %collective-permute-start.1) | collective-permute-done | bytes 278560 | tf_op jit(solution)/shard_map/ppermute | solution.py:690
  25.9 0.1 add_convert_fusion.proj_ref
  26.0 2.7 %collective-permute-start.2 = (bf16[544,256]{1,0:T(8,128)(2,1)S(1)}, bf16[544,256]{1,0:T(8,128)(2,1)S(1)}, u32[]{:S(2)}, u32[]{:S(2)}) collective-permute-start(bf16[544,256]{1,0:T(8,128)(2,1)S(1)} %add_convert_fusion.proj_ref), channel_id=1, source_target_pairs={{0,2},{1,3},{2,0},{3,1},{4,6},{5,7},{6,4},{7,5},{8,10},{9,11},{10,... | collective-permute-start | bytes 835592 | tf_op jit(solution)/shard_map/ppermute | solution.py:690
  28.7 0.0 collective-permute-done.5.keys_theirs.values_theirs
  28.7 5.5 %attend.1 = bf16[256,2048]{1,0:T(8,128)(2,1)} custom-call(s32[4]{0:T(128)} %lengths_ref.5, s32[8,256]{1,0:T(8,128)S(1)} %reshape.19.place_ref, bf16[256,2048]{1,0:T(8,128)(2,1)S(1)} %copy-done, bf16[3,256,512]{2,1,0:T(8,128)(2,1)S(1)} %pad_maximum_fusion.keys_mine.values_mine, bf16[3,256,512]{2,1,0:T(8,128)(2,1)S(1)} %collective-permute-done.5.keys_theirs.values_theirs, ...), custom_call_target="tpu_custom_call" | custom-call | flops 524288 | bytes 524288 | tf_op jit(solution)/shard_map/attend/pallas_call | solution.py:609
  34.1 5.7 %collective-permute-done.2.other_ref = bf16[544,256]{1,0:T(8,128)(2,1)S(1)} collective-permute-done((bf16[544,256]{1,0:T(8,128)(2,1)S(1)}, bf16[544,256]{1,0:T(8,128)(2,1)S(1)}, u32[]{:S(2)}, u32[]{:S(2)}) %collective-permute-start.2) | collective-permute-done | bytes 278560 | tf_op jit(solution)/shard_map/ppermute | solution.py:690
  39.8 4.2 %all-to-all-start = ((bf16[8,32,2048]{2,1,0:T(8,128)(2,1)}), bf16[8,32,2048]{2,1,0:T(8,128)(2,1)S(1)}, u32[]{:S(2)}, u32[]{:S(2)}) async-start(bf16[8,32,2048]{2,1,0:T(8,128)(2,1)} %bitcast.7), calls=%async_computation | async-start | bytes 2097152 | tf_op jit(solution)/shard_map/all_to_all | solution.py:693
  44.0 13.8 %local_scan.1 = (f32[256,16,128]{2,1,0:T(8,128)}, f32[256,16,128]{2,1,0:T(8,128)}, bf16[288,128]{1,0:T(8,128)(2,1)S(1)}) custom-call(s32[4]{0:T(128)} %lengths_ref.5, bf16[544,256]{1,0:T(8,128)(2,1)S(1)} %add_convert_fusion.proj_ref, bf16[544,256]{1,0:T(8,128)(2,1)S(1)} %collective-permute-done.2.other_ref, bf16[512,2048]{1,0:T(8,128)(2,1)} %dtw_ref.1, ...), custom_call_target="tpu_custom_call" | custom-call | flops 100663296 | bytes 6291456 | tf_op jit(solution)/shard_map/local_scan/pallas_call | solution.py:318
  57.8 3.9 %collective-permute-start.7 = (bf16[288,128]{1,0:T(8,128)(2,1)S(1)}, bf16[288,128]{1,0:T(8,128)(2,1)S(1)}, u32[]{:S(2)}, u32[]{:S(2)}) collective-permute-start(bf16[288,128]{1,0:T(8,128)(2,1)S(1)} %get-tuple-element.31), channel_id=1, source_target_pairs={{0,16},{4,20},{8,24},{12,28},{1,17},{5,21},{9,25},{13,29},{2,18},{... | collective-permute-start | bytes 221192 | tf_op jit(solution)/shard_map/ppermute | solution.py:637
  61.7 3.4 %collective-permute-start.6 = (bf16[288,128]{1,0:T(8,128)(2,1)S(1)}, bf16[288,128]{1,0:T(8,128)(2,1)S(1)}, u32[]{:S(2)}, u32[]{:S(2)}) collective-permute-start(bf16[288,128]{1,0:T(8,128)(2,1)S(1)} %get-tuple-element.31), channel_id=1, source_target_pairs={{0,8},{4,12},{8,16},{12,20},{16,24},{20,28},{1,9},{5,13},{9,17},{1... | collective-permute-start | bytes 221192 | tf_op jit(solution)/shard_map/ppermute | solution.py:637
  65.1 0.0 collective-permute-done.7
  65.1 2.0 %collective-permute-done.6 = bf16[288,128]{1,0:T(8,128)(2,1)S(1)} collective-permute-done((bf16[288,128]{1,0:T(8,128)(2,1)S(1)}, bf16[288,128]{1,0:T(8,128)(2,1)S(1)}, u32[]{:S(2)}, u32[]{:S(2)}) %collective-permute-start.6) | collective-permute-done | bytes 73760 | tf_op jit(solution)/shard_map/ppermute | solution.py:637
  67.1 0.1 collective-permute-start.8
  67.2 1.5 %collective-permute-done.8.theirs_ref = bf16[3,288,128]{2,1,0:T(8,128)(2,1)S(1)} collective-permute-done((bf16[3,288,128]{2,1,0:T(8,128)(2,1)S(1)}, bf16[3,288,128]{2,1,0:T(8,128)(2,1)S(1)}, u32[]{:S(2)}, u32[]{:S(2)}) %collective-permute-start.8) | collective-permute-done | bytes 221216 | tf_op jit(solution)/shard_map/ppermute | solution.py:643
  68.6 0.0 all-to-all-done
  68.6 9.6 %join_states.1 = (bf16[256,2048]{1,0:T(8,128)(2,1)}, bf16[256,2048]{1,0:T(8,128)(2,1)}) custom-call(bf16[544,256]{1,0:T(8,128)(2,1)S(1)} %add_convert_fusion.proj_ref, bf16[544,256]{1,0:T(8,128)(2,1)S(1)} %collective-permute-done.2.other_ref, f32[256,16,128]{2,1,0:T(8,128)} %get-tuple-element.28.y_ref, f32[256,16,128]{2,1,0:T(8,128)} %get-tuple-element.29.sum_ref, ...), custom_call_target="tpu_custom_call" | custom-call | flops 67108864 | bytes 7340032 | tf_op jit(solution)/shard_map/join_states/pallas_call | solution.py:439
  (6 shorter events, 0.1 us)
Async XLA Ops:
  2.4 10.2 %collective-permute-start = (bf16[16,2048]{1,0:T(8,128)(2,1)}, bf16[16,2048]{1,0:T(8,128)(2,1)S(1)}, u32[]{:S(2)}, u32[]{:S(2)}) collective-permute-start(bf16[16,2048]{1,0:T(8,128)(2,1)} %get-tuple-element.17), channel_id=1, source_target_pairs={{0,4},{4,8},{8,12},{12,16},{16,20},{20,24},{24,28},{1,5},{5,9},{9,... | collective-permute-start | bytes 196616 | tf_op jit(solution)/shard_map/ppermute | solution.py:637
  4.7 16.5 %collective-permute-start.4 = (bf16[256,512]{1,0:T(8,128)(2,1)}, bf16[256,512]{1,0:T(8,128)(2,1)S(1)}, u32[]{:S(2)}, u32[]{:S(2)}) collective-permute-start(bf16[256,512]{1,0:T(8,128)(2,1)} %get-tuple-element.22), channel_id=1, source_target_pairs={{0,16},{4,20},{8,24},{12,28},{1,17},{5,21},{9,25},{13,29},{2,18},{... | collective-permute-start | bytes 786440 | tf_op jit(solution)/shard_map/ppermute | solution.py:637
  9.2 12.0 %collective-permute-start.3 = (bf16[256,512]{1,0:T(8,128)(2,1)}, bf16[256,512]{1,0:T(8,128)(2,1)S(1)}, u32[]{:S(2)}, u32[]{:S(2)}) collective-permute-start(bf16[256,512]{1,0:T(8,128)(2,1)} %get-tuple-element.22), channel_id=1, source_target_pairs={{0,8},{4,12},{8,16},{12,20},{16,24},{20,28},{1,9},{5,13},{9,17},{1... | collective-permute-start | bytes 786440 | tf_op jit(solution)/shard_map/ppermute | solution.py:637
  12.6 8.6 %copy-start.2 = (bf16[256,512]{1,0:T(8,128)(2,1)S(1)}, bf16[256,512]{1,0:T(8,128)(2,1)}, u32[]{:S(2)}) copy-start(bf16[256,512]{1,0:T(8,128)(2,1)} %get-tuple-element.22) | copy-start | bytes 786436
  12.6 9.4 %copy-start.3 = (s32[2048]{0:T(1024)S(1)}, s32[2048]{0:T(1024)}, u32[]{:S(2)}) copy-start(s32[2048]{0:T(1024)} %param.27) | copy-start | bytes 24580
  18.1 4.0 %copy-start.1 = (bf16[256,2048]{1,0:T(8,128)(2,1)}, bf16[256,2048]{1,0:T(8,128)(2,1)S(1)}, u32[]{:S(2)}) copy-start(bf16[256,2048]{1,0:T(8,128)(2,1)S(1)} %get-tuple-element.27.inner_ref) | copy-start | bytes 3145732
  18.1 10.6 %copy-start = (bf16[256,2048]{1,0:T(8,128)(2,1)S(1)}, bf16[256,2048]{1,0:T(8,128)(2,1)}, u32[]{:S(2)}) copy-start(bf16[256,2048]{1,0:T(8,128)(2,1)} %q_ref.1) | copy-start | bytes 3145732
  18.1 7.8 %collective-permute-start.1 = (bf16[544,256]{1,0:T(8,128)(2,1)S(1)}, bf16[544,256]{1,0:T(8,128)(2,1)S(1)}, u32[]{:S(2)}, u32[]{:S(2)}) collective-permute-start(bf16[544,256]{1,0:T(8,128)(2,1)S(1)} %get-tuple-element.18), channel_id=1, source_target_pairs={{0,1},{1,0},{2,3},{3,2},{4,5},{5,4},{6,7},{7,6},{8,9},{9,8},{10,11... | collective-permute-start | bytes 835592 | tf_op jit(solution)/shard_map/ppermute | solution.py:690
  21.3 7.4 %collective-permute-start.5 = (bf16[3,256,512]{2,1,0:T(8,128)(2,1)S(1)}, bf16[3,256,512]{2,1,0:T(8,128)(2,1)S(1)}, u32[]{:S(2)}, u32[]{:S(2)}) collective-permute-start(bf16[3,256,512]{2,1,0:T(8,128)(2,1)S(1)} %pad_maximum_fusion.keys_mine.values_mine), channel_id=1, source_target_pairs={{0,4},{4,0},{8,12},{12,8},{16,20},{20,16},{24,28},{28,24},{1,5},{5... | collective-permute-start | bytes 2359304 | tf_op jit(solution)/shard_map/ppermute | solution.py:643
  26.0 13.8 %collective-permute-start.2 = (bf16[544,256]{1,0:T(8,128)(2,1)S(1)}, bf16[544,256]{1,0:T(8,128)(2,1)S(1)}, u32[]{:S(2)}, u32[]{:S(2)}) collective-permute-start(bf16[544,256]{1,0:T(8,128)(2,1)S(1)} %add_convert_fusion.proj_ref), channel_id=1, source_target_pairs={{0,2},{1,3},{2,0},{3,1},{4,6},{5,7},{6,4},{7,5},{8,10},{9,11},{10,... | collective-permute-start | bytes 835592 | tf_op jit(solution)/shard_map/ppermute | solution.py:690
  39.8 28.8 %all-to-all-start = ((bf16[8,32,2048]{2,1,0:T(8,128)(2,1)}), bf16[8,32,2048]{2,1,0:T(8,128)(2,1)S(1)}, u32[]{:S(2)}, u32[]{:S(2)}) async-start(bf16[8,32,2048]{2,1,0:T(8,128)(2,1)} %bitcast.7), calls=%async_computation | async-start | bytes 2097152 | tf_op jit(solution)/shard_map/all_to_all | solution.py:693
  57.8 7.3 %collective-permute-start.7 = (bf16[288,128]{1,0:T(8,128)(2,1)S(1)}, bf16[288,128]{1,0:T(8,128)(2,1)S(1)}, u32[]{:S(2)}, u32[]{:S(2)}) collective-permute-start(bf16[288,128]{1,0:T(8,128)(2,1)S(1)} %get-tuple-element.31), channel_id=1, source_target_pairs={{0,16},{4,20},{8,24},{12,28},{1,17},{5,21},{9,25},{13,29},{2,18},{... | collective-permute-start | bytes 221192 | tf_op jit(solution)/shard_map/ppermute | solution.py:637
  61.7 5.3 %collective-permute-start.6 = (bf16[288,128]{1,0:T(8,128)(2,1)S(1)}, bf16[288,128]{1,0:T(8,128)(2,1)S(1)}, u32[]{:S(2)}, u32[]{:S(2)}) collective-permute-start(bf16[288,128]{1,0:T(8,128)(2,1)S(1)} %get-tuple-element.31), channel_id=1, source_target_pairs={{0,8},{4,12},{8,16},{12,20},{16,24},{20,28},{1,9},{5,13},{9,17},{1... | collective-permute-start | bytes 221192 | tf_op jit(solution)/shard_map/ppermute | solution.py:637
  67.1 1.5 %collective-permute-start.8 = (bf16[3,288,128]{2,1,0:T(8,128)(2,1)S(1)}, bf16[3,288,128]{2,1,0:T(8,128)(2,1)S(1)}, u32[]{:S(2)}, u32[]{:S(2)}) collective-permute-start(bf16[3,288,128]{2,1,0:T(8,128)(2,1)S(1)} %pad_maximum_fusion.1.mine_ref), channel_id=1, source_target_pairs={{0,4},{4,0},{8,12},{12,8},{16,20},{20,16},{24,28},{28,24},{1,5},{5... | collective-permute-start | bytes 663560 | tf_op jit(solution)/shard_map/ppermute | solution.py:643

commit v13 on v12

--- a/solution.py
+++ b/solution.py
@@ -67,10 +67,10 @@
             jax.ShapeDtypeStruct((HALO, channels), x_branch.dtype),
             jax.ShapeDtypeStruct((tok, 2 * width), key_rows.dtype),
         ],
-        compiler_params=pltpu.CompilerParams(vmem_limit_bytes=VMEM_MOST),
+        compiler_params=pltpu.CompilerParams(vmem_limit_bytes=VMEM_LIMIT),
         cost_estimate=pl.CostEstimate(flops=0, bytes_accessed=16 * tok * width, transcendentals=0),
         name="pack",
-    )(x_branch, key_rows, value_rows)
+    )(in_hbm(x_branch), in_hbm(key_rows), in_hbm(value_rows))
 
 
 def conv_kernel(
@@ -689,8 +689,8 @@
             total, send_place = fence((total, send_place))
         other = lax.ppermute(total, "mp", [(source, source ^ step) for source in range(n_mp)])
     attended = attend(lengths, send_place, query_rows, mine, theirs)
-    total, other, attended = fence((total, other, attended))
     regrouped = lax.all_to_all(attended, "seq", split_axis=0, concat_axis=0, tiled=True)
+    total, other, _ = fence((total, other, attended))
 
     y, sums, state = local_scan(lengths, total, other, dt_weight, dt_bias, decay_rate, inner_act)
     states = with_partner(even_back(state, reach))

time: 78.6 us -> 94.6 us (1.20)
  waiting for transfers between devices: 14.4 us -> 26.7 us
  starting transfers between devices: 26.8 us -> 31.3 us
    ppermute x2, waiting for transfers between devices: 9.5 us -> 20.4 us  [local(): lax.ppermute(total, 'mp', [(source, source ^ step) for source in range(n_...]
    all_to_all x1, starting transfers between devices: 4.22 us -> 9.14 us  [local(): lax.all_to_all(attended, 'seq', split_axis=0, concat_axis=0, tiled=True)]
    ppermute x5, waiting for transfers between devices: 3.43 us -> 4.81 us  [shifted(): lax.ppermute(value, 'seq', [(source, source + steps) for source in range(...]
  transfers between devices with their start and end apart: 10 -> 10, of which waited for: 5 -> 5; matrix products, arithmetic and copies ran while one was open for 0% -> 0% of each run, Pallas kernels for 32% -> 20%
where the time goes in v13:
time: 94.6 us; the launch traced here: 94.2 us
  Pallas kernels  35.2 us (37%)
  starting transfers between devices  31.3 us (33%)
  waiting for transfers between devices  26.7 us (28%)
    ppermute x2, waiting for transfers between devices, local(): lax.ppermute(total, 'mp', [(source, source ^ step) for source in range(n_...  20.4 us
    ppermute x5, starting transfers between devices, shifted(): lax.ppermute(value, 'seq', [(source, source + steps) for source in range(...  17.2 us
    pallas_call x1, Pallas kernels, local_scan(): pl.pallas_call(local_kernel, grid=(tok // BLOCK,), in_specs=[pl.BlockSpec...  13.8 us
    pallas_call x1, Pallas kernels, join_states(): pl.pallas_call(functools.partial(join_kernel, reach), grid=(tok // BLOCK,...  9.56 us
    all_to_all x1, starting transfers between devices, local(): lax.all_to_all(attended, 'seq', split_axis=0, concat_axis=0, tiled=True)  9.14 us
    pallas_call x1, Pallas kernels, attend(): pl.pallas_call(attend_kernel, grid=(kv_local,), in_specs=[pl.BlockSpec(me...  5.49 us
    pallas_call x1, Pallas kernels, conv_project(): pl.pallas_call(conv_kernel, grid=(channels // chunk,), in_specs=[pl.Block...  5.39 us
    ppermute x5, waiting for transfers between devices, shifted(): lax.ppermute(value, 'seq', [(source, source + steps) for source in range(...  4.81 us
  transfers between devices with their start and end apart: 10, of which 5 were waited for; matrix products, arithmetic and copies ran while one was open for 0% of the time, Pallas kernels for 20%

profile of v13, /device:TPU:0, one launch (start us, length us, event | category | flops | bytes accessed | tf_op | source)
XLA Modules:
  0.0 94.2 jit_solution(11408164761776870153)
XLA Ops:
  0.6 1.0 %pack.1 = (bf16[16,2048]{1,0:T(8,128)(2,1)S(1)}, bf16[256,512]{1,0:T(8,128)(2,1)S(1)}) custom-call(bf16[256,2048]{1,0:T(8,128)(2,1)} %x_ref.3, bf16[256,256]{1,0:T(8,128)(2,1)} %k_ref.1, bf16[256,256]{1,0:T(8,128)(2,1)} %v_ref.1), custom_call_target="tpu_custom_call" | custom-call | bytes 1048576 | tf_op jit(solution)/shard_map/pack/pallas_call | solution.py:57
  1.7 2.4 %collective-permute-start = (bf16[16,2048]{1,0:T(8,128)(2,1)S(1)}, bf16[16,2048]{1,0:T(8,128)(2,1)S(1)}, u32[]{:S(2)}, u32[]{:S(2)}) collective-permute-start(bf16[16,2048]{1,0:T(8,128)(2,1)S(1)} %get-tuple-element.16), channel_id=1, source_target_pairs={{0,4},{4,8},{8,12},{12,16},{16,20},{20,24},{24,28},{1,5},{5,9},{9,... | collective-permute-start | bytes 196616 | tf_op jit(solution)/shard_map/ppermute | solution.py:637
  4.0 4.4 %collective-permute-start.4 = (bf16[256,512]{1,0:T(8,128)(2,1)S(1)}, bf16[256,512]{1,0:T(8,128)(2,1)S(1)}, u32[]{:S(2)}, u32[]{:S(2)}) collective-permute-start(bf16[256,512]{1,0:T(8,128)(2,1)S(1)} %get-tuple-element.21), channel_id=1, source_target_pairs={{0,16},{4,20},{8,24},{12,28},{1,17},{5,21},{9,25},{13,29},{2,18},{... | collective-permute-start | bytes 786440 | tf_op jit(solution)/shard_map/ppermute | solution.py:637
  8.5 3.4 %collective-permute-start.3 = (bf16[256,512]{1,0:T(8,128)(2,1)S(1)}, bf16[256,512]{1,0:T(8,128)(2,1)S(1)}, u32[]{:S(2)}, u32[]{:S(2)}) collective-permute-start(bf16[256,512]{1,0:T(8,128)(2,1)S(1)} %get-tuple-element.21), channel_id=1, source_target_pairs={{0,8},{4,12},{8,16},{12,20},{16,24},{20,28},{1,9},{5,13},{9,17},{1... | collective-permute-start | bytes 786440 | tf_op jit(solution)/shard_map/ppermute | solution.py:637
  11.9 0.0 collective-permute-done.halo_ref
  11.9 0.0 copy-start.2
  11.9 5.4 %conv_project.1 = (bf16[256,2048]{1,0:T(8,128)(2,1)S(1)}, bf16[544,256]{1,0:T(8,128)(2,1)S(1)}) custom-call(s32[4]{0:T(128)} %lengths_ref.5, bf16[256,2048]{1,0:T(8,128)(2,1)} %x_ref.3, bf16[16,2048]{1,0:T(8,128)(2,1)S(1)} %collective-permute-done.halo_ref, f32[4,2048]{1,0:T(4,128)} %w_hbm.1, f32[1,2048]{1,0:T(1,128)} %bitcast.20, bf16[544,2048]{1,0:T(8,128)(2,1)} %bitcast.19), custom_call_target="tpu_custom_call" | custom-call | flops 22817013760 | bytes 4194304 | tf_op jit(solution)/shard_map/conv_project/pallas_call | solution.py:134
  17.3 0.0 copy-start.1
  17.3 0.0 copy-start
  17.3 2.8 %collective-permute-done.4 = bf16[256,512]{1,0:T(8,128)(2,1)S(1)} collective-permute-done((bf16[256,512]{1,0:T(8,128)(2,1)S(1)}, bf16[256,512]{1,0:T(8,128)(2,1)S(1)}, u32[]{:S(2)}, u32[]{:S(2)}) %collective-permute-start.4) | collective-permute-done | bytes 262176 | tf_op jit(solution)/shard_map/ppermute | solution.py:637
  20.2 0.0 collective-permute-done.3
  20.2 0.1 pad_maximum_fusion.keys_mine.values_mine
  20.3 0.8 collective-permute-start.5
  21.0 1.6 %collective-permute-start.1 = (bf16[544,256]{1,0:T(8,128)(2,1)S(1)}, bf16[544,256]{1,0:T(8,128)(2,1)S(1)}, u32[]{:S(2)}, u32[]{:S(2)}) collective-permute-start(bf16[544,256]{1,0:T(8,128)(2,1)S(1)} %get-tuple-element.17), channel_id=1, source_target_pairs={{0,1},{1,0},{2,3},{3,2},{4,5},{5,4},{6,7},{7,6},{8,9},{9,8},{10,11... | collective-permute-start | bytes 835592 | tf_op jit(solution)/shard_map/ppermute | solution.py:690
  22.6 0.0 copy-done.1
  22.6 0.0 copy-done.2
  22.7 7.0 %collective-permute-done.1 = bf16[544,256]{1,0:T(8,128)(2,1)S(1)} collective-permute-done((bf16[544,256]{1,0:T(8,128)(2,1)S(1)}, bf16[544,256]{1,0:T(8,128)(2,1)S(1)}, u32[]{:S(2)}, u32[]{:S(2)}) %collective-permute-start.1) | collective-permute-done | bytes 278560 | tf_op jit(solution)/shard_map/ppermute | solution.py:690
  29.7 0.1 add_convert_fusion.proj_ref
  29.8 0.0 collective-permute-done.5.keys_theirs.values_theirs
  29.8 5.5 %attend.1 = bf16[256,2048]{1,0:T(8,128)(2,1)} custom-call(s32[4]{0:T(128)} %lengths_ref.5, s32[8,256]{1,0:T(8,128)S(1)} %reshape.19.place_ref, bf16[256,2048]{1,0:T(8,128)(2,1)S(1)} %copy-done, bf16[3,256,512]{2,1,0:T(8,128)(2,1)S(1)} %pad_maximum_fusion.keys_mine.values_mine, bf16[3,256,512]{2,1,0:T(8,128)(2,1)S(1)} %collective-permute-done.5.keys_theirs.values_theirs, ...), custom_call_target="tpu_custom_call" | custom-call | flops 524288 | bytes 524288 | tf_op jit(solution)/shard_map/attend/pallas_call | solution.py:609
  35.3 9.1 %all-to-all-start = ((bf16[8,32,2048]{2,1,0:T(8,128)(2,1)}), bf16[8,32,2048]{2,1,0:T(8,128)(2,1)S(1)}, u32[]{:S(2)}, u32[]{:S(2)}) async-start(bf16[8,32,2048]{2,1,0:T(8,128)(2,1)} %bitcast.7), calls=%async_computation | async-start | bytes 2097152 | tf_op jit(solution)/shard_map/all_to_all | solution.py:692
  44.4 2.6 %collective-permute-start.2 = (bf16[544,256]{1,0:T(8,128)(2,1)S(1)}, bf16[544,256]{1,0:T(8,128)(2,1)S(1)}, u32[]{:S(2)}, u32[]{:S(2)}) collective-permute-start(bf16[544,256]{1,0:T(8,128)(2,1)S(1)} %add_convert_fusion.proj_ref), channel_id=1, source_target_pairs={{0,2},{1,3},{2,0},{3,1},{4,6},{5,7},{6,4},{7,5},{8,10},{9,11},{10,... | collective-permute-start | bytes 835592 | tf_op jit(solution)/shard_map/ppermute | solution.py:690
  47.0 13.4 %collective-permute-done.2.other_ref = bf16[544,256]{1,0:T(8,128)(2,1)S(1)} collective-permute-done((bf16[544,256]{1,0:T(8,128)(2,1)S(1)}, bf16[544,256]{1,0:T(8,128)(2,1)S(1)}, u32[]{:S(2)}, u32[]{:S(2)}) %collective-permute-start.2) | collective-permute-done | bytes 278560 | tf_op jit(solution)/shard_map/ppermute | solution.py:690
  60.4 13.8 %local_scan.1 = (f32[256,16,128]{2,1,0:T(8,128)}, f32[256,16,128]{2,1,0:T(8,128)}, bf16[288,128]{1,0:T(8,128)(2,1)S(1)}) custom-call(s32[4]{0:T(128)} %lengths_ref.5, bf16[544,256]{1,0:T(8,128)(2,1)S(1)} %add_convert_fusion.proj_ref, bf16[544,256]{1,0:T(8,128)(2,1)S(1)} %collective-permute-done.2.other_ref, bf16[512,2048]{1,0:T(8,128)(2,1)} %dtw_ref.1, ...), custom_call_target="tpu_custom_call" | custom-call | flops 100663296 | bytes 6291456 | tf_op jit(solution)/shard_map/local_scan/pallas_call | solution.py:318
  74.1 3.6 %collective-permute-start.7 = (bf16[288,128]{1,0:T(8,128)(2,1)S(1)}, bf16[288,128]{1,0:T(8,128)(2,1)S(1)}, u32[]{:S(2)}, u32[]{:S(2)}) collective-permute-start(bf16[288,128]{1,0:T(8,128)(2,1)S(1)} %get-tuple-element.29), channel_id=1, source_target_pairs={{0,16},{4,20},{8,24},{12,28},{1,17},{5,21},{9,25},{13,29},{2,18},{... | collective-permute-start | bytes 221192 | tf_op jit(solution)/shard_map/ppermute | solution.py:637
  77.7 3.4 %collective-permute-start.6 = (bf16[288,128]{1,0:T(8,128)(2,1)S(1)}, bf16[288,128]{1,0:T(8,128)(2,1)S(1)}, u32[]{:S(2)}, u32[]{:S(2)}) collective-permute-start(bf16[288,128]{1,0:T(8,128)(2,1)S(1)} %get-tuple-element.29), channel_id=1, source_target_pairs={{0,8},{4,12},{8,16},{12,20},{16,24},{20,28},{1,9},{5,13},{9,17},{1... | collective-permute-start | bytes 221192 | tf_op jit(solution)/shard_map/ppermute | solution.py:637
  81.1 0.0 collective-permute-done.7
  81.1 2.0 %collective-permute-done.6 = bf16[288,128]{1,0:T(8,128)(2,1)S(1)} collective-permute-done((bf16[288,128]{1,0:T(8,128)(2,1)S(1)}, bf16[288,128]{1,0:T(8,128)(2,1)S(1)}, u32[]{:S(2)}, u32[]{:S(2)}) %collective-permute-start.6) | collective-permute-done | bytes 73760 | tf_op jit(solution)/shard_map/ppermute | solution.py:637
  83.1 0.1 collective-permute-start.8
  83.2 1.5 %collective-permute-done.8.theirs_ref = bf16[3,288,128]{2,1,0:T(8,128)(2,1)S(1)} collective-permute-done((bf16[3,288,128]{2,1,0:T(8,128)(2,1)S(1)}, bf16[3,288,128]{2,1,0:T(8,128)(2,1)S(1)}, u32[]{:S(2)}, u32[]{:S(2)}) %collective-permute-start.8) | collective-permute-done | bytes 221216 | tf_op jit(solution)/shard_map/ppermute | solution.py:643
  84.6 0.0 all-to-all-done
  84.6 9.6 %join_states.1 = (bf16[256,2048]{1,0:T(8,128)(2,1)}, bf16[256,2048]{1,0:T(8,128)(2,1)}) custom-call(bf16[544,256]{1,0:T(8,128)(2,1)S(1)} %add_convert_fusion.proj_ref, bf16[544,256]{1,0:T(8,128)(2,1)S(1)} %collective-permute-done.2.other_ref, f32[256,16,128]{2,1,0:T(8,128)} %get-tuple-element.27.y_ref, f32[256,16,128]{2,1,0:T(8,128)} %get-tuple-element.28.sum_ref, ...), custom_call_target="tpu_custom_call" | custom-call | flops 67108864 | bytes 7340032 | tf_op jit(solution)/shard_map/join_states/pallas_call | solution.py:439
  (4 shorter events, 0.0 us)
Async XLA Ops:
  1.7 10.2 %collective-permute-start = (bf16[16,2048]{1,0:T(8,128)(2,1)S(1)}, bf16[16,2048]{1,0:T(8,128)(2,1)S(1)}, u32[]{:S(2)}, u32[]{:S(2)}) collective-permute-start(bf16[16,2048]{1,0:T(8,128)(2,1)S(1)} %get-tuple-element.16), channel_id=1, source_target_pairs={{0,4},{4,8},{8,12},{12,16},{16,20},{20,24},{24,28},{1,5},{5,9},{9,... | collective-permute-start | bytes 196616 | tf_op jit(solution)/shard_map/ppermute | solution.py:637
  4.0 16.2 %collective-permute-start.4 = (bf16[256,512]{1,0:T(8,128)(2,1)S(1)}, bf16[256,512]{1,0:T(8,128)(2,1)S(1)}, u32[]{:S(2)}, u32[]{:S(2)}) collective-permute-start(bf16[256,512]{1,0:T(8,128)(2,1)S(1)} %get-tuple-element.21), channel_id=1, source_target_pairs={{0,16},{4,20},{8,24},{12,28},{1,17},{5,21},{9,25},{13,29},{2,18},{... | collective-permute-start | bytes 786440 | tf_op jit(solution)/shard_map/ppermute | solution.py:637
  8.5 11.7 %collective-permute-start.3 = (bf16[256,512]{1,0:T(8,128)(2,1)S(1)}, bf16[256,512]{1,0:T(8,128)(2,1)S(1)}, u32[]{:S(2)}, u32[]{:S(2)}) collective-permute-start(bf16[256,512]{1,0:T(8,128)(2,1)S(1)} %get-tuple-element.21), channel_id=1, source_target_pairs={{0,8},{4,12},{8,16},{12,20},{16,24},{20,28},{1,9},{5,13},{9,17},{1... | collective-permute-start | bytes 786440 | tf_op jit(solution)/shard_map/ppermute | solution.py:637
  11.9 10.7 %copy-start.2 = (s32[2048]{0:T(1024)S(1)}, s32[2048]{0:T(1024)}, u32[]{:S(2)}) copy-start(s32[2048]{0:T(1024)} %param.27) | copy-start | bytes 24580
  17.3 5.3 %copy-start.1 = (bf16[256,2048]{1,0:T(8,128)(2,1)}, bf16[256,2048]{1,0:T(8,128)(2,1)S(1)}, u32[]{:S(2)}) copy-start(bf16[256,2048]{1,0:T(8,128)(2,1)S(1)} %get-tuple-element.26.inner_ref) | copy-start | bytes 3145732
  17.3 12.4 %copy-start = (bf16[256,2048]{1,0:T(8,128)(2,1)S(1)}, bf16[256,2048]{1,0:T(8,128)(2,1)}, u32[]{:S(2)}) copy-start(bf16[256,2048]{1,0:T(8,128)(2,1)} %q_ref.1) | copy-start | bytes 3145732
  20.3 9.5 %collective-permute-start.5 = (bf16[3,256,512]{2,1,0:T(8,128)(2,1)S(1)}, bf16[3,256,512]{2,1,0:T(8,128)(2,1)S(1)}, u32[]{:S(2)}, u32[]{:S(2)}) collective-permute-start(bf16[3,256,512]{2,1,0:T(8,128)(2,1)S(1)} %pad_maximum_fusion.keys_mine.values_mine), channel_id=1, source_target_pairs={{0,4},{4,0},{8,12},{12,8},{16,20},{20,16},{24,28},{28,24},{1,5},{5... | collective-permute-start | bytes 2359304 | tf_op jit(solution)/shard_map/ppermute | solution.py:643
  21.0 8.6 %collective-permute-start.1 = (bf16[544,256]{1,0:T(8,128)(2,1)S(1)}, bf16[544,256]{1,0:T(8,128)(2,1)S(1)}, u32[]{:S(2)}, u32[]{:S(2)}) collective-permute-start(bf16[544,256]{1,0:T(8,128)(2,1)S(1)} %get-tuple-element.17), channel_id=1, source_target_pairs={{0,1},{1,0},{2,3},{3,2},{4,5},{5,4},{6,7},{7,6},{8,9},{9,8},{10,11... | collective-permute-start | bytes 835592 | tf_op jit(solution)/shard_map/ppermute | solution.py:690
  35.3 49.3 %all-to-all-start = ((bf16[8,32,2048]{2,1,0:T(8,128)(2,1)}), bf16[8,32,2048]{2,1,0:T(8,128)(2,1)S(1)}, u32[]{:S(2)}, u32[]{:S(2)}) async-start(bf16[8,32,2048]{2,1,0:T(8,128)(2,1)} %bitcast.7), calls=%async_computation | async-start | bytes 2097152 | tf_op jit(solution)/shard_map/all_to_all | solution.py:692
  44.4 15.9 %collective-permute-start.2 = (bf16[544,256]{1,0:T(8,128)(2,1)S(1)}, bf16[544,256]{1,0:T(8,128)(2,1)S(1)}, u32[]{:S(2)}, u32[]{:S(2)}) collective-permute-start(bf16[544,256]{1,0:T(8,128)(2,1)S(1)} %add_convert_fusion.proj_ref), channel_id=1, source_target_pairs={{0,2},{1,3},{2,0},{3,1},{4,6},{5,7},{6,4},{7,5},{8,10},{9,11},{10,... | collective-permute-start | bytes 835592 | tf_op jit(solution)/shard_map/ppermute | solution.py:690
  74.1 7.0 %collective-permute-start.7 = (bf16[288,128]{1,0:T(8,128)(2,1)S(1)}, bf16[288,128]{1,0:T(8,128)(2,1)S(1)}, u32[]{:S(2)}, u32[]{:S(2)}) collective-permute-start(bf16[288,128]{1,0:T(8,128)(2,1)S(1)} %get-tuple-element.29), channel_id=1, source_target_pairs={{0,16},{4,20},{8,24},{12,28},{1,17},{5,21},{9,25},{13,29},{2,18},{... | collective-permute-start | bytes 221192 | tf_op jit(solution)/shard_map/ppermute | solution.py:637
  77.7 5.3 %collective-permute-start.6 = (bf16[288,128]{1,0:T(8,128)(2,1)S(1)}, bf16[288,128]{1,0:T(8,128)(2,1)S(1)}, u32[]{:S(2)}, u32[]{:S(2)}) collective-permute-start(bf16[288,128]{1,0:T(8,128)(2,1)S(1)} %get-tuple-element.29), channel_id=1, source_target_pairs={{0,8},{4,12},{8,16},{12,20},{16,24},{20,28},{1,9},{5,13},{9,17},{1... | collective-permute-start | bytes 221192 | tf_op jit(solution)/shard_map/ppermute | solution.py:637
  83.1 1.5 %collective-permute-start.8 = (bf16[3,288,128]{2,1,0:T(8,128)(2,1)S(1)}, bf16[3,288,128]{2,1,0:T(8,128)(2,1)S(1)}, u32[]{:S(2)}, u32[]{:S(2)}) collective-permute-start(bf16[3,288,128]{2,1,0:T(8,128)(2,1)S(1)} %pad_maximum_fusion.1.mine_ref), channel_id=1, source_target_pairs={{0,4},{4,0},{8,12},{12,8},{16,20},{20,16},{24,28},{28,24},{1,5},{5... | collective-permute-start | bytes 663560 | tf_op jit(solution)/shard_map/ppermute | solution.py:643

commit v14 on v13

--- a/solution.py
+++ b/solution.py
@@ -689,8 +689,8 @@
             total, send_place = fence((total, send_place))
         other = lax.ppermute(total, "mp", [(source, source ^ step) for source in range(n_mp)])
     attended = attend(lengths, send_place, query_rows, mine, theirs)
+    total, other, attended = fence((total, other, attended))
     regrouped = lax.all_to_all(attended, "seq", split_axis=0, concat_axis=0, tiled=True)
-    total, other, _ = fence((total, other, attended))
 
     y, sums, state = local_scan(lengths, total, other, dt_weight, dt_bias, decay_rate, inner_act)
     states = with_partner(even_back(state, reach))

time: 94.6 us -> 77.8 us (0.82)
  waiting for transfers between devices: 26.7 us -> 14.4 us
  starting transfers between devices: 31.3 us -> 26.9 us
    ppermute x2, waiting for transfers between devices: 20.4 us -> 9.76 us  [local(): lax.ppermute(total, 'mp', [(source, source ^ step) for source in range(n_...]
    all_to_all x1, starting transfers between devices: 9.14 us -> 4.23 us  [local(): lax.all_to_all(attended, 'seq', split_axis=0, concat_axis=0, tiled=True)]
    ppermute x5, waiting for transfers between devices: 4.81 us -> 3.16 us  [shifted(): lax.ppermute(value, 'seq', [(source, source + steps) for source in range(...]
  transfers between devices with their start and end apart: 10 -> 10, of which waited for: 5 -> 5; matrix products, arithmetic and copies ran while one was open for 0% -> 0% of each run, Pallas kernels for 20% -> 32%
where the time goes in v14:
time: 77.8 us; the launch traced here: 77.5 us
  Pallas kernels  35.2 us (45%)
  starting transfers between devices  26.9 us (35%)
  waiting for transfers between devices  14.4 us (19%)
    ppermute x5, starting transfers between devices, shifted(): lax.ppermute(value, 'seq', [(source, source + steps) for source in range(...  17.5 us
    pallas_call x1, Pallas kernels, local_scan(): pl.pallas_call(local_kernel, grid=(tok // BLOCK,), in_specs=[pl.BlockSpec...  13.8 us
    ppermute x2, waiting for transfers between devices, local(): lax.ppermute(total, 'mp', [(source, source ^ step) for source in range(n_...  9.76 us
    pallas_call x1, Pallas kernels, join_states(): pl.pallas_call(functools.partial(join_kernel, reach), grid=(tok // BLOCK,...  9.56 us
    pallas_call x1, Pallas kernels, attend(): pl.pallas_call(attend_kernel, grid=(kv_local,), in_specs=[pl.BlockSpec(me...  5.47 us
    pallas_call x1, Pallas kernels, conv_project(): pl.pallas_call(conv_kernel, grid=(channels // chunk,), in_specs=[pl.Block...  5.39 us
    ppermute x2, starting transfers between devices, local(): lax.ppermute(total, 'mp', [(source, source ^ step) for source in range(n_...  4.3 us
    all_to_all x1, starting transfers between devices, local(): lax.all_to_all(attended, 'seq', split_axis=0, concat_axis=0, tiled=True)  4.23 us
  transfers between devices with their start and end apart: 10, of which 5 were waited for; matrix products, arithmetic and copies ran while one was open for 0% of the time, Pallas kernels for 32%

profile of v14, /device:TPU:0, one launch (start us, length us, event | category | flops | bytes accessed | tf_op | source)
XLA Modules:
  0.0 77.5 jit_solution(5560716398431828696)
XLA Ops:
  0.6 1.0 %pack.1 = (bf16[16,2048]{1,0:T(8,128)(2,1)S(1)}, bf16[256,512]{1,0:T(8,128)(2,1)S(1)}) custom-call(bf16[256,2048]{1,0:T(8,128)(2,1)} %x_ref.3, bf16[256,256]{1,0:T(8,128)(2,1)} %k_ref.1, bf16[256,256]{1,0:T(8,128)(2,1)} %v_ref.1), custom_call_target="tpu_custom_call" | custom-call | bytes 1048576 | tf_op jit(solution)/shard_map/pack/pallas_call | solution.py:57
  1.7 2.4 %collective-permute-start = (bf16[16,2048]{1,0:T(8,128)(2,1)S(1)}, bf16[16,2048]{1,0:T(8,128)(2,1)S(1)}, u32[]{:S(2)}, u32[]{:S(2)}) collective-permute-start(bf16[16,2048]{1,0:T(8,128)(2,1)S(1)} %get-tuple-element.17), channel_id=1, source_target_pairs={{0,4},{4,8},{8,12},{12,16},{16,20},{20,24},{24,28},{1,5},{5,9},{9,... | collective-permute-start | bytes 196616 | tf_op jit(solution)/shard_map/ppermute | solution.py:637
  4.0 4.4 %collective-permute-start.4 = (bf16[256,512]{1,0:T(8,128)(2,1)S(1)}, bf16[256,512]{1,0:T(8,128)(2,1)S(1)}, u32[]{:S(2)}, u32[]{:S(2)}) collective-permute-start(bf16[256,512]{1,0:T(8,128)(2,1)S(1)} %get-tuple-element.22), channel_id=1, source_target_pairs={{0,16},{4,20},{8,24},{12,28},{1,17},{5,21},{9,25},{13,29},{2,18},{... | collective-permute-start | bytes 786440 | tf_op jit(solution)/shard_map/ppermute | solution.py:637
  8.5 3.4 %collective-permute-start.3 = (bf16[256,512]{1,0:T(8,128)(2,1)S(1)}, bf16[256,512]{1,0:T(8,128)(2,1)S(1)}, u32[]{:S(2)}, u32[]{:S(2)}) collective-permute-start(bf16[256,512]{1,0:T(8,128)(2,1)S(1)} %get-tuple-element.22), channel_id=1, source_target_pairs={{0,8},{4,12},{8,16},{12,20},{16,24},{20,28},{1,9},{5,13},{9,17},{1... | collective-permute-start | bytes 786440 | tf_op jit(solution)/shard_map/ppermute | solution.py:637
  11.9 0.0 collective-permute-done.halo_ref
  11.9 0.0 copy-start.2
  11.9 5.4 %conv_project.1 = (bf16[256,2048]{1,0:T(8,128)(2,1)S(1)}, bf16[544,256]{1,0:T(8,128)(2,1)S(1)}) custom-call(s32[4]{0:T(128)} %lengths_ref.5, bf16[256,2048]{1,0:T(8,128)(2,1)} %x_ref.3, bf16[16,2048]{1,0:T(8,128)(2,1)S(1)} %collective-permute-done.halo_ref, f32[4,2048]{1,0:T(4,128)} %w_hbm.1, f32[1,2048]{1,0:T(1,128)} %bitcast.20, bf16[544,2048]{1,0:T(8,128)(2,1)} %bitcast.19), custom_call_target="tpu_custom_call" | custom-call | flops 22817013760 | bytes 4194304 | tf_op jit(solution)/shard_map/conv_project/pallas_call | solution.py:134
  17.3 0.0 copy-start.1
  17.3 0.0 copy-start
  17.3 1.6 %collective-permute-start.1 = (bf16[544,256]{1,0:T(8,128)(2,1)S(1)}, bf16[544,256]{1,0:T(8,128)(2,1)S(1)}, u32[]{:S(2)}, u32[]{:S(2)}) collective-permute-start(bf16[544,256]{1,0:T(8,128)(2,1)S(1)} %get-tuple-element.18), channel_id=1, source_target_pairs={{0,1},{1,0},{2,3},{3,2},{4,5},{5,4},{6,7},{7,6},{8,9},{9,8},{10,11... | collective-permute-start | bytes 835592 | tf_op jit(solution)/shard_map/ppermute | solution.py:690
  19.0 1.2 %collective-permute-done.4 = bf16[256,512]{1,0:T(8,128)(2,1)S(1)} collective-permute-done((bf16[256,512]{1,0:T(8,128)(2,1)S(1)}, bf16[256,512]{1,0:T(8,128)(2,1)S(1)}, u32[]{:S(2)}, u32[]{:S(2)}) %collective-permute-start.4) | collective-permute-done | bytes 262176 | tf_op jit(solution)/shard_map/ppermute | solution.py:637
  20.2 0.0 collective-permute-done.3
  20.2 0.1 pad_maximum_fusion.keys_mine.values_mine
  20.3 0.8 collective-permute-start.5
  21.0 0.0 copy-done.1
  21.1 4.1 %collective-permute-done.1 = bf16[544,256]{1,0:T(8,128)(2,1)S(1)} collective-permute-done((bf16[544,256]{1,0:T(8,128)(2,1)S(1)}, bf16[544,256]{1,0:T(8,128)(2,1)S(1)}, u32[]{:S(2)}, u32[]{:S(2)}) %collective-permute-start.1) | collective-permute-done | bytes 278560 | tf_op jit(solution)/shard_map/ppermute | solution.py:690
  25.2 0.1 add_convert_fusion.proj_ref
  25.3 2.7 %collective-permute-start.2 = (bf16[544,256]{1,0:T(8,128)(2,1)S(1)}, bf16[544,256]{1,0:T(8,128)(2,1)S(1)}, u32[]{:S(2)}, u32[]{:S(2)}) collective-permute-start(bf16[544,256]{1,0:T(8,128)(2,1)S(1)} %add_convert_fusion.proj_ref), channel_id=1, source_target_pairs={{0,2},{1,3},{2,0},{3,1},{4,6},{5,7},{6,4},{7,5},{8,10},{9,11},{10,... | collective-permute-start | bytes 835592 | tf_op jit(solution)/shard_map/ppermute | solution.py:690
  27.9 0.0 collective-permute-done.5.keys_theirs.values_theirs
  27.9 0.0 copy-done
  27.9 5.5 %attend.1 = bf16[256,2048]{1,0:T(8,128)(2,1)} custom-call(s32[4]{0:T(128)} %lengths_ref.5, s32[8,256]{1,0:T(8,128)S(1)} %reshape.19.place_ref, bf16[256,2048]{1,0:T(8,128)(2,1)S(1)} %copy-done, bf16[3,256,512]{2,1,0:T(8,128)(2,1)S(1)} %pad_maximum_fusion.keys_mine.values_mine, bf16[3,256,512]{2,1,0:T(8,128)(2,1)S(1)} %collective-permute-done.5.keys_theirs.values_theirs, ...), custom_call_target="tpu_custom_call" | custom-call | flops 524288 | bytes 524288 | tf_op jit(solution)/shard_map/attend/pallas_call | solution.py:609
  33.4 5.7 %collective-permute-done.2.other_ref = bf16[544,256]{1,0:T(8,128)(2,1)S(1)} collective-permute-done((bf16[544,256]{1,0:T(8,128)(2,1)S(1)}, bf16[544,256]{1,0:T(8,128)(2,1)S(1)}, u32[]{:S(2)}, u32[]{:S(2)}) %collective-permute-start.2) | collective-permute-done | bytes 278560 | tf_op jit(solution)/shard_map/ppermute | solution.py:690
  39.0 4.2 %all-to-all-start = ((bf16[8,32,2048]{2,1,0:T(8,128)(2,1)}), bf16[8,32,2048]{2,1,0:T(8,128)(2,1)S(1)}, u32[]{:S(2)}, u32[]{:S(2)}) async-start(bf16[8,32,2048]{2,1,0:T(8,128)(2,1)} %bitcast.7), calls=%async_computation | async-start | bytes 2097152 | tf_op jit(solution)/shard_map/all_to_all | solution.py:693
  43.3 13.8 %local_scan.1 = (f32[256,16,128]{2,1,0:T(8,128)}, f32[256,16,128]{2,1,0:T(8,128)}, bf16[288,128]{1,0:T(8,128)(2,1)S(1)}) custom-call(s32[4]{0:T(128)} %lengths_ref.5, bf16[544,256]{1,0:T(8,128)(2,1)S(1)} %add_convert_fusion.proj_ref, bf16[544,256]{1,0:T(8,128)(2,1)S(1)} %collective-permute-done.2.other_ref, bf16[512,2048]{1,0:T(8,128)(2,1)} %dtw_ref.1, ...), custom_call_target="tpu_custom_call" | custom-call | flops 100663296 | bytes 6291456 | tf_op jit(solution)/shard_map/local_scan/pallas_call | solution.py:318
  57.0 3.9 %collective-permute-start.7 = (bf16[288,128]{1,0:T(8,128)(2,1)S(1)}, bf16[288,128]{1,0:T(8,128)(2,1)S(1)}, u32[]{:S(2)}, u32[]{:S(2)}) collective-permute-start(bf16[288,128]{1,0:T(8,128)(2,1)S(1)} %get-tuple-element.31), channel_id=1, source_target_pairs={{0,16},{4,20},{8,24},{12,28},{1,17},{5,21},{9,25},{13,29},{2,18},{... | collective-permute-start | bytes 221192 | tf_op jit(solution)/shard_map/ppermute | solution.py:637
  61.0 3.4 %collective-permute-start.6 = (bf16[288,128]{1,0:T(8,128)(2,1)S(1)}, bf16[288,128]{1,0:T(8,128)(2,1)S(1)}, u32[]{:S(2)}, u32[]{:S(2)}) collective-permute-start(bf16[288,128]{1,0:T(8,128)(2,1)S(1)} %get-tuple-element.31), channel_id=1, source_target_pairs={{0,8},{4,12},{8,16},{12,20},{16,24},{20,28},{1,9},{5,13},{9,17},{1... | collective-permute-start | bytes 221192 | tf_op jit(solution)/shard_map/ppermute | solution.py:637
  64.4 0.0 collective-permute-done.7
  64.4 2.0 %collective-permute-done.6 = bf16[288,128]{1,0:T(8,128)(2,1)S(1)} collective-permute-done((bf16[288,128]{1,0:T(8,128)(2,1)S(1)}, bf16[288,128]{1,0:T(8,128)(2,1)S(1)}, u32[]{:S(2)}, u32[]{:S(2)}) %collective-permute-start.6) | collective-permute-done | bytes 73760 | tf_op jit(solution)/shard_map/ppermute | solution.py:637
  66.4 0.1 collective-permute-start.8
  66.4 1.5 %collective-permute-done.8.theirs_ref = bf16[3,288,128]{2,1,0:T(8,128)(2,1)S(1)} collective-permute-done((bf16[3,288,128]{2,1,0:T(8,128)(2,1)S(1)}, bf16[3,288,128]{2,1,0:T(8,128)(2,1)S(1)}, u32[]{:S(2)}, u32[]{:S(2)}) %collective-permute-start.8) | collective-permute-done | bytes 221216 | tf_op jit(solution)/shard_map/ppermute | solution.py:643
  67.9 0.0 all-to-all-done
  67.9 9.6 %join_states.1 = (bf16[256,2048]{1,0:T(8,128)(2,1)}, bf16[256,2048]{1,0:T(8,128)(2,1)}) custom-call(bf16[544,256]{1,0:T(8,128)(2,1)S(1)} %add_convert_fusion.proj_ref, bf16[544,256]{1,0:T(8,128)(2,1)S(1)} %collective-permute-done.2.other_ref, f32[256,16,128]{2,1,0:T(8,128)} %get-tuple-element.28.y_ref, f32[256,16,128]{2,1,0:T(8,128)} %get-tuple-element.29.sum_ref, ...), custom_call_target="tpu_custom_call" | custom-call | flops 67108864 | bytes 7340032 | tf_op jit(solution)/shard_map/join_states/pallas_call | solution.py:439
  (4 shorter events, 0.0 us)
Async XLA Ops:
  1.7 10.2 %collective-permute-start = (bf16[16,2048]{1,0:T(8,128)(2,1)S(1)}, bf16[16,2048]{1,0:T(8,128)(2,1)S(1)}, u32[]{:S(2)}, u32[]{:S(2)}) collective-permute-start(bf16[16,2048]{1,0:T(8,128)(2,1)S(1)} %get-tuple-element.17), channel_id=1, source_target_pairs={{0,4},{4,8},{8,12},{12,16},{16,20},{20,24},{24,28},{1,5},{5,9},{9,... | collective-permute-start | bytes 196616 | tf_op jit(solution)/shard_map/ppermute | solution.py:637
  4.0 16.2 %collective-permute-start.4 = (bf16[256,512]{1,0:T(8,128)(2,1)S(1)}, bf16[256,512]{1,0:T(8,128)(2,1)S(1)}, u32[]{:S(2)}, u32[]{:S(2)}) collective-permute-start(bf16[256,512]{1,0:T(8,128)(2,1)S(1)} %get-tuple-element.22), channel_id=1, source_target_pairs={{0,16},{4,20},{8,24},{12,28},{1,17},{5,21},{9,25},{13,29},{2,18},{... | collective-permute-start | bytes 786440 | tf_op jit(solution)/shard_map/ppermute | solution.py:637
  8.5 11.7 %collective-permute-start.3 = (bf16[256,512]{1,0:T(8,128)(2,1)S(1)}, bf16[256,512]{1,0:T(8,128)(2,1)S(1)}, u32[]{:S(2)}, u32[]{:S(2)}) collective-permute-start(bf16[256,512]{1,0:T(8,128)(2,1)S(1)} %get-tuple-element.22), channel_id=1, source_target_pairs={{0,8},{4,12},{8,16},{12,20},{16,24},{20,28},{1,9},{5,13},{9,17},{1... | collective-permute-start | bytes 786440 | tf_op jit(solution)/shard_map/ppermute | solution.py:637
  11.9 9.1 %copy-start.2 = (s32[2048]{0:T(1024)S(1)}, s32[2048]{0:T(1024)}, u32[]{:S(2)}) copy-start(s32[2048]{0:T(1024)} %param.27) | copy-start | bytes 24580
  17.3 3.7 %copy-start.1 = (bf16[256,2048]{1,0:T(8,128)(2,1)}, bf16[256,2048]{1,0:T(8,128)(2,1)S(1)}, u32[]{:S(2)}) copy-start(bf16[256,2048]{1,0:T(8,128)(2,1)S(1)} %get-tuple-element.27.inner_ref) | copy-start | bytes 3145732
  17.3 10.6 %copy-start = (bf16[256,2048]{1,0:T(8,128)(2,1)S(1)}, bf16[256,2048]{1,0:T(8,128)(2,1)}, u32[]{:S(2)}) copy-start(bf16[256,2048]{1,0:T(8,128)(2,1)} %q_ref.1) | copy-start | bytes 3145732
  17.3 7.8 %collective-permute-start.1 = (bf16[544,256]{1,0:T(8,128)(2,1)S(1)}, bf16[544,256]{1,0:T(8,128)(2,1)S(1)}, u32[]{:S(2)}, u32[]{:S(2)}) collective-permute-start(bf16[544,256]{1,0:T(8,128)(2,1)S(1)} %get-tuple-element.18), channel_id=1, source_target_pairs={{0,1},{1,0},{2,3},{3,2},{4,5},{5,4},{6,7},{7,6},{8,9},{9,8},{10,11... | collective-permute-start | bytes 835592 | tf_op jit(solution)/shard_map/ppermute | solution.py:690
  20.3 7.6 %collective-permute-start.5 = (bf16[3,256,512]{2,1,0:T(8,128)(2,1)S(1)}, bf16[3,256,512]{2,1,0:T(8,128)(2,1)S(1)}, u32[]{:S(2)}, u32[]{:S(2)}) collective-permute-start(bf16[3,256,512]{2,1,0:T(8,128)(2,1)S(1)} %pad_maximum_fusion.keys_mine.values_mine), channel_id=1, source_target_pairs={{0,4},{4,0},{8,12},{12,8},{16,20},{20,16},{24,28},{28,24},{1,5},{5... | collective-permute-start | bytes 2359304 | tf_op jit(solution)/shard_map/ppermute | solution.py:643
  25.3 13.8 %collective-permute-start.2 = (bf16[544,256]{1,0:T(8,128)(2,1)S(1)}, bf16[544,256]{1,0:T(8,128)(2,1)S(1)}, u32[]{:S(2)}, u32[]{:S(2)}) collective-permute-start(bf16[544,256]{1,0:T(8,128)(2,1)S(1)} %add_convert_fusion.proj_ref), channel_id=1, source_target_pairs={{0,2},{1,3},{2,0},{3,1},{4,6},{5,7},{6,4},{7,5},{8,10},{9,11},{10,... | collective-permute-start | bytes 835592 | tf_op jit(solution)/shard_map/ppermute | solution.py:690
  39.0 28.9 %all-to-all-start = ((bf16[8,32,2048]{2,1,0:T(8,128)(2,1)}), bf16[8,32,2048]{2,1,0:T(8,128)(2,1)S(1)}, u32[]{:S(2)}, u32[]{:S(2)}) async-start(bf16[8,32,2048]{2,1,0:T(8,128)(2,1)} %bitcast.7), calls=%async_computation | async-start | bytes 2097152 | tf_op jit(solution)/shard_map/all_to_all | solution.py:693
  57.0 7.3 %collective-permute-start.7 = (bf16[288,128]{1,0:T(8,128)(2,1)S(1)}, bf16[288,128]{1,0:T(8,128)(2,1)S(1)}, u32[]{:S(2)}, u32[]{:S(2)}) collective-permute-start(bf16[288,128]{1,0:T(8,128)(2,1)S(1)} %get-tuple-element.31), channel_id=1, source_target_pairs={{0,16},{4,20},{8,24},{12,28},{1,17},{5,21},{9,25},{13,29},{2,18},{... | collective-permute-start | bytes 221192 | tf_op jit(solution)/shard_map/ppermute | solution.py:637
  61.0 5.3 %collective-permute-start.6 = (bf16[288,128]{1,0:T(8,128)(2,1)S(1)}, bf16[288,128]{1,0:T(8,128)(2,1)S(1)}, u32[]{:S(2)}, u32[]{:S(2)}) collective-permute-start(bf16[288,128]{1,0:T(8,128)(2,1)S(1)} %get-tuple-element.31), channel_id=1, source_target_pairs={{0,8},{4,12},{8,16},{12,20},{16,24},{20,28},{1,9},{5,13},{9,17},{1... | collective-permute-start | bytes 221192 | tf_op jit(solution)/shard_map/ppermute | solution.py:637
  66.4 1.5 %collective-permute-start.8 = (bf16[3,288,128]{2,1,0:T(8,128)(2,1)S(1)}, bf16[3,288,128]{2,1,0:T(8,128)(2,1)S(1)}, u32[]{:S(2)}, u32[]{:S(2)}) collective-permute-start(bf16[3,288,128]{2,1,0:T(8,128)(2,1)S(1)} %pad_maximum_fusion.1.mine_ref), channel_id=1, source_target_pairs={{0,4},{4,0},{8,12},{12,8},{16,20},{20,16},{24,28},{28,24},{1,5},{5... | collective-permute-start | bytes 663560 | tf_op jit(solution)/shard_map/ppermute | solution.py:643

commit v15 on v14

--- a/solution.py
+++ b/solution.py
@@ -174,7 +174,7 @@
 
 ROWS = 8
 PAIR = 2 * ROWS
-BLOCK = 64
+BLOCK = 128
 
 
 def spread(columns):

time: 77.8 us -> 79 us (1.015)
  Pallas kernels: 35.2 us -> 36.4 us
    pallas_call x1, Pallas kernels: 9.56 us -> 10.4 us  [join_states(): pl.pallas_call(functools.partial(join_kernel, reach), grid=(tok // BLOCK,...]
where the time goes in v15:
time: 79 us; the launch traced here: 78.7 us
  Pallas kernels  36.4 us (46%)
  starting transfers between devices  26.9 us (34%)
  waiting for transfers between devices  14.4 us (18%)
    ppermute x5, starting transfers between devices, shifted(): lax.ppermute(value, 'seq', [(source, source + steps) for source in range(...  17.5 us
    pallas_call x1, Pallas kernels, local_scan(): pl.pallas_call(local_kernel, grid=(tok // BLOCK,), in_specs=[pl.BlockSpec...  14.1 us
    pallas_call x1, Pallas kernels, join_states(): pl.pallas_call(functools.partial(join_kernel, reach), grid=(tok // BLOCK,...  10.4 us
    ppermute x2, waiting for transfers between devices, local(): lax.ppermute(total, 'mp', [(source, source ^ step) for source in range(n_...  9.76 us
    pallas_call x1, Pallas kernels, attend(): pl.pallas_call(attend_kernel, grid=(kv_local,), in_specs=[pl.BlockSpec(me...  5.47 us
    pallas_call x1, Pallas kernels, conv_project(): pl.pallas_call(conv_kernel, grid=(channels // chunk,), in_specs=[pl.Block...  5.39 us
    ppermute x2, starting transfers between devices, local(): lax.ppermute(total, 'mp', [(source, source ^ step) for source in range(n_...  4.3 us
    all_to_all x1, starting transfers between devices, local(): lax.all_to_all(attended, 'seq', split_axis=0, concat_axis=0, tiled=True)  4.23 us
  transfers between devices with their start and end apart: 10, of which 5 were waited for; matrix products, arithmetic and copies ran while one was open for 0% of the time, Pallas kernels for 32%

profile of v15, /device:TPU:0, one launch (start us, length us, event | category | flops | bytes accessed | tf_op | source)
XLA Modules:
  0.0 78.7 jit_solution(5484712685835214096)
XLA Ops:
  0.6 1.0 %pack.1 = (bf16[16,2048]{1,0:T(8,128)(2,1)S(1)}, bf16[256,512]{1,0:T(8,128)(2,1)S(1)}) custom-call(bf16[256,2048]{1,0:T(8,128)(2,1)} %x_ref.3, bf16[256,256]{1,0:T(8,128)(2,1)} %k_ref.1, bf16[256,256]{1,0:T(8,128)(2,1)} %v_ref.1), custom_call_target="tpu_custom_call" | custom-call | bytes 1048576 | tf_op jit(solution)/shard_map/pack/pallas_call | solution.py:57
  1.7 2.4 %collective-permute-start = (bf16[16,2048]{1,0:T(8,128)(2,1)S(1)}, bf16[16,2048]{1,0:T(8,128)(2,1)S(1)}, u32[]{:S(2)}, u32[]{:S(2)}) collective-permute-start(bf16[16,2048]{1,0:T(8,128)(2,1)S(1)} %get-tuple-element.17), channel_id=1, source_target_pairs={{0,4},{4,8},{8,12},{12,16},{16,20},{20,24},{24,28},{1,5},{5,9},{9,... | collective-permute-start | bytes 196616 | tf_op jit(solution)/shard_map/ppermute | solution.py:637
  4.0 4.4 %collective-permute-start.4 = (bf16[256,512]{1,0:T(8,128)(2,1)S(1)}, bf16[256,512]{1,0:T(8,128)(2,1)S(1)}, u32[]{:S(2)}, u32[]{:S(2)}) collective-permute-start(bf16[256,512]{1,0:T(8,128)(2,1)S(1)} %get-tuple-element.22), channel_id=1, source_target_pairs={{0,16},{4,20},{8,24},{12,28},{1,17},{5,21},{9,25},{13,29},{2,18},{... | collective-permute-start | bytes 786440 | tf_op jit(solution)/shard_map/ppermute | solution.py:637
  8.5 3.4 %collective-permute-start.3 = (bf16[256,512]{1,0:T(8,128)(2,1)S(1)}, bf16[256,512]{1,0:T(8,128)(2,1)S(1)}, u32[]{:S(2)}, u32[]{:S(2)}) collective-permute-start(bf16[256,512]{1,0:T(8,128)(2,1)S(1)} %get-tuple-element.22), channel_id=1, source_target_pairs={{0,8},{4,12},{8,16},{12,20},{16,24},{20,28},{1,9},{5,13},{9,17},{1... | collective-permute-start | bytes 786440 | tf_op jit(solution)/shard_map/ppermute | solution.py:637
  11.9 0.0 collective-permute-done.halo_ref
  11.9 0.0 copy-start.2
  11.9 5.4 %conv_project.1 = (bf16[256,2048]{1,0:T(8,128)(2,1)S(1)}, bf16[544,256]{1,0:T(8,128)(2,1)S(1)}) custom-call(s32[4]{0:T(128)} %lengths_ref.5, bf16[256,2048]{1,0:T(8,128)(2,1)} %x_ref.3, bf16[16,2048]{1,0:T(8,128)(2,1)S(1)} %collective-permute-done.halo_ref, f32[4,2048]{1,0:T(4,128)} %w_hbm.1, f32[1,2048]{1,0:T(1,128)} %bitcast.20, bf16[544,2048]{1,0:T(8,128)(2,1)} %bitcast.19), custom_call_target="tpu_custom_call" | custom-call | flops 22817013760 | bytes 4194304 | tf_op jit(solution)/shard_map/conv_project/pallas_call | solution.py:134
  17.3 0.0 copy-start.1
  17.3 0.0 copy-start
  17.3 1.6 %collective-permute-start.1 = (bf16[544,256]{1,0:T(8,128)(2,1)S(1)}, bf16[544,256]{1,0:T(8,128)(2,1)S(1)}, u32[]{:S(2)}, u32[]{:S(2)}) collective-permute-start(bf16[544,256]{1,0:T(8,128)(2,1)S(1)} %get-tuple-element.18), channel_id=1, source_target_pairs={{0,1},{1,0},{2,3},{3,2},{4,5},{5,4},{6,7},{7,6},{8,9},{9,8},{10,11... | collective-permute-start | bytes 835592 | tf_op jit(solution)/shard_map/ppermute | solution.py:690
  19.0 1.2 %collective-permute-done.4 = bf16[256,512]{1,0:T(8,128)(2,1)S(1)} collective-permute-done((bf16[256,512]{1,0:T(8,128)(2,1)S(1)}, bf16[256,512]{1,0:T(8,128)(2,1)S(1)}, u32[]{:S(2)}, u32[]{:S(2)}) %collective-permute-start.4) | collective-permute-done | bytes 262176 | tf_op jit(solution)/shard_map/ppermute | solution.py:637
  20.2 0.0 collective-permute-done.3
  20.2 0.1 pad_maximum_fusion.keys_mine.values_mine
  20.3 0.8 collective-permute-start.5
  21.0 0.0 copy-done.1
  21.0 0.0 copy-done.2
  21.1 4.1 %collective-permute-done.1 = bf16[544,256]{1,0:T(8,128)(2,1)S(1)} collective-permute-done((bf16[544,256]{1,0:T(8,128)(2,1)S(1)}, bf16[544,256]{1,0:T(8,128)(2,1)S(1)}, u32[]{:S(2)}, u32[]{:S(2)}) %collective-permute-start.1) | collective-permute-done | bytes 278560 | tf_op jit(solution)/shard_map/ppermute | solution.py:690
  25.2 0.1 add_convert_fusion.proj_ref
  25.3 2.7 %collective-permute-start.2 = (bf16[544,256]{1,0:T(8,128)(2,1)S(1)}, bf16[544,256]{1,0:T(8,128)(2,1)S(1)}, u32[]{:S(2)}, u32[]{:S(2)}) collective-permute-start(bf16[544,256]{1,0:T(8,128)(2,1)S(1)} %add_convert_fusion.proj_ref), channel_id=1, source_target_pairs={{0,2},{1,3},{2,0},{3,1},{4,6},{5,7},{6,4},{7,5},{8,10},{9,11},{10,... | collective-permute-start | bytes 835592 | tf_op jit(solution)/shard_map/ppermute | solution.py:690
  27.9 0.0 collective-permute-done.5.keys_theirs.values_theirs
  27.9 5.5 %attend.1 = bf16[256,2048]{1,0:T(8,128)(2,1)} custom-call(s32[4]{0:T(128)} %lengths_ref.5, s32[8,256]{1,0:T(8,128)S(1)} %reshape.19.place_ref, bf16[256,2048]{1,0:T(8,128)(2,1)S(1)} %copy-done, bf16[3,256,512]{2,1,0:T(8,128)(2,1)S(1)} %pad_maximum_fusion.keys_mine.values_mine, bf16[3,256,512]{2,1,0:T(8,128)(2,1)S(1)} %collective-permute-done.5.keys_theirs.values_theirs, ...), custom_call_target="tpu_custom_call" | custom-call | flops 524288 | bytes 524288 | tf_op jit(solution)/shard_map/attend/pallas_call | solution.py:609
  33.4 5.7 %collective-permute-done.2.other_ref = bf16[544,256]{1,0:T(8,128)(2,1)S(1)} collective-permute-done((bf16[544,256]{1,0:T(8,128)(2,1)S(1)}, bf16[544,256]{1,0:T(8,128)(2,1)S(1)}, u32[]{:S(2)}, u32[]{:S(2)}) %collective-permute-start.2) | collective-permute-done | bytes 278560 | tf_op jit(solution)/shard_map/ppermute | solution.py:690
  39.0 4.2 %all-to-all-start = ((bf16[8,32,2048]{2,1,0:T(8,128)(2,1)}), bf16[8,32,2048]{2,1,0:T(8,128)(2,1)S(1)}, u32[]{:S(2)}, u32[]{:S(2)}) async-start(bf16[8,32,2048]{2,1,0:T(8,128)(2,1)} %bitcast.7), calls=%async_computation | async-start | bytes 2097152 | tf_op jit(solution)/shard_map/all_to_all | solution.py:693
  43.3 14.1 %local_scan.1 = (f32[256,16,128]{2,1,0:T(8,128)}, f32[256,16,128]{2,1,0:T(8,128)}, bf16[288,128]{1,0:T(8,128)(2,1)S(1)}) custom-call(s32[4]{0:T(128)} %lengths_ref.5, bf16[544,256]{1,0:T(8,128)(2,1)S(1)} %add_convert_fusion.proj_ref, bf16[544,256]{1,0:T(8,128)(2,1)S(1)} %collective-permute-done.2.other_ref, bf16[512,2048]{1,0:T(8,128)(2,1)} %dtw_ref.1, ...), custom_call_target="tpu_custom_call" | custom-call | flops 100663296 | bytes 6291456 | tf_op jit(solution)/shard_map/local_scan/pallas_call | solution.py:318
  57.4 3.9 %collective-permute-start.7 = (bf16[288,128]{1,0:T(8,128)(2,1)S(1)}, bf16[288,128]{1,0:T(8,128)(2,1)S(1)}, u32[]{:S(2)}, u32[]{:S(2)}) collective-permute-start(bf16[288,128]{1,0:T(8,128)(2,1)S(1)} %get-tuple-element.31), channel_id=1, source_target_pairs={{0,16},{4,20},{8,24},{12,28},{1,17},{5,21},{9,25},{13,29},{2,18},{... | collective-permute-start | bytes 221192 | tf_op jit(solution)/shard_map/ppermute | solution.py:637
  61.3 3.4 %collective-permute-start.6 = (bf16[288,128]{1,0:T(8,128)(2,1)S(1)}, bf16[288,128]{1,0:T(8,128)(2,1)S(1)}, u32[]{:S(2)}, u32[]{:S(2)}) collective-permute-start(bf16[288,128]{1,0:T(8,128)(2,1)S(1)} %get-tuple-element.31), channel_id=1, source_target_pairs={{0,8},{4,12},{8,16},{12,20},{16,24},{20,28},{1,9},{5,13},{9,17},{1... | collective-permute-start | bytes 221192 | tf_op jit(solution)/shard_map/ppermute | solution.py:637
  64.7 0.0 collective-permute-done.7
  64.7 2.0 %collective-permute-done.6 = bf16[288,128]{1,0:T(8,128)(2,1)S(1)} collective-permute-done((bf16[288,128]{1,0:T(8,128)(2,1)S(1)}, bf16[288,128]{1,0:T(8,128)(2,1)S(1)}, u32[]{:S(2)}, u32[]{:S(2)}) %collective-permute-start.6) | collective-permute-done | bytes 73760 | tf_op jit(solution)/shard_map/ppermute | solution.py:637
  66.7 0.1 collective-permute-start.8
  66.8 1.5 %collective-permute-done.8.theirs_ref = bf16[3,288,128]{2,1,0:T(8,128)(2,1)S(1)} collective-permute-done((bf16[3,288,128]{2,1,0:T(8,128)(2,1)S(1)}, bf16[3,288,128]{2,1,0:T(8,128)(2,1)S(1)}, u32[]{:S(2)}, u32[]{:S(2)}) %collective-permute-start.8) | collective-permute-done | bytes 221216 | tf_op jit(solution)/shard_map/ppermute | solution.py:643
  68.2 0.0 all-to-all-done
  68.3 10.4 %join_states.1 = (bf16[256,2048]{1,0:T(8,128)(2,1)}, bf16[256,2048]{1,0:T(8,128)(2,1)}) custom-call(bf16[544,256]{1,0:T(8,128)(2,1)S(1)} %add_convert_fusion.proj_ref, bf16[544,256]{1,0:T(8,128)(2,1)S(1)} %collective-permute-done.2.other_ref, f32[256,16,128]{2,1,0:T(8,128)} %get-tuple-element.28.y_ref, f32[256,16,128]{2,1,0:T(8,128)} %get-tuple-element.29.sum_ref, ...), custom_call_target="tpu_custom_call" | custom-call | flops 67108864 | bytes 7340032 | tf_op jit(solution)/shard_map/join_states/pallas_call | solution.py:439
  (4 shorter events, 0.0 us)
Async XLA Ops:
  1.7 10.2 %collective-permute-start = (bf16[16,2048]{1,0:T(8,128)(2,1)S(1)}, bf16[16,2048]{1,0:T(8,128)(2,1)S(1)}, u32[]{:S(2)}, u32[]{:S(2)}) collective-permute-start(bf16[16,2048]{1,0:T(8,128)(2,1)S(1)} %get-tuple-element.17), channel_id=1, source_target_pairs={{0,4},{4,8},{8,12},{12,16},{16,20},{20,24},{24,28},{1,5},{5,9},{9,... | collective-permute-start | bytes 196616 | tf_op jit(solution)/shard_map/ppermute | solution.py:637
  4.0 16.2 %collective-permute-start.4 = (bf16[256,512]{1,0:T(8,128)(2,1)S(1)}, bf16[256,512]{1,0:T(8,128)(2,1)S(1)}, u32[]{:S(2)}, u32[]{:S(2)}) collective-permute-start(bf16[256,512]{1,0:T(8,128)(2,1)S(1)} %get-tuple-element.22), channel_id=1, source_target_pairs={{0,16},{4,20},{8,24},{12,28},{1,17},{5,21},{9,25},{13,29},{2,18},{... | collective-permute-start | bytes 786440 | tf_op jit(solution)/shard_map/ppermute | solution.py:637
  8.5 11.7 %collective-permute-start.3 = (bf16[256,512]{1,0:T(8,128)(2,1)S(1)}, bf16[256,512]{1,0:T(8,128)(2,1)S(1)}, u32[]{:S(2)}, u32[]{:S(2)}) collective-permute-start(bf16[256,512]{1,0:T(8,128)(2,1)S(1)} %get-tuple-element.22), channel_id=1, source_target_pairs={{0,8},{4,12},{8,16},{12,20},{16,24},{20,28},{1,9},{5,13},{9,17},{1... | collective-permute-start | bytes 786440 | tf_op jit(solution)/shard_map/ppermute | solution.py:637
  11.9 9.1 %copy-start.2 = (s32[2048]{0:T(1024)S(1)}, s32[2048]{0:T(1024)}, u32[]{:S(2)}) copy-start(s32[2048]{0:T(1024)} %param.27) | copy-start | bytes 24580
  17.3 3.7 %copy-start.1 = (bf16[256,2048]{1,0:T(8,128)(2,1)}, bf16[256,2048]{1,0:T(8,128)(2,1)S(1)}, u32[]{:S(2)}) copy-start(bf16[256,2048]{1,0:T(8,128)(2,1)S(1)} %get-tuple-element.27.inner_ref) | copy-start | bytes 3145732
  17.3 10.6 %copy-start = (bf16[256,2048]{1,0:T(8,128)(2,1)S(1)}, bf16[256,2048]{1,0:T(8,128)(2,1)}, u32[]{:S(2)}) copy-start(bf16[256,2048]{1,0:T(8,128)(2,1)} %q_ref.1) | copy-start | bytes 3145732
  17.3 7.8 %collective-permute-start.1 = (bf16[544,256]{1,0:T(8,128)(2,1)S(1)}, bf16[544,256]{1,0:T(8,128)(2,1)S(1)}, u32[]{:S(2)}, u32[]{:S(2)}) collective-permute-start(bf16[544,256]{1,0:T(8,128)(2,1)S(1)} %get-tuple-element.18), channel_id=1, source_target_pairs={{0,1},{1,0},{2,3},{3,2},{4,5},{5,4},{6,7},{7,6},{8,9},{9,8},{10,11... | collective-permute-start | bytes 835592 | tf_op jit(solution)/shard_map/ppermute | solution.py:690
  20.3 7.6 %collective-permute-start.5 = (bf16[3,256,512]{2,1,0:T(8,128)(2,1)S(1)}, bf16[3,256,512]{2,1,0:T(8,128)(2,1)S(1)}, u32[]{:S(2)}, u32[]{:S(2)}) collective-permute-start(bf16[3,256,512]{2,1,0:T(8,128)(2,1)S(1)} %pad_maximum_fusion.keys_mine.values_mine), channel_id=1, source_target_pairs={{0,4},{4,0},{8,12},{12,8},{16,20},{20,16},{24,28},{28,24},{1,5},{5... | collective-permute-start | bytes 2359304 | tf_op jit(solution)/shard_map/ppermute | solution.py:643
  25.3 13.8 %collective-permute-start.2 = (bf16[544,256]{1,0:T(8,128)(2,1)S(1)}, bf16[544,256]{1,0:T(8,128)(2,1)S(1)}, u32[]{:S(2)}, u32[]{:S(2)}) collective-permute-start(bf16[544,256]{1,0:T(8,128)(2,1)S(1)} %add_convert_fusion.proj_ref), channel_id=1, source_target_pairs={{0,2},{1,3},{2,0},{3,1},{4,6},{5,7},{6,4},{7,5},{8,10},{9,11},{10,... | collective-permute-start | bytes 835592 | tf_op jit(solution)/shard_map/ppermute | solution.py:690
  39.0 29.2 %all-to-all-start = ((bf16[8,32,2048]{2,1,0:T(8,128)(2,1)}), bf16[8,32,2048]{2,1,0:T(8,128)(2,1)S(1)}, u32[]{:S(2)}, u32[]{:S(2)}) async-start(bf16[8,32,2048]{2,1,0:T(8,128)(2,1)} %bitcast.7), calls=%async_computation | async-start | bytes 2097152 | tf_op jit(solution)/shard_map/all_to_all | solution.py:693
  57.4 7.3 %collective-permute-start.7 = (bf16[288,128]{1,0:T(8,128)(2,1)S(1)}, bf16[288,128]{1,0:T(8,128)(2,1)S(1)}, u32[]{:S(2)}, u32[]{:S(2)}) collective-permute-start(bf16[288,128]{1,0:T(8,128)(2,1)S(1)} %get-tuple-element.31), channel_id=1, source_target_pairs={{0,16},{4,20},{8,24},{12,28},{1,17},{5,21},{9,25},{13,29},{2,18},{... | collective-permute-start | bytes 221192 | tf_op jit(solution)/shard_map/ppermute | solution.py:637
  61.3 5.3 %collective-permute-start.6 = (bf16[288,128]{1,0:T(8,128)(2,1)S(1)}, bf16[288,128]{1,0:T(8,128)(2,1)S(1)}, u32[]{:S(2)}, u32[]{:S(2)}) collective-permute-start(bf16[288,128]{1,0:T(8,128)(2,1)S(1)} %get-tuple-element.31), channel_id=1, source_target_pairs={{0,8},{4,12},{8,16},{12,20},{16,24},{20,28},{1,9},{5,13},{9,17},{1... | collective-permute-start | bytes 221192 | tf_op jit(solution)/shard_map/ppermute | solution.py:637
  66.7 1.5 %collective-permute-start.8 = (bf16[3,288,128]{2,1,0:T(8,128)(2,1)S(1)}, bf16[3,288,128]{2,1,0:T(8,128)(2,1)S(1)}, u32[]{:S(2)}, u32[]{:S(2)}) collective-permute-start(bf16[3,288,128]{2,1,0:T(8,128)(2,1)S(1)} %pad_maximum_fusion.1.mine_ref), channel_id=1, source_target_pairs={{0,4},{4,0},{8,12},{12,8},{16,20},{20,16},{24,28},{28,24},{1,5},{5... | collective-permute-start | bytes 663560 | tf_op jit(solution)/shard_map/ppermute | solution.py:643
